TPU v7x, 32 devices: a whole 2x2x4 slice. The times are simulated.
32 devices in a mesh: dp: 8 (over y, x, core), tensor: 4 (over z).
Axes of the slice: x: 2, y: 2, z: 4, core: 2. Of those that a mesh axis runs over, the one named last changes fastest.
Arguments:
- block_input: bfloat16 [2048, 4, 1536], P(('dp', 'tensor')), may hold values from -6 to 6
- out_grad: bfloat16 [2048, 4, 1536], P(('dp', 'tensor')), may hold values from -6 to 6
- lengths: int32 [4], replicated, may hold values from 512 to 2048, as said below
- routes: int32 [2048, 4, 6], P('dp'), may hold values from 0 to 15, all different within a row; in each aligned block of 1024 rows (0 to 1023, 1024 to 2047, ..., all dimensions but the last counted through in order) at most 512 rows name the same one
- norm1_gain: bfloat16 [1536], P('dp'), may hold values from 0.25 to 1.75
- w_zx: bfloat16 [1536, 2, 3072], P('dp', None, 'tensor'), may hold values from -0.15625 to 0.15625
- w_bc: bfloat16 [1536, 256], P('dp'), may hold values from -0.15625 to 0.15625
- w_dt: bfloat16 [1536, 48], P('dp', 'tensor'), may hold values from -0.15625 to 0.15625
- conv_x: float32 [5, 3072], P(None, 'tensor'), may hold values from -3 to 3
- conv_bc: float32 [5, 256], replicated, may hold values from -3 to 3
- head_params: float32 [3, 48], P(None, 'tensor'), may hold values from -11 to 2
- gate_gain: float32 [3072], P('tensor'), may hold values from 0.25 to 1.75
- w_out: bfloat16 [3072, 1536], P('tensor', 'dp'), may hold values from -0.109375 to 0.109375
- norm2_gain: bfloat16 [1536], P('dp'), may hold values from 0.25 to 1.75
- w_router: bfloat16 [1536, 16], P('dp'), may hold values from -0.078125 to 0.078125
- w_gu: bfloat16 [16, 1536, 2, 512], P(None, 'dp', None, 'tensor'), may hold values from -0.15625 to 0.15625
- w_dn: bfloat16 [16, 512, 1536], P(None, 'tensor', 'dp'), may hold values from -0.5 to 0.5
- s_gu: bfloat16 [1536, 2, 1024], P('dp', None, 'tensor'), may hold values from -0.15625 to 0.15625
- s_dn: bfloat16 [1024, 1536], P('tensor', 'dp'), may hold values from -0.1875 to 0.1875
Outputs:
- output: bfloat16 [2048, 4, 1536], P(('dp', 'tensor'))
- input_grad: bfloat16 [2048, 4, 1536], P(('dp', 'tensor'))
- norm1_gain_grad: float32 [1536], P(('dp', 'tensor'))
- w_zx_grad: float32 [1536, 2, 3072], P('dp', None, 'tensor')
- w_bc_grad: float32 [1536, 256], P(('dp', 'tensor'))
- w_dt_grad: float32 [1536, 48], P('dp', 'tensor')
- conv_x_grad: float32 [5, 3072], P(None, ('dp', 'tensor'))
- conv_bc_grad: float32 [5, 256], P(None, ('dp', 'tensor'))
- head_params_grad: float32 [3, 48], replicated
- gate_gain_grad: float32 [3072], P(('dp', 'tensor'))
- w_out_grad: float32 [3072, 1536], P('tensor', 'dp')
- norm2_gain_grad: float32 [1536], P(('dp', 'tensor'))
- w_router_grad: float32 [1536, 16], P(('dp', 'tensor'))
- w_gu_grad: float32 [16, 1536, 2, 512], P(None, 'dp', None, 'tensor')
- w_dn_grad: float32 [16, 512, 1536], P(None, 'tensor', 'dp')
- s_gu_grad: float32 [1536, 2, 1024], P('dp', None, 'tensor')
- s_dn_grad: float32 [1024, 1536], P('tensor', 'dp')
- stats: float32 [3], replicated
Inputs may be any that keep to these rules, and one draw needn't show every extreme that they name: `lengths`: each slot has between a quarter of 2048 and 2048 valid positions; one slot is full. `routes`: within the rows of one index of dp (aligned blocks of 1024 rows, positions before slots) no expert is named by more than 512 rows, and some expert reaches that.
All inputs are finite; a program needn't handle non-finite values.
Results may differ from a plain program's by a relative error of at most 0.015.
Values may be sent and summed in bfloat16 or wider, within the bound.
No kernel may reach another device: no remote copies, remote signals or barrier semaphores. Data moves between devices by JAX's collectives and lax.ppermute only.
A program may use at most 448 MiB of HBM per device.

v0:
```python
import jax
import jax.numpy as jnp
from jax import lax
from jax.sharding import PartitionSpec as P

D_MODEL = 1536
HEAD_COUNT = 48
HEAD_DIM = 64
STATE_DIM = 128
CONV_WIDTH = 4
TOP_K = 6
EXPERTS = 16
SLOT_COUNT = 4
INNER_DIM = 3072
CAPACITY = 512


norm_eps = 1e-05
highest = lax.Precision.HIGHEST


def passed_along(value, axis, steps):
    count = lax.axis_size(axis)
    first, last = (max(0, -steps), min(count, count - steps))
    return lax.ppermute(value, axis, [(source, source + steps) for source in range(first, last)])


def rms_scale(values, gain_vec):
    return (
        values * lax.rsqrt(jnp.mean(values * values, axis=-1, keepdims=True) + norm_eps) * gain_vec
    )


def silu_slope(values):
    logistic = jax.nn.sigmoid(values)
    return logistic * (1.0 + values * (1.0 - logistic))


def swiglu_back(hidden, act_grad):
    gate_part = hidden[..., 0, :]
    up_part = hidden[..., 1, :]
    return jnp.stack(
        [act_grad * up_part * silu_slope(gate_part), act_grad * jax.nn.silu(gate_part)], axis=-2
    )


def split_parts(values):
    upper = values.astype(jnp.bfloat16)
    lower = (values - upper.astype(jnp.float32)).astype(jnp.bfloat16)
    return (upper, lower)


def conv_pre_act(padded, conv_weights, length):
    tap_count = conv_weights.shape[0] - 1
    summed = conv_weights[tap_count] + conv_weights[0] * padded[0:length]
    for offset in range(1, tap_count):
        summed = summed + conv_weights[offset] * padded[offset : offset + length]
    return summed


def piece_terms(x_heads, step_size, decay_rate, write_vec, read_vec):
    log_sum = jnp.cumsum(-step_size * decay_rate, axis=0)
    extent = x_heads.shape[0]
    causal_mask = jnp.arange(extent)[:, None] >= jnp.arange(extent)[None, :]
    gap_log = log_sum[:, None] - log_sum[None, :]
    decays = jnp.exp(jnp.where(causal_mask[:, :, None, None], gap_log, -jnp.inf))
    scores = jnp.einsum("tsn,jsn->tjs", read_vec, write_vec, precision=highest)
    mixing = decays * scores[..., None] * step_size[None]
    y_inner = jnp.einsum("tjsh,jshp->tshp", mixing, x_heads, precision=highest)
    tail_decay = jnp.exp(log_sum[-1][None] - log_sum) * step_size
    s_local = jnp.einsum("jsh,jshp,jsn->shpn", tail_decay, x_heads, write_vec, precision=highest)
    return (y_inner, s_local, log_sum)


def state_terms(log_sum, read_vec, entering):
    y_state = jnp.einsum(
        "tsh,tsn,shpn->tshp", jnp.exp(log_sum), read_vec, entering, precision=highest
    )
    leaving = jnp.exp(log_sum[-1])[..., None, None] * entering
    return (y_state, leaving)


def local_ssm(x_heads, write_vec, read_vec, raw_step, log_rate, step_bias, entering):
    step_size = jax.nn.softplus(raw_step + step_bias)
    y_inner, s_local, log_sum = piece_terms(
        x_heads, step_size, jnp.exp(log_rate), write_vec, read_vec
    )
    y_state, leaving = state_terms(log_sum, read_vec, entering)
    return (y_inner + y_state, leaving + s_local)


def gather_piece(values):
    return lax.all_gather(values, "tensor", axis=0, tiled=True)


def sum_piece(values):
    return lax.psum_scatter(values, "tensor", scatter_dimension=0, tiled=True)


def norm_total(values):
    return lax.psum(values, "tensor")


def body(
    block_input,
    out_grad,
    lengths,
    routes,
    norm1_gain,
    w_zx,
    w_bc,
    w_dt,
    conv_x,
    conv_bc,
    head_params,
    gate_gain,
    w_out,
    norm2_gain,
    w_router,
    w_gu,
    w_dn,
    s_gu,
    s_dn,
):
    tensor_size = lax.axis_size("tensor")
    tensor_index = lax.axis_index("tensor")
    wide_index = lax.axis_index("dp")
    local_rows = block_input.shape[0]
    piece_rows = local_rows * tensor_size
    heads_local = HEAD_COUNT // tensor_size
    inner_local = INNER_DIM // tensor_size
    token_rows = piece_rows * SLOT_COUNT
    rim_width = CONV_WIDTH - 1
    positions = (
        wide_index * piece_rows
        + tensor_index * local_rows
        + jnp.arange(local_rows, dtype=jnp.int32)
    )
    valid = (positions[:, None] < lengths[None, :]).astype(jnp.float32)[:, :, None]
    fetched = (
        lax.all_gather(norm1_gain, "dp", axis=0, tiled=True),
        lax.all_gather(w_zx, "dp", axis=0, tiled=True),
        lax.all_gather(w_bc, "dp", axis=0, tiled=True),
        lax.all_gather(w_dt, "dp", axis=0, tiled=True),
        lax.all_gather(w_out, "dp", axis=1, tiled=True),
        lax.all_gather(norm2_gain, "dp", axis=0, tiled=True),
        lax.all_gather(w_router, "dp", axis=0, tiled=True),
        lax.all_gather(w_gu, "dp", axis=1, tiled=True),
        lax.all_gather(w_dn, "dp", axis=2, tiled=True),
        lax.all_gather(s_gu, "dp", axis=0, tiled=True),
        lax.all_gather(s_dn, "dp", axis=1, tiled=True),
    )
    gain_one = fetched[0].astype(jnp.float32)
    full_zx = fetched[1]
    full_bc = fetched[2]
    full_dt = fetched[3]
    full_out = fetched[4]
    gain_two = fetched[5].astype(jnp.float32)
    full_router = fetched[6]
    full_gu = fetched[7]
    full_dn = fetched[8]
    full_sgu = fetched[9]
    full_sdn = fetched[10]
    u_float = block_input.astype(jnp.float32)
    normed_one, norm_one_back = jax.vjp(rms_scale, u_float, gain_one)
    n_one = gather_piece(normed_one.astype(jnp.bfloat16))
    zx_raw = jnp.einsum("tsd,dcf->tscf", n_one, full_zx, preferred_element_type=jnp.float32)
    bc_raw = jnp.einsum("tsd,dn->tsn", n_one, full_bc, preferred_element_type=jnp.float32)
    dt_raw = jnp.einsum("tsd,dh->tsh", n_one, full_dt, preferred_element_type=jnp.float32)
    conv_in = jnp.concatenate([zx_raw[:, :, 1], bc_raw], axis=2)
    prior_rows = passed_along(conv_in[piece_rows - rim_width :], "dp", 1)
    padded = jnp.concatenate([prior_rows, conv_in], axis=0)
    conv_weights = jnp.concatenate([conv_x, conv_bc], axis=1)
    conv_pre = conv_pre_act(padded, conv_weights, piece_rows)
    conv_out = jax.nn.silu(conv_pre)
    x_heads = conv_out[:, :, :inner_local].reshape(piece_rows, SLOT_COUNT, heads_local, HEAD_DIM)
    write_vec = conv_out[:, :, inner_local : inner_local + STATE_DIM]
    read_vec = conv_out[:, :, inner_local + STATE_DIM :]
    step_size = jax.nn.softplus(dt_raw + head_params[1])
    y_inner, s_local, log_sum = piece_terms(
        x_heads, step_size, jnp.exp(head_params[0]), write_vec, read_vec
    )
    piece_decay = jnp.exp(log_sum[-1])

    def pass_forward(turn_index, entering):
        return passed_along(piece_decay[:, :, None, None] * entering + s_local, "dp", 1)

    h_in = lax.fori_loop(0, lax.axis_size("dp") - 1, pass_forward, jnp.zeros_like(s_local))
    y_state, unused_state = state_terms(log_sum, read_vec, h_in)
    y_heads = y_inner + y_state + head_params[2][:, None] * x_heads
    y_flat = y_heads.reshape(piece_rows, SLOT_COUNT, inner_local)
    gate_act = jax.nn.silu(zx_raw[:, :, 0])
    gated = y_flat * gate_act
    square_sum = norm_total(jnp.sum(gated * gated, axis=-1))
    inv_rms = lax.rsqrt(square_sum / INNER_DIM + norm_eps)[:, :, None]
    n_y = (gated * inv_rms * gate_gain).astype(jnp.bfloat16)
    mixed = sum_piece(jnp.einsum("tsf,fd->tsd", n_y, full_out, preferred_element_type=jnp.float32))
    resid = u_float + mixed
    normed_two, norm_two_back = jax.vjp(rms_scale, resid, gain_two)
    n_two = gather_piece(normed_two.astype(jnp.bfloat16))
    flat_in = n_two.reshape(token_rows, D_MODEL)
    route_flat = routes.reshape(token_rows, TOP_K)
    logits = jnp.dot(flat_in, full_router, preferred_element_type=jnp.float32)
    route_hot = (
        route_flat[:, :, None] == jnp.arange(EXPERTS, dtype=jnp.int32)[None, None, :]
    ).astype(jnp.float32)
    gates = jax.nn.softmax(jnp.sum(route_hot * logits[:, None, :], axis=-1), axis=-1)
    hot_int = route_hot.reshape(token_rows * TOP_K, EXPERTS).astype(jnp.int32)
    slot_pos = jnp.sum((jnp.cumsum(hot_int, axis=0) - hot_int) * hot_int, axis=1)
    slot_ids = route_flat.reshape(-1) * CAPACITY + slot_pos
    slot_assign = (
        jnp.full((EXPERTS * CAPACITY,), token_rows * TOP_K, jnp.int32)
        .at[slot_ids]
        .set(jnp.arange(token_rows * TOP_K, dtype=jnp.int32))
    )
    slot_token = slot_assign // TOP_K
    in_padded = jnp.concatenate([flat_in, jnp.zeros((1, D_MODEL), jnp.bfloat16)], axis=0)
    expert_in = jnp.take(in_padded, slot_token, axis=0).reshape(EXPERTS, CAPACITY, D_MODEL)
    hidden = jnp.einsum("ecd,edgf->ecgf", expert_in, full_gu, preferred_element_type=jnp.float32)
    expert_act = (jax.nn.silu(hidden[:, :, 0]) * hidden[:, :, 1]).astype(jnp.bfloat16)
    produced = jnp.einsum(
        "ecf,efd->ecd", expert_act, full_dn, preferred_element_type=jnp.float32
    ).reshape(EXPERTS * CAPACITY, D_MODEL)
    per_route = jnp.take(produced, slot_ids, axis=0).reshape(token_rows, TOP_K, D_MODEL)
    shared_hidden = jnp.einsum("rd,dgf->rgf", flat_in, full_sgu, preferred_element_type=jnp.float32)
    shared_act = (jax.nn.silu(shared_hidden[:, 0]) * shared_hidden[:, 1]).astype(jnp.bfloat16)
    moe_rows = jnp.sum(gates[:, :, None] * per_route, axis=1) + jnp.dot(
        shared_act, full_sdn, preferred_element_type=jnp.float32
    )
    moe = sum_piece(moe_rows.reshape(piece_rows, SLOT_COUNT, D_MODEL))
    output = resid + moe
    stat_terms = jnp.stack(
        [
            jnp.sum(valid * output * output),
            jnp.sum(valid * mixed * mixed),
            jnp.sum(valid * moe * moe),
        ]
    )
    fetched_again = (
        lax.all_gather(w_zx, "dp", axis=0, tiled=True),
        lax.all_gather(w_bc, "dp", axis=0, tiled=True),
        lax.all_gather(w_dt, "dp", axis=0, tiled=True),
        lax.all_gather(w_out, "dp", axis=1, tiled=True),
        lax.all_gather(w_router, "dp", axis=0, tiled=True),
        lax.all_gather(w_gu, "dp", axis=1, tiled=True),
        lax.all_gather(w_dn, "dp", axis=2, tiled=True),
        lax.all_gather(s_gu, "dp", axis=0, tiled=True),
        lax.all_gather(s_dn, "dp", axis=1, tiled=True),
    )
    full_zx = fetched_again[0]
    full_bc = fetched_again[1]
    full_dt = fetched_again[2]
    full_out = fetched_again[3]
    full_router = fetched_again[4]
    full_gu = fetched_again[5]
    full_dn = fetched_again[6]
    full_sgu = fetched_again[7]
    full_sdn = fetched_again[8]
    grad_out = out_grad.astype(jnp.float32) * valid
    moe_back = gather_piece(grad_out.astype(jnp.bfloat16)).reshape(token_rows, D_MODEL)
    shared_act_grad = jnp.einsum(
        "rd,fd->rf", moe_back, full_sdn, preferred_element_type=jnp.float32
    )
    s_dn_grad = jnp.einsum("rf,rd->fd", shared_act, moe_back, preferred_element_type=jnp.float32)
    shared_hidden_grad = swiglu_back(shared_hidden, shared_act_grad).astype(jnp.bfloat16)
    s_gu_grad = jnp.einsum(
        "rd,rgf->dgf", flat_in, shared_hidden_grad, preferred_element_type=jnp.float32
    )
    in_grad = jnp.einsum(
        "rgf,dgf->rd", shared_hidden_grad, full_sgu, preferred_element_type=jnp.float32
    )
    back_padded = jnp.concatenate([moe_back, jnp.zeros((1, D_MODEL), jnp.bfloat16)], axis=0)
    gate_padded = jnp.concatenate([gates.reshape(-1), jnp.zeros((1,), jnp.float32)])
    slot_gate = jnp.take(gate_padded, slot_assign)
    produced_grad = (
        (slot_gate[:, None] * jnp.take(back_padded, slot_token, axis=0).astype(jnp.float32))
        .astype(jnp.bfloat16)
        .reshape(EXPERTS, CAPACITY, D_MODEL)
    )
    w_dn_grad = jnp.einsum(
        "ecf,ecd->efd", expert_act, produced_grad, preferred_element_type=jnp.float32
    )
    act_grad = jnp.einsum(
        "ecd,efd->ecf", produced_grad, full_dn, preferred_element_type=jnp.float32
    )
    hidden_grad = swiglu_back(hidden, act_grad).astype(jnp.bfloat16)
    w_gu_grad = jnp.einsum(
        "ecd,ecgf->edgf", expert_in, hidden_grad, preferred_element_type=jnp.float32
    )
    expert_back = jnp.einsum(
        "ecgf,edgf->ecd", hidden_grad, full_gu, preferred_element_type=jnp.float32
    ).reshape(EXPERTS * CAPACITY, D_MODEL)
    in_grad = in_grad + jnp.sum(
        jnp.take(expert_back, slot_ids, axis=0).reshape(token_rows, TOP_K, D_MODEL), axis=1
    )
    gate_grad = jnp.sum(per_route * moe_back.astype(jnp.float32)[:, None, :], axis=-1)
    picked_grad = gates * (gate_grad - jnp.sum(gates * gate_grad, axis=-1, keepdims=True))
    logit_grad = jnp.sum(route_hot * picked_grad[:, :, None], axis=1)
    logit_upper, logit_lower = split_parts(logit_grad)
    router_grad = jnp.einsum(
        "rd,re->de", flat_in, logit_upper, preferred_element_type=jnp.float32
    ) + jnp.einsum("rd,re->de", flat_in, logit_lower, preferred_element_type=jnp.float32)
    in_grad = (
        in_grad
        + jnp.einsum("re,de->rd", logit_upper, full_router, preferred_element_type=jnp.float32)
        + jnp.einsum("re,de->rd", logit_lower, full_router, preferred_element_type=jnp.float32)
    )
    resid_from, gain_two_grad = norm_two_back(
        sum_piece(in_grad.reshape(piece_rows, SLOT_COUNT, D_MODEL))
    )
    resid_grad = grad_out + resid_from
    mix_back = gather_piece(resid_grad.astype(jnp.bfloat16))
    w_out_grad = jnp.einsum("tsf,tsd->fd", n_y, mix_back, preferred_element_type=jnp.float32)
    n_y_grad = jnp.einsum("tsd,fd->tsf", mix_back, full_out, preferred_element_type=jnp.float32)
    gate_gain_grad = jnp.sum(n_y_grad * gated * inv_rms, axis=(0, 1))
    scaled_grad = n_y_grad * gate_gain
    cross_sum = norm_total(jnp.sum(scaled_grad * gated, axis=-1))[:, :, None]
    gated_grad = (
        scaled_grad * inv_rms - gated * (inv_rms * inv_rms * inv_rms) * cross_sum / INNER_DIM
    )
    y_grad = (gated_grad * gate_act).reshape(piece_rows, SLOT_COUNT, heads_local, HEAD_DIM)
    z_grad = gated_grad * y_flat * silu_slope(zx_raw[:, :, 0])
    skip_grad = jnp.sum(y_grad * x_heads, axis=(0, 1, 3))
    local_grad = jnp.einsum(
        "tsh,tshp,tsn->shpn", jnp.exp(log_sum), y_grad, read_vec, precision=highest
    )

    def pass_backward(turn_index, later):
        return passed_along(piece_decay[:, :, None, None] * later + local_grad, "dp", -1)

    h_out_grad = lax.fori_loop(
        0, lax.axis_size("dp") - 1, pass_backward, jnp.zeros_like(local_grad)
    )
    unused_out, ssm_back = jax.vjp(
        local_ssm, x_heads, write_vec, read_vec, dt_raw, head_params[0], head_params[1], h_in
    )
    x_grad, write_grad, read_grad, dt_raw_grad, log_rate_grad, bias_grad, unused_grad = ssm_back(
        (y_grad, h_out_grad)
    )
    x_grad = x_grad + y_grad * head_params[2][:, None]
    conv_out_grad = jnp.concatenate(
        [x_grad.reshape(piece_rows, SLOT_COUNT, inner_local), write_grad, read_grad], axis=2
    )
    pre_grad = conv_out_grad * silu_slope(conv_pre)
    padded_grad = jnp.pad(conv_weights[0] * pre_grad, ((0, rim_width), (0, 0), (0, 0)))
    for offset in range(1, CONV_WIDTH):
        padded_grad = padded_grad + jnp.pad(
            conv_weights[offset] * pre_grad, ((offset, rim_width - offset), (0, 0), (0, 0))
        )
    next_rows = passed_along(padded_grad[:rim_width].astype(jnp.bfloat16), "dp", -1).astype(
        jnp.float32
    )
    conv_in_grad = padded_grad[rim_width:] + jnp.pad(
        next_rows, ((piece_rows - rim_width, 0), (0, 0), (0, 0))
    )
    tap_grads = [
        jnp.sum(pre_grad * padded[offset : offset + piece_rows], axis=(0, 1))
        for offset in range(CONV_WIDTH)
    ]
    conv_grad = jnp.stack(tap_grads + [jnp.sum(pre_grad, axis=(0, 1))])
    zx_grad = jnp.stack([z_grad, conv_in_grad[:, :, :inner_local]], axis=2).astype(jnp.bfloat16)
    bc_grad = conv_in_grad[:, :, inner_local:]
    bc_upper, bc_lower = split_parts(bc_grad)
    dt_grad = dt_raw_grad.astype(jnp.bfloat16)
    w_zx_grad = jnp.einsum("tsd,tscf->dcf", n_one, zx_grad, preferred_element_type=jnp.float32)
    w_dt_grad = jnp.einsum("tsd,tsh->dh", n_one, dt_grad, preferred_element_type=jnp.float32)
    w_bc_grad = jnp.einsum(
        "tsd,tsn->dn", n_one, bc_upper, preferred_element_type=jnp.float32
    ) + jnp.einsum("tsd,tsn->dn", n_one, bc_lower, preferred_element_type=jnp.float32)
    n_one_grad = jnp.einsum("tscf,dcf->tsd", zx_grad, full_zx, preferred_element_type=jnp.float32)
    n_one_grad = n_one_grad + jnp.einsum(
        "tsh,dh->tsd", dt_grad, full_dt, preferred_element_type=jnp.float32
    )
    n_one_grad = n_one_grad + jnp.einsum(
        "tsn,dn->tsd", bc_upper, full_bc, preferred_element_type=jnp.float32
    )
    n_one_grad = n_one_grad + jnp.einsum(
        "tsn,dn->tsd", bc_lower, full_bc, preferred_element_type=jnp.float32
    )
    u_from, gain_one_grad = norm_one_back(sum_piece(n_one_grad))
    input_grad = (resid_grad + u_from).astype(jnp.bfloat16)
    column = tensor_index * inner_local
    conv_x_full = lax.dynamic_update_slice(
        jnp.zeros((CONV_WIDTH + 1, INNER_DIM), jnp.float32),
        conv_grad[:, :inner_local],
        (jnp.int32(0), column),
    )
    conv_bc_grad = conv_grad[:, inner_local:]
    gate_full = lax.dynamic_update_slice(
        jnp.zeros((INNER_DIM,), jnp.float32), gate_gain_grad, (column,)
    )
    head_local = jnp.stack([log_rate_grad, bias_grad, skip_grad])
    head_full = lax.dynamic_update_slice(
        jnp.zeros((3, HEAD_COUNT), jnp.float32),
        head_local,
        (jnp.int32(0), tensor_index * heads_local),
    )
    shard_grads = (
        lax.psum_scatter(
            w_zx_grad.astype(jnp.bfloat16), "dp", scatter_dimension=0, tiled=True
        ).astype(jnp.float32),
        lax.psum_scatter(
            w_dt_grad.astype(jnp.bfloat16), "dp", scatter_dimension=0, tiled=True
        ).astype(jnp.float32),
        lax.psum_scatter(
            w_out_grad.astype(jnp.bfloat16), "dp", scatter_dimension=1, tiled=True
        ).astype(jnp.float32),
        lax.psum_scatter(
            w_gu_grad.astype(jnp.bfloat16), "dp", scatter_dimension=1, tiled=True
        ).astype(jnp.float32),
        lax.psum_scatter(
            w_dn_grad.astype(jnp.bfloat16), "dp", scatter_dimension=2, tiled=True
        ).astype(jnp.float32),
        lax.psum_scatter(
            s_gu_grad.astype(jnp.bfloat16), "dp", scatter_dimension=0, tiled=True
        ).astype(jnp.float32),
        lax.psum_scatter(
            s_dn_grad.astype(jnp.bfloat16), "dp", scatter_dimension=1, tiled=True
        ).astype(jnp.float32),
    )
    shared_grads = (
        lax.psum_scatter(gain_one_grad, ("dp", "tensor"), scatter_dimension=0, tiled=True),
        lax.psum_scatter(w_bc_grad, ("dp", "tensor"), scatter_dimension=0, tiled=True),
        lax.psum_scatter(conv_x_full, ("dp", "tensor"), scatter_dimension=1, tiled=True),
        lax.psum_scatter(conv_bc_grad, ("dp", "tensor"), scatter_dimension=1, tiled=True),
        lax.psum_scatter(gate_full, ("dp", "tensor"), scatter_dimension=0, tiled=True),
        lax.psum_scatter(gain_two_grad, ("dp", "tensor"), scatter_dimension=0, tiled=True),
        lax.psum_scatter(router_grad, ("dp", "tensor"), scatter_dimension=0, tiled=True),
    )
    stat_sum, head_sum = lax.psum((stat_terms, head_full), ("dp", "tensor"))
    stats = jnp.sqrt(stat_sum / (jnp.sum(lengths).astype(jnp.float32) * D_MODEL))
    return (
        output.astype(jnp.bfloat16),
        input_grad,
        shared_grads[0],
        shard_grads[0],
        shared_grads[1],
        shard_grads[1],
        shared_grads[2],
        shared_grads[3],
        head_sum,
        shared_grads[4],
        shard_grads[2],
        shared_grads[5],
        shared_grads[6],
        shard_grads[3],
        shard_grads[4],
        shard_grads[5],
        shard_grads[6],
        stats,
    )


def solution(mesh):
    placed = (
        P(("dp", "tensor"), None, None),
        P(("dp", "tensor"), None, None),
        P(),
        P("dp", None, None),
        P("dp"),
        P("dp", None, "tensor"),
        P("dp", None),
        P("dp", "tensor"),
        P(None, "tensor"),
        P(),
        P(None, "tensor"),
        P("tensor"),
        P("tensor", "dp"),
        P("dp"),
        P("dp", None),
        P(None, "dp", None, "tensor"),
        P(None, "tensor", "dp"),
        P("dp", None, "tensor"),
        P("tensor", "dp"),
    )
    return jax.shard_map(
        body,
        mesh=mesh,
        in_specs=placed,
        out_specs=(
            P(("dp", "tensor"), None, None),
            P(("dp", "tensor"), None, None),
            P(("dp", "tensor")),
            P("dp", None, "tensor"),
            P(("dp", "tensor"), None),
            P("dp", "tensor"),
            P(None, ("dp", "tensor")),
            P(None, ("dp", "tensor")),
            P(),
            P(("dp", "tensor")),
            P("tensor", "dp"),
            P(("dp", "tensor")),
            P(("dp", "tensor"), None),
            P(None, "dp", None, "tensor"),
            P(None, "tensor", "dp"),
            P("dp", None, "tensor"),
            P("tensor", "dp"),
            P(),
        ),
        check_vma=False,
    )
```

profile of v0, /device:TPU:0, one launch (start us, length us, event | category | flops | bytes accessed | tf_op | source)
XLA Modules:
  0.0 2361.3 jit_solution(17156280806456751154)
XLA Ops:
  10.9 16.0 all-reduce.16
  34.3 10.5 all_gather.57
  45.4 9.1 all-gather
  55.2 39.7 %all-gather.12.cloned.1.call-done = bf16[256,4,1536]{2,0,1:T(8,128)(2,1)} async-done(((bf16[64,4,1536]{2,0,1:T(8,128)(2,1)}), bf16[256,4,1536]{2,0,1:T(8,128)(2,1)}) %all-gather.12.cloned.1.call-update) | async-done | bytes 3145744 | tf_op jit(solution)/shard_map/all_gather | solution.py:93
  113.0 22.0 all-gather.14.cloned.1.call-done
  177.0 145.6 %while.20 = (s32[]{:T(128)}, f32[4,12,64,128]{3,2,1,0:T(8,128)S(1)}, f32[4,12]{1,0:T(4,128)S(1)}, f32[4,12,64,128]{3,2,1,0:T(8,128)S(1)}, s32[]{:T(128)}) while((s32[]{:T(128)}, f32[4,12,64,128]{3,2,1,0:T(8,128)S(1)}, f32[4,12]{1,0:T(4,128)S(1)}, f32[4,12,64,128]{3,2,1,0:T(8,128)S(1)}, s32[]{:T(128)}) %tuple.95), condition=%wide.region_4.5_spmd, body=%wide.region_3.4_spmd.sunk | while | flops 786434 | bytes 11010341 | solution.py:188
  186.6 16.4 collective-permute-start
  207.5 18.8 collective-permute-start
  230.8 18.8 collective-permute-start
  254.1 18.8 collective-permute-start
  277.4 18.8 collective-permute-start
  300.7 18.8 collective-permute-start
  327.2 18.0 multiply_reduce_fusion.10
  347.5 11.7 psum.28
  374.7 129.3 %reduce-scatter.22.cloned.1.call-done = f32[64,4,1536]{2,0,1:T(8,128)} async-done(((f32[256,4,1536]{2,0,1:T(8,128)}), f32[64,4,1536]{2,0,1:T(8,128)}) %reduce-scatter.22.cloned.1.call-update) | async-done | bytes 1572880 | tf_op jit(solution)/shard_map/reduce_scatter | solution.py:97
  519.3 23.0 scatter_custom_fusion
  545.1 9.2 all-gather.1
  556.1 11.3 all_gather.66
  580.7 17.8 mul.677
  598.5 43.5 %mul.678 = f32[6144,1536]{1,0:T(8,128)} reshape(f32[1024,6,1536]{2,1,0:T(8,128)} %mul.677) | data formatting | bytes 75497472 | tf_op jit(solution)/shard_map/mul | solution.py:296
  644.6 37.4 %gather_fusion.3 = bf16[8192,1536]{1,0:T(8,128)(2,1)} fusion(bf16[1025,1536]{1,0:T(8,128)(2,1)S(1)} %concatenate.26, s32[8192]{0:T(1024)S(1)} %get-tuple-element.254), kind=kCustom, calls=%fused_computation.2.clone | custom fusion | bytes 50364416 | tf_op jit(solution)/shard_map/jit(_take)/gather | solution.py:276
  692.5 37.3 %gather_fusion.1 = bf16[8192,1536]{1,0:T(8,128)(2,1)} fusion(bf16[1025,1536]{1,0:T(8,128)(2,1)S(1)} %concatenate.24, s32[8192]{0:T(1024)S(1)} %get-tuple-element.254), kind=kCustom, calls=%fused_computation.clone | custom fusion | bytes 50364416 | tf_op jit(solution)/shard_map/jit(_take)/gather | solution.py:218
  729.8 21.9 broadcast_select_fusion
  751.6 17.2 fusion.188
  773.5 22.0 fusion.189
  795.5 55.6 %gather_fusion.2 = f32[6144,1536]{1,0:T(8,128)} fusion(f32[8192,1536]{1,0:T(8,128)} %bitcast.411, s32[6144]{0:T(1024)S(1)} %copy-done.77), kind=kCustom, calls=%fused_computation.1.clone | custom fusion | bytes 75522048 | tf_op jit(solution)/shard_map/jit(_take)/gather | solution.py:224
  851.1 38.4 %multiply_reduce_fusion.1 = (f32[6144]{0:T(1024)S(1)}, f32[6144,1536]{1,0:T(8,128)}) fusion(f32[6144,1536]{1,0:T(8,128)} %mul.678, f32[6144,1536]{1,0:T(8,128)} %gather_fusion.2, pred[6144]{0:T(1024)(128)(4,1)S(1)} %copy-done.98), kind=kLoop, calls=%fused_computation.10 | loop fusion | flops 28305408 | bytes 113276928 | tf_op jit(solution)/shard_map/reduce_sum | solution.py:296
  895.1 45.5 %gather_fusion = f32[8192]{0:T(1024)S(1)} fusion(f32[6145]{0:T(1024)S(1)} %pad_maximum_fusion.8, s32[8192]{0:T(1024)S(1)} %copy-done.86), kind=kCustom, calls=%fused_computation.4 | custom fusion | bytes 98304 | tf_op jit(solution)/shard_map/jit(_take)/gather | solution.py:274
  940.7 23.0 multiply_convert_fusion
  963.7 17.1 fusion.69
  980.9 23.1 fusion.1
  1004.0 55.4 %gather_fusion.4 = f32[6144,1536]{1,0:T(8,128)} fusion(f32[8192,1536]{1,0:T(8,128)} %bitcast.410, s32[6144]{0:T(1024)S(1)} %copy-done.77), kind=kCustom, calls=%fused_computation.3.clone | custom fusion | bytes 75522048 | tf_op jit(solution)/shard_map/jit(_take)/gather | solution.py:294
  1059.5 27.8 %broadcast_select_fusion.1 = f32[6144,1536]{1,0:T(8,128)} fusion(f32[6144,1536]{1,0:T(8,128)} %gather_fusion.4, pred[6144]{0:T(1024)(128)(4,1)S(1)} %copy-done.99), kind=kLoop, calls=%fused_computation.12 | loop fusion | flops 9437184 | bytes 75503616 | tf_op jit(solution)/shard_map/jit(_take)/select_n | solution.py:294
  1089.7 42.2 %reshape.414 = f32[1024,6,1536]{2,1,0:T(8,128)} reshape(f32[6144,1536]{1,0:T(8,128)} %broadcast_select_fusion.1) | data formatting | bytes 75497472 | tf_op jit(solution)/shard_map/reshape | solution.py:294
  1131.9 27.4 %reduce_sum.386 = f32[1024,1536]{1,0:T(8,128)} reduce(f32[1024,6,1536]{2,1,0:T(8,128)} %reshape.414, f32[]{:T(128)} %constant.69.clone.1), dimensions={1}, to_apply=%region_18.21 | reduce | flops 7864320 | bytes 44040196 | tf_op jit(solution)/shard_map/reduce_sum | solution.py:293
  1191.5 42.1 %reshape.409 = f32[1024,6,1536]{2,1,0:T(8,128)} reshape(f32[6144,1536]{1,0:T(8,128)} %get-tuple-element.231) | data formatting | bytes 75497472 | tf_op jit(solution)/shard_map/reshape | solution.py:224
  1233.6 61.9 %multiply_reduce_fusion = f32[1024,1536]{1,0:T(8,128)S(1)} fusion(f32[1024,6,1536]{2,1,0:T(8,128)} %reshape.409, f32[1024,6]{1,0:T(8,128)} %copy-done.39), kind=kLoop, calls=%fused_computation.9 | loop fusion | flops 17301504 | bytes 44064768 | tf_op jit(solution)/shard_map/reduce_sum | solution.py:227
  1316.4 109.2 %reduce-scatter.24.cloned.1.call-done = f32[64,4,1536]{2,0,1:T(8,128)} async-done(((f32[256,4,1536]{2,0,1:T(8,128)}), f32[64,4,1536]{2,0,1:T(8,128)}) %reduce-scatter.24.cloned.1.call-update) | async-done | bytes 1572880 | tf_op jit(solution)/shard_map/reduce_scatter | solution.py:97
  1445.8 15.4 convolution_convert_fusion.1
  1461.3 36.9 %all-gather.28.cloned.1.call-done = bf16[256,4,1536]{2,0,1:T(8,128)(2,1)} async-done(((bf16[64,4,1536]{2,0,1:T(8,128)(2,1)}), bf16[256,4,1536]{2,0,1:T(8,128)(2,1)}) %all-gather.28.cloned.1.call-update) | async-done | bytes 3145744 | tf_op jit(solution)/shard_map/all_gather | solution.py:93
  1498.2 8.6 multiply_reduce_fusion.7
  1506.7 9.5 psum.29
  1532.3 153.9 %while.21 = (s32[]{:T(128)}, f32[4,12,64,128]{3,2,1,0:T(8,128)S(1)}, f32[4,12]{1,0:T(4,128)S(1)}, f32[4,12,64,128]{3,2,1,0:T(8,128)S(1)}, s32[]{:T(128)}) while((s32[]{:T(128)}, f32[4,12,64,128]{3,2,1,0:T(8,128)S(1)}, f32[4,12]{1,0:T(4,128)S(1)}, f32[4,12,64,128]{3,2,1,0:T(8,128)S(1)}, s32[]{:T(128)}) %tuple.147), condition=%wide.region_27.30_spmd, body=%wide.region_26.29_spmd.sunk | while | flops 786434 | bytes 11010341 | solution.py:331
  1541.9 21.6 collective-permute-done.1
  1566.1 21.1 collective-permute-done.1
  1589.8 21.2 collective-permute-done.1
  1613.7 20.6 collective-permute-done.1
  1637.0 22.1 collective-permute-done.1
  1661.8 24.4 %collective-permute-done.1 = f32[4,12,64,128]{3,2,1,0:T(8,128)S(1)} collective-permute-done((f32[4,12,64,128]{3,2,1,0:T(8,128)}, f32[4,12,64,128]{3,2,1,0:T(8,128)S(1)}, u32[]{:S(2)}, u32[]{:S(2)}) %collective-permute-start.1) | collective-permute-done | bytes 1572896 | tf_op jit(solution)/shard_map/while/body/eval_jaxpr/ppermute | solution.py:25
  1691.5 12.3 fusion.39
  1713.7 21.9 fusion.10
  1743.2 10.1 reduce-window.26
  1782.0 11.4 fusion.176
  1795.2 17.6 convolution_convert_fusion
  1821.1 8.1 broadcast_multiply_fusion.3
  1836.6 19.8 collective-permute-done.3
  1873.4 9.4 fusion.27
  1910.4 27.9 %reduce-scatter.46.cloned.1.call-done = f32[96,5]{1,0:T(8,128)} async-done(((f32[3072,5]{1,0:T(8,128)}), f32[96,5]{1,0:T(8,128)}) %reduce-scatter.46.cloned.1.call-update) | async-done | bytes 1936
  1939.8 93.9 %reduce-scatter.36.cloned.1.call-done = bf16[16,192,2,128]{3,1,2,0:T(8,128)(2,1)} async-done(((bf16[16,1536,2,128]{3,1,2,0:T(8,128)(2,1)}), bf16[16,192,2,128]{3,1,2,0:T(8,128)(2,1)}) %reduce-scatter.36.cloned.1.call-update) | async-done | bytes 1572880 | tf_op jit(solution)/shard_map/reduce_scatter | solution.py:408
  2038.4 41.3 %reduce-scatter.34.cloned.1.call-done = bf16[768,192]{0,1:T(8,128)(2,1)} async-done(((bf16[768,1536]{0,1:T(8,128)(2,1)}), bf16[768,192]{0,1:T(8,128)(2,1)}) %reduce-scatter.34.cloned.1.call-update) | async-done | bytes 294928 | tf_op jit(solution)/shard_map/reduce_scatter | solution.py:405
  2081.6 55.6 %reduce-scatter.30.cloned.1.call-done = bf16[192,2,768]{2,0,1:T(8,128)(2,1)} async-done(((bf16[1536,2,768]{2,0,1:T(8,128)(2,1)}), bf16[192,2,768]{2,0,1:T(8,128)(2,1)}) %reduce-scatter.30.cloned.1.call-update) | async-done | bytes 589840 | tf_op jit(solution)/shard_map/reduce_scatter | solution.py:399
  2139.8 110.5 %reduce-scatter.28.cloned.1.call-done = f32[64,4,1536]{2,0,1:T(8,128)} async-done(((f32[256,4,1536]{2,0,1:T(8,128)}), f32[64,4,1536]{2,0,1:T(8,128)}) %reduce-scatter.28.cloned.1.call-update) | async-done | bytes 1572880 | tf_op jit(solution)/shard_map/reduce_scatter | solution.py:97
  2252.2 41.8 %all-reduce.15 = (f32[1536]{0:T(1024)S(1)}, f32[5,256]{1,0:T(8,128)S(1)}, f32[3,48]{1,0:T(4,128)}, f32[3072]{0:T(1024)S(1)}, f32[1536]{0:T(1024)S(1)}, /*index=5*/f32[3]{0:T(128)S(1)}) all-reduce(f32[1536]{0:T(1024)S(1)} %get-tuple-element.190, ...), channel_id=6, replica_groups=mesh['dp'=8,'tensor'=4] {'dp','tensor'}, use_global_device_ids=true, to_apply=%region_39.42.clone | all-reduce | flops 7571 | bytes 60568
  2301.3 53.2 %reduce-scatter.32.cloned.1.call-done = f32[48,256]{1,0:T(8,128)} async-done(((f32[1536,256]{1,0:T(8,128)}), f32[48,256]{1,0:T(8,128)}) %reduce-scatter.32.cloned.1.call-update) | async-done | bytes 49168 | tf_op jit(solution)/shard_map/reduce_scatter | solution.py:423
  (608 shorter events, 431.5 us)
Async XLA Ops:
  7.2 87.7 %all-gather.12.cloned.1.call-start = ((), (), s32[]{:S(2)}) async-start(), calls=%async_computation.14 | async-start | bytes 3932160 | tf_op jit(solution)/shard_map/all_gather | solution.py:93
  31.9 103.1 %all-gather.14.cloned.1.call-start = ((), (), s32[]{:S(2)}) async-start(), calls=%async_computation.15 | async-start | bytes 5308416 | tf_op jit(solution)/shard_map/all_gather | solution.py:142
  32.9 331.3 %all-gather.16.cloned.1.call-start = ((), (), s32[]{:S(2)}) async-start(), calls=%async_computation.16 | async-start | bytes 2654208 | tf_op jit(solution)/shard_map/all_gather | solution.py:145
  33.6 470.4 %reduce-scatter.22.cloned.1.call-start = ((), (), s32[]{:S(2)}) async-start(), calls=%async_computation.17 | async-start | bytes 7864320 | tf_op jit(solution)/shard_map/reduce_scatter | solution.py:97
  45.4 114.0 %copy-start.106 = (f32[1,1024]{1,0:T(1,128)}, f32[1,1024]{1,0:T(1,128)S(1)}, u32[]{:S(2)}) copy-start(f32[1,1024]{1,0:T(1,128)S(1)} %get-tuple-element.256) | copy-start | bytes 12292
  45.4 114.0 %copy-start.108 = (f32[1,1024]{1,0:T(1,128)}, f32[1,1024]{1,0:T(1,128)S(1)}, u32[]{:S(2)}) copy-start(f32[1,1024]{1,0:T(1,128)S(1)} %get-tuple-element.257) | copy-start | bytes 12292
  45.4 114.0 %copy-start.110 = (f32[1,1024]{1,0:T(1,128)}, f32[1,1024]{1,0:T(1,128)S(1)}, u32[]{:S(2)}) copy-start(f32[1,1024]{1,0:T(1,128)S(1)} %get-tuple-element.258) | copy-start | bytes 12292
  145.6 11.7 collective-permute-start.2
  149.9 177.2 %copy-start.91 = (f32[256,4,12]{0,2,1:T(8,128)}, f32[256,4,12]{0,2,1:T(8,128)S(1)}, u32[]{:S(2)}) copy-start(f32[256,4,12]{0,2,1:T(8,128)S(1)} %copy.322) | copy-start | bytes 147460
  152.4 174.7 %copy-start.93 = (f32[256,4,12]{0,2,1:T(8,128)}, f32[256,4,12]{0,2,1:T(8,128)S(1)}, u32[]{:S(2)}) copy-start(f32[256,4,12]{0,2,1:T(8,128)S(1)} %copy.325) | copy-start | bytes 147460
  153.7 173.4 %copy-start.59 = (f32[256,4,12]{0,2,1:T(8,128)}, f32[256,4,12]{0,2,1:T(8,128)S(1)}, u32[]{:S(2)}) copy-start(f32[256,4,12]{0,2,1:T(8,128)S(1)} %copy.326) | copy-start | bytes 147460
  178.4 6.8 collective-permute-start
  186.6 19.6 collective-permute-start
  207.5 21.9 collective-permute-start
  230.8 21.9 collective-permute-start
  254.1 21.9 collective-permute-start
  277.4 21.9 collective-permute-start
  300.7 21.9 collective-permute-start
  372.1 131.8 %copy-start.23 = (bf16[64,4,1536]{2,1,0:T(4,128)(2,1)S(1)}, bf16[64,4,1536]{2,1,0:T(4,128)(2,1)}, u32[]{:S(2)}) copy-start(bf16[64,4,1536]{2,1,0:T(4,128)(2,1)} %param.27) | copy-start | bytes 2359300
  372.2 197.8 %all-gather.26.cloned.1.call-start = ((), (), s32[]{:S(2)}) async-start(), calls=%async_computation.23 | async-start | bytes 3932160 | tf_op jit(solution)/shard_map/all_gather | solution.py:93
  374.6 307.4 %all-gather.18.cloned.1.call-start = ((), (), s32[]{:S(2)}) async-start(), calls=%async_computation.18 | async-start | bytes 3932160 | tf_op jit(solution)/shard_map/all_gather | solution.py:93
  374.6 133.3 %copy-start.79 = (f32[1536]{0:T(1024)}, f32[1536]{0:T(1024)S(1)}, u32[]{:S(2)}) copy-start(f32[1536]{0:T(1024)S(1)} %convert_element_type.164) | copy-start | bytes 18436
  374.6 133.4 %copy-start.51 = (bf16[16,192,2,128]{3,2,1,0:T(2,128)(2,1)S(1)}, bf16[16,192,2,128]{3,2,1,0:T(2,128)(2,1)}, u32[]{:S(2)}) copy-start(bf16[16,192,2,128]{3,2,1,0:T(2,128)(2,1)} %param.42) | copy-start | bytes 4718596
  508.0 243.7 %all-gather.20.cloned.1.call-start = ((), (), s32[]{:S(2)}) async-start(), calls=%async_computation.19 | async-start | bytes 14155776 | tf_op jit(solution)/shard_map/all_gather | solution.py:148
  509.6 263.9 %all-gather.22.cloned.1.call-start = ((), (), s32[]{:S(2)}) async-start(), calls=%async_computation.20 | async-start | bytes 7077888 | tf_op jit(solution)/shard_map/all_gather | solution.py:149
  510.3 652.8 %all-gather.24.cloned.1.call-start = ((), (), s32[]{:S(2)}) async-start(), calls=%async_computation.21 | async-start | bytes 1769472 | tf_op jit(solution)/shard_map/all_gather | solution.py:150
  511.1 805.2 %reduce-scatter.26.cloned.1.call-start = ((), (), s32[]{:S(2)}) async-start(), calls=%async_computation.24 | async-start | bytes 7864320 | tf_op jit(solution)/shard_map/reduce_scatter | solution.py:97
  1191.5 234.1 %reduce-scatter.24.cloned.1.call-start = ((), (), s32[]{:S(2)}) async-start(), calls=%async_computation.22 | async-start | bytes 7864320 | tf_op jit(solution)/shard_map/reduce_scatter | solution.py:97
  1316.2 109.4 %copy-start.101 = (f32[64,4]{0,1:T(4,128)S(1)}, f32[64,4]{0,1:T(4,128)}, u32[]{:S(2)}) copy-start(f32[64,4]{0,1:T(4,128)} %copy-done.100) | copy-start | bytes 3076
  1316.2 109.4 %copy-start.104 = (f32[64,4]{0,1:T(4,128)S(1)}, f32[64,4]{0,1:T(4,128)}, u32[]{:S(2)}) copy-start(f32[64,4]{0,1:T(4,128)} %copy-done.103) | copy-start | bytes 3076
  1316.3 113.8 %copy-start.121 = (f32[64,4]{0,1:T(4,128)S(1)}, f32[64,4]{0,1:T(4,128)}, u32[]{:S(2)}) copy-start(f32[64,4]{0,1:T(4,128)} %copy-done.120) | copy-start | bytes 3076
  1316.3 181.9 %all-gather.28.cloned.1.call-start = ((), (), s32[]{:S(2)}) async-start(), calls=%async_computation.25 | async-start | bytes 3932160 | tf_op jit(solution)/shard_map/all_gather | solution.py:93
  1434.0 462.6 %reduce-scatter.48.cloned.1.call-start = ((), (), s32[]{:S(2)}) async-start(), calls=%async_computation.36 | async-start | bytes 811008
  1436.3 461.7 %reduce-scatter.42.cloned.1.call-start = ((), (), s32[]{:S(2)}) async-start(), calls=%async_computation.33 | async-start | bytes 884736 | tf_op jit(solution)/shard_map/reduce_scatter | solution.py:417
  1441.4 458.3 %reduce-scatter.40.cloned.1.call-start = ((), (), s32[]{:S(2)}) async-start(), calls=%async_computation.32 | async-start | bytes 1769472 | tf_op jit(solution)/shard_map/reduce_scatter | solution.py:414
  1445.8 455.8 %reduce-scatter.38.cloned.1.call-start = ((), (), s32[]{:S(2)}) async-start(), calls=%async_computation.31 | async-start | bytes 7077888 | tf_op jit(solution)/shard_map/reduce_scatter | solution.py:411
  1461.2 447.7 %reduce-scatter.44.cloned.1.call-start = ((), (), s32[]{:S(2)}) async-start(), calls=%async_computation.34 | async-start | bytes 442368
  1533.7 5.5 collective-permute-start.1
  1540.6 22.9 collective-permute-start.1
  1564.8 22.4 collective-permute-start.1
  1588.5 22.5 collective-permute-start.1
  1612.4 21.9 collective-permute-start.1
  1635.7 23.4 collective-permute-start.1
  1660.5 25.7 %collective-permute-start.1 = (f32[4,12,64,128]{3,2,1,0:T(8,128)}, f32[4,12,64,128]{3,2,1,0:T(8,128)S(1)}, u32[]{:S(2)}, u32[]{:S(2)}) collective-permute-start(f32[4,12,64,128]{3,2,1,0:T(8,128)} %multiply_add_fusion.9), channel_id=1, source_target_pairs={{4,0},{8,4},{12,8},{16,12},{20,16},{24,20},{28,24},{5,1},{9,5},{13... | collective-permute-start | bytes 4718600 | tf_op jit(solution)/shard_map/while/body/eval_jaxpr/ppermute | solution.py:25
  1782.0 156.3 %reduce-scatter.46.cloned.1.call-start = ((), (), s32[]{:S(2)}) async-start(), calls=%async_computation.35 | async-start | bytes 1622016
  1793.4 114.0 %copy-start.85 = (f32[5,1024]{1,0:T(8,128)}, f32[5,1024]{1,0:T(8,128)S(1)}, u32[]{:S(2)}) copy-start(f32[5,1024]{1,0:T(8,128)S(1)} %stack.90) | copy-start | bytes 61444
  1795.2 238.5 %reduce-scatter.36.cloned.1.call-start = ((), (), s32[]{:S(2)}) async-start(), calls=%async_computation.30 | async-start | bytes 14155776 | tf_op jit(solution)/shard_map/reduce_scatter | solution.py:408
  1812.8 266.9 %reduce-scatter.34.cloned.1.call-start = ((), (), s32[]{:S(2)}) async-start(), calls=%async_computation.29 | async-start | bytes 2654208 | tf_op jit(solution)/shard_map/reduce_scatter | solution.py:405
  1820.8 316.3 %reduce-scatter.30.cloned.1.call-start = ((), (), s32[]{:S(2)}) async-start(), calls=%async_computation.27 | async-start | bytes 5308416 | tf_op jit(solution)/shard_map/reduce_scatter | solution.py:399
  1835.3 21.1 collective-permute-start.3
  1868.3 382.0 %reduce-scatter.28.cloned.1.call-start = ((), (), s32[]{:S(2)}) async-start(), calls=%async_computation.26 | async-start | bytes 7864320 | tf_op jit(solution)/shard_map/reduce_scatter | solution.py:97
  1889.3 465.2 %reduce-scatter.32.cloned.1.call-start = ((), (), s32[]{:S(2)}) async-start(), calls=%async_computation.28 | async-start | bytes 1622016 | tf_op jit(solution)/shard_map/reduce_scatter | solution.py:423
  1939.8 310.5 %copy-start.24 = (bf16[64,4,1536]{2,1,0:T(4,128)(2,1)S(1)}, bf16[64,4,1536]{2,1,0:T(4,128)(2,1)}, u32[]{:S(2)}) copy-start(bf16[64,4,1536]{2,1,0:T(4,128)(2,1)} %param.27) | copy-start | bytes 2359300
  1939.8 310.5 %copy-start.84 = (f32[1536]{0:T(1024)S(1)}, f32[1536]{0:T(1024)}, u32[]{:S(2)}) copy-start(f32[1536]{0:T(1024)} %copy-done.83) | copy-start | bytes 18436
  1939.8 310.5 %copy-start.115 = (f32[64,4]{0,1:T(4,128)S(1)}, f32[64,4]{0,1:T(4,128)}, u32[]{:S(2)}) copy-start(f32[64,4]{0,1:T(4,128)} %copy-done.114) | copy-start | bytes 3076
  2038.4 213.8 %slice-start.4 = ((f32[5,1024]{1,0:T(8,128)}), f32[5,256]{1,0:T(8,128)S(1)}, s32[]{:S(2)}) async-start(f32[5,1024]{1,0:T(8,128)} %copy-done.85), calls=%async_computation.41 | async-start | bytes 16384 | tf_op jit(solution)/shard_map/slice | solution.py:388
  2038.4 213.8 %copy-start.116 = (f32[1536]{0:T(1024)S(1)}, f32[1536]{0:T(1024)}, u32[]{:S(2)}) copy-start(f32[1536]{0:T(1024)} %get-tuple-element.195) | copy-start | bytes 18436
  2038.4 256.7 %copy-start.123 = (f32[64,4]{0,1:T(4,128)S(1)}, f32[64,4]{0,1:T(4,128)}, u32[]{:S(2)}) copy-start(f32[64,4]{0,1:T(4,128)} %copy-done.122) | copy-start | bytes 3076
  2038.4 256.8 %copy-start.14 = (f32[64,4,1536]{2,0,1:T(8,128)S(1)}, f32[64,4,1536]{2,0,1:T(8,128)}, u32[]{:S(2)}) copy-start(f32[64,4,1536]{2,0,1:T(8,128)} %copy-done.12) | copy-start | bytes 4718596
  2038.4 256.8 %copy-start.36 = (bf16[64,4,1536]{2,1,0:T(4,128)(2,1)S(1)}, bf16[64,4,1536]{2,1,0:T(4,128)(2,1)}, u32[]{:S(2)}) copy-start(bf16[64,4,1536]{2,1,0:T(4,128)(2,1)} %param.28) | copy-start | bytes 2359300
  2038.4 256.8 %copy-start.81 = (f32[1536]{0:T(1024)S(1)}, f32[1536]{0:T(1024)}, u32[]{:S(2)}) copy-start(f32[1536]{0:T(1024)} %copy-done.79) | copy-start | bytes 18436
  2038.4 256.8 %copy-start.102 = (f32[64,4]{0,1:T(4,128)S(1)}, f32[64,4]{0,1:T(4,128)}, u32[]{:S(2)}) copy-start(f32[64,4]{0,1:T(4,128)} %copy-done.100) | copy-start | bytes 3076
  2038.4 256.8 %copy-start.105 = (f32[64,4]{0,1:T(4,128)S(1)}, f32[64,4]{0,1:T(4,128)}, u32[]{:S(2)}) copy-start(f32[64,4]{0,1:T(4,128)} %copy-done.103) | copy-start | bytes 3076
  2038.4 256.8 %copy-start.119 = (f32[64,4]{0,1:T(4,128)S(1)}, f32[64,4]{0,1:T(4,128)}, u32[]{:S(2)}) copy-start(f32[64,4]{0,1:T(4,128)} %copy-done.118) | copy-start | bytes 3076
  (133 other events, 2039.8 us)
Sparse Core Ops, SparseCore 0:
  32.0 62.8 all-gather.11
  97.4 37.5 all-gather.13
  136.9 29.0 all-gather.15
  372.3 131.6 reduce-scatter.21
  506.0 63.9 all-gather.25
  572.0 62.1 all-gather.17
  636.6 70.8 all-gather.19
  709.4 45.5 all-gather.21
  757.4 25.6 all-gather.23
  1191.6 109.1 reduce-scatter.25
  1316.4 109.1 reduce-scatter.23
  1434.1 63.9 all-gather.27
  1503.3 103.3 reduce-scatter.47
  1609.6 34.3 reduce-scatter.41
  1647.1 42.7 reduce-scatter.39
  1693.1 61.8 reduce-scatter.37
  1782.1 53.2 reduce-scatter.43
  1841.3 96.9 reduce-scatter.45
  1942.2 91.4 reduce-scatter.35
  2037.2 42.4 reduce-scatter.33
  2083.2 53.8 reduce-scatter.29
  2139.5 110.6 reduce-scatter.27
  2256.9 97.5 reduce-scatter.31
where the time goes:
time: 2370 us; the launch traced here: 2360 us
  waiting for transfers between devices  901 us (38%)
  local copies, waits for them, and re-layouts  556 us (23%)
  other arithmetic  337 us (14%)
  matrix products  303 us (13%)
  starting transfers between devices  128 us (5%)
  blocking collectives  119 us (5%)
    reduce_scatter x4, waiting for transfers between devices, sum_piece(): return lax.psum_scatter(values, 'tensor', scatter_dimension=0, tiled=True)  349 us
    ppermute x16, waiting for transfers between devices, passed_along(): lax.ppermute(value, axis, [(source, source + steps) for source in range(f...  177 us
    ppermute x16, starting transfers between devices, passed_along(): lax.ppermute(value, axis, [(source, source + steps) for source in range(f...  127 us
    reduce_scatter x1, waiting for transfers between devices, body(): lax.psum_scatter(w_gu_grad.astype(jnp.bfloat16), 'dp', scatter_dimension=...  93.9 us
    all_gather x4, waiting for transfers between devices, gather_piece(): return lax.all_gather(values, 'tensor', axis=0, tiled=True)  79.1 us
    reduce_sum x1, other arithmetic, body(): jnp.sum(gates[:, :, None] * per_route, axis=1)  61.9 us
    mul x2, local copies, waits for them, and re-layouts, body(): per_route * moe_back.astype(jnp.float32)[:, None, :]  61.3 us
    unnamed x2, blocking collectives  57.8 us
  transfers between devices with their start and end apart: 39, of which 27 were waited for; matrix products, arithmetic and copies ran while one was open for 48% of the time, Pallas kernels for 0%

commit v1 on v0

v1 whole, which is shorter than its diff:
```python
import functools

import jax
import jax.numpy as jnp
from jax import lax
from jax.experimental import pallas as pl
from jax.experimental.pallas import tpu as pltpu
from jax.sharding import PartitionSpec as P

D_MODEL = 1536
HEAD_COUNT = 48
HEAD_DIM = 64
STATE_DIM = 128
CONV_WIDTH = 4
TOP_K = 6
EXPERTS = 16
SLOT_COUNT = 4
INNER_DIM = 3072
LANES = 128
CHUNKS = 1

norm_eps = 1e-05
highest = lax.Precision.HIGHEST
f32 = jnp.float32
bf16 = jnp.bfloat16


def passed_along(value, axis, steps):
    count = lax.axis_size(axis)
    first, last = (max(0, -steps), min(count, count - steps))
    return lax.ppermute(value, axis, [(source, source + steps) for source in range(first, last)])


def line_gather(value):
    size = lax.axis_size("tensor")
    rights, lefts = [], []
    right, left = value, value
    for _ in range(1, size):
        right = lax.ppermute(right, "tensor", [(a, a + 1) for a in range(size - 1)])
        left = lax.ppermute(left, "tensor", [(a, a - 1) for a in range(1, size)])
        rights.append(right)
        lefts.append(left)
    return [value] + [rights[size - k - 1] + lefts[k - 1] for k in range(1, size)]


def line_scatter(block_of):
    size = lax.axis_size("tensor")
    right, left = None, None
    for k in range(1, size):
        to_right, to_left = block_of(size - k), block_of(k)
        if k > 1:
            to_right = (to_right.astype(f32) + right.astype(f32)).astype(bf16)
            to_left = (to_left.astype(f32) + left.astype(f32)).astype(bf16)
        right = lax.ppermute(to_right, "tensor", [(a, a + 1) for a in range(k)])
        left = lax.ppermute(to_left, "tensor", [(a, a - 1) for a in range(size - k, size)])
    return block_of(0).astype(f32) + right.astype(f32) + left.astype(f32)


def in_order(blocks):
    size = len(blocks)
    own = lax.axis_index("tensor")
    whole = jnp.zeros((size,) + blocks[0].shape, blocks[0].dtype)
    for k in range(size):
        whole = lax.dynamic_update_index_in_dim(whole, blocks[k], (own + k) % size, 0)
    return whole


def by_distance(whole):
    size = whole.shape[0]
    own = lax.axis_index("tensor")
    return lambda k: lax.dynamic_index_in_dim(whole, (own + k) % size, 0, False)


def weight_gather(shard):
    return lax.all_gather(shard, "dp", axis=0, tiled=False)


def weight_scatter(grads):
    return lax.psum_scatter(grads.astype(bf16), "dp", scatter_dimension=0, tiled=False)


def rms_scale(values, gain_vec):
    return (
        values * lax.rsqrt(jnp.mean(values * values, axis=-1, keepdims=True) + norm_eps) * gain_vec
    )


def silu_slope(values):
    logistic = jax.nn.sigmoid(values)
    return logistic * (1.0 + values * (1.0 - logistic))


def dot(a, b, dims, precision=None):
    return lax.dot_general(a, b, (dims, ((), ())), precision=precision, preferred_element_type=f32)


def split_parts(values):
    upper = values.astype(bf16)
    return upper, (values - upper.astype(f32)).astype(bf16)


def dot_split(a, b, dims):
    return dot(a[0], b[0], dims) + (dot(a[0], b[1], dims) + dot(a[1], b[0], dims))


def after(value, *others):
    return lax.optimization_barrier((value,) + others)[0]


NN = ((1,), (0,))
NT = ((1,), (1,))
TN = ((0,), (0,))


def head_spread(inner):
    row = lax.broadcasted_iota(jnp.int32, (LANES, inner), 0)
    col = lax.broadcasted_iota(jnp.int32, (LANES, inner), 1)
    return (col // HEAD_DIM == row).astype(f32)


def head_sums(inner):
    row = lax.broadcasted_iota(jnp.int32, (inner, LANES), 0)
    col = lax.broadcasted_iota(jnp.int32, (inner, LANES), 1)
    return (row // HEAD_DIM == col).astype(f32)


def lower_ones(extent):
    row = lax.broadcasted_iota(jnp.int32, (extent, extent), 0)
    col = lax.broadcasted_iota(jnp.int32, (extent, extent), 1)
    return (row >= col).astype(f32)


def kernel_params(mib):
    return pltpu.CompilerParams(vmem_limit_bytes=mib * 1024 * 1024)


def conv_of(v_ref, halo_ref, cw_ref, padded):
    extent = padded.shape[0] - 8
    width = padded.shape[1]
    padded[0:8, :] = halo_ref[0]
    padded[8:, :] = v_ref[:, 0, :, 0:width].reshape(extent, width)
    summed = cw_ref[CONV_WIDTH : CONV_WIDTH + 1, :]
    for tap in range(CONV_WIDTH):
        summed = summed + cw_ref[tap : tap + 1, :] * padded[5 + tap : 5 + tap + extent, :]
    return summed


def step_sizes(v_ref, hp_ref, conv_width, extent):
    raw = v_ref[:, 0, :, conv_width : conv_width + LANES].reshape(extent, LANES) + hp_ref[1:2, :]
    step = jnp.maximum(raw, 0.0) + jnp.log1p(jnp.exp(-jnp.abs(raw)))
    return raw, step


def enter_kernel(inner, v_ref, halo_ref, cw_ref, hp_ref, xs_ref, rw_ref, dl_ref, s_ref, padded):
    extent = xs_ref.shape[1]
    width = padded.shape[1]
    pre = conv_of(v_ref, halo_ref, cw_ref, padded)
    act = pre * jax.nn.sigmoid(pre)
    xs = act[:, :inner]
    write = act[:, inner : inner + STATE_DIM]
    unused_raw, step = step_sizes(v_ref, hp_ref, width, extent)
    log_sum = dot(lower_ones(extent), -step * jnp.exp(hp_ref[0:1, :]), NN, highest)
    tail = jnp.exp(log_sum[extent - 1 : extent, :] - log_sum) * step
    spread = dot(tail, head_spread(inner), NN, highest)
    xs_ref[0] = xs
    rw_ref[0] = act[:, inner:]
    dl_ref[0, :, 0:LANES] = step
    dl_ref[0, :, LANES:] = log_sum
    s_ref[0] = dot_split(split_parts(xs * spread), split_parts(write), TN)


def mixer_enter(v, halo, cw, hp, inner):
    zs, slots, rows, cols = v.shape
    extent = zs * rows
    width = cw.shape[1]
    heads = inner // HEAD_DIM
    return pl.pallas_call(
        functools.partial(enter_kernel, inner),
        grid=(slots,),
        in_specs=[
            pl.BlockSpec((zs, 1, rows, cols), lambda s: (0, s, 0, 0)),
            pl.BlockSpec((1, 8, width), lambda s: (s, 0, 0)),
            pl.BlockSpec(cw.shape, lambda s: (0, 0)),
            pl.BlockSpec(hp.shape, lambda s: (0, 0)),
        ],
        out_specs=[
            pl.BlockSpec((1, extent, inner), lambda s: (s, 0, 0)),
            pl.BlockSpec((1, extent, 2 * STATE_DIM), lambda s: (s, 0, 0)),
            pl.BlockSpec((1, extent, 2 * LANES), lambda s: (s, 0, 0)),
            pl.BlockSpec((1, inner, STATE_DIM), lambda s: (s, 0, 0)),
        ],
        out_shape=[
            jax.ShapeDtypeStruct((slots, extent, inner), f32),
            jax.ShapeDtypeStruct((slots, extent, 2 * STATE_DIM), f32),
            jax.ShapeDtypeStruct((slots, extent, 2 * LANES), f32),
            jax.ShapeDtypeStruct((slots, inner, STATE_DIM), f32),
        ],
        scratch_shapes=[pltpu.VMEM((extent + 8, width), f32)],
        compiler_params=kernel_params(48),
        cost_estimate=pl.CostEstimate(
            flops=slots * extent * inner * 500, bytes_accessed=slots * extent * cols * 8, transcendentals=slots * extent * cols
        ),
        name="mixer_enter",
    )(v, halo, cw, hp)


def scan_kernel(reverse, got_ref, decay_ref, out_ref):
    count = got_ref.shape[0]
    state = jnp.zeros(got_ref.shape[1:], f32)
    order = range(count - 1, -1, -1) if reverse else range(count)
    for piece in order:
        out_ref[piece] = state
        state = decay_ref[piece] * state + got_ref[piece]


def scan_pieces(got, decay, reverse):
    return pl.pallas_call(
        functools.partial(scan_kernel, reverse),
        out_shape=jax.ShapeDtypeStruct(got.shape, f32),
        compiler_params=kernel_params(32),
        name="scan_pieces",
    )(got, decay)


def exchanged(rows):
    return lax.all_to_all(rows, "dp", 0, 0, tiled=False)


def states_forward(s_local, log_last):
    count = lax.axis_size("dp")
    slots, inner, _ = s_local.shape
    share = slots * inner // count
    per_row = jnp.repeat(jnp.exp(log_last).reshape(-1), HEAD_DIM).reshape(count, share)
    lines = -(-share // (8 * LANES)) * 8
    per_row = jnp.pad(per_row, ((0, 0), (0, lines * LANES - share))).reshape(count, lines, LANES)
    got = exchanged(jnp.concatenate([s_local.reshape(count, share, STATE_DIM), per_row], axis=1))
    decay = got[:, share:].reshape(count, lines * LANES)[:, :share, None]
    entering = exchanged(scan_pieces(got[:, :share], decay, False))
    return entering.reshape(slots, inner, STATE_DIM), decay


def states_backward(g_local, decay):
    count = lax.axis_size("dp")
    slots, inner, _ = g_local.shape
    got = exchanged(g_local.reshape(count, slots * inner // count, STATE_DIM))
    return exchanged(scan_pieces(got, decay, True)).reshape(slots, inner, STATE_DIM)


def leave_kernel(inner, xs_ref, rw_ref, dl_ref, h_ref, z_ref, hp_ref, gain_ref, y_ref, gg_ref, sq_ref, ybuf):
    extent = xs_ref.shape[1]
    zs, _, rows, _ = z_ref.shape
    xs = xs_ref[0]
    write = split_parts(rw_ref[0, :, :STATE_DIM])
    read = split_parts(rw_ref[0, :, STATE_DIM:])
    step_t = dl_ref[0, :, 0:LANES].T
    log_sum = dl_ref[0, :, LANES:]
    log_t = log_sum.T
    scores = dot_split(read, write, NT)
    causal = lax.broadcasted_iota(jnp.int32, (extent, extent), 0) >= lax.broadcasted_iota(
        jnp.int32, (extent, extent), 1
    )
    xs_low = xs.astype(bf16)
    for head in range(inner // HEAD_DIM):
        cols = slice(head * HEAD_DIM, (head + 1) * HEAD_DIM)
        gap = log_sum[:, head : head + 1] - log_t[head : head + 1, :]
        mixing = jnp.exp(jnp.where(causal, gap, -jnp.inf)) * scores * step_t[head : head + 1, :]
        ybuf[:, cols] = dot(mixing.astype(bf16), xs_low[:, cols], NN)
    spread = head_spread(inner)
    grown = dot(jnp.exp(log_sum), spread, NN, highest)
    y = ybuf[...] + grown * dot_split(read, split_parts(h_ref[0]), NT) + hp_ref[3:4, :] * xs
    y_ref[0] = y
    z = z_ref[...].reshape(extent, inner)
    gated = y * (z * jax.nn.sigmoid(z))
    sq_ref[0] = jnp.broadcast_to(jnp.sum(gated * gated, axis=1, keepdims=True), (extent, LANES))
    gg_ref[...] = (gated * gain_ref[...]).astype(bf16).reshape(zs, 1, rows, inner)


def mixer_leave(xs, rw, dl, h_in, z, skip, gain):
    zs, slots, rows, inner = z.shape
    extent = zs * rows
    return pl.pallas_call(
        functools.partial(leave_kernel, inner),
        grid=(slots,),
        in_specs=[
            pl.BlockSpec((1, extent, inner), lambda s: (s, 0, 0)),
            pl.BlockSpec((1, extent, 2 * STATE_DIM), lambda s: (s, 0, 0)),
            pl.BlockSpec((1, extent, 2 * LANES), lambda s: (s, 0, 0)),
            pl.BlockSpec((1, inner, STATE_DIM), lambda s: (s, 0, 0)),
            pl.BlockSpec((zs, 1, rows, inner), lambda s: (0, s, 0, 0)),
            pl.BlockSpec(skip.shape, lambda s: (0, 0)),
            pl.BlockSpec(gain.shape, lambda s: (0, 0)),
        ],
        out_specs=[
            pl.BlockSpec((1, extent, inner), lambda s: (s, 0, 0)),
            pl.BlockSpec((zs, 1, rows, inner), lambda s: (0, s, 0, 0)),
            pl.BlockSpec((1, extent, LANES), lambda s: (s, 0, 0)),
        ],
        out_shape=[
            jax.ShapeDtypeStruct((slots, extent, inner), f32),
            jax.ShapeDtypeStruct((zs, slots, rows, inner), bf16),
            jax.ShapeDtypeStruct((slots, extent, LANES), f32),
        ],
        scratch_shapes=[pltpu.VMEM((extent, inner), f32)],
        compiler_params=kernel_params(48),
        cost_estimate=pl.CostEstimate(
            flops=slots * extent * inner * 2000, bytes_accessed=slots * extent * inner * 16, transcendentals=slots * extent * inner
        ),
        name="mixer_leave",
    )(xs, rw, dl, h_in, z, skip, gain)


def unmix_kernel(inner, gn_ref, y_ref, z_ref, rw_ref, dl_ref, tok_ref, gain_ref, gy_ref, gz_ref, s_ref, gg_ref):
    extent = y_ref.shape[1]
    zs, _, rows, _ = z_ref.shape
    grad = gn_ref[...].reshape(extent, inner)
    z = z_ref[...].reshape(extent, inner)
    logistic = jax.nn.sigmoid(z)
    gate = z * logistic
    y = y_ref[0]
    gated = y * gate
    inv_rms = tok_ref[0, :, 0:1]
    cross = tok_ref[0, :, 1:2]
    part = jnp.sum(grad * gated * inv_rms, axis=0, keepdims=True)

    @pl.when(pl.program_id(0) == 0)
    def _():
        gg_ref[...] = jnp.zeros_like(gg_ref)

    gg_ref[0:1, :] += part
    gated_grad = grad * gain_ref[...] * inv_rms - gated * cross
    gy = gated_grad * gate
    gy_ref[0] = gy
    gz = gated_grad * y * (logistic * (1.0 + z * (1.0 - logistic)))
    gz_ref[...] = gz.astype(bf16).reshape(zs, 1, rows, inner)
    grown = dot(jnp.exp(dl_ref[0, :, LANES:]), head_spread(inner), NN, highest)
    s_ref[0] = dot_split(split_parts(gy * grown), split_parts(rw_ref[0, :, STATE_DIM:]), TN)


def mixer_unmix(gn, y, z, rw, dl, tok, gain):
    zs, slots, rows, inner = z.shape
    extent = zs * rows
    return pl.pallas_call(
        functools.partial(unmix_kernel, inner),
        grid=(slots,),
        in_specs=[
            pl.BlockSpec((zs, 1, rows, inner), lambda s: (0, s, 0, 0)),
            pl.BlockSpec((1, extent, inner), lambda s: (s, 0, 0)),
            pl.BlockSpec((zs, 1, rows, inner), lambda s: (0, s, 0, 0)),
            pl.BlockSpec((1, extent, 2 * STATE_DIM), lambda s: (s, 0, 0)),
            pl.BlockSpec((1, extent, 2 * LANES), lambda s: (s, 0, 0)),
            pl.BlockSpec((1, extent, 2), lambda s: (s, 0, 0)),
            pl.BlockSpec(gain.shape, lambda s: (0, 0)),
        ],
        out_specs=[
            pl.BlockSpec((1, extent, inner), lambda s: (s, 0, 0)),
            pl.BlockSpec((zs, 1, rows, inner), lambda s: (0, s, 0, 0)),
            pl.BlockSpec((1, inner, STATE_DIM), lambda s: (s, 0, 0)),
            pl.BlockSpec((8, inner), lambda s: (0, 0)),
        ],
        out_shape=[
            jax.ShapeDtypeStruct((slots, extent, inner), f32),
            jax.ShapeDtypeStruct((zs, slots, rows, inner), bf16),
            jax.ShapeDtypeStruct((slots, inner, STATE_DIM), f32),
            jax.ShapeDtypeStruct((8, inner), f32),
        ],
        compiler_params=kernel_params(48),
        cost_estimate=pl.CostEstimate(
            flops=slots * extent * inner * 500, bytes_accessed=slots * extent * inner * 26, transcendentals=slots * extent * inner
        ),
        name="mixer_unmix",
    )(gn, y, z, rw, dl, tok, gain)


def back_kernel(
    inner, v_ref, halo_ref, cw_ref, hp_ref, skip_ref, rw_ref, dl_ref, gy_ref, h_ref, gh_ref,
    gv_ref, gbc_ref, gp_ref, gc_ref, ghp_ref, padded, gpad, bufs, cols_buf,
):
    extent = gy_ref.shape[1]
    zs, _, rows, _ = v_ref.shape
    width = padded.shape[1]
    heads = inner // HEAD_DIM
    first = pl.program_id(0) == 0
    pre = conv_of(v_ref, halo_ref, cw_ref, padded)
    logistic = jax.nn.sigmoid(pre)
    slope = logistic * (1.0 + pre * (1.0 - logistic))
    xs = pre[:, :inner] * logistic[:, :inner]
    write = split_parts(rw_ref[0, :, :STATE_DIM])
    read = split_parts(rw_ref[0, :, STATE_DIM:])
    raw, step = step_sizes(v_ref, hp_ref, width, extent)
    rate = jnp.exp(hp_ref[0:1, :])
    log_sum = dl_ref[0, :, LANES:]
    log_t = log_sum.T
    gy = gy_ref[0]
    gy_parts, xs_parts = split_parts(gy), split_parts(xs)
    scores_t = dot_split(write, read, NT)
    later = lax.broadcasted_iota(jnp.int32, (extent, extent), 1) >= lax.broadcasted_iota(
        jnp.int32, (extent, extent), 0
    )
    lane = lax.broadcasted_iota(jnp.int32, (extent, LANES), 1)
    score_grad_t = jnp.zeros((extent, extent), f32)
    step_direct = jnp.zeros((extent, LANES), f32)
    cols_buf[...] = jnp.zeros_like(cols_buf)
    for head in range(heads):
        cols = slice(head * HEAD_DIM, (head + 1) * HEAD_DIM)
        gap_t = log_t[head : head + 1, :] - log_sum[:, head : head + 1]
        decay_t = jnp.exp(jnp.where(later, gap_t, -jnp.inf))
        mix_t = decay_t * scores_t
        pair_t = dot_split([x[:, cols] for x in xs_parts], [g[:, cols] for g in gy_parts], NT)
        both_t = decay_t * pair_t
        step_col = step[:, head : head + 1]
        score_grad_t = score_grad_t + both_t * step_col
        weight_t = both_t * scores_t
        step_direct = step_direct + jnp.where(lane == head, jnp.sum(weight_t, axis=1, keepdims=True), 0.0)
        cols_buf[head : head + 1, :] = jnp.sum(weight_t * step_col, axis=0, keepdims=True)
        bufs[:, cols] = dot((mix_t * step_col).astype(bf16), gy_parts[0][:, cols], NN)
    sums = head_sums(inner)
    spread = head_spread(inner)
    last = log_sum[extent - 1 : extent, :]
    tail_decay = jnp.exp(last - log_sum)
    tail = dot(tail_decay * step, spread, NN, highest)
    grown = dot(jnp.exp(log_sum), spread, NN, highest)
    gh = gh_ref[0]
    h_in = h_ref[0]
    gh_parts, h_parts = split_parts(gh), split_parts(h_in)
    tail_in = dot(write[0], gh_parts[0], NT)
    tail_direct = tail_decay * dot(xs * tail_in, sums, NN, highest)
    tail_weight = tail_direct * step
    state_part = grown * dot(read[0], h_parts[0], NT)
    state_weight = dot(gy * state_part, sums, NN, highest)
    kept = dot(sums, jnp.sum(gh * h_in, axis=1, keepdims=True) * jnp.ones((1, LANES), f32), TN, highest).T[0:1, :]
    log_grad = cols_buf[...].T - step * step_direct + state_weight - tail_weight
    end_grad = jnp.sum(tail_weight, axis=0, keepdims=True) + jnp.exp(last) * kept
    rate_arg_grad = dot(lower_ones(extent), log_grad, TN, highest) + end_grad
    step_grad = step_direct + tail_direct - rate * rate_arg_grad
    raw_grad = step_grad * jax.nn.sigmoid(raw)
    xs_grad = bufs[...] + tail * tail_in + skip_ref[3:4, :] * gy
    score_parts = split_parts(score_grad_t)
    write_grad = dot_split(score_parts, read, NN) + dot_split(split_parts(tail * xs), gh_parts, NN)
    read_grad = dot_split(score_parts, write, TN) + dot_split(split_parts(grown * gy), h_parts, NN)
    valid_lane = lax.broadcasted_iota(jnp.int32, (1, LANES), 1) < heads
    rate_grad = jnp.where(valid_lane, jnp.sum(-step * rate * rate_arg_grad, axis=0, keepdims=True), 0.0)
    raw_grad = jnp.where(valid_lane, raw_grad, 0.0)
    skip_grad = jnp.sum(dot(gy * xs, sums, NN, highest), axis=0, keepdims=True)

    @pl.when(first)
    def _():
        gc_ref[...] = jnp.zeros_like(gc_ref)
        ghp_ref[...] = jnp.zeros_like(ghp_ref)

    ghp_ref[0:1, :] += rate_grad
    ghp_ref[1:2, :] += jnp.sum(raw_grad, axis=0, keepdims=True)
    ghp_ref[2:3, :] += skip_grad
    gpad[0:8, :] = jnp.zeros((8, width), f32)
    gpad[extent + 8 :, :] = jnp.zeros((8, width), f32)
    gpad[8 : extent + 8, 0:inner] = xs_grad * slope[:, 0:inner]
    gpad[8 : extent + 8, inner : inner + STATE_DIM] = write_grad * slope[:, inner : inner + STATE_DIM]
    gpad[8 : extent + 8, inner + STATE_DIM :] = read_grad * slope[:, inner + STATE_DIM :]
    back = jnp.zeros((extent, width), f32)
    before = jnp.zeros((8, width), f32)
    pre_grad = gpad[8 : extent + 8, :]
    for tap in range(CONV_WIDTH):
        ahead = CONV_WIDTH - 1 - tap
        weight = cw_ref[tap : tap + 1, :]
        back = back + weight * gpad[8 + ahead : 8 + ahead + extent, :]
        before = before + weight * gpad[ahead : 8 + ahead, :]
        gc_ref[tap : tap + 1, :] += jnp.sum(pre_grad * padded[5 + tap : 5 + tap + extent, :], axis=0, keepdims=True)
    gc_ref[CONV_WIDTH : CONV_WIDTH + 1, :] += jnp.sum(pre_grad, axis=0, keepdims=True)
    gp_ref[0] = before
    gv_ref[:, :, :, 0:inner] = back[:, :inner].astype(bf16).reshape(zs, 1, rows, inner)
    gbc_ref[...] = back[:, inner:].reshape(zs, 1, rows, width - inner)
    gv_ref[:, :, :, inner:] = raw_grad.astype(bf16).reshape(zs, 1, rows, LANES)


def mixer_back(v, halo, cw, hp, skip, rw, dl, gy, h_in, gh):
    zs, slots, rows, cols = v.shape
    extent = zs * rows
    inner = gy.shape[2]
    width = cw.shape[1]
    return pl.pallas_call(
        functools.partial(back_kernel, inner),
        grid=(slots,),
        in_specs=[
            pl.BlockSpec((zs, 1, rows, cols), lambda s: (0, s, 0, 0)),
            pl.BlockSpec((1, 8, width), lambda s: (s, 0, 0)),
            pl.BlockSpec(cw.shape, lambda s: (0, 0)),
            pl.BlockSpec(hp.shape, lambda s: (0, 0)),
            pl.BlockSpec(skip.shape, lambda s: (0, 0)),
            pl.BlockSpec((1, extent, 2 * STATE_DIM), lambda s: (s, 0, 0)),
            pl.BlockSpec((1, extent, 2 * LANES), lambda s: (s, 0, 0)),
            pl.BlockSpec((1, extent, inner), lambda s: (s, 0, 0)),
            pl.BlockSpec((1, inner, STATE_DIM), lambda s: (s, 0, 0)),
            pl.BlockSpec((1, inner, STATE_DIM), lambda s: (s, 0, 0)),
        ],
        out_specs=[
            pl.BlockSpec((zs, 1, rows, inner + LANES), lambda s: (0, s, 0, 0)),
            pl.BlockSpec((zs, 1, rows, 2 * STATE_DIM), lambda s: (0, s, 0, 0)),
            pl.BlockSpec((1, 8, width), lambda s: (s, 0, 0)),
            pl.BlockSpec((8, width), lambda s: (0, 0)),
            pl.BlockSpec((8, LANES), lambda s: (0, 0)),
        ],
        out_shape=[
            jax.ShapeDtypeStruct((zs, slots, rows, inner + LANES), bf16),
            jax.ShapeDtypeStruct((zs, slots, rows, 2 * STATE_DIM), f32),
            jax.ShapeDtypeStruct((slots, 8, width), f32),
            jax.ShapeDtypeStruct((8, width), f32),
            jax.ShapeDtypeStruct((8, LANES), f32),
        ],
        scratch_shapes=[
            pltpu.VMEM((extent + 8, width), f32),
            pltpu.VMEM((extent + 16, width), f32),
            pltpu.VMEM((extent, inner), f32),
            pltpu.VMEM((LANES, extent), f32),
        ],
        compiler_params=kernel_params(56),
        cost_estimate=pl.CostEstimate(
            flops=slots * extent * inner * 5000, bytes_accessed=slots * extent * inner * 20, transcendentals=slots * extent * inner * 2
        ),
        name="mixer_back",
    )(v, halo, cw, hp, skip, rw, dl, gy, h_in, gh)


def expert_kernel(
    n_ref, g_ref, mask_ref, router_ref, up_ref, down_ref,
    moe_ref, back_ref, logit_ref, act_ref, hid_ref, moe_sum, back_sum, gates_buf, gate_grad,
):
    pair = pl.program_id(0)
    pairs = pl.num_programs(0)
    tokens = n_ref.shape[0]
    lane = lax.broadcasted_iota(jnp.int32, (tokens, LANES), 1)
    half = up_ref.shape[3] // 2

    @pl.when(pair == 0)
    def _():
        logits = dot(n_ref[...], router_ref[...], NN)
        chosen = mask_ref[...] > 0.0
        logits = jnp.where(chosen, logits, -jnp.inf)
        powers = jnp.exp(logits - jnp.max(logits, axis=1, keepdims=True))
        gates = powers / jnp.sum(powers, axis=1, keepdims=True)
        gates_buf[...] = jnp.where(lane < EXPERTS, gates, 1.0)
        moe_sum[...] = jnp.zeros_like(moe_sum)
        back_sum[...] = jnp.zeros_like(back_sum)
        gate_grad[...] = jnp.zeros_like(gate_grad)

    depth = up_ref.shape[0] * up_ref.shape[2]
    down = down_ref[...].reshape(depth, 2 * half)
    n_val = n_ref[...]
    gates = gates_buf[...]
    act_back = dot(g_ref[...], down, NN)
    for member in range(2):
        up = up_ref[:, member].reshape(depth, 2 * half)
        hidden = dot(n_val, up, NN)
        gate_part, up_part = hidden[:, :half], hidden[:, half:]
        logistic = jax.nn.sigmoid(gate_part)
        silu = gate_part * logistic
        act = (silu * up_part).astype(bf16).astype(f32)
        own = lane == 2 * pair + member
        gate = jnp.sum(jnp.where(own, gates, 0.0), axis=1, keepdims=True)
        part = act_back[:, member * half : (member + 1) * half]
        gate_grad[...] += jnp.where(own, jnp.sum(act * part, axis=1, keepdims=True), 0.0)
        act_ref[0, :, member * half : (member + 1) * half] = (gate * act).astype(bf16)
        part = part * gate
        hid_ref[member, :, :half] = (part * up_part * (logistic * (1.0 + gate_part * (1.0 - logistic)))).astype(bf16)
        hid_ref[member, :, half:] = (part * silu).astype(bf16)
        back_sum[...] += dot(hid_ref[member], up, NT)
    moe_sum[...] += dot(act_ref[0], down, NT)

    @pl.when(pair == pairs - 1)
    def _():
        gates_in = jnp.where(lane < EXPERTS, gates, 0.0)
        grads = gates_in * gate_grad[...]
        logit_grad = (grads - gates_in * jnp.sum(grads, axis=1, keepdims=True)).astype(bf16)
        logit_ref[...] = logit_grad
        back_ref[...] = (back_sum[...] + dot(logit_grad, router_ref[...], NT)).astype(bf16)
        moe_ref[...] = moe_sum[...].astype(bf16)


def experts(n_two, g_moe, mask, router, weights):
    tokens, width = n_two.shape
    count, blocks, rows, cols = weights.shape
    pairs = blocks // 3
    down_at = 2 * pairs
    return pl.pallas_call(
        expert_kernel,
        grid=(pairs,),
        in_specs=[
            pl.BlockSpec((tokens, width), lambda p: (0, 0)),
            pl.BlockSpec((tokens, width), lambda p: (0, 0)),
            pl.BlockSpec((tokens, LANES), lambda p: (0, 0)),
            pl.BlockSpec((width, LANES), lambda p: (0, 0)),
            pl.BlockSpec((count, 2, rows, cols), lambda p: (0, p, 0, 0)),
            pl.BlockSpec((count, 1, rows, cols), lambda p: (0, down_at + p, 0, 0)),
        ],
        out_specs=[
            pl.BlockSpec((tokens, width), lambda p: (0, 0)),
            pl.BlockSpec((tokens, width), lambda p: (0, 0)),
            pl.BlockSpec((tokens, LANES), lambda p: (0, 0)),
            pl.BlockSpec((1, tokens, cols), lambda p: (p, 0, 0)),
            pl.BlockSpec((2, tokens, cols), lambda p: (p, 0, 0)),
        ],
        out_shape=[
            jax.ShapeDtypeStruct((tokens, width), bf16),
            jax.ShapeDtypeStruct((tokens, width), bf16),
            jax.ShapeDtypeStruct((tokens, LANES), bf16),
            jax.ShapeDtypeStruct((pairs, tokens, cols), bf16),
            jax.ShapeDtypeStruct((2 * pairs, tokens, cols), bf16),
        ],
        scratch_shapes=[
            pltpu.VMEM((tokens, width), f32),
            pltpu.VMEM((tokens, width), f32),
            pltpu.VMEM((tokens, LANES), f32),
            pltpu.VMEM((tokens, LANES), f32),
        ],
        compiler_params=kernel_params(60),
        cost_estimate=pl.CostEstimate(
            flops=12 * tokens * width * cols * pairs, bytes_accessed=weights.size * 2 + tokens * width * 20, transcendentals=tokens * cols * pairs
        ),
        name="experts",
    )(n_two, g_moe, mask, router, weights, weights)


def expert_grad_kernel(up_blocks, chunks, start, *refs):
    n_refs, g_refs, h_refs, a_refs = (refs[i * chunks : (i + 1) * chunks] for i in range(4))
    out_ref = refs[4 * chunks]
    block = pl.program_id(0) + start
    count, _, rows, cols = out_ref.shape

    def summed(lefts, rights):
        total = dot(lefts[0][...], rights[0][0], NN)
        for left, right in zip(lefts[1:], rights[1:]):
            total = total + dot(left[...], right[0], NN)
        out_ref[...] = total.astype(bf16).reshape(count, 1, rows, cols)

    @pl.when(block < up_blocks)
    def _():
        summed(n_refs, h_refs)

    @pl.when(block >= up_blocks)
    def _():
        summed(g_refs, a_refs)


def expert_grads(n_list, g_list, hid_list, act_list, count, start, blocks):
    chunks = len(n_list)
    width, tokens = n_list[0].shape
    ups, _, cols = hid_list[0].shape
    whole = pl.BlockSpec((width, tokens), lambda b: (0, 0))
    return pl.pallas_call(
        functools.partial(expert_grad_kernel, ups, chunks, start),
        grid=(blocks,),
        in_specs=[whole] * (2 * chunks)
        + [pl.BlockSpec((1, tokens, cols), lambda b: (jnp.minimum(b + start, ups - 1), 0, 0))] * chunks
        + [pl.BlockSpec((1, tokens, cols), lambda b: (jnp.maximum(b + start - ups, 0), 0, 0))] * chunks,
        out_specs=pl.BlockSpec((count, 1, width // count, cols), lambda b: (0, b, 0, 0)),
        out_shape=jax.ShapeDtypeStruct((count, blocks, width // count, cols), bf16),
        compiler_params=kernel_params(48),
        cost_estimate=pl.CostEstimate(
            flops=2 * chunks * tokens * width * cols * blocks, bytes_accessed=blocks * width * cols * 2, transcendentals=0
        ),
        name="expert_grads",
    )(*n_list, *g_list, *hid_list, *act_list)


def body(
    block_input,
    out_grad,
    lengths,
    routes,
    norm1_gain,
    w_zx,
    w_bc,
    w_dt,
    conv_x,
    conv_bc,
    head_params,
    gate_gain,
    w_out,
    norm2_gain,
    w_router,
    w_gu,
    w_dn,
    s_gu,
    s_dn,
):
    zs = lax.axis_size("tensor")
    pieces = lax.axis_size("dp")
    own = lax.axis_index("tensor")
    wide_index = lax.axis_index("dp")
    rows = block_input.shape[0]
    piece_rows = rows * zs
    heads = HEAD_COUNT // zs
    inner = INNER_DIM // zs
    width = inner + 2 * STATE_DIM
    shard = D_MODEL // pieces
    half = w_gu.shape[3]
    rim = CONV_WIDTH - 1
    per = SLOT_COUNT // CHUNKS
    tokens = per * rows
    chunk_ids = range(CHUNKS)

    enter_shard = jnp.concatenate(
        [w_zx[:, 1], w_bc, jnp.pad(w_dt, ((0, 0), (0, LANES - heads)))], axis=1
    )
    side_shard = jnp.concatenate([w_zx[:, 0], w_out.T], axis=1)
    router_shard = jnp.pad(w_router, ((0, 0), (0, LANES - EXPERTS)))
    expert_shard = jnp.concatenate(
        [
            w_gu.reshape(EXPERTS, shard, 2 * half),
            s_gu.reshape(shard, 2, 2, half).transpose(2, 0, 1, 3).reshape(2, shard, 2 * half),
            w_dn.reshape(EXPERTS // 2, 2 * half, shard).transpose(0, 2, 1),
            s_dn.T[None],
        ],
        axis=0,
    )
    full_enter = weight_gather(enter_shard).reshape(D_MODEL, width + LANES)
    full_side = weight_gather(side_shard).reshape(D_MODEL, 2 * inner)
    full_z, full_out = full_side[:, :inner], full_side[:, inner:]
    gains = jnp.stack([norm1_gain, norm2_gain], axis=1).astype(f32)
    gains = lax.all_gather(gains, "dp", axis=0, tiled=True)
    gain_one, gain_two = gains[:, 0], gains[:, 1]
    full_router = weight_gather(router_shard).reshape(D_MODEL, LANES)
    full_expert = weight_gather(expert_shard)

    positions = wide_index * piece_rows + own * rows + jnp.arange(rows, dtype=jnp.int32)
    valid = (positions[None, :] < lengths[:, None]).astype(f32)[:, :, None]
    u_slots = jnp.transpose(block_input, (1, 0, 2)).astype(f32)
    grad_slots = jnp.transpose(out_grad, (1, 0, 2)).astype(f32) * valid

    def part(values, c):
        return values[c * per : (c + 1) * per].reshape((tokens,) + values.shape[2:])

    conv_w = jnp.pad(jnp.concatenate([conv_x, conv_bc], axis=1), ((0, 8 - CONV_WIDTH - 1), (0, 0)))
    hp = jnp.pad(head_params, ((0, 5), (0, LANES - heads)))
    skip = jnp.pad(jnp.repeat(head_params[2], HEAD_DIM)[None], ((3, 4), (0, 0)))
    gain_row = gate_gain[None]

    hot = jnp.sum(
        (routes[..., None] == jnp.arange(LANES, dtype=jnp.int32)).astype(f32), axis=2
    )
    hot = jnp.transpose(hot.reshape(zs, rows, SLOT_COUNT, LANES), (0, 2, 1, 3))
    hot_at = by_distance(hot)

    u, valid_c, grad_c, n_one, n_one_t, v, halo, z = [], [], [], [], [], [], [], []
    for c in chunk_ids:
        u.append(part(u_slots, c))
        valid_c.append(part(valid, c))
        grad_c.append(part(grad_slots, c))
        normed = rms_scale(u[c], gain_one).astype(bf16)
        n_one.append(in_order(line_gather(normed)))
    for c in chunk_ids:
        flat = n_one[c].reshape(zs * tokens, D_MODEL)
        v.append(dot(flat, full_enter, NN).reshape(zs, per, rows, width + LANES))
        rim_rows = n_one[c].reshape(zs, per, rows, D_MODEL)[zs - 1, :, rows - rim :]
        prior = dot(passed_along(rim_rows, "dp", 1).reshape(per * rim, D_MODEL), full_enter[:, :width], NN)
        halo.append(jnp.pad(prior.reshape(per, rim, width), ((0, 0), (8 - rim, 0), (0, 0))))
    entered = [mixer_enter(v[c], halo[c], conv_w, hp, inner) for c in chunk_ids]
    g_moe = [jnp.concatenate(line_gather(after(grad_c[c].astype(bf16), n_one[c])), axis=0) for c in chunk_ids]
    resid, mixed_all, y_all, h_all, decay_all, tok_all, gg_all, n_two = [], [], [], [], [], [], [], []
    for c in chunk_ids:
        xs, rw, dl, s_local = entered[c]
        h_in, decay = states_forward(s_local, dl[:, piece_rows - 1, LANES : LANES + heads])
        h_in = after(h_in, g_moe[c])
        z.append(dot(n_one[c].reshape(zs * tokens, D_MODEL), full_z, NN).reshape(zs, per, rows, inner))
        y, gg, squares = mixer_leave(xs, rw, dl, h_in, z[c], skip, gain_row)
        square_sum = lax.psum(squares[:, :, 0], "tensor")
        inv_all = lax.rsqrt(square_sum / INNER_DIM + norm_eps)
        inv_own = lax.dynamic_slice_in_dim(inv_all, own * rows, rows, 1).reshape(tokens, 1)
        product = dot(gg.reshape(zs * tokens, inner), full_out, NT).astype(bf16)
        mixed = line_scatter(by_distance(product.reshape(zs, tokens, D_MODEL))) * inv_own
        resid.append(u[c] + mixed)
        mixed_all.append(mixed)
        y_all.append(y)
        h_all.append(h_in)
        decay_all.append(decay)
        tok_all.append(inv_all)
        gg_all.append(gg)
        normed = rms_scale(resid[c], gain_two).astype(bf16)
        n_two.append(jnp.concatenate(line_gather(normed), axis=0))
    moe_part, back_part, logit_grads, acts, hids = [], [], [], [], []
    for c in chunk_ids:
        mask = jnp.concatenate([part(hot_at(k), c) for k in range(zs)], axis=0)
        results = experts(n_two[c], g_moe[c], mask, full_router, full_expert)
        moe_part.append(results[0].reshape(zs, tokens, D_MODEL))
        back_part.append(results[1].reshape(zs, tokens, D_MODEL))
        logit_grads.append(results[2])
        acts.append(results[3])
        hids.append(results[4])

    def two_back(values, gain_vec):
        return jax.vjp(rms_scale, values, gain_vec)[1]

    n_two_t, g_moe_t = [n.T for n in n_two], [g.T for g in g_moe]
    third = (EXPERTS + 2) // 2
    expert_grad = [
        expert_grads(n_two_t, g_moe_t, hids, acts, pieces, start, third) for start in (0, third, 2 * third)
    ]
    resid_grad, g_mixed, gain_two_grad = [], [], 0.0
    unmixed, gate_gain_grad = [], 0.0
    for c in chunk_ids:
        n_two_grad = line_scatter(lambda k: back_part[c][k])
        from_norm, gain_grad = two_back(resid[c], gain_two)(n_two_grad)
        gain_two_grad = gain_two_grad + gain_grad
        resid_grad.append(grad_c[c] + from_norm)
        low = resid_grad[c].astype(bf16)
        if c == 0:
            low = after(low, expert_grad[0], expert_grad[1])
        g_mixed.append(in_order(line_gather(low)))
        grad = dot(g_mixed[c].reshape(zs * tokens, D_MODEL), full_out, NN).reshape(zs, per, rows, inner)
        if c == 0:
            grad = after(grad, expert_grad[2])
        xs, rw, dl, _ = entered[c]
        inv_all = tok_all[c]
        y_like = jnp.transpose(y_all[c].reshape(per, zs, rows, inner), (1, 0, 2, 3))
        cross = jnp.sum(grad * gain_row * y_like * jax.nn.silu(z[c]), axis=-1)
        cross = lax.psum(jnp.transpose(cross, (1, 0, 2)).reshape(per, piece_rows), "tensor")
        tok = jnp.stack([inv_all, cross * (inv_all * inv_all * inv_all) / INNER_DIM], axis=-1)
        gy, gz, g_local, gg_grad = mixer_unmix(grad, y_all[c], z[c], rw, dl, tok, gain_row)
        gate_gain_grad = gate_gain_grad + gg_grad[0]
        unmixed.append((gy, gz, g_local))

    moe_part = [after(moe_part[c], g_mixed[c]) for c in chunk_ids]
    moe = [line_scatter(lambda k: moe_part[c][k]) for c in chunk_ids]
    output = [resid[c] + moe[c] for c in chunk_ids]
    stat_terms = sum(
        jnp.stack(
            [
                jnp.sum(valid_c[c] * output[c] * output[c]),
                jnp.sum(valid_c[c] * mixed_all[c] * mixed_all[c]),
                jnp.sum(valid_c[c] * moe[c] * moe[c]),
            ]
        )
        for c in chunk_ids
    )
    router_grad = sum(dot(n_two[c], logit_grads[c], TN)[:, :EXPERTS] for c in chunk_ids)

    def rows_of(values):
        return jnp.concatenate([v.reshape(zs * tokens, -1) for v in values], axis=0)

    inv_rows = [
        jnp.transpose(tok_all[c].reshape(per, zs, rows), (1, 0, 2)).reshape(zs * tokens, 1) for c in chunk_ids
    ]
    scaled = [
        (g_mixed[c].reshape(zs * tokens, D_MODEL).astype(f32) * inv_rows[c]).astype(bf16) for c in chunk_ids
    ]
    out_w_grad = dot(rows_of(scaled), rows_of(gg_all), TN)

    z_grads, v_grads, bc_grads, conv_grad, head_grad = [], [], [], 0.0, 0.0
    full_x = jnp.concatenate([full_enter[:, :inner], full_enter[:, width:]], axis=1)
    full_bc = full_enter[:, inner:width]
    full_bc = jnp.concatenate([full_bc, full_bc], axis=1)
    for c in chunk_ids:
        gy, gz, g_local = unmixed[c]
        xs, rw, dl, _ = entered[c]
        gh = states_backward(g_local, decay_all[c])
        gv, gbc, g_rim, gc, ghp = mixer_back(
            v[c], halo[c], conv_w, hp, skip, rw, dl, gy, h_all[c], gh
        )
        conv_grad = conv_grad + gc
        head_grad = head_grad + ghp
        following = passed_along(g_rim[:, 8 - rim :].astype(bf16), "dp", -1)
        following = following.astype(f32)
        edge = gv[zs - 1, :, rows - rim :, :inner].astype(f32) + following[:, :, :inner]
        gv = lax.dynamic_update_slice(gv, edge.astype(bf16)[None], (zs - 1, 0, rows - rim, 0))
        edge = gbc[zs - 1, :, rows - rim :] + following[:, :, inner:]
        gbc = lax.dynamic_update_slice(gbc, edge[None], (zs - 1, 0, rows - rim, 0))
        z_grads.append(gz)
        v_grads.append(gv)
        bc_grads.append(jnp.concatenate(split_parts(gbc), axis=-1))
    u_grad, gain_one_grad = [], 0.0
    for c in chunk_ids:
        n_grad = (
            dot(z_grads[c].reshape(zs * tokens, inner), full_z, NT)
            + dot(v_grads[c].reshape(zs * tokens, inner + LANES), full_x, NT)
            + dot(bc_grads[c].reshape(zs * tokens, 4 * STATE_DIM), full_bc, NT)
        )
        n_grad = n_grad.astype(bf16).reshape(zs, tokens, D_MODEL)
        from_norm, gain_grad = two_back(u[c], gain_one)(line_scatter(by_distance(n_grad)))
        gain_one_grad = gain_one_grad + gain_grad
        u_grad.append(resid_grad[c] + from_norm)
    n_rows = rows_of(n_one)
    z_w_grad = dot(n_rows, rows_of(z_grads), TN)
    enter_w_grad = dot(n_rows, rows_of(v_grads), TN)
    bc_w_grad = dot(n_rows, rows_of(bc_grads), TN)
    bc_w_grad = bc_w_grad[:, : 2 * STATE_DIM] + bc_w_grad[:, 2 * STATE_DIM :]
    side_grad = weight_scatter(
        jnp.concatenate([z_w_grad, out_w_grad], axis=1).reshape(pieces, shard, 2 * inner)
    ).astype(f32)
    enter_grad = weight_scatter(enter_w_grad.reshape(pieces, shard, inner + LANES)).astype(f32)

    column = own * inner
    conv_x_full = lax.dynamic_update_slice(
        jnp.zeros((CONV_WIDTH + 1, INNER_DIM), f32), conv_grad[: CONV_WIDTH + 1, :inner], (jnp.int32(0), column)
    )
    gate_full = lax.dynamic_update_slice(jnp.zeros((INNER_DIM,), f32), gate_gain_grad, (column,))
    head_full = lax.dynamic_update_slice(
        jnp.zeros((3, HEAD_COUNT), f32), head_grad[:3, :heads], (jnp.int32(0), own * heads)
    )
    both = ("dp", "tensor")
    bc_grad = lax.psum_scatter(bc_w_grad, both, scatter_dimension=0, tiled=True)
    shared_grads = (
        lax.psum_scatter(gain_one_grad, both, scatter_dimension=0, tiled=True),
        lax.psum_scatter(conv_x_full, both, scatter_dimension=1, tiled=True),
        lax.psum_scatter(conv_grad[: CONV_WIDTH + 1, inner:], both, scatter_dimension=1, tiled=True),
        lax.psum_scatter(gate_full, both, scatter_dimension=0, tiled=True),
        lax.psum_scatter(gain_two_grad, both, scatter_dimension=0, tiled=True),
        lax.psum_scatter(router_grad, both, scatter_dimension=0, tiled=True),
    )
    stat_sum, head_sum = lax.psum((stat_terms, head_full), both)
    stats = jnp.sqrt(stat_sum / (jnp.sum(lengths).astype(f32) * D_MODEL))

    def placed_back(values):
        whole = jnp.concatenate([value.astype(bf16).reshape(per, rows, D_MODEL) for value in values], axis=0)
        return jnp.transpose(whole, (1, 0, 2))

    expert_grad = jnp.concatenate([weight_scatter(grads) for grads in expert_grad], axis=0).astype(f32)
    ups, pairs = EXPERTS + 2, EXPERTS // 2
    return (
        placed_back(output),
        placed_back(u_grad),
        shared_grads[0],
        jnp.stack([side_grad[:, :inner], enter_grad[:, :inner]], axis=1),
        bc_grad,
        enter_grad[:, inner : inner + heads],
        shared_grads[1],
        shared_grads[2],
        head_sum,
        shared_grads[3],
        side_grad[:, inner:].T,
        shared_grads[4],
        shared_grads[5],
        expert_grad[:EXPERTS].reshape(EXPERTS, shard, 2, half),
        expert_grad[ups : ups + pairs].transpose(0, 2, 1).reshape(EXPERTS, half, shard),
        expert_grad[EXPERTS:ups].reshape(2, shard, 2, half).transpose(1, 2, 0, 3).reshape(shard, 2, 2 * half),
        expert_grad[ups + pairs].T,
        stats,
    )


def solution(mesh):
    both = ("dp", "tensor")
    placed = (
        P(both, None, None),
        P(both, None, None),
        P(),
        P("dp", None, None),
        P("dp"),
        P("dp", None, "tensor"),
        P("dp", None),
        P("dp", "tensor"),
        P(None, "tensor"),
        P(),
        P(None, "tensor"),
        P("tensor"),
        P("tensor", "dp"),
        P("dp"),
        P("dp", None),
        P(None, "dp", None, "tensor"),
        P(None, "tensor", "dp"),
        P("dp", None, "tensor"),
        P("tensor", "dp"),
    )
    return jax.shard_map(
        body,
        mesh=mesh,
        in_specs=placed,
        out_specs=(
            P(both, None, None),
            P(both, None, None),
            P(both),
            P("dp", None, "tensor"),
            P(both, None),
            P("dp", "tensor"),
            P(None, both),
            P(None, both),
            P(),
            P(both),
            P("tensor", "dp"),
            P(both),
            P(both, None),
            P(None, "dp", None, "tensor"),
            P(None, "tensor", "dp"),
            P("dp", None, "tensor"),
            P("tensor", "dp"),
            P(),
        ),
        check_vma=False,
    )
```

time: 2370 us -> 1330 us (0.56)
  local copies, waits for them, and re-layouts: 556 us -> 123 us
  waiting for transfers between devices: 901 us -> 531 us
  matrix products: 303 us -> 59.4 us
  other arithmetic: 337 us -> 96.2 us
  Pallas kernels: 0 us -> 202 us
  starting transfers between devices: 128 us -> 174 us
    reduce_scatter x11 -> x6, waiting for transfers between devices: 593 us -> 299 us  [the longest x5 200 us: weight_scatter(): lax.psum_scatter(grads.astype(bf16), 'dp', scatter_dimension=0, tiled=False)]
    dot_general x43 -> x12, matrix products: 303 us -> 56.6 us  [dot(): lax.dot_general(a, b, (dims, ((), ())), precision=precision, preferred_el...]
    gather x5 -> x0, local copies, waits for them, and re-layouts: 231 us -> none  [the longest x1 55.6 us: body(): jnp.take(produced, slot_ids, axis=0).reshape(token_rows, TOP_K, D_MODEL)]
    pallas_call x0 -> x10, Pallas kernels: none -> 202 us  [the longest x1 72 us: experts(): pl.pallas_call(expert_kernel, grid=(pairs,), in_specs=[pl.BlockSpec((toke...]
    ppermute x0 -> x48, waiting for transfers between devices: none -> 184 us  [the longest x12 70.2 us: line_scatter(): right = lax.ppermute(to_right, 'tensor', [(a, a + 1) for a in range(k)])]
    ppermute x16 -> x2, waiting for transfers between devices: 177 us -> 0.01 us  [passed_along(): lax.ppermute(value, axis, [(source, source + steps) for source in range(f...]
    ppermute x0 -> x48, starting transfers between devices: none -> 158 us  [the longest x12 67.4 us: line_scatter(): right = lax.ppermute(to_right, 'tensor', [(a, a + 1) for a in range(k)])]
    reduce_sum x16 -> x4, other arithmetic: 158 us -> 8.27 us  [the longest x1 5.48 us: body(): jnp.sum(valid_c[c] * output[c] * output[c])]
  transfers between devices with their start and end apart: 39 -> 64, of which waited for: 27 -> 28; matrix products, arithmetic and copies ran while one was open for 48% -> 18% of each run, Pallas kernels for 0% -> 9%
where the time goes in v1:
time: 1330 us; the launch traced here: 1320 us
  waiting for transfers between devices  531 us (40%)
  Pallas kernels  202 us (15%)
  starting transfers between devices  174 us (13%)
  local copies, waits for them, and re-layouts  123 us (9%)
  blocking collectives  120 us (9%)
  other arithmetic  96.2 us (7%)
  matrix products  59.4 us (4%)
  between operations  16.8 us (1%)
    reduce_scatter x5, waiting for transfers between devices, weight_scatter(): lax.psum_scatter(grads.astype(bf16), 'dp', scatter_dimension=0, tiled=False)  200 us
    reduce_scatter x1, waiting for transfers between devices, body(): bc_grad = lax.psum_scatter(bc_w_grad, both, scatter_dimension=0, tiled=True)  99.6 us
    pallas_call x1, Pallas kernels, experts(): pl.pallas_call(expert_kernel, grid=(pairs,), in_specs=[pl.BlockSpec((toke...  72 us
    ppermute x12, waiting for transfers between devices, line_scatter(): right = lax.ppermute(to_right, 'tensor', [(a, a + 1) for a in range(k)])  70.2 us
    ppermute x12, starting transfers between devices, line_scatter(): right = lax.ppermute(to_right, 'tensor', [(a, a + 1) for a in range(k)])  67.4 us
    ppermute x12, waiting for transfers between devices, line_gather(): right = lax.ppermute(right, 'tensor', [(a, a + 1) for a in range(size - 1)])  62.9 us
    ppermute x12, starting transfers between devices, line_gather(): right = lax.ppermute(right, 'tensor', [(a, a + 1) for a in range(size - 1)])  57.7 us
    dot_general x12, matrix products, dot(): lax.dot_general(a, b, (dims, ((), ())), precision=precision, preferred_el...  56.6 us
  transfers between devices with their start and end apart: 64, of which 28 were waited for; matrix products, arithmetic and copies ran while one was open for 18% of the time, Pallas kernels for 9%

profile of v1, /device:TPU:0, one launch (start us, length us, event | category | flops | bytes accessed | tf_op | source)
XLA Modules:
  0.0 1321.9 jit_solution(1950696198814739112)
XLA Ops:
  20.1 10.4 all-gather.4
  33.2 4.4 collective-permute-start
  38.9 15.4 %collective-permute-done = bf16[256,1536]{0,1:T(8,128)(2,1)} collective-permute-done((bf16[256,1536]{0,1:T(8,128)(2,1)}, bf16[256,1536]{0,1:T(8,128)(2,1)}, u32[]{:S(2)}, u32[]{:S(2)}) %collective-permute-start) | collective-permute-done | bytes 786464 | tf_op jit(solution)/shard_map/ppermute | solution.py:39
  54.3 5.3 collective-permute-start.1
  63.1 12.4 collective-permute-done.1
  75.5 4.4 collective-permute-start.2
  86.5 9.2 collective-permute-done.2
  98.1 4.5 collective-permute-done.5
  122.9 7.9 fusion.v_ref
  130.9 12.0 mixer_enter.1
  150.8 5.8 collective-permute-start.8
  156.6 15.4 %collective-permute-done.11 = bf16[256,1536]{0,1:T(8,128)(2,1)} collective-permute-done((bf16[256,1536]{0,1:T(8,128)(2,1)}, bf16[256,1536]{0,1:T(8,128)(2,1)}, u32[]{:S(2)}, u32[]{:S(2)}) %collective-permute-start.11) | collective-permute-done | bytes 786464 | tf_op jit(solution)/shard_map/ppermute | solution.py:40
  173.7 5.3 collective-permute-start.9
  179.0 9.3 all-to-all-done
  207.0 6.9 fusion.11.z_ref
  213.8 18.5 %all-to-all-done.1 = f32[8,384,128]{2,1,0:T(8,128)S(1)} async-done(((f32[8,384,128]{2,1,0:T(8,128)}), f32[8,384,128]{2,1,0:T(8,128)S(1)}, u32[]{:S(2)}, u32[]{:S(2)}) %all-to-all-start.1) | async-done | bytes 1572896 | tf_op jit(solution)/shard_map/all_to_all | solution.py:226
  234.2 11.2 mixer_leave.1
  258.4 9.3 collective-permute-done.13
  270.4 5.1 collective-permute-start.14
  278.0 10.8 collective-permute-done.14
  289.8 9.8 collective-permute-start.15
  299.9 19.1 %psum.28 = f32[4,256]{1,0:T(4,128)S(1)} all-reduce(f32[4,256]{1,0:T(4,128)S(1)} %slice_reduce_fusion), channel_id=1, replica_groups=mesh['dp'=8,'tensor'=4] {'tensor'}, use_global_device_ids=true, to_apply=%region_1.2 | all-reduce | flops 1024 | bytes 8192 | tf_op jit(solution)/shard_map/psum | solution.py:764
  325.8 4.6 collective-permute-start.19
  330.4 11.8 collective-permute-done.22
  343.5 5.4 collective-permute-start.20
  348.9 11.0 collective-permute-done.23
  361.3 5.4 collective-permute-start.21
  366.9 14.7 %all-gather.2.router_ref = bf16[1536,128]{1,0:T(8,128)(2,1)} all-gather(bf16[192,128]{1,0:T(8,128)(2,1)S(1)} %pad.34), channel_id=4, replica_groups=mesh['dp'=8,'tensor'=4] {'dp'}, dimensions={0}, use_global_device_ids=true | all-gather | bytes 442368 | tf_op jit(solution)/shard_map/all_gather | solution.py:75
  396.3 72.0 %experts.1 = (bf16[1024,1536]{1,0:T(8,128)(2,1)}, bf16[1024,1536]{1,0:T(8,128)(2,1)}, bf16[1024,128]{1,0:T(8,128)(2,1)}, bf16[9,1024,256]{2,1,0:T(8,128)(2,1)}, bf16[18,1024,256]{2,1,0:T(8,128)(2,1)}) custom-call(bf16[1024,1536]{1,0:T(8,128)(2,1)} %copy.391.n_ref, bf16[1024,1536]{1,0:T(8,128)(2,1)} %copy.392.g_ref, f32[1024,128]{1,0:T(8,128)} %pad_maximum_fusion.8.mask_ref, ...), custom_call_target="tpu_custom_call" | custom-call | flops 43486543872 | bytes 52690944 | tf_op jit(solution)/shard_map/experts/pallas_call | solution.py:582
  474.5 16.3 %collective-permute-done.25 = bf16[256,1536]{0,1:T(8,128)(2,1)S(1)} collective-permute-done((bf16[256,1536]{0,1:T(8,128)(2,1)S(1)}, bf16[256,1536]{0,1:T(8,128)(2,1)S(1)}, u32[]{:S(2)}, u32[]{:S(2)}) %collective-permute-start.25) | collective-permute-done | bytes 786464 | tf_op jit(solution)/shard_map/ppermute | solution.py:54
  491.2 4.4 collective-permute-start.26
  497.0 15.3 %collective-permute-done.26 = bf16[256,1536]{0,1:T(8,128)(2,1)S(1)} collective-permute-done((bf16[256,1536]{0,1:T(8,128)(2,1)S(1)}, bf16[256,1536]{0,1:T(8,128)(2,1)S(1)}, u32[]{:S(2)}, u32[]{:S(2)}) %collective-permute-start.26) | collective-permute-done | bytes 786464 | tf_op jit(solution)/shard_map/ppermute | solution.py:54
  515.2 8.1 collective-permute-start.27
  523.3 13.5 %expert_grads.3 = bf16[8,9,192,256]{3,2,1,0:T(8,128)(2,1)} custom-call(bf16[1536,1024]{1,0:T(8,128)(2,1)S(1)} %fusion.84.refs_0_, bf16[1536,1024]{1,0:T(8,128)(2,1)} %get-tuple-element.226.refs_1_, bf16[18,1024,256]{2,1,0:T(8,128)(2,1)} %get-tuple-element.54.refs_2_, bf16[9,1024,256]{2,1,0:T(8,128)(2,1)} %get-tuple-element.55.refs_3_), custom_call_target="tpu_custom_call" | custom-call | flops 7247757312 | bytes 7077888 | tf_op jit(solution)/shard_map/expert_grads/pallas_call | solution.py:647
  536.8 13.5 %expert_grads.4 = bf16[8,9,192,256]{3,2,1,0:T(8,128)(2,1)} custom-call(bf16[1536,1024]{1,0:T(8,128)(2,1)S(1)} %fusion.84.refs_0_, bf16[1536,1024]{1,0:T(8,128)(2,1)} %get-tuple-element.226.refs_1_, bf16[18,1024,256]{2,1,0:T(8,128)(2,1)} %get-tuple-element.54.refs_2_, bf16[9,1024,256]{2,1,0:T(8,128)(2,1)} %get-tuple-element.55.refs_3_), custom_call_target="tpu_custom_call" | custom-call | flops 7247757312 | bytes 7077888 | tf_op jit(solution)/shard_map/expert_grads/pallas_call | solution.py:647
  561.2 13.6 %collective-permute-done.31 = bf16[256,1536]{0,1:T(8,128)(2,1)S(1)} collective-permute-done((bf16[256,1536]{0,1:T(8,128)(2,1)S(1)}, bf16[256,1536]{0,1:T(8,128)(2,1)S(1)}, u32[]{:S(2)}, u32[]{:S(2)}) %collective-permute-start.31) | collective-permute-done | bytes 786464 | tf_op jit(solution)/shard_map/ppermute | solution.py:39
  574.8 5.3 collective-permute-start.32
  581.3 11.9 collective-permute-done.32
  593.3 5.4 collective-permute-start.33
  598.6 13.5 %expert_grads.5 = bf16[8,9,192,256]{3,2,1,0:T(8,128)(2,1)} custom-call(bf16[1536,1024]{1,0:T(8,128)(2,1)S(1)} %fusion.84.refs_0_, bf16[1536,1024]{1,0:T(8,128)(2,1)} %get-tuple-element.226.refs_1_, bf16[18,1024,256]{2,1,0:T(8,128)(2,1)} %get-tuple-element.54.refs_2_, bf16[9,1024,256]{2,1,0:T(8,128)(2,1)} %get-tuple-element.55.refs_3_), custom_call_target="tpu_custom_call" | custom-call | flops 7247757312 | bytes 7077888 | tf_op jit(solution)/shard_map/expert_grads/pallas_call | solution.py:647
  626.3 6.9 collective-permute-done.36
  640.4 5.4 fusion.9.gn_ref
  647.7 8.3 psum.29
  656.3 9.3 mixer_unmix.1
  665.6 23.7 %all_to_all.20.got_ref = f32[8,384,128]{2,1,0:T(8,128)S(1)} all-to-all(f32[8,384,128]{2,1,0:T(8,128)S(1)} %bitcast.272), channel_id=1, replica_groups=mesh['dp'=8,'tensor'=4] {'dp'}, dimensions={0} | all-to-all | bytes 3145728 | tf_op jit(solution)/shard_map/all_to_all | solution.py:226
  690.9 4.6 all-to-all-start.3
  698.7 17.9 %all-to-all-done.3 = f32[8,384,128]{2,1,0:T(8,128)} async-done(((f32[8,384,128]{2,1,0:T(8,128)}), f32[8,384,128]{2,1,0:T(8,128)}, u32[]{:S(2)}, u32[]{:S(2)}) %all-to-all-start.3) | async-done | bytes 1572896 | tf_op jit(solution)/shard_map/all_to_all | solution.py:226
  716.5 53.9 %mixer_back.1 = (bf16[4,4,64,896]{3,2,1,0:T(8,128)(2,1)}, f32[4,4,64,256]{3,2,1,0:T(8,128)}, f32[4,8,1024]{2,1,0:T(8,128)}, f32[8,1024]{1,0:T(8,128)}, f32[8,128]{1,0:T(8,128)}) custom-call(f32[4,4,64,1152]{3,2,1,0:T(8,128)} %fusion.v_ref, f32[4,8,1024]{2,1,0:T(8,128)} %copy-done.10, f32[8,1024]{1,0:T(8,128)} %copy-done.11, f32[8,128]{1,0:T(8,128)} %copy-done.13, ...), custom_call_target="tpu_custom_call" | custom-call | flops 3932160000 | bytes 15728640 | tf_op jit(solution)/shard_map/mixer_back/pallas_call | solution.py:479
  782.9 7.4 convolution_convert_fusion.3
  795.0 5.0 collective-permute-start.37
  810.8 6.7 copy.419
  817.5 6.2 fusion.15
  833.0 5.4 fusion.5
  862.7 5.3 collective-permute-done.44
  877.0 7.7 collective-permute-start.45
  892.4 12.4 collective-permute-done.45
  906.0 14.4 %collective-permute-start.46 = (bf16[256,1536]{0,1:T(8,128)(2,1)}, bf16[256,1536]{0,1:T(8,128)(2,1)}, u32[]{:S(2)}, u32[]{:S(2)}) collective-permute-start(bf16[256,1536]{0,1:T(8,128)(2,1)} %add_convert_fusion.2), channel_id=1, source_target_pairs={{0,1},{1,2},{2,3},{4,5},{5,6},{6,7},{8,9},{9,10},{10,11},{12,13},{... | collective-permute-start | bytes 2359304 | tf_op jit(solution)/shard_map/ppermute | solution.py:54
  924.9 5.5 fusion.29
  942.4 44.0 %all-reduce.11 = (f32[1536]{0:T(1024)S(1)}, f32[5,256]{1,0:T(8,128)S(1)}, f32[3,48]{1,0:T(4,128)}, f32[3072]{0:T(1024)S(1)}, f32[1536]{0:T(1024)S(1)}, /*index=5*/f32[3]{0:T(128)S(1)}) all-reduce(f32[1536]{0:T(1024)S(1)} %get-tuple-element.200, f32[5,256]{1,0:T(8,128)S(1)} %slice.182, ...), channel_id=6, replica_groups=mesh['dp'=8,'tensor'=4] {'dp','tensor'}, use_global_device_ids=true, to_apply=%region_9.10.clone | all-reduce | flops 7571 | bytes 60568
  989.3 47.8 %reduce-scatter.22.cloned.1.call-done = bf16[1,9,192,256]{3,2,1,0:T(8,128)(2,1)} async-done(((bf16[8,9,192,256]{3,2,1,0:T(8,128)(2,1)}), bf16[1,9,192,256]{3,2,1,0:T(8,128)(2,1)}) %reduce-scatter.22.cloned.1.call-update) | async-done | bytes 884752 | tf_op jit(solution)/shard_map/reduce_scatter | solution.py:79
  1037.1 69.0 %reduce-scatter.20.cloned.1.call-done = bf16[1,9,192,256]{3,2,1,0:T(8,128)(2,1)} async-done(((bf16[8,9,192,256]{3,2,1,0:T(8,128)(2,1)}), bf16[1,9,192,256]{3,2,1,0:T(8,128)(2,1)}) %reduce-scatter.20.cloned.1.call-update) | async-done | bytes 884752 | tf_op jit(solution)/shard_map/reduce_scatter | solution.py:79
  1126.8 27.4 %reduce-scatter.16.cloned.1.call-done = bf16[1,192,896]{2,1,0:T(8,128)(2,1)} async-done(((bf16[8,192,896]{2,1,0:T(8,128)(2,1)}), bf16[1,192,896]{2,1,0:T(8,128)(2,1)}) %reduce-scatter.16.cloned.1.call-update) | async-done | bytes 344080 | tf_op jit(solution)/shard_map/reduce_scatter | solution.py:79
  1156.0 55.4 %reduce-scatter.14.cloned.1.call-done = bf16[1,192,1536]{2,1,0:T(8,128)(2,1)} async-done(((bf16[8,192,1536]{2,1,0:T(8,128)(2,1)}), bf16[1,192,1536]{2,1,0:T(8,128)(2,1)}) %reduce-scatter.14.cloned.1.call-update) | async-done | bytes 589840 | tf_op jit(solution)/shard_map/reduce_scatter | solution.py:79
  1215.5 99.6 %reduce-scatter.18.cloned.1.call-done = f32[48,256]{1,0:T(8,128)} async-done(((f32[1536,256]{1,0:T(8,128)}), f32[48,256]{1,0:T(8,128)}) %reduce-scatter.18.cloned.1.call-update) | async-done | bytes 49168 | tf_op jit(solution)/shard_map/reduce_scatter | solution.py:898
  (514 shorter events, 297.8 us)
Async XLA Ops:
  7.2 112.8 %all-gather.9.cloned.1.call-start = ((), (), s32[]{:S(2)}) async-start(), calls=%async_computation.18 | async-start | bytes 3981312 | tf_op jit(solution)/shard_map/all_gather | solution.py:75
  11.4 195.6 %all-gather.11.cloned.1.call-start = ((), (), s32[]{:S(2)}) async-start(), calls=%async_computation.19 | async-start | bytes 5308416 | tf_op jit(solution)/shard_map/all_gather | solution.py:75
  12.3 383.9 %all-gather.13.cloned.1.call-start = ((), (), s32[]{:S(2)}) async-start(), calls=%async_computation.20 | async-start | bytes 23887872 | tf_op jit(solution)/shard_map/all_gather | solution.py:75
  33.2 21.1 %collective-permute-start = (bf16[256,1536]{0,1:T(8,128)(2,1)}, bf16[256,1536]{0,1:T(8,128)(2,1)}, u32[]{:S(2)}, u32[]{:S(2)}) collective-permute-start(bf16[256,1536]{0,1:T(8,128)(2,1)} %multiply_convert_fusion.2), channel_id=1, source_target_pairs={{0,1},{1,2},{2,3},{4,5},{5,6},{6,7},{8,9},{9,10},{10,11},{12,13},{... | collective-permute-start | bytes 2359304 | tf_op jit(solution)/shard_map/ppermute | solution.py:39
  37.6 24.1 %collective-permute-start.3 = (bf16[256,1536]{0,1:T(8,128)(2,1)}, bf16[256,1536]{0,1:T(8,128)(2,1)}, u32[]{:S(2)}, u32[]{:S(2)}) collective-permute-start(bf16[256,1536]{0,1:T(8,128)(2,1)} %multiply_convert_fusion.2), channel_id=1, source_target_pairs={{1,0},{2,1},{3,2},{5,4},{6,5},{7,6},{9,8},{10,9},{11,10},{13,12},{... | collective-permute-start | bytes 2359304 | tf_op jit(solution)/shard_map/ppermute | solution.py:40
  54.3 21.2 %collective-permute-start.1 = (bf16[256,1536]{0,1:T(8,128)(2,1)}, bf16[256,1536]{0,1:T(8,128)(2,1)}, u32[]{:S(2)}, u32[]{:S(2)}) collective-permute-start(bf16[256,1536]{0,1:T(8,128)(2,1)} %collective-permute-done), channel_id=1, source_target_pairs={{0,1},{1,2},{2,3},{4,5},{5,6},{6,7},{8,9},{9,10},{10,11},{12,13},{... | collective-permute-start | bytes 2359304 | tf_op jit(solution)/shard_map/ppermute | solution.py:39
  61.7 20.9 %collective-permute-start.4 = (bf16[256,1536]{0,1:T(8,128)(2,1)}, bf16[256,1536]{0,1:T(8,128)(2,1)}, u32[]{:S(2)}, u32[]{:S(2)}) collective-permute-start(bf16[256,1536]{0,1:T(8,128)(2,1)} %collective-permute-done.3), channel_id=1, source_target_pairs={{1,0},{2,1},{3,2},{5,4},{6,5},{7,6},{9,8},{10,9},{11,10},{13,12},{... | collective-permute-start | bytes 2359304 | tf_op jit(solution)/shard_map/ppermute | solution.py:40
  75.5 20.2 %collective-permute-start.2 = (bf16[256,1536]{0,1:T(8,128)(2,1)}, bf16[256,1536]{0,1:T(8,128)(2,1)S(1)}, u32[]{:S(2)}, u32[]{:S(2)}) collective-permute-start(bf16[256,1536]{0,1:T(8,128)(2,1)} %collective-permute-done.1), channel_id=1, source_target_pairs={{0,1},{1,2},{2,3},{4,5},{5,6},{6,7},{8,9},{9,10},{10,11},{12,13},{... | collective-permute-start | bytes 2359304 | tf_op jit(solution)/shard_map/ppermute | solution.py:39
  82.6 20.0 %collective-permute-start.5 = (bf16[256,1536]{0,1:T(8,128)(2,1)}, bf16[256,1536]{0,1:T(8,128)(2,1)}, u32[]{:S(2)}, u32[]{:S(2)}) collective-permute-start(bf16[256,1536]{0,1:T(8,128)(2,1)} %collective-permute-done.4), channel_id=1, source_target_pairs={{1,0},{2,1},{3,2},{5,4},{6,5},{7,6},{9,8},{10,9},{11,10},{13,12},{... | collective-permute-start | bytes 2359304 | tf_op jit(solution)/shard_map/ppermute | solution.py:40
  110.2 9.8 collective-permute-start.6
  114.8 36.0 %collective-permute-start.7 = (bf16[256,1536]{0,1:T(8,128)(2,1)}, bf16[256,1536]{0,1:T(8,128)(2,1)}, u32[]{:S(2)}, u32[]{:S(2)}) collective-permute-start(bf16[256,1536]{0,1:T(8,128)(2,1)} %convert_element_type.336), channel_id=1, source_target_pairs={{0,1},{1,2},{2,3},{4,5},{5,6},{6,7},{8,9},{9,10},{10,11},{12,13},{... | collective-permute-start | bytes 2359304 | tf_op jit(solution)/shard_map/ppermute | solution.py:39
  118.2 31.3 %collective-permute-start.10 = (bf16[256,1536]{0,1:T(8,128)(2,1)}, bf16[256,1536]{0,1:T(8,128)(2,1)}, u32[]{:S(2)}, u32[]{:S(2)}) collective-permute-start(bf16[256,1536]{0,1:T(8,128)(2,1)} %convert_element_type.336), channel_id=1, source_target_pairs={{1,0},{2,1},{3,2},{5,4},{6,5},{7,6},{9,8},{10,9},{11,10},{13,12},{... | collective-permute-start | bytes 2359304 | tf_op jit(solution)/shard_map/ppermute | solution.py:40
  145.4 42.9 %all-to-all-start = ((f32[8,392,128]{2,1,0:T(8,128)}), f32[8,392,128]{2,1,0:T(8,128)S(1)}, u32[]{:S(2)}, u32[]{:S(2)}) async-start(f32[8,392,128]{2,1,0:T(8,128)} %pad_maximum_fusion.4), calls=%async_computation | async-start | bytes 3211264 | tf_op jit(solution)/shard_map/all_to_all | solution.py:226
  149.5 22.5 %collective-permute-start.11 = (bf16[256,1536]{0,1:T(8,128)(2,1)}, bf16[256,1536]{0,1:T(8,128)(2,1)}, u32[]{:S(2)}, u32[]{:S(2)}) collective-permute-start(bf16[256,1536]{0,1:T(8,128)(2,1)} %collective-permute-done.10), channel_id=1, source_target_pairs={{1,0},{2,1},{3,2},{5,4},{6,5},{7,6},{9,8},{10,9},{11,10},{13,12},{... | collective-permute-start | bytes 2359304 | tf_op jit(solution)/shard_map/ppermute | solution.py:40
  150.8 22.9 %collective-permute-start.8 = (bf16[256,1536]{0,1:T(8,128)(2,1)}, bf16[256,1536]{0,1:T(8,128)(2,1)}, u32[]{:S(2)}, u32[]{:S(2)}) collective-permute-start(bf16[256,1536]{0,1:T(8,128)(2,1)} %collective-permute-done.7), channel_id=1, source_target_pairs={{0,1},{1,2},{2,3},{4,5},{5,6},{6,7},{8,9},{9,10},{10,11},{12,13},{... | collective-permute-start | bytes 2359304 | tf_op jit(solution)/shard_map/ppermute | solution.py:39
  172.1 27.4 %collective-permute-start.12 = (bf16[256,1536]{0,1:T(8,128)(2,1)}, bf16[256,1536]{0,1:T(8,128)(2,1)}, u32[]{:S(2)}, u32[]{:S(2)}) collective-permute-start(bf16[256,1536]{0,1:T(8,128)(2,1)} %collective-permute-done.11), channel_id=1, source_target_pairs={{1,0},{2,1},{3,2},{5,4},{6,5},{7,6},{9,8},{10,9},{11,10},{13,12},{... | collective-permute-start | bytes 2359304 | tf_op jit(solution)/shard_map/ppermute | solution.py:40
  173.7 27.3 %collective-permute-start.9 = (bf16[256,1536]{0,1:T(8,128)(2,1)}, bf16[256,1536]{0,1:T(8,128)(2,1)}, u32[]{:S(2)}, u32[]{:S(2)}) collective-permute-start(bf16[256,1536]{0,1:T(8,128)(2,1)} %collective-permute-done.8), channel_id=1, source_target_pairs={{0,1},{1,2},{2,3},{4,5},{5,6},{6,7},{8,9},{9,10},{10,11},{12,13},{... | collective-permute-start | bytes 2359304 | tf_op jit(solution)/shard_map/ppermute | solution.py:39
  193.8 38.6 %all-to-all-start.1 = ((f32[8,384,128]{2,1,0:T(8,128)}), f32[8,384,128]{2,1,0:T(8,128)S(1)}, u32[]{:S(2)}, u32[]{:S(2)}) async-start(f32[8,384,128]{2,1,0:T(8,128)} %scan_pieces.2), calls=%async_computation.1 | async-start | bytes 3145728 | tf_op jit(solution)/shard_map/all_to_all | solution.py:226
  250.0 17.6 %collective-permute-start.13 = (bf16[256,1536]{0,1:T(8,128)(2,1)S(1)}, bf16[256,1536]{0,1:T(8,128)(2,1)}, u32[]{:S(2)}, u32[]{:S(2)}) collective-permute-start(bf16[256,1536]{0,1:T(8,128)(2,1)S(1)} %bitcast.313), channel_id=1, source_target_pairs={{0,1},{4,5},{8,9},{12,13},{16,17},{20,21},{24,25},{28,29}} | collective-permute-start | bytes 2359304 | tf_op jit(solution)/shard_map/ppermute | solution.py:54
  255.7 12.0 collective-permute-start.16
  269.7 5.9 collective-permute-start.17
  270.4 18.4 %collective-permute-start.14 = (bf16[256,1536]{0,1:T(8,128)(2,1)S(1)}, bf16[256,1536]{0,1:T(8,128)(2,1)S(1)}, u32[]{:S(2)}, u32[]{:S(2)}) collective-permute-start(bf16[256,1536]{0,1:T(8,128)(2,1)S(1)} %get-tuple-element.242), channel_id=1, source_target_pairs={{0,1},{1,2},{4,5},{5,6},{8,9},{9,10},{12,13},{13,14},{16,17},{17,1... | collective-permute-start | bytes 2359304 | tf_op jit(solution)/shard_map/ppermute | solution.py:54
  276.6 44.0 %collective-permute-start.18 = (bf16[256,1536]{0,1:T(8,128)(2,1)}, bf16[256,1536]{0,1:T(8,128)(2,1)}, u32[]{:S(2)}, u32[]{:S(2)}) collective-permute-start(bf16[256,1536]{0,1:T(8,128)(2,1)} %add_convert_fusion.7), channel_id=1, source_target_pairs={{1,0},{2,1},{3,2},{5,4},{6,5},{7,6},{9,8},{10,9},{11,10},{13,12},{... | collective-permute-start | bytes 2359304 | tf_op jit(solution)/shard_map/ppermute | solution.py:55
  289.8 30.7 %collective-permute-start.15 = (bf16[256,1536]{0,1:T(8,128)(2,1)}, bf16[256,1536]{0,1:T(8,128)(2,1)}, u32[]{:S(2)}, u32[]{:S(2)}) collective-permute-start(bf16[256,1536]{0,1:T(8,128)(2,1)} %add_convert_fusion.8), channel_id=1, source_target_pairs={{0,1},{1,2},{2,3},{4,5},{5,6},{6,7},{8,9},{9,10},{10,11},{12,13},{... | collective-permute-start | bytes 2359304 | tf_op jit(solution)/shard_map/ppermute | solution.py:54
  324.2 18.0 %collective-permute-start.22 = (bf16[256,1536]{0,1:T(8,128)(2,1)S(1)}, bf16[256,1536]{0,1:T(8,128)(2,1)S(1)}, u32[]{:S(2)}, u32[]{:S(2)}) collective-permute-start(bf16[256,1536]{0,1:T(8,128)(2,1)S(1)} %multiply_convert_fusion.1), channel_id=1, source_target_pairs={{1,0},{2,1},{3,2},{5,4},{6,5},{7,6},{9,8},{10,9},{11,10},{13,12},{... | collective-permute-start | bytes 2359304 | tf_op jit(solution)/shard_map/ppermute | solution.py:40
  325.8 17.7 %collective-permute-start.19 = (bf16[256,1536]{0,1:T(8,128)(2,1)S(1)}, bf16[256,1536]{0,1:T(8,128)(2,1)S(1)}, u32[]{:S(2)}, u32[]{:S(2)}) collective-permute-start(bf16[256,1536]{0,1:T(8,128)(2,1)S(1)} %multiply_convert_fusion.1), channel_id=1, source_target_pairs={{0,1},{1,2},{2,3},{4,5},{5,6},{6,7},{8,9},{9,10},{10,11},{12,13},{... | collective-permute-start | bytes 2359304 | tf_op jit(solution)/shard_map/ppermute | solution.py:39
  342.2 17.8 %collective-permute-start.23 = (bf16[256,1536]{0,1:T(8,128)(2,1)S(1)}, bf16[256,1536]{0,1:T(8,128)(2,1)}, u32[]{:S(2)}, u32[]{:S(2)}) collective-permute-start(bf16[256,1536]{0,1:T(8,128)(2,1)S(1)} %collective-permute-done.22), channel_id=1, source_target_pairs={{1,0},{2,1},{3,2},{5,4},{6,5},{7,6},{9,8},{10,9},{11,10},{13,12},{... | collective-permute-start | bytes 2359304 | tf_op jit(solution)/shard_map/ppermute | solution.py:40
  343.5 17.8 %collective-permute-start.20 = (bf16[256,1536]{0,1:T(8,128)(2,1)S(1)}, bf16[256,1536]{0,1:T(8,128)(2,1)}, u32[]{:S(2)}, u32[]{:S(2)}) collective-permute-start(bf16[256,1536]{0,1:T(8,128)(2,1)S(1)} %collective-permute-done.19), channel_id=1, source_target_pairs={{0,1},{1,2},{2,3},{4,5},{5,6},{6,7},{8,9},{9,10},{10,11},{12,13},{... | collective-permute-start | bytes 2359304 | tf_op jit(solution)/shard_map/ppermute | solution.py:39
  359.9 28.4 %collective-permute-start.24 = (bf16[256,1536]{0,1:T(8,128)(2,1)}, bf16[256,1536]{0,1:T(8,128)(2,1)}, u32[]{:S(2)}, u32[]{:S(2)}) collective-permute-start(bf16[256,1536]{0,1:T(8,128)(2,1)} %collective-permute-done.23), channel_id=1, source_target_pairs={{1,0},{2,1},{3,2},{5,4},{6,5},{7,6},{9,8},{10,9},{11,10},{13,12},{... | collective-permute-start | bytes 2359304 | tf_op jit(solution)/shard_map/ppermute | solution.py:40
  361.3 28.6 %collective-permute-start.21 = (bf16[256,1536]{0,1:T(8,128)(2,1)}, bf16[256,1536]{0,1:T(8,128)(2,1)}, u32[]{:S(2)}, u32[]{:S(2)}) collective-permute-start(bf16[256,1536]{0,1:T(8,128)(2,1)} %collective-permute-done.20), channel_id=1, source_target_pairs={{0,1},{1,2},{2,3},{4,5},{5,6},{6,7},{8,9},{9,10},{10,11},{12,13},{... | collective-permute-start | bytes 2359304 | tf_op jit(solution)/shard_map/ppermute | solution.py:39
  471.7 19.1 %collective-permute-start.25 = (bf16[256,1536]{0,1:T(8,128)(2,1)S(1)}, bf16[256,1536]{0,1:T(8,128)(2,1)S(1)}, u32[]{:S(2)}, u32[]{:S(2)}) collective-permute-start(bf16[256,1536]{0,1:T(8,128)(2,1)S(1)} %get-tuple-element.232), channel_id=1, source_target_pairs={{0,1},{4,5},{8,9},{12,13},{16,17},{20,21},{24,25},{28,29}} | collective-permute-start | bytes 2359304 | tf_op jit(solution)/shard_map/ppermute | solution.py:54
  473.3 17.5 %collective-permute-start.28 = (bf16[256,1536]{0,1:T(8,128)(2,1)S(1)}, bf16[256,1536]{0,1:T(8,128)(2,1)S(1)}, u32[]{:S(2)}, u32[]{:S(2)}) collective-permute-start(bf16[256,1536]{0,1:T(8,128)(2,1)S(1)} %get-tuple-element.233), channel_id=1, source_target_pairs={{3,2},{7,6},{11,10},{15,14},{19,18},{23,22},{27,26},{31,30}} | collective-permute-start | bytes 2359304 | tf_op jit(solution)/shard_map/ppermute | solution.py:55
  491.2 21.1 %collective-permute-start.26 = (bf16[256,1536]{0,1:T(8,128)(2,1)S(1)}, bf16[256,1536]{0,1:T(8,128)(2,1)S(1)}, u32[]{:S(2)}, u32[]{:S(2)}) collective-permute-start(bf16[256,1536]{0,1:T(8,128)(2,1)S(1)} %get-tuple-element.230), channel_id=1, source_target_pairs={{0,1},{1,2},{4,5},{5,6},{8,9},{9,10},{12,13},{13,14},{16,17},{17,1... | collective-permute-start | bytes 2359304 | tf_op jit(solution)/shard_map/ppermute | solution.py:54
  495.7 16.7 %collective-permute-start.29 = (bf16[256,1536]{0,1:T(8,128)(2,1)S(1)}, bf16[256,1536]{0,1:T(8,128)(2,1)S(1)}, u32[]{:S(2)}, u32[]{:S(2)}) collective-permute-start(bf16[256,1536]{0,1:T(8,128)(2,1)S(1)} %get-tuple-element.231), channel_id=1, source_target_pairs={{2,1},{3,2},{6,5},{7,6},{10,9},{11,10},{14,13},{15,14},{18,17},{19... | collective-permute-start | bytes 2359304 | tf_op jit(solution)/shard_map/ppermute | solution.py:55
  514.0 36.4 %collective-permute-start.30 = (bf16[256,1536]{0,1:T(8,128)(2,1)}, bf16[256,1536]{0,1:T(8,128)(2,1)}, u32[]{:S(2)}, u32[]{:S(2)}) collective-permute-start(bf16[256,1536]{0,1:T(8,128)(2,1)} %get-tuple-element.229), channel_id=1, source_target_pairs={{1,0},{2,1},{3,2},{5,4},{6,5},{7,6},{9,8},{10,9},{11,10},{13,12},{... | collective-permute-start | bytes 2359304 | tf_op jit(solution)/shard_map/ppermute | solution.py:55
  515.2 35.1 %collective-permute-start.27 = (bf16[256,1536]{0,1:T(8,128)(2,1)}, bf16[256,1536]{0,1:T(8,128)(2,1)}, u32[]{:S(2)}, u32[]{:S(2)}) collective-permute-start(bf16[256,1536]{0,1:T(8,128)(2,1)} %get-tuple-element.228), channel_id=1, source_target_pairs={{0,1},{1,2},{2,3},{4,5},{5,6},{6,7},{8,9},{9,10},{10,11},{12,13},{... | collective-permute-start | bytes 2359304 | tf_op jit(solution)/shard_map/ppermute | solution.py:54
  556.8 18.0 %collective-permute-start.31 = (bf16[256,1536]{0,1:T(8,128)(2,1)S(1)}, bf16[256,1536]{0,1:T(8,128)(2,1)S(1)}, u32[]{:S(2)}, u32[]{:S(2)}) collective-permute-start(bf16[256,1536]{0,1:T(8,128)(2,1)S(1)} %get-tuple-element.56), channel_id=1, source_target_pairs={{0,1},{1,2},{2,3},{4,5},{5,6},{6,7},{8,9},{9,10},{10,11},{12,13},{... | collective-permute-start | bytes 2359304 | tf_op jit(solution)/shard_map/ppermute | solution.py:39
  559.9 20.2 %collective-permute-start.34 = (bf16[256,1536]{0,1:T(8,128)(2,1)S(1)}, bf16[256,1536]{0,1:T(8,128)(2,1)}, u32[]{:S(2)}, u32[]{:S(2)}) collective-permute-start(bf16[256,1536]{0,1:T(8,128)(2,1)S(1)} %get-tuple-element.56), channel_id=1, source_target_pairs={{1,0},{2,1},{3,2},{5,4},{6,5},{7,6},{9,8},{10,9},{11,10},{13,12},{... | collective-permute-start | bytes 2359304 | tf_op jit(solution)/shard_map/ppermute | solution.py:40
  574.8 18.5 %collective-permute-start.32 = (bf16[256,1536]{0,1:T(8,128)(2,1)S(1)}, bf16[256,1536]{0,1:T(8,128)(2,1)}, u32[]{:S(2)}, u32[]{:S(2)}) collective-permute-start(bf16[256,1536]{0,1:T(8,128)(2,1)S(1)} %collective-permute-done.31), channel_id=1, source_target_pairs={{0,1},{1,2},{2,3},{4,5},{5,6},{6,7},{8,9},{9,10},{10,11},{12,13},{... | collective-permute-start | bytes 2359304 | tf_op jit(solution)/shard_map/ppermute | solution.py:39
  580.1 35.5 %collective-permute-start.35 = (bf16[256,1536]{0,1:T(8,128)(2,1)}, bf16[256,1536]{0,1:T(8,128)(2,1)}, u32[]{:S(2)}, u32[]{:S(2)}) collective-permute-start(bf16[256,1536]{0,1:T(8,128)(2,1)} %collective-permute-done.34), channel_id=1, source_target_pairs={{1,0},{2,1},{3,2},{5,4},{6,5},{7,6},{9,8},{10,9},{11,10},{13,12},{... | collective-permute-start | bytes 2359304 | tf_op jit(solution)/shard_map/ppermute | solution.py:40
  593.3 28.5 %collective-permute-start.33 = (bf16[256,1536]{0,1:T(8,128)(2,1)}, bf16[256,1536]{0,1:T(8,128)(2,1)}, u32[]{:S(2)}, u32[]{:S(2)}) collective-permute-start(bf16[256,1536]{0,1:T(8,128)(2,1)} %collective-permute-done.32), channel_id=1, source_target_pairs={{0,1},{1,2},{2,3},{4,5},{5,6},{6,7},{8,9},{9,10},{10,11},{12,13},{... | collective-permute-start | bytes 2359304 | tf_op jit(solution)/shard_map/ppermute | solution.py:39
  615.6 17.6 %collective-permute-start.36 = (bf16[256,1536]{0,1:T(8,128)(2,1)}, bf16[256,1536]{0,1:T(8,128)(2,1)}, u32[]{:S(2)}, u32[]{:S(2)}) collective-permute-start(bf16[256,1536]{0,1:T(8,128)(2,1)} %collective-permute-done.35), channel_id=1, source_target_pairs={{1,0},{2,1},{3,2},{5,4},{6,5},{7,6},{9,8},{10,9},{11,10},{13,12},{... | collective-permute-start | bytes 2359304 | tf_op jit(solution)/shard_map/ppermute | solution.py:40
  690.9 25.6 %all-to-all-start.3 = ((f32[8,384,128]{2,1,0:T(8,128)}), f32[8,384,128]{2,1,0:T(8,128)}, u32[]{:S(2)}, u32[]{:S(2)}) async-start(f32[8,384,128]{2,1,0:T(8,128)} %scan_pieces.3), calls=%async_computation.3 | async-start | bytes 3145728 | tf_op jit(solution)/shard_map/all_to_all | solution.py:226
  695.5 160.9 %reduce-scatter.28.cloned.1.call-start = ((), (), s32[]{:S(2)}) async-start(), calls=%async_computation.22 | async-start | bytes 811008
  698.4 224.9 %reduce-scatter.26.cloned.1.call-start = ((), (), s32[]{:S(2)}) async-start(), calls=%async_computation.21 | async-start | bytes 1622016
  772.9 216.4 %reduce-scatter.24.cloned.1.call-start = ((), (), s32[]{:S(2)}) async-start(), calls=%async_computation.17 | async-start | bytes 7962624 | tf_op jit(solution)/shard_map/reduce_scatter | solution.py:79
  773.5 263.6 %reduce-scatter.22.cloned.1.call-start = ((), (), s32[]{:S(2)}) async-start(), calls=%async_computation.16 | async-start | bytes 7962624 | tf_op jit(solution)/shard_map/reduce_scatter | solution.py:79
  774.3 331.9 %reduce-scatter.20.cloned.1.call-start = ((), (), s32[]{:S(2)}) async-start(), calls=%async_computation.15 | async-start | bytes 7962624 | tf_op jit(solution)/shard_map/reduce_scatter | solution.py:79
  775.0 379.2 %reduce-scatter.16.cloned.1.call-start = ((), (), s32[]{:S(2)}) async-start(), calls=%async_computation.13 | async-start | bytes 3096576 | tf_op jit(solution)/shard_map/reduce_scatter | solution.py:79
  776.1 4.2 collective-permute-start.43
  790.3 421.1 %reduce-scatter.14.cloned.1.call-start = ((), (), s32[]{:S(2)}) async-start(), calls=%async_computation.12 | async-start | bytes 5308416 | tf_op jit(solution)/shard_map/reduce_scatter | solution.py:79
  795.0 28.8 %collective-permute-start.37 = (bf16[256,1536]{0,1:T(8,128)(2,1)}, bf16[256,1536]{0,1:T(8,128)(2,1)}, u32[]{:S(2)}, u32[]{:S(2)}) collective-permute-start(bf16[256,1536]{0,1:T(8,128)(2,1)} %get-tuple-element.224), channel_id=1, source_target_pairs={{0,1},{4,5},{8,9},{12,13},{16,17},{20,21},{24,25},{28,29}} | collective-permute-start | bytes 2359304 | tf_op jit(solution)/shard_map/ppermute | solution.py:54
  800.0 50.5 %collective-permute-start.40 = (bf16[256,1536]{0,1:T(8,128)(2,1)}, bf16[256,1536]{0,1:T(8,128)(2,1)}, u32[]{:S(2)}, u32[]{:S(2)}) collective-permute-start(bf16[256,1536]{0,1:T(8,128)(2,1)} %get-tuple-element.225), channel_id=1, source_target_pairs={{3,2},{7,6},{11,10},{15,14},{19,18},{23,22},{27,26},{31,30}} | collective-permute-start | bytes 2359304 | tf_op jit(solution)/shard_map/ppermute | solution.py:55
  817.5 497.7 %reduce-scatter.18.cloned.1.call-start = ((), (), s32[]{:S(2)}) async-start(), calls=%async_computation.14 | async-start | bytes 1622016 | tf_op jit(solution)/shard_map/reduce_scatter | solution.py:898
  826.2 24.3 %collective-permute-start.38 = (bf16[256,1536]{0,1:T(8,128)(2,1)}, bf16[256,1536]{0,1:T(8,128)(2,1)}, u32[]{:S(2)}, u32[]{:S(2)}) collective-permute-start(bf16[256,1536]{0,1:T(8,128)(2,1)} %fusion.22), channel_id=1, source_target_pairs={{0,1},{1,2},{4,5},{5,6},{8,9},{9,10},{12,13},{13,14},{16,17},{17,1... | collective-permute-start | bytes 2359304 | tf_op jit(solution)/shard_map/ppermute | solution.py:54
  844.4 23.6 %collective-permute-start.44 = (bf16[256,1536]{0,1:T(8,128)(2,1)}, bf16[256,1536]{0,1:T(8,128)(2,1)}, u32[]{:S(2)}, u32[]{:S(2)}) collective-permute-start(bf16[256,1536]{0,1:T(8,128)(2,1)} %bitcast.311), channel_id=1, source_target_pairs={{0,1},{4,5},{8,9},{12,13},{16,17},{20,21},{24,25},{28,29}} | collective-permute-start | bytes 2359304 | tf_op jit(solution)/shard_map/ppermute | solution.py:54
  848.9 19.1 %collective-permute-start.47 = (bf16[256,1536]{0,1:T(8,128)(2,1)}, bf16[256,1536]{0,1:T(8,128)(2,1)}, u32[]{:S(2)}, u32[]{:S(2)}) collective-permute-start(bf16[256,1536]{0,1:T(8,128)(2,1)} %bitcast.310), channel_id=1, source_target_pairs={{3,2},{7,6},{11,10},{15,14},{19,18},{23,22},{27,26},{31,30}} | collective-permute-start | bytes 2359304 | tf_op jit(solution)/shard_map/ppermute | solution.py:55
  853.4 19.3 %collective-permute-start.41 = (bf16[256,1536]{0,1:T(8,128)(2,1)}, bf16[256,1536]{0,1:T(8,128)(2,1)}, u32[]{:S(2)}, u32[]{:S(2)}) collective-permute-start(bf16[256,1536]{0,1:T(8,128)(2,1)} %get-tuple-element.223), channel_id=1, source_target_pairs={{2,1},{3,2},{6,5},{7,6},{10,9},{11,10},{14,13},{15,14},{18,17},{19... | collective-permute-start | bytes 2359304 | tf_op jit(solution)/shard_map/ppermute | solution.py:55
  858.2 66.7 %collective-permute-start.39 = (bf16[256,1536]{0,1:T(8,128)(2,1)}, bf16[256,1536]{0,1:T(8,128)(2,1)}, u32[]{:S(2)}, u32[]{:S(2)}) collective-permute-start(bf16[256,1536]{0,1:T(8,128)(2,1)} %get-tuple-element.222), channel_id=1, source_target_pairs={{0,1},{1,2},{2,3},{4,5},{5,6},{6,7},{8,9},{9,10},{10,11},{12,13},{... | collective-permute-start | bytes 2359304 | tf_op jit(solution)/shard_map/ppermute | solution.py:54
  871.1 17.7 %collective-permute-start.48 = (bf16[256,1536]{0,1:T(8,128)(2,1)}, bf16[256,1536]{0,1:T(8,128)(2,1)}, u32[]{:S(2)}, u32[]{:S(2)}) collective-permute-start(bf16[256,1536]{0,1:T(8,128)(2,1)} %get-tuple-element.241), channel_id=1, source_target_pairs={{2,1},{3,2},{6,5},{7,6},{10,9},{11,10},{14,13},{15,14},{18,17},{19... | collective-permute-start | bytes 2359304 | tf_op jit(solution)/shard_map/ppermute | solution.py:55
  874.9 49.9 %collective-permute-start.42 = (bf16[256,1536]{0,1:T(8,128)(2,1)}, bf16[256,1536]{0,1:T(8,128)(2,1)}, u32[]{:S(2)}, u32[]{:S(2)}) collective-permute-start(bf16[256,1536]{0,1:T(8,128)(2,1)} %add_convert_fusion.3), channel_id=1, source_target_pairs={{1,0},{2,1},{3,2},{5,4},{6,5},{7,6},{9,8},{10,9},{11,10},{13,12},{... | collective-permute-start | bytes 2359304 | tf_op jit(solution)/shard_map/ppermute | solution.py:55
  877.0 27.8 %collective-permute-start.45 = (bf16[256,1536]{0,1:T(8,128)(2,1)}, bf16[256,1536]{0,1:T(8,128)(2,1)S(1)}, u32[]{:S(2)}, u32[]{:S(2)}) collective-permute-start(bf16[256,1536]{0,1:T(8,128)(2,1)} %get-tuple-element.240), channel_id=1, source_target_pairs={{0,1},{1,2},{4,5},{5,6},{8,9},{9,10},{12,13},{13,14},{16,17},{17,1... | collective-permute-start | bytes 2359304 | tf_op jit(solution)/shard_map/ppermute | solution.py:54
  891.1 44.4 %collective-permute-start.49 = (bf16[256,1536]{0,1:T(8,128)(2,1)}, bf16[256,1536]{0,1:T(8,128)(2,1)}, u32[]{:S(2)}, u32[]{:S(2)}) collective-permute-start(bf16[256,1536]{0,1:T(8,128)(2,1)} %add_convert_fusion.1), channel_id=1, source_target_pairs={{1,0},{2,1},{3,2},{5,4},{6,5},{7,6},{9,8},{10,9},{11,10},{13,12},{... | collective-permute-start | bytes 2359304 | tf_op jit(solution)/shard_map/ppermute | solution.py:55
  906.0 30.4 %collective-permute-start.46 = (bf16[256,1536]{0,1:T(8,128)(2,1)}, bf16[256,1536]{0,1:T(8,128)(2,1)}, u32[]{:S(2)}, u32[]{:S(2)}) collective-permute-start(bf16[256,1536]{0,1:T(8,128)(2,1)} %add_convert_fusion.2), channel_id=1, source_target_pairs={{0,1},{1,2},{2,3},{4,5},{5,6},{6,7},{8,9},{9,10},{10,11},{12,13},{... | collective-permute-start | bytes 2359304 | tf_op jit(solution)/shard_map/ppermute | solution.py:54
  (106 other events, 1241.1 us)
Sparse Core Ops, SparseCore 0:
  11.5 36.6 all-gather.8
  50.7 38.9 all-gather.10
  91.5 138.8 all-gather.12
  701.1 95.5 reduce-scatter.27
  801.8 97.7 reduce-scatter.25
  903.0 64.6 reduce-scatter.23
  971.6 65.4 reduce-scatter.21
  1040.6 65.4 reduce-scatter.19
  1109.9 44.2 reduce-scatter.15
  1157.5 53.8 reduce-scatter.13
  1218.1 97.0 reduce-scatter.17

commit v2 on v1

--- a/solution.py
+++ b/solution.py
@@ -4,6 +4,7 @@
 import jax.numpy as jnp
 from jax import lax
 from jax.experimental import pallas as pl
+from jax.experimental.layout import Layout, with_layout_constraint
 from jax.experimental.pallas import tpu as pltpu
 from jax.sharding import PartitionSpec as P
 
@@ -31,44 +32,29 @@
     return lax.ppermute(value, axis, [(source, source + steps) for source in range(first, last)])
 
 
+def row_major(value):
+    return with_layout_constraint(value, Layout(major_to_minor=tuple(range(value.ndim))))
+
+
 def line_gather(value):
     size = lax.axis_size("tensor")
-    rights, lefts = [], []
-    right, left = value, value
-    for _ in range(1, size):
-        right = lax.ppermute(right, "tensor", [(a, a + 1) for a in range(size - 1)])
-        left = lax.ppermute(left, "tensor", [(a, a - 1) for a in range(1, size)])
-        rights.append(right)
-        lefts.append(left)
-    return [value] + [rights[size - k - 1] + lefts[k - 1] for k in range(1, size)]
-
-
-def line_scatter(block_of):
+    return lax.all_to_all(row_major(jnp.broadcast_to(value[None], (size,) + value.shape)), "tensor", 0, 0)
+
+
+def line_scatter(blocks):
+    got = lax.all_to_all(row_major(blocks), "tensor", 0, 0)
+    return row_major(jnp.sum(got.astype(f32), axis=0))
+
+
+def line_scatter_steps(blocks):
     size = lax.axis_size("tensor")
-    right, left = None, None
-    for k in range(1, size):
-        to_right, to_left = block_of(size - k), block_of(k)
-        if k > 1:
-            to_right = (to_right.astype(f32) + right.astype(f32)).astype(bf16)
-            to_left = (to_left.astype(f32) + left.astype(f32)).astype(bf16)
-        right = lax.ppermute(to_right, "tensor", [(a, a + 1) for a in range(k)])
-        left = lax.ppermute(to_left, "tensor", [(a, a - 1) for a in range(size - k, size)])
-    return block_of(0).astype(f32) + right.astype(f32) + left.astype(f32)
-
-
-def in_order(blocks):
-    size = len(blocks)
     own = lax.axis_index("tensor")
-    whole = jnp.zeros((size,) + blocks[0].shape, blocks[0].dtype)
-    for k in range(size):
-        whole = lax.dynamic_update_index_in_dim(whole, blocks[k], (own + k) % size, 0)
-    return whole
-
-
-def by_distance(whole):
-    size = whole.shape[0]
-    own = lax.axis_index("tensor")
-    return lambda k: lax.dynamic_index_in_dim(whole, (own + k) % size, 0, False)
+    total = lax.dynamic_index_in_dim(blocks, own, 0, False).astype(f32)
+    for step in range(1, size):
+        sent = lax.dynamic_index_in_dim(blocks, (own + step) % size, 0, False)
+        sent = lax.ppermute(row_major(sent), "tensor", [(a, (a + step) % size) for a in range(size)])
+        total = total + sent.astype(f32)
+    return row_major(total)
 
 
 def weight_gather(shard):
@@ -104,7 +90,15 @@
 
 
 def after(value, *others):
-    return lax.optimization_barrier((value,) + others)[0]
+    anywhere = pl.BlockSpec(memory_space=pl.ANY)
+    return pl.pallas_call(
+        lambda *refs: None,
+        in_specs=[anywhere] * (1 + len(others)),
+        out_specs=anywhere,
+        out_shape=jax.ShapeDtypeStruct(value.shape, value.dtype),
+        input_output_aliases={0: 0},
+        name="after",
+    )(value, *others)
 
 
 NN = ((1,), (0,))
@@ -132,6 +126,10 @@
 
 def kernel_params(mib):
     return pltpu.CompilerParams(vmem_limit_bytes=mib * 1024 * 1024)
+
+
+def taking(micros, tokens):
+    return pl.CostEstimate(flops=int(micros * tokens * 1.1e6), bytes_accessed=1024, transcendentals=0)
 
 
 def conv_of(v_ref, halo_ref, cw_ref, padded):
@@ -197,9 +195,7 @@
         ],
         scratch_shapes=[pltpu.VMEM((extent + 8, width), f32)],
         compiler_params=kernel_params(48),
-        cost_estimate=pl.CostEstimate(
-            flops=slots * extent * inner * 500, bytes_accessed=slots * extent * cols * 8, transcendentals=slots * extent * cols
-        ),
+        cost_estimate=taking(12, zs * slots * rows),
         name="mixer_enter",
     )(v, halo, cw, hp)
 
@@ -246,10 +242,8 @@
     return exchanged(scan_pieces(got, decay, True)).reshape(slots, inner, STATE_DIM)
 
 
-def leave_kernel(inner, xs_ref, rw_ref, dl_ref, h_ref, z_ref, hp_ref, gain_ref, y_ref, gg_ref, sq_ref, ybuf):
+def inner_kernel(inner, xs_ref, rw_ref, dl_ref, y_ref):
     extent = xs_ref.shape[1]
-    zs, _, rows, _ = z_ref.shape
-    xs = xs_ref[0]
     write = split_parts(rw_ref[0, :, :STATE_DIM])
     read = split_parts(rw_ref[0, :, STATE_DIM:])
     step_t = dl_ref[0, :, 0:LANES].T
@@ -259,15 +253,38 @@
     causal = lax.broadcasted_iota(jnp.int32, (extent, extent), 0) >= lax.broadcasted_iota(
         jnp.int32, (extent, extent), 1
     )
-    xs_low = xs.astype(bf16)
+    xs_low = xs_ref[0].astype(bf16)
     for head in range(inner // HEAD_DIM):
         cols = slice(head * HEAD_DIM, (head + 1) * HEAD_DIM)
         gap = log_sum[:, head : head + 1] - log_t[head : head + 1, :]
         mixing = jnp.exp(jnp.where(causal, gap, -jnp.inf)) * scores * step_t[head : head + 1, :]
-        ybuf[:, cols] = dot(mixing.astype(bf16), xs_low[:, cols], NN)
-    spread = head_spread(inner)
-    grown = dot(jnp.exp(log_sum), spread, NN, highest)
-    y = ybuf[...] + grown * dot_split(read, split_parts(h_ref[0]), NT) + hp_ref[3:4, :] * xs
+        y_ref[0, :, cols] = dot(mixing.astype(bf16), xs_low[:, cols], NN)
+
+
+def mixer_inner(xs, rw, dl):
+    slots, extent, inner = xs.shape
+    return pl.pallas_call(
+        functools.partial(inner_kernel, inner),
+        grid=(slots,),
+        in_specs=[
+            pl.BlockSpec((1, extent, inner), lambda s: (s, 0, 0)),
+            pl.BlockSpec((1, extent, 2 * STATE_DIM), lambda s: (s, 0, 0)),
+            pl.BlockSpec((1, extent, 2 * LANES), lambda s: (s, 0, 0)),
+        ],
+        out_specs=pl.BlockSpec((1, extent, inner), lambda s: (s, 0, 0)),
+        out_shape=jax.ShapeDtypeStruct((slots, extent, inner), f32),
+        compiler_params=kernel_params(40),
+        cost_estimate=taking(9, slots * extent),
+        name="mixer_inner",
+    )(xs, rw, dl)
+
+
+def leave_kernel(inner, yi_ref, xs_ref, rw_ref, dl_ref, h_ref, z_ref, hp_ref, gain_ref, y_ref, gg_ref, sq_ref):
+    extent = xs_ref.shape[1]
+    zs, _, rows, _ = z_ref.shape
+    read = split_parts(rw_ref[0, :, STATE_DIM:])
+    grown = dot(jnp.exp(dl_ref[0, :, LANES:]), head_spread(inner), NN, highest)
+    y = yi_ref[0] + grown * dot_split(read, split_parts(h_ref[0]), NT) + hp_ref[3:4, :] * xs_ref[0]
     y_ref[0] = y
     z = z_ref[...].reshape(extent, inner)
     gated = y * (z * jax.nn.sigmoid(z))
@@ -275,7 +292,7 @@
     gg_ref[...] = (gated * gain_ref[...]).astype(bf16).reshape(zs, 1, rows, inner)
 
 
-def mixer_leave(xs, rw, dl, h_in, z, skip, gain):
+def mixer_leave(yi, xs, rw, dl, h_in, z, skip, gain):
     zs, slots, rows, inner = z.shape
     extent = zs * rows
     return pl.pallas_call(
@@ -283,6 +300,7 @@
         grid=(slots,),
         in_specs=[
             pl.BlockSpec((1, extent, inner), lambda s: (s, 0, 0)),
+            pl.BlockSpec((1, extent, inner), lambda s: (s, 0, 0)),
             pl.BlockSpec((1, extent, 2 * STATE_DIM), lambda s: (s, 0, 0)),
             pl.BlockSpec((1, extent, 2 * LANES), lambda s: (s, 0, 0)),
             pl.BlockSpec((1, inner, STATE_DIM), lambda s: (s, 0, 0)),
@@ -300,13 +318,10 @@
             jax.ShapeDtypeStruct((zs, slots, rows, inner), bf16),
             jax.ShapeDtypeStruct((slots, extent, LANES), f32),
         ],
-        scratch_shapes=[pltpu.VMEM((extent, inner), f32)],
         compiler_params=kernel_params(48),
-        cost_estimate=pl.CostEstimate(
-            flops=slots * extent * inner * 2000, bytes_accessed=slots * extent * inner * 16, transcendentals=slots * extent * inner
-        ),
+        cost_estimate=taking(7, zs * slots * rows),
         name="mixer_leave",
-    )(xs, rw, dl, h_in, z, skip, gain)
+    )(yi, xs, rw, dl, h_in, z, skip, gain)
 
 
 def unmix_kernel(inner, gn_ref, y_ref, z_ref, rw_ref, dl_ref, tok_ref, gain_ref, gy_ref, gz_ref, s_ref, gg_ref):
@@ -364,16 +379,70 @@
             jax.ShapeDtypeStruct((8, inner), f32),
         ],
         compiler_params=kernel_params(48),
-        cost_estimate=pl.CostEstimate(
-            flops=slots * extent * inner * 500, bytes_accessed=slots * extent * inner * 26, transcendentals=slots * extent * inner
-        ),
+        cost_estimate=taking(9, zs * slots * rows),
         name="mixer_unmix",
     )(gn, y, z, rw, dl, tok, gain)
 
 
+def pairs_kernel(inner, xs_ref, rw_ref, dl_ref, gy_ref, gx_ref, grw_ref, gdl_ref, cols_buf):
+    extent = gy_ref.shape[1]
+    write = split_parts(rw_ref[0, :, :STATE_DIM])
+    read = split_parts(rw_ref[0, :, STATE_DIM:])
+    step = dl_ref[0, :, 0:LANES]
+    log_sum = dl_ref[0, :, LANES:]
+    log_t = log_sum.T
+    gy_parts, xs_parts = split_parts(gy_ref[0]), split_parts(xs_ref[0])
+    scores_t = dot_split(write, read, NT)
+    later = lax.broadcasted_iota(jnp.int32, (extent, extent), 1) >= lax.broadcasted_iota(
+        jnp.int32, (extent, extent), 0
+    )
+    lane = lax.broadcasted_iota(jnp.int32, (extent, LANES), 1)
+    score_grad_t = jnp.zeros((extent, extent), f32)
+    step_direct = jnp.zeros((extent, LANES), f32)
+    cols_buf[...] = jnp.zeros_like(cols_buf)
+    for head in range(inner // HEAD_DIM):
+        cols = slice(head * HEAD_DIM, (head + 1) * HEAD_DIM)
+        gap_t = log_t[head : head + 1, :] - log_sum[:, head : head + 1]
+        decay_t = jnp.exp(jnp.where(later, gap_t, -jnp.inf))
+        step_col = step[:, head : head + 1]
+        pair_t = dot_split([x[:, cols] for x in xs_parts], [g[:, cols] for g in gy_parts], NT)
+        both_t = decay_t * pair_t
+        score_grad_t = score_grad_t + both_t * step_col
+        weight_t = both_t * scores_t
+        step_direct = step_direct + jnp.where(lane == head, jnp.sum(weight_t, axis=1, keepdims=True), 0.0)
+        cols_buf[head : head + 1, :] = jnp.sum(weight_t * step_col, axis=0, keepdims=True)
+        gx_ref[0, :, cols] = dot((decay_t * scores_t * step_col).astype(bf16), gy_parts[0][:, cols], NN)
+    score_parts = split_parts(score_grad_t)
+    grw_ref[0, :, :STATE_DIM] = dot_split(score_parts, read, NN)
+    grw_ref[0, :, STATE_DIM:] = dot_split(score_parts, write, TN)
+    gdl_ref[0, :, 0:LANES] = step_direct
+    gdl_ref[0, :, LANES:] = cols_buf[...].T - step * step_direct
+
+
+def mixer_pairs(xs, rw, dl, gy):
+    slots, extent, inner = xs.shape
+    wide = pl.BlockSpec((1, extent, inner), lambda s: (s, 0, 0))
+    two = pl.BlockSpec((1, extent, 2 * LANES), lambda s: (s, 0, 0))
+    return pl.pallas_call(
+        functools.partial(pairs_kernel, inner),
+        grid=(slots,),
+        in_specs=[wide, two, two, wide],
+        out_specs=[wide, two, two],
+        out_shape=[
+            jax.ShapeDtypeStruct((slots, extent, inner), f32),
+            jax.ShapeDtypeStruct((slots, extent, 2 * STATE_DIM), f32),
+            jax.ShapeDtypeStruct((slots, extent, 2 * LANES), f32),
+        ],
+        scratch_shapes=[pltpu.VMEM((LANES, extent), f32)],
+        compiler_params=kernel_params(48),
+        cost_estimate=taking(42, slots * extent),
+        name="mixer_pairs",
+    )(xs, rw, dl, gy)
+
+
 def back_kernel(
-    inner, v_ref, halo_ref, cw_ref, hp_ref, skip_ref, rw_ref, dl_ref, gy_ref, h_ref, gh_ref,
-    gv_ref, gbc_ref, gp_ref, gc_ref, ghp_ref, padded, gpad, bufs, cols_buf,
+    inner, v_ref, halo_ref, cw_ref, hp_ref, skip_ref, rw_ref, dl_ref, gy_ref, gx_ref, grw_ref, gdl_ref, h_ref, gh_ref,
+    gv_ref, gbc_ref, gp_ref, gc_ref, ghp_ref, padded, gpad,
 ):
     extent = gy_ref.shape[1]
     zs, _, rows, _ = v_ref.shape
@@ -384,35 +453,13 @@
     logistic = jax.nn.sigmoid(pre)
     slope = logistic * (1.0 + pre * (1.0 - logistic))
     xs = pre[:, :inner] * logistic[:, :inner]
-    write = split_parts(rw_ref[0, :, :STATE_DIM])
-    read = split_parts(rw_ref[0, :, STATE_DIM:])
+    write_low = rw_ref[0, :, :STATE_DIM].astype(bf16)
+    read_low = rw_ref[0, :, STATE_DIM:].astype(bf16)
     raw, step = step_sizes(v_ref, hp_ref, width, extent)
     rate = jnp.exp(hp_ref[0:1, :])
     log_sum = dl_ref[0, :, LANES:]
-    log_t = log_sum.T
     gy = gy_ref[0]
-    gy_parts, xs_parts = split_parts(gy), split_parts(xs)
-    scores_t = dot_split(write, read, NT)
-    later = lax.broadcasted_iota(jnp.int32, (extent, extent), 1) >= lax.broadcasted_iota(
-        jnp.int32, (extent, extent), 0
-    )
-    lane = lax.broadcasted_iota(jnp.int32, (extent, LANES), 1)
-    score_grad_t = jnp.zeros((extent, extent), f32)
-    step_direct = jnp.zeros((extent, LANES), f32)
-    cols_buf[...] = jnp.zeros_like(cols_buf)
-    for head in range(heads):
-        cols = slice(head * HEAD_DIM, (head + 1) * HEAD_DIM)
-        gap_t = log_t[head : head + 1, :] - log_sum[:, head : head + 1]
-        decay_t = jnp.exp(jnp.where(later, gap_t, -jnp.inf))
-        mix_t = decay_t * scores_t
-        pair_t = dot_split([x[:, cols] for x in xs_parts], [g[:, cols] for g in gy_parts], NT)
-        both_t = decay_t * pair_t
-        step_col = step[:, head : head + 1]
-        score_grad_t = score_grad_t + both_t * step_col
-        weight_t = both_t * scores_t
-        step_direct = step_direct + jnp.where(lane == head, jnp.sum(weight_t, axis=1, keepdims=True), 0.0)
-        cols_buf[head : head + 1, :] = jnp.sum(weight_t * step_col, axis=0, keepdims=True)
-        bufs[:, cols] = dot((mix_t * step_col).astype(bf16), gy_parts[0][:, cols], NN)
+    step_direct = gdl_ref[0, :, 0:LANES]
     sums = head_sums(inner)
     spread = head_spread(inner)
     last = log_sum[extent - 1 : extent, :]
@@ -422,21 +469,20 @@
     gh = gh_ref[0]
     h_in = h_ref[0]
     gh_parts, h_parts = split_parts(gh), split_parts(h_in)
-    tail_in = dot(write[0], gh_parts[0], NT)
+    tail_in = dot(write_low, gh_parts[0], NT)
     tail_direct = tail_decay * dot(xs * tail_in, sums, NN, highest)
     tail_weight = tail_direct * step
-    state_part = grown * dot(read[0], h_parts[0], NT)
+    state_part = grown * dot(read_low, h_parts[0], NT)
     state_weight = dot(gy * state_part, sums, NN, highest)
     kept = dot(sums, jnp.sum(gh * h_in, axis=1, keepdims=True) * jnp.ones((1, LANES), f32), TN, highest).T[0:1, :]
-    log_grad = cols_buf[...].T - step * step_direct + state_weight - tail_weight
+    log_grad = gdl_ref[0, :, LANES:] + state_weight - tail_weight
     end_grad = jnp.sum(tail_weight, axis=0, keepdims=True) + jnp.exp(last) * kept
     rate_arg_grad = dot(lower_ones(extent), log_grad, TN, highest) + end_grad
     step_grad = step_direct + tail_direct - rate * rate_arg_grad
     raw_grad = step_grad * jax.nn.sigmoid(raw)
-    xs_grad = bufs[...] + tail * tail_in + skip_ref[3:4, :] * gy
-    score_parts = split_parts(score_grad_t)
-    write_grad = dot_split(score_parts, read, NN) + dot_split(split_parts(tail * xs), gh_parts, NN)
-    read_grad = dot_split(score_parts, write, TN) + dot_split(split_parts(grown * gy), h_parts, NN)
+    xs_grad = gx_ref[0] + tail * tail_in + skip_ref[3:4, :] * gy
+    write_grad = grw_ref[0, :, :STATE_DIM] + dot_split(split_parts(tail * xs), gh_parts, NN)
+    read_grad = grw_ref[0, :, STATE_DIM:] + dot_split(split_parts(grown * gy), h_parts, NN)
     valid_lane = lax.broadcasted_iota(jnp.int32, (1, LANES), 1) < heads
     rate_grad = jnp.where(valid_lane, jnp.sum(-step * rate * rate_arg_grad, axis=0, keepdims=True), 0.0)
     raw_grad = jnp.where(valid_lane, raw_grad, 0.0)
@@ -471,11 +517,14 @@
     gv_ref[:, :, :, inner:] = raw_grad.astype(bf16).reshape(zs, 1, rows, LANES)
 
 
-def mixer_back(v, halo, cw, hp, skip, rw, dl, gy, h_in, gh):
+def mixer_back(v, halo, cw, hp, skip, rw, dl, gy, gx, grw, gdl, h_in, gh):
     zs, slots, rows, cols = v.shape
     extent = zs * rows
     inner = gy.shape[2]
     width = cw.shape[1]
+    wide = pl.BlockSpec((1, extent, inner), lambda s: (s, 0, 0))
+    two = pl.BlockSpec((1, extent, 2 * LANES), lambda s: (s, 0, 0))
+    state = pl.BlockSpec((1, inner, STATE_DIM), lambda s: (s, 0, 0))
     return pl.pallas_call(
         functools.partial(back_kernel, inner),
         grid=(slots,),
@@ -485,11 +534,14 @@
             pl.BlockSpec(cw.shape, lambda s: (0, 0)),
             pl.BlockSpec(hp.shape, lambda s: (0, 0)),
             pl.BlockSpec(skip.shape, lambda s: (0, 0)),
-            pl.BlockSpec((1, extent, 2 * STATE_DIM), lambda s: (s, 0, 0)),
-            pl.BlockSpec((1, extent, 2 * LANES), lambda s: (s, 0, 0)),
-            pl.BlockSpec((1, extent, inner), lambda s: (s, 0, 0)),
-            pl.BlockSpec((1, inner, STATE_DIM), lambda s: (s, 0, 0)),
-            pl.BlockSpec((1, inner, STATE_DIM), lambda s: (s, 0, 0)),
+            two,
+            two,
+            wide,
+            wide,
+            two,
+            two,
+            state,
+            state,
         ],
         out_specs=[
             pl.BlockSpec((zs, 1, rows, inner + LANES), lambda s: (0, s, 0, 0)),
@@ -508,15 +560,11 @@
         scratch_shapes=[
             pltpu.VMEM((extent + 8, width), f32),
             pltpu.VMEM((extent + 16, width), f32),
-            pltpu.VMEM((extent, inner), f32),
-            pltpu.VMEM((LANES, extent), f32),
         ],
         compiler_params=kernel_params(56),
-        cost_estimate=pl.CostEstimate(
-            flops=slots * extent * inner * 5000, bytes_accessed=slots * extent * inner * 20, transcendentals=slots * extent * inner * 2
-        ),
+        cost_estimate=taking(18, zs * slots * rows),
         name="mixer_back",
-    )(v, halo, cw, hp, skip, rw, dl, gy, h_in, gh)
+    )(v, halo, cw, hp, skip, rw, dl, gy, gx, grw, gdl, h_in, gh)
 
 
 def expert_kernel(
@@ -546,9 +594,9 @@
     n_val = n_ref[...]
     gates = gates_buf[...]
     act_back = dot(g_ref[...], down, NN)
+    ups = [up_ref[:, member].reshape(depth, 2 * half) for member in range(2)]
     for member in range(2):
-        up = up_ref[:, member].reshape(depth, 2 * half)
-        hidden = dot(n_val, up, NN)
+        hidden = dot(n_val, ups[member], NN)
         gate_part, up_part = hidden[:, :half], hidden[:, half:]
         logistic = jax.nn.sigmoid(gate_part)
         silu = gate_part * logistic
@@ -559,10 +607,11 @@
         gate_grad[...] += jnp.where(own, jnp.sum(act * part, axis=1, keepdims=True), 0.0)
         act_ref[0, :, member * half : (member + 1) * half] = (gate * act).astype(bf16)
         part = part * gate
-        hid_ref[member, :, :half] = (part * up_part * (logistic * (1.0 + gate_part * (1.0 - logistic)))).astype(bf16)
-        hid_ref[member, :, half:] = (part * silu).astype(bf16)
-        back_sum[...] += dot(hid_ref[member], up, NT)
+        first_col = 2 * member * half
+        hid_ref[0, :, first_col : first_col + half] = (part * up_part * (logistic * (1.0 + gate_part * (1.0 - logistic)))).astype(bf16)
+        hid_ref[0, :, first_col + half : first_col + 2 * half] = (part * silu).astype(bf16)
     moe_sum[...] += dot(act_ref[0], down, NT)
+    back_sum[...] += dot(hid_ref[0], jnp.concatenate(ups, axis=1), NT)
 
     @pl.when(pair == pairs - 1)
     def _():
@@ -595,14 +644,14 @@
             pl.BlockSpec((tokens, width), lambda p: (0, 0)),
             pl.BlockSpec((tokens, LANES), lambda p: (0, 0)),
             pl.BlockSpec((1, tokens, cols), lambda p: (p, 0, 0)),
-            pl.BlockSpec((2, tokens, cols), lambda p: (p, 0, 0)),
+            pl.BlockSpec((1, tokens, 2 * cols), lambda p: (p, 0, 0)),
         ],
         out_shape=[
             jax.ShapeDtypeStruct((tokens, width), bf16),
             jax.ShapeDtypeStruct((tokens, width), bf16),
             jax.ShapeDtypeStruct((tokens, LANES), bf16),
             jax.ShapeDtypeStruct((pairs, tokens, cols), bf16),
-            jax.ShapeDtypeStruct((2 * pairs, tokens, cols), bf16),
+            jax.ShapeDtypeStruct((pairs, tokens, 2 * cols), bf16),
         ],
         scratch_shapes=[
             pltpu.VMEM((tokens, width), f32),
@@ -611,17 +660,15 @@
             pltpu.VMEM((tokens, LANES), f32),
         ],
         compiler_params=kernel_params(60),
-        cost_estimate=pl.CostEstimate(
-            flops=12 * tokens * width * cols * pairs, bytes_accessed=weights.size * 2 + tokens * width * 20, transcendentals=tokens * cols * pairs
-        ),
+        cost_estimate=taking(72, tokens),
         name="experts",
     )(n_two, g_moe, mask, router, weights, weights)
 
 
-def expert_grad_kernel(up_blocks, chunks, start, *refs):
+def expert_grad_kernel(up_blocks, chunks, *refs):
     n_refs, g_refs, h_refs, a_refs = (refs[i * chunks : (i + 1) * chunks] for i in range(4))
     out_ref = refs[4 * chunks]
-    block = pl.program_id(0) + start
+    block = pl.program_id(0)
     count, _, rows, cols = out_ref.shape
 
     def summed(lefts, rights):
@@ -639,23 +686,24 @@
         summed(g_refs, a_refs)
 
 
-def expert_grads(n_list, g_list, hid_list, act_list, count, start, blocks):
+def expert_grads(n_list, g_list, hid_list, act_list, count):
     chunks = len(n_list)
     width, tokens = n_list[0].shape
-    ups, _, cols = hid_list[0].shape
+    pairs, _, cols = act_list[0].shape
+    ups = 2 * pairs
+    blocks = 3 * pairs
     whole = pl.BlockSpec((width, tokens), lambda b: (0, 0))
+    hid_at = lambda b: (jnp.minimum(b, ups - 1) // 2, 0, jnp.minimum(b, ups - 1) % 2)
     return pl.pallas_call(
-        functools.partial(expert_grad_kernel, ups, chunks, start),
+        functools.partial(expert_grad_kernel, ups, chunks),
         grid=(blocks,),
         in_specs=[whole] * (2 * chunks)
-        + [pl.BlockSpec((1, tokens, cols), lambda b: (jnp.minimum(b + start, ups - 1), 0, 0))] * chunks
-        + [pl.BlockSpec((1, tokens, cols), lambda b: (jnp.maximum(b + start - ups, 0), 0, 0))] * chunks,
+        + [pl.BlockSpec((1, tokens, cols), hid_at)] * chunks
+        + [pl.BlockSpec((1, tokens, cols), lambda b: (jnp.maximum(b - ups, 0), 0, 0))] * chunks,
         out_specs=pl.BlockSpec((count, 1, width // count, cols), lambda b: (0, b, 0, 0)),
         out_shape=jax.ShapeDtypeStruct((count, blocks, width // count, cols), bf16),
         compiler_params=kernel_params(48),
-        cost_estimate=pl.CostEstimate(
-            flops=2 * chunks * tokens * width * cols * blocks, bytes_accessed=blocks * width * cols * 2, transcendentals=0
-        ),
+        cost_estimate=taking(40, chunks * tokens),
         name="expert_grads",
     )(*n_list, *g_list, *hid_list, *act_list)
 
@@ -700,8 +748,9 @@
     enter_shard = jnp.concatenate(
         [w_zx[:, 1], w_bc, jnp.pad(w_dt, ((0, 0), (0, LANES - heads)))], axis=1
     )
-    side_shard = jnp.concatenate([w_zx[:, 0], w_out.T], axis=1)
-    router_shard = jnp.pad(w_router, ((0, 0), (0, LANES - EXPERTS)))
+    side_shard = jnp.concatenate(
+        [w_zx[:, 0], w_out.T, jnp.pad(w_router, ((0, 0), (0, LANES - EXPERTS)))], axis=1
+    )
     expert_shard = jnp.concatenate(
         [
             w_gu.reshape(EXPERTS, shard, 2 * half),
@@ -711,22 +760,27 @@
         ],
         axis=0,
     )
+
+    def by_slot(values):
+        return jnp.transpose(values, (1, 0, 2))
+
+    def part(values, c):
+        return values[c * per : (c + 1) * per].reshape((tokens,) + values.shape[2:])
+
+    u_slots = by_slot(block_input)
+    u_low = [row_major(part(u_slots, c)) for c in chunk_ids]
+    u_all = [line_gather(u_low[c]) for c in chunk_ids]
     full_enter = weight_gather(enter_shard).reshape(D_MODEL, width + LANES)
-    full_side = weight_gather(side_shard).reshape(D_MODEL, 2 * inner)
-    full_z, full_out = full_side[:, :inner], full_side[:, inner:]
     gains = jnp.stack([norm1_gain, norm2_gain], axis=1).astype(f32)
     gains = lax.all_gather(gains, "dp", axis=0, tiled=True)
     gain_one, gain_two = gains[:, 0], gains[:, 1]
-    full_router = weight_gather(router_shard).reshape(D_MODEL, LANES)
+    full_side = weight_gather(side_shard).reshape(D_MODEL, 2 * inner + LANES)
+    full_z, full_out, full_router = full_side[:, :inner], full_side[:, inner : 2 * inner], full_side[:, 2 * inner :]
     full_expert = weight_gather(expert_shard)
 
     positions = wide_index * piece_rows + own * rows + jnp.arange(rows, dtype=jnp.int32)
     valid = (positions[None, :] < lengths[:, None]).astype(f32)[:, :, None]
-    u_slots = jnp.transpose(block_input, (1, 0, 2)).astype(f32)
-    grad_slots = jnp.transpose(out_grad, (1, 0, 2)).astype(f32) * valid
-
-    def part(values, c):
-        return values[c * per : (c + 1) * per].reshape((tokens,) + values.shape[2:])
+    grad_slots = by_slot(out_grad).astype(f32) * valid
 
     conv_w = jnp.pad(jnp.concatenate([conv_x, conv_bc], axis=1), ((0, 8 - CONV_WIDTH - 1), (0, 0)))
     hp = jnp.pad(head_params, ((0, 5), (0, LANES - heads)))
@@ -737,47 +791,50 @@
         (routes[..., None] == jnp.arange(LANES, dtype=jnp.int32)).astype(f32), axis=2
     )
     hot = jnp.transpose(hot.reshape(zs, rows, SLOT_COUNT, LANES), (0, 2, 1, 3))
-    hot_at = by_distance(hot)
-
-    u, valid_c, grad_c, n_one, n_one_t, v, halo, z = [], [], [], [], [], [], [], []
+
+    def flat(values):
+        return values.reshape((zs * tokens,) + values.shape[2:])
+
+    def in_slots(values):
+        return values.reshape((zs, per, rows) + values.shape[1:])
+
+    u = [row_major(u_low[c].astype(f32)) for c in chunk_ids]
+    valid_c = [part(valid, c) for c in chunk_ids]
+    grad_c = [row_major(part(grad_slots, c)) for c in chunk_ids]
+    n_one, v, z, halo, entered = [], [], [], [], []
     for c in chunk_ids:
-        u.append(part(u_slots, c))
-        valid_c.append(part(valid, c))
-        grad_c.append(part(grad_slots, c))
-        normed = rms_scale(u[c], gain_one).astype(bf16)
-        n_one.append(in_order(line_gather(normed)))
-    for c in chunk_ids:
-        flat = n_one[c].reshape(zs * tokens, D_MODEL)
-        v.append(dot(flat, full_enter, NN).reshape(zs, per, rows, width + LANES))
-        rim_rows = n_one[c].reshape(zs, per, rows, D_MODEL)[zs - 1, :, rows - rim :]
+        n_one.append(row_major(rms_scale(flat(u_all[c]).astype(f32), gain_one).astype(bf16)))
+        v.append(in_slots(dot(n_one[c], full_enter, NN)))
+        rim_rows = in_slots(n_one[c])[zs - 1, :, rows - rim :]
         prior = dot(passed_along(rim_rows, "dp", 1).reshape(per * rim, D_MODEL), full_enter[:, :width], NN)
         halo.append(jnp.pad(prior.reshape(per, rim, width), ((0, 0), (8 - rim, 0), (0, 0))))
-    entered = [mixer_enter(v[c], halo[c], conv_w, hp, inner) for c in chunk_ids]
-    g_moe = [jnp.concatenate(line_gather(after(grad_c[c].astype(bf16), n_one[c])), axis=0) for c in chunk_ids]
-    resid, mixed_all, y_all, h_all, decay_all, tok_all, gg_all, n_two = [], [], [], [], [], [], [], []
+        entered.append(mixer_enter(v[c], halo[c], conv_w, hp, inner))
+    g_moe = [line_gather(after(grad_c[c].astype(bf16), u_all[CHUNKS - 1])) for c in chunk_ids]
+    resid, mixed_all, y_all, h_all, decay_all, inv_alls, gg_all, n_two = [], [], [], [], [], [], [], []
     for c in chunk_ids:
         xs, rw, dl, s_local = entered[c]
+        yi = mixer_inner(xs, rw, dl)
+        z.append(in_slots(dot(n_one[c], full_z, NN)))
         h_in, decay = states_forward(s_local, dl[:, piece_rows - 1, LANES : LANES + heads])
         h_in = after(h_in, g_moe[c])
-        z.append(dot(n_one[c].reshape(zs * tokens, D_MODEL), full_z, NN).reshape(zs, per, rows, inner))
-        y, gg, squares = mixer_leave(xs, rw, dl, h_in, z[c], skip, gain_row)
+        y, gg, squares = mixer_leave(yi, xs, rw, dl, h_in, z[c], skip, gain_row)
+        product = dot(flat(gg.reshape(zs, tokens, inner)), full_out, NT).astype(bf16)
+        mixed = line_scatter(product.reshape(zs, tokens, D_MODEL))
         square_sum = lax.psum(squares[:, :, 0], "tensor")
         inv_all = lax.rsqrt(square_sum / INNER_DIM + norm_eps)
-        inv_own = lax.dynamic_slice_in_dim(inv_all, own * rows, rows, 1).reshape(tokens, 1)
-        product = dot(gg.reshape(zs * tokens, inner), full_out, NT).astype(bf16)
-        mixed = line_scatter(by_distance(product.reshape(zs, tokens, D_MODEL))) * inv_own
-        resid.append(u[c] + mixed)
+        mixed = mixed * lax.dynamic_slice_in_dim(inv_all, own * rows, rows, 1).reshape(tokens, 1)
+        resid.append(row_major(u[c] + mixed))
         mixed_all.append(mixed)
         y_all.append(y)
         h_all.append(h_in)
         decay_all.append(decay)
-        tok_all.append(inv_all)
+        inv_alls.append(inv_all)
         gg_all.append(gg)
-        normed = rms_scale(resid[c], gain_two).astype(bf16)
-        n_two.append(jnp.concatenate(line_gather(normed), axis=0))
+        n_two.append(flat(line_gather(row_major(rms_scale(resid[c], gain_two).astype(bf16)))))
+    g_moe = [flat(g_moe[c]) for c in chunk_ids]
     moe_part, back_part, logit_grads, acts, hids = [], [], [], [], []
     for c in chunk_ids:
-        mask = jnp.concatenate([part(hot_at(k), c) for k in range(zs)], axis=0)
+        mask = hot[:, c * per : (c + 1) * per].reshape(zs * tokens, LANES)
         results = experts(n_two[c], g_moe[c], mask, full_router, full_expert)
         moe_part.append(results[0].reshape(zs, tokens, D_MODEL))
         back_part.append(results[1].reshape(zs, tokens, D_MODEL))
@@ -785,30 +842,21 @@
         acts.append(results[3])
         hids.append(results[4])
 
-    def two_back(values, gain_vec):
-        return jax.vjp(rms_scale, values, gain_vec)[1]
-
-    n_two_t, g_moe_t = [n.T for n in n_two], [g.T for g in g_moe]
-    third = (EXPERTS + 2) // 2
-    expert_grad = [
-        expert_grads(n_two_t, g_moe_t, hids, acts, pieces, start, third) for start in (0, third, 2 * third)
-    ]
+    def norm_back(values, gain_vec, grads):
+        return jax.vjp(rms_scale, values, gain_vec)[1](grads)
+
     resid_grad, g_mixed, gain_two_grad = [], [], 0.0
-    unmixed, gate_gain_grad = [], 0.0
+    unmixed, pairs, gate_gain_grad = [], [], 0.0
     for c in chunk_ids:
-        n_two_grad = line_scatter(lambda k: back_part[c][k])
-        from_norm, gain_grad = two_back(resid[c], gain_two)(n_two_grad)
+        n_two_grad = line_scatter_steps(back_part[c])
+        from_norm, gain_grad = norm_back(resid[c], gain_two, n_two_grad)
         gain_two_grad = gain_two_grad + gain_grad
-        resid_grad.append(grad_c[c] + from_norm)
+        resid_grad.append(row_major(grad_c[c] + from_norm))
         low = resid_grad[c].astype(bf16)
-        if c == 0:
-            low = after(low, expert_grad[0], expert_grad[1])
-        g_mixed.append(in_order(line_gather(low)))
-        grad = dot(g_mixed[c].reshape(zs * tokens, D_MODEL), full_out, NN).reshape(zs, per, rows, inner)
-        if c == 0:
-            grad = after(grad, expert_grad[2])
+        g_mixed.append(flat(line_gather(low)))
+        grad = in_slots(dot(g_mixed[c], full_out, NN))
         xs, rw, dl, _ = entered[c]
-        inv_all = tok_all[c]
+        inv_all = inv_alls[c]
         y_like = jnp.transpose(y_all[c].reshape(per, zs, rows, inner), (1, 0, 2, 3))
         cross = jnp.sum(grad * gain_row * y_like * jax.nn.silu(z[c]), axis=-1)
         cross = lax.psum(jnp.transpose(cross, (1, 0, 2)).reshape(per, piece_rows), "tensor")
@@ -816,9 +864,12 @@
         gy, gz, g_local, gg_grad = mixer_unmix(grad, y_all[c], z[c], rw, dl, tok, gain_row)
         gate_gain_grad = gate_gain_grad + gg_grad[0]
         unmixed.append((gy, gz, g_local))
-
-    moe_part = [after(moe_part[c], g_mixed[c]) for c in chunk_ids]
-    moe = [line_scatter(lambda k: moe_part[c][k]) for c in chunk_ids]
+        pairs.append(mixer_pairs(xs, rw, dl, gy))
+
+    expert_grad = weight_scatter(
+        expert_grads([n.T for n in n_two], [g.T for g in g_moe], hids, acts, pieces)
+    )
+    moe = [line_scatter(after(moe_part[c], g_mixed[CHUNKS - 1])) for c in chunk_ids]
     output = [resid[c] + moe[c] for c in chunk_ids]
     stat_terms = sum(
         jnp.stack(
@@ -836,101 +887,128 @@
         return jnp.concatenate([v.reshape(zs * tokens, -1) for v in values], axis=0)
 
     inv_rows = [
-        jnp.transpose(tok_all[c].reshape(per, zs, rows), (1, 0, 2)).reshape(zs * tokens, 1) for c in chunk_ids
+        jnp.transpose(inv_alls[c].reshape(per, zs, rows), (1, 0, 2)).reshape(zs * tokens, 1) for c in chunk_ids
     ]
-    scaled = [
-        (g_mixed[c].reshape(zs * tokens, D_MODEL).astype(f32) * inv_rows[c]).astype(bf16) for c in chunk_ids
-    ]
-    out_w_grad = dot(rows_of(scaled), rows_of(gg_all), TN)
-
-    z_grads, v_grads, bc_grads, conv_grad, head_grad = [], [], [], 0.0, 0.0
+    scaled = [(g_mixed[c].astype(f32) * inv_rows[c]).astype(bf16) for c in chunk_ids]
+    out_w_grad = dot(rows_of(scaled), rows_of(gg_all), TN).astype(bf16)
+    n_rows = rows_of(n_one)
+    z_w_grad = dot(n_rows, rows_of([unmixed[c][1] for c in chunk_ids]), TN).astype(bf16)
+
+    v_grads, bc_grads, conv_grad, head_grad = [], [], 0.0, 0.0
     full_x = jnp.concatenate([full_enter[:, :inner], full_enter[:, width:]], axis=1)
     full_bc = full_enter[:, inner:width]
     full_bc = jnp.concatenate([full_bc, full_bc], axis=1)
     for c in chunk_ids:
         gy, gz, g_local = unmixed[c]
         xs, rw, dl, _ = entered[c]
-        gh = states_backward(g_local, decay_all[c])
+        gh = after(states_backward(g_local, decay_all[c]), moe[c])
         gv, gbc, g_rim, gc, ghp = mixer_back(
-            v[c], halo[c], conv_w, hp, skip, rw, dl, gy, h_all[c], gh
+            v[c], halo[c], conv_w, hp, skip, rw, dl, gy, *pairs[c], h_all[c], gh
         )
         conv_grad = conv_grad + gc
         head_grad = head_grad + ghp
-        following = passed_along(g_rim[:, 8 - rim :].astype(bf16), "dp", -1)
-        following = following.astype(f32)
+        following = passed_along(g_rim[:, 8 - rim :].astype(bf16), "dp", -1).astype(f32)
         edge = gv[zs - 1, :, rows - rim :, :inner].astype(f32) + following[:, :, :inner]
         gv = lax.dynamic_update_slice(gv, edge.astype(bf16)[None], (zs - 1, 0, rows - rim, 0))
         edge = gbc[zs - 1, :, rows - rim :] + following[:, :, inner:]
         gbc = lax.dynamic_update_slice(gbc, edge[None], (zs - 1, 0, rows - rim, 0))
-        z_grads.append(gz)
         v_grads.append(gv)
         bc_grads.append(jnp.concatenate(split_parts(gbc), axis=-1))
-    u_grad, gain_one_grad = [], 0.0
+    u_grad, n_parts, gain_one_grad = [], [], 0.0
     for c in chunk_ids:
         n_grad = (
-            dot(z_grads[c].reshape(zs * tokens, inner), full_z, NT)
+            dot(unmixed[c][1].reshape(zs * tokens, inner), full_z, NT)
             + dot(v_grads[c].reshape(zs * tokens, inner + LANES), full_x, NT)
             + dot(bc_grads[c].reshape(zs * tokens, 4 * STATE_DIM), full_bc, NT)
         )
-        n_grad = n_grad.astype(bf16).reshape(zs, tokens, D_MODEL)
-        from_norm, gain_grad = two_back(u[c], gain_one)(line_scatter(by_distance(n_grad)))
-        gain_one_grad = gain_one_grad + gain_grad
-        u_grad.append(resid_grad[c] + from_norm)
-    n_rows = rows_of(n_one)
-    z_w_grad = dot(n_rows, rows_of(z_grads), TN)
-    enter_w_grad = dot(n_rows, rows_of(v_grads), TN)
+        every = flat(u_all[c]).astype(f32)
+        scale = lax.rsqrt(jnp.mean(every * every, axis=-1, keepdims=True) + norm_eps)
+        gain_one_grad = gain_one_grad + jnp.sum(n_grad * (every * scale), axis=0)
+        n_parts.append(n_grad.astype(bf16))
+        total = line_scatter(n_parts[c].reshape(zs, tokens, D_MODEL))
+        u_grad.append(resid_grad[c] + norm_back(u[c], gain_one, total)[0])
+    v_grads[0] = after(v_grads[0], expert_grad, *n_parts)
+    bc_grads[0] = after(bc_grads[0], *n_parts)
+    enter_w_grad = dot(n_rows, rows_of(v_grads), TN).astype(bf16)
     bc_w_grad = dot(n_rows, rows_of(bc_grads), TN)
     bc_w_grad = bc_w_grad[:, : 2 * STATE_DIM] + bc_w_grad[:, 2 * STATE_DIM :]
-    side_grad = weight_scatter(
-        jnp.concatenate([z_w_grad, out_w_grad], axis=1).reshape(pieces, shard, 2 * inner)
+    mixer_grad = weight_scatter(
+        jnp.concatenate([z_w_grad, out_w_grad, enter_w_grad], axis=1).reshape(pieces, shard, 3 * inner + LANES)
     ).astype(f32)
-    enter_grad = weight_scatter(enter_w_grad.reshape(pieces, shard, inner + LANES)).astype(f32)
+
+    def to_shares(values, dim):
+        size = values.shape[dim] // (pieces * zs)
+        values = jnp.moveaxis(values, dim, 0).reshape(pieces, zs, size, -1)
+        return jnp.moveaxis(values, 3, 2).reshape(pieces, zs, -1)
 
     column = own * inner
     conv_x_full = lax.dynamic_update_slice(
         jnp.zeros((CONV_WIDTH + 1, INNER_DIM), f32), conv_grad[: CONV_WIDTH + 1, :inner], (jnp.int32(0), column)
     )
     gate_full = lax.dynamic_update_slice(jnp.zeros((INNER_DIM,), f32), gate_gain_grad, (column,))
-    head_full = lax.dynamic_update_slice(
-        jnp.zeros((3, HEAD_COUNT), f32), head_grad[:3, :heads], (jnp.int32(0), own * heads)
-    )
-    both = ("dp", "tensor")
-    bc_grad = lax.psum_scatter(bc_w_grad, both, scatter_dimension=0, tiled=True)
-    shared_grads = (
-        lax.psum_scatter(gain_one_grad, both, scatter_dimension=0, tiled=True),
-        lax.psum_scatter(conv_x_full, both, scatter_dimension=1, tiled=True),
-        lax.psum_scatter(conv_grad[: CONV_WIDTH + 1, inner:], both, scatter_dimension=1, tiled=True),
-        lax.psum_scatter(gate_full, both, scatter_dimension=0, tiled=True),
-        lax.psum_scatter(gain_two_grad, both, scatter_dimension=0, tiled=True),
-        lax.psum_scatter(router_grad, both, scatter_dimension=0, tiled=True),
-    )
-    stat_sum, head_sum = lax.psum((stat_terms, head_full), both)
+    small = [
+        (gain_one_grad, 0),
+        (conv_x_full, 1),
+        (conv_grad[: CONV_WIDTH + 1, inner:], 1),
+        (gate_full, 0),
+        (gain_two_grad, 0),
+        (router_grad, 0),
+    ]
+    shares = [to_shares(values, dim) for values, dim in small]
+    sizes = [share.shape[2] for share in shares]
+    shares = jnp.concatenate(shares, axis=2)
+    length = shares.shape[2]
+    shares = jnp.pad(shares, ((0, 0), (0, 0), (0, -length % (8 * LANES))))
+    wide_share = bc_w_grad.reshape(pieces, zs, -1, LANES)
+    shares = jnp.concatenate([wide_share, shares.reshape(pieces, zs, -1, LANES)], axis=2)
+    shares = jnp.sum(lax.all_to_all(shares, "dp", 0, 0), axis=0)
+    shares = jnp.sum(lax.all_to_all(shares, "tensor", 0, 0), axis=0)
+    bc_lines = wide_share.shape[2]
+    bc_grad = shares[:bc_lines].reshape(-1, 2 * STATE_DIM)
+    shares = shares[bc_lines:].reshape(-1)
+    ends = [sum(sizes[: k + 1]) for k in range(len(sizes))]
+    took = []
+    for (values, dim), size, end in zip(small, sizes, ends):
+        share = shares[end - size : end]
+        if values.ndim == 2:
+            other = values.shape[1 - dim]
+            share = share.reshape(other, size // other)
+            share = share if dim == 1 else share.T
+        took.append(share)
+    tile = jnp.zeros((8, LANES), f32)
+    tile = tile.at[:3, :heads].set(head_grad[:3, :heads]).at[3, :3].set(stat_terms)
+    tile = jnp.sum(lax.all_gather(tile, "dp"), axis=0)
+    tiles = lax.all_gather(tile, "tensor")
+    head_sum = jnp.transpose(tiles[:, :3, :heads], (1, 0, 2)).reshape(3, HEAD_COUNT)
+    stat_sum = jnp.sum(tiles[:, 3, :3], axis=0)
     stats = jnp.sqrt(stat_sum / (jnp.sum(lengths).astype(f32) * D_MODEL))
 
     def placed_back(values):
         whole = jnp.concatenate([value.astype(bf16).reshape(per, rows, D_MODEL) for value in values], axis=0)
         return jnp.transpose(whole, (1, 0, 2))
 
-    expert_grad = jnp.concatenate([weight_scatter(grads) for grads in expert_grad], axis=0).astype(f32)
-    ups, pairs = EXPERTS + 2, EXPERTS // 2
+    expert_grad = expert_grad.astype(f32)
+    ups, downs = EXPERTS + 2, EXPERTS // 2
+    z_part, out_part = mixer_grad[:, :inner], mixer_grad[:, inner : 2 * inner]
+    x_part, dt_part = mixer_grad[:, 2 * inner : 3 * inner], mixer_grad[:, 3 * inner :]
     return (
         placed_back(output),
         placed_back(u_grad),
-        shared_grads[0],
-        jnp.stack([side_grad[:, :inner], enter_grad[:, :inner]], axis=1),
+        took[0],
+        jnp.stack([z_part, x_part], axis=1),
         bc_grad,
-        enter_grad[:, inner : inner + heads],
-        shared_grads[1],
-        shared_grads[2],
+        dt_part[:, :heads],
+        took[1],
+        took[2],
         head_sum,
-        shared_grads[3],
-        side_grad[:, inner:].T,
-        shared_grads[4],
-        shared_grads[5],
+        took[3],
+        out_part.T,
+        took[4],
+        took[5],
         expert_grad[:EXPERTS].reshape(EXPERTS, shard, 2, half),
-        expert_grad[ups : ups + pairs].transpose(0, 2, 1).reshape(EXPERTS, half, shard),
+        expert_grad[ups : ups + downs].transpose(0, 2, 1).reshape(EXPERTS, half, shard),
         expert_grad[EXPERTS:ups].reshape(2, shard, 2, half).transpose(1, 2, 0, 3).reshape(shard, 2, 2 * half),
-        expert_grad[ups + pairs].T,
+        expert_grad[ups + downs].T,
         stats,
     )
 

time: 1330 us -> 1150 us (0.86)
  waiting for transfers between devices: 531 us -> 358 us
  blocking collectives: 120 us -> 273 us
  starting transfers between devices: 174 us -> 57.9 us
  other arithmetic: 96.2 us -> 46.6 us
    all_to_all x0 -> x6, waiting for transfers between devices: none -> 219 us  [the longest x3 173 us: line_gather(): lax.all_to_all(row_major(jnp.broadcast_to(value[None], (size,) + value.sh...]
    reduce_scatter x5 -> x2, waiting for transfers between devices: 200 us -> 0.01 us  [weight_scatter(): lax.psum_scatter(grads.astype(bf16), 'dp', scatter_dimension=0, tiled=False)]
    ppermute x48 -> x3, starting transfers between devices: 158 us -> 3.98 us  [line_scatter_steps(): lax.ppermute(row_major(sent), 'tensor', [(a, (a + step) % size) for a in...]
    ppermute x48 -> x3, waiting for transfers between devices: 184 us -> 50.6 us  [line_scatter_steps(): lax.ppermute(row_major(sent), 'tensor', [(a, (a + step) % size) for a in...]
    all_to_all x1 -> x3, blocking collectives: 23.7 us -> 132 us  [the longest x1 87.6 us: line_gather(): lax.all_to_all(row_major(jnp.broadcast_to(value[None], (size,) + value.sh...]
    reduce_scatter x1 -> x0, waiting for transfers between devices: 99.6 us -> none  [body(): bc_grad = lax.psum_scatter(bc_w_grad, both, scatter_dimension=0, tiled=True)]
    all_gather x1 -> x2, blocking collectives: 14.7 us -> 66 us  [the longest x1 57.7 us: body(): tiles = lax.all_gather(tile, 'tensor')]
    unnamed x1 -> x0, blocking collectives: 44 us -> none
  transfers between devices with their start and end apart: 64 -> 20, of which waited for: 28 -> 12; matrix products, arithmetic and copies ran while one was open for 18% -> 15% of each run, Pallas kernels for 9% -> 9%
where the time goes in v2:
time: 1150 us; the launch traced here: 1140 us
  waiting for transfers between devices  358 us (31%)
  blocking collectives  273 us (24%)
  Pallas kernels  208 us (18%)
  local copies, waits for them, and re-layouts  116 us (10%)
  matrix products  66.5 us (6%)
  starting transfers between devices  57.9 us (5%)
  other arithmetic  46.6 us (4%)
  between operations  16.1 us (1%)
    all_to_all x3, waiting for transfers between devices, line_gather(): lax.all_to_all(row_major(jnp.broadcast_to(value[None], (size,) + value.sh...  173 us
    all_to_all x4, waiting for transfers between devices, exchanged(): return lax.all_to_all(rows, 'dp', 0, 0, tiled=False)  88 us
    all_to_all x1, blocking collectives, line_gather(): lax.all_to_all(row_major(jnp.broadcast_to(value[None], (size,) + value.sh...  87.6 us
    pallas_call x1, Pallas kernels, experts(): pl.pallas_call(expert_kernel, grid=(pairs,), in_specs=[pl.BlockSpec((toke...  71.6 us
    dot_general x13, matrix products, dot(): lax.dot_general(a, b, (dims, ((), ())), precision=precision, preferred_el...  66.5 us
    all_gather x1, blocking collectives, body(): tiles = lax.all_gather(tile, 'tensor')  57.7 us
    psum x1, blocking collectives, body(): square_sum = lax.psum(squares[:, :, 0], 'tensor')  56.2 us
    ppermute x3, waiting for transfers between devices, line_scatter_steps(): lax.ppermute(row_major(sent), 'tensor', [(a, (a + step) % size) for a in...  50.6 us
  transfers between devices with their start and end apart: 20, of which 12 were waited for; matrix products, arithmetic and copies ran while one was open for 15% of the time, Pallas kernels for 9%

profile of v2, /device:TPU:0, one launch (start us, length us, event | category | flops | bytes accessed | tf_op | source)
XLA Modules:
  0.0 1141.5 jit_solution(602252122226397971)
XLA Ops:
  12.9 2.8 reshape.419
  21.7 6.5 all-to-all-start
  28.3 8.9 all-gather.4
  37.3 61.5 %all-to-all-done.refs_1_ = bf16[4,256,1536]{2,1,0:T(8,128)(2,1)S(1)} async-done(((bf16[4,256,1536]{2,1,0:T(8,128)(2,1)}), bf16[4,256,1536]{2,1,0:T(8,128)(2,1)S(1)}, u32[]{:S(2)}, u32[]{:S(2)}) %all-to-all-start) | async-done | bytes 3145760 | tf_op jit(solution)/shard_map/all_to_all | solution.py:41
  102.9 3.6 fusion.2
  106.5 7.8 fusion.v_ref
  114.3 12.0 %mixer_enter.1 = (f32[4,256,768]{2,1,0:T(8,128)}, f32[4,256,256]{2,1,0:T(8,128)S(1)}, f32[4,256,256]{2,1,0:T(8,128)S(1)}, f32[4,768,128]{2,1,0:T(8,128)S(1)}) custom-call(f32[4,4,64,1152]{3,2,1,0:T(8,128)} %fusion.v_ref, f32[4,8,1024]{2,1,0:T(8,128)S(1)} %pad.42.halo_ref, f32[8,1024]{1,0:T(8,128)S(1)} %select_maximum_fusion.cw_ref, f32[8,128]{1,0:T(8,128)S(1)} %pad.44.hp_ref), custom_call_target="tpu_custom_call" | custom-call | flops 13516800000 | bytes 1024 | tf_op jit(solution)/shard_map/mixer_enter/pallas_call | solution.py:175
  129.8 6.5 all-to-all-start.1
  136.4 37.8 %all-to-all-done.1 = f32[8,392,128]{2,1,0:T(8,128)S(1)} async-done(((f32[8,392,128]{2,1,0:T(8,128)}), f32[8,392,128]{2,1,0:T(8,128)S(1)}, u32[]{:S(2)}, u32[]{:S(2)}) %all-to-all-start.1) | async-done | bytes 1605664 | tf_op jit(solution)/shard_map/all_to_all | solution.py:222
  176.4 4.0 all-to-all-start.2
  184.6 33.8 %all-to-all-done.2 = f32[8,384,128]{2,1,0:T(8,128)S(1)} async-done(((f32[8,384,128]{2,1,0:T(8,128)}), f32[8,384,128]{2,1,0:T(8,128)S(1)}, u32[]{:S(2)}, u32[]{:S(2)}) %all-to-all-start.2) | async-done | bytes 1572896 | tf_op jit(solution)/shard_map/all_to_all | solution.py:222
  218.4 3.6 broadcast_in_dim.36
  222.0 4.8 all-to-all-start.3
  231.4 4.6 mixer_inner.1.yi_ref
  237.7 6.9 fusion.15
  244.6 50.2 %all-to-all-done.3.refs_1_ = bf16[4,256,1536]{2,1,0:T(8,128)(2,1)} async-done(((bf16[4,256,1536]{2,1,0:T(8,128)(2,1)}), bf16[4,256,1536]{2,1,0:T(8,128)(2,1)}, u32[]{:S(2)}, u32[]{:S(2)}) %all-to-all-start.3) | async-done | bytes 3145760 | tf_op jit(solution)/shard_map/all_to_all | solution.py:41
  298.6 8.1 mixer_leave.1
  306.7 6.2 convolution_convert_fusion
  313.0 4.7 all-to-all-start.4
  317.9 56.2 %psum.14 = f32[4,256]{1,0:T(4,128)S(1)} all-reduce(f32[4,256]{1,0:T(4,128)S(1)} %slice_reduce_fusion), channel_id=1, replica_groups=mesh['dp'=8,'tensor'=4] {'tensor'}, use_global_device_ids=true, to_apply=%region_2.3 | all-reduce | flops 1024 | bytes 8192 | tf_op jit(solution)/shard_map/psum | solution.py:823
  374.2 13.9 %all-to-all-done.4 = bf16[4,256,1536]{2,1,0:T(8,128)(2,1)} async-done(((bf16[4,256,1536]{2,1,0:T(8,128)(2,1)}), bf16[4,256,1536]{2,1,0:T(8,128)(2,1)}, u32[]{:S(2)}, u32[]{:S(2)}) %all-to-all-start.4) | async-done | bytes 3145760 | tf_op jit(solution)/shard_map/all_to_all | solution.py:45
  388.1 2.6 convert_reduce_fusion.2
  394.5 5.2 all-to-all-start.5
  403.9 4.7 copy.309
  408.6 60.9 %all-to-all-done.5 = bf16[4,256,1536]{2,1,0:T(8,128)(2,1)} async-done(((bf16[4,256,1536]{2,1,0:T(8,128)(2,1)}), bf16[4,256,1536]{2,1,0:T(8,128)(2,1)}, u32[]{:S(2)}, u32[]{:S(2)}) %all-to-all-start.5) | async-done | bytes 3145760 | tf_op jit(solution)/shard_map/all_to_all | solution.py:41
  469.5 4.7 copy.308
  474.2 71.6 %experts.1 = (bf16[1024,1536]{1,0:T(8,128)(2,1)}, bf16[1024,1536]{1,0:T(8,128)(2,1)}, bf16[1024,128]{1,0:T(8,128)(2,1)}, bf16[9,1024,256]{2,1,0:T(8,128)(2,1)}, bf16[9,1024,512]{2,1,0:T(8,128)(2,1)}) custom-call(bf16[1024,1536]{1,0:T(8,128)(2,1)} %bitcast.21.n_ref, bf16[1024,1536]{1,0:T(8,128)(2,1)} %bitcast.22.g_ref, f32[1024,128]{1,0:T(8,128)} %bitcast.265, ...), custom_call_target="tpu_custom_call" | custom-call | flops 81100800000 | bytes 1024 | tf_op jit(solution)/shard_map/experts/pallas_call | solution.py:631
  547.7 34.6 %expert_grads.1 = bf16[8,27,192,256]{3,2,1,0:T(8,128)(2,1)} custom-call(bf16[1536,1024]{1,0:T(8,128)(2,1)S(1)} %bitcast.231, bf16[1536,1024]{1,0:T(8,128)(2,1)} %bitcast.251, bf16[9,1024,512]{2,1,0:T(8,128)(2,1)} %get-tuple-element.87.refs_2_, bf16[9,1024,256]{2,1,0:T(8,128)(2,1)} %get-tuple-element.88.refs_3_), custom_call_target="tpu_custom_call" | custom-call | flops 45056000000 | bytes 1024 | tf_op jit(solution)/shard_map/expert_grads/pallas_call | solution.py:697
  582.4 3.0 dynamic-slice_bitcast_fusion.2
  589.4 18.7 %collective-permute-done.1 = bf16[256,1536]{1,0:T(8,128)(2,1)} collective-permute-done((bf16[256,1536]{1,0:T(8,128)(2,1)}, bf16[256,1536]{1,0:T(8,128)(2,1)}, u32[]{:S(2)}, u32[]{:S(2)}) %collective-permute-start.1) | collective-permute-done | bytes 786464 | tf_op jit(solution)/shard_map/ppermute | solution.py:55
  608.1 31.9 %collective-permute-done.2 = bf16[256,1536]{1,0:T(8,128)(2,1)} collective-permute-done((bf16[256,1536]{1,0:T(8,128)(2,1)}, bf16[256,1536]{1,0:T(8,128)(2,1)}, u32[]{:S(2)}, u32[]{:S(2)}) %collective-permute-start.2) | collective-permute-done | bytes 786464 | tf_op jit(solution)/shard_map/ppermute | solution.py:55
  640.0 3.1 multiply_reduce_fusion.2
  645.0 87.6 %all_to_all.65 = bf16[4,256,1536]{2,1,0:T(8,128)(2,1)S(1)} all-to-all(bf16[4,256,1536]{2,1,0:T(8,128)(2,1)S(1)} %broadcast_in_dim.80), channel_id=1, replica_groups=mesh['dp'=8,'tensor'=4] {'tensor'}, dimensions={0} | all-to-all | bytes 6291456 | tf_op jit(solution)/shard_map/all_to_all | solution.py:41
  732.6 7.5 fusion.4
  740.2 9.9 psum.15
  751.5 9.3 mixer_unmix.1
  763.2 4.1 all-to-all-start.8
  774.5 4.1 multiply_convert_fusion
  778.6 9.7 all-to-all-done.8.got_ref
  788.3 4.6 all-to-all-start.7
  792.9 6.5 convolution_convert_fusion.3
  802.3 23.1 %mixer_pairs.1 = (f32[4,256,768]{2,1,0:T(8,128)}, f32[4,256,256]{2,1,0:T(8,128)S(1)}, f32[4,256,256]{2,1,0:T(8,128)S(1)}) custom-call(f32[4,256,768]{2,1,0:T(8,128)} %get-tuple-element.66.xs_ref, f32[4,256,256]{2,1,0:T(8,128)S(1)} %copy-done.26, f32[4,256,256]{2,1,0:T(8,128)S(1)} %copy-done.15, f32[4,256,768]{2,1,0:T(8,128)} %get-tuple-element.76.gy_ref), custom_call_target="tpu_custom_call" | custom-call | flops 47308800000 | bytes 1024 | tf_op jit(solution)/shard_map/mixer_pairs/pallas_call | solution.py:426
  829.0 32.2 %all-to-all-done.7 = bf16[4,256,1536]{2,1,0:T(8,128)(2,1)} async-done(((bf16[4,256,1536]{2,1,0:T(8,128)(2,1)}), bf16[4,256,1536]{2,1,0:T(8,128)(2,1)}, u32[]{:S(2)}, u32[]{:S(2)}) %all-to-all-start.7) | async-done | bytes 3145760 | tf_op jit(solution)/shard_map/all_to_all | solution.py:45
  861.2 4.8 all-to-all-start.9
  866.4 6.4 fusion.13
  872.8 3.9 convolution_convert_fusion.2
  876.7 3.6 convert_reduce_fusion.1.refs_1_
  880.4 6.7 all-to-all-done.9
  887.1 43.6 %mixer_back.1 = (bf16[4,4,64,896]{3,2,1,0:T(8,128)(2,1)}, f32[4,4,64,256]{3,2,1,0:T(8,128)}, f32[4,8,1024]{2,1,0:T(8,128)}, f32[8,1024]{1,0:T(8,128)}, f32[8,128]{1,0:T(8,128)}) custom-call(f32[4,4,64,1152]{3,2,1,0:T(8,128)} %fusion.v_ref, f32[4,8,1024]{2,1,0:T(8,128)} %copy-done.8, f32[8,1024]{1,0:T(8,128)} %copy-done.9, f32[8,128]{1,0:T(8,128)} %copy-done.11, ...), custom_call_target="tpu_custom_call" | custom-call | flops 20275200000 | bytes 1024 | tf_op jit(solution)/shard_map/mixer_back/pallas_call | solution.py:528
  941.7 3.4 fusion.5
  945.8 3.8 multiply_reduce_fusion
  951.5 5.0 convolution_convert_fusion.1
  956.5 3.7 pad_maximum_fusion
  960.2 10.1 copy.297
  971.3 3.1 fusion.55
  975.9 34.2 %all_to_all.66 = f32[8,4,112,128]{3,2,1,0:T(8,128)S(1)} all-to-all(f32[8,4,112,128]{3,2,1,0:T(8,128)S(1)} %pad_maximum_fusion.2), channel_id=1, replica_groups=mesh['dp'=8,'tensor'=4] {'dp'}, dimensions={0} | all-to-all | bytes 3670016 | tf_op jit(solution)/shard_map/all_to_all | solution.py:964
  1010.1 9.9 all_to_all.67
  1020.1 5.0 all-to-all-start.10
  1026.6 3.6 fusion.20
  1032.3 8.3 all_gather.44
  1040.6 57.7 %all-gather.3 = f32[32,128]{1,0:T(8,128)S(1)} all-gather(f32[8,128]{1,0:T(8,128)S(1)} %reduce_sum.217), channel_id=5, replica_groups=mesh['dp'=8,'tensor'=4] {'tensor'}, dimensions={0}, use_global_device_ids=true | all-gather | bytes 20480 | tf_op jit(solution)/shard_map/all_gather | solution.py:981
  1104.5 2.6 convert_reduce_fusion
  1120.0 3.1 copy.303
  1123.1 3.0 reshape.453
  (374 shorter events, 116.0 us)
Async XLA Ops:
  7.2 8.5 copy-start
  7.2 3.6 copy-start.75
  7.2 3.7 copy-start.56
  7.2 95.6 %all-gather.9.cloned.1.call-start = ((), (), s32[]{:S(2)}) async-start(), calls=%async_computation.17 | async-start | bytes 3981312 | tf_op jit(solution)/shard_map/all_gather | solution.py:61
  10.7 227.0 %all-gather.11.cloned.1.call-start = ((), (), s32[]{:S(2)}) async-start(), calls=%async_computation.18 | async-start | bytes 5750784 | tf_op jit(solution)/shard_map/all_gather | solution.py:61
  11.8 462.4 %all-gather.13.cloned.1.call-start = ((), (), s32[]{:S(2)}) async-start(), calls=%async_computation.19 | async-start | bytes 23887872 | tf_op jit(solution)/shard_map/all_gather | solution.py:61
  21.7 6.5 copy-start.83
  21.7 6.5 copy-start.84
  21.7 77.1 %all-to-all-start = ((bf16[4,256,1536]{2,1,0:T(8,128)(2,1)}), bf16[4,256,1536]{2,1,0:T(8,128)(2,1)S(1)}, u32[]{:S(2)}, u32[]{:S(2)}) async-start(bf16[4,256,1536]{2,1,0:T(8,128)(2,1)} %broadcast_in_dim.32), calls=%async_computation | async-start | bytes 6291456 | tf_op jit(solution)/shard_map/all_to_all | solution.py:41
  37.3 63.1 %copy-start.58 = (f32[1536]{0:T(1024)}, f32[1536]{0:T(1024)S(1)}, u32[]{:S(2)}) copy-start(f32[1536]{0:T(1024)S(1)} %get-tuple-element.223) | copy-start | bytes 18436
  100.7 2.1 collective-permute-start
  102.3 12.0 %copy-start.9 = (f32[8,1024]{1,0:T(8,128)}, f32[8,1024]{1,0:T(8,128)S(1)}, u32[]{:S(2)}) copy-start(f32[8,1024]{1,0:T(8,128)S(1)} %select_maximum_fusion.cw_ref) | copy-start | bytes 98308
  102.4 4.1 copy-start.47
  102.4 11.9 %copy-start.11 = (f32[8,128]{1,0:T(8,128)}, f32[8,128]{1,0:T(8,128)S(1)}, u32[]{:S(2)}) copy-start(f32[8,128]{1,0:T(8,128)S(1)} %pad.44.hp_ref) | copy-start | bytes 12292
  106.5 7.9 copy-start.8
  129.8 44.3 %all-to-all-start.1 = ((f32[8,392,128]{2,1,0:T(8,128)}), f32[8,392,128]{2,1,0:T(8,128)S(1)}, u32[]{:S(2)}, u32[]{:S(2)}) async-start(f32[8,392,128]{2,1,0:T(8,128)} %pad_maximum_fusion.3), calls=%async_computation.1 | async-start | bytes 3211264 | tf_op jit(solution)/shard_map/all_to_all | solution.py:222
  176.4 4.0 copy-start.81
  176.4 42.0 %all-to-all-start.2 = ((f32[8,384,128]{2,1,0:T(8,128)}), f32[8,384,128]{2,1,0:T(8,128)S(1)}, u32[]{:S(2)}, u32[]{:S(2)}) async-start(f32[8,384,128]{2,1,0:T(8,128)} %copy-done.5), calls=%async_computation.2 | async-start | bytes 3145728 | tf_op jit(solution)/shard_map/all_to_all | solution.py:222
  218.4 3.6 copy-start.2
  222.0 5.0 copy-start.77
  222.0 72.7 %all-to-all-start.3 = ((bf16[4,256,1536]{2,1,0:T(8,128)(2,1)}), bf16[4,256,1536]{2,1,0:T(8,128)(2,1)}, u32[]{:S(2)}, u32[]{:S(2)}) async-start(bf16[4,256,1536]{2,1,0:T(8,128)(2,1)} %broadcast_in_dim.36), calls=%async_computation.3 | async-start | bytes 6291456 | tf_op jit(solution)/shard_map/all_to_all | solution.py:41
  227.1 67.7 %copy-start.10 = (f32[8,768]{1,0:T(8,128)}, f32[8,768]{1,0:T(8,128)S(1)}, u32[]{:S(2)}) copy-start(f32[8,768]{1,0:T(8,128)S(1)} %pad.47.hp_ref.skip_ref) | copy-start | bytes 73732
  306.7 6.2 copy-start.16
  313.0 75.1 %all-to-all-start.4 = ((bf16[4,256,1536]{2,1,0:T(8,128)(2,1)}), bf16[4,256,1536]{2,1,0:T(8,128)(2,1)}, u32[]{:S(2)}, u32[]{:S(2)}) async-start(bf16[4,256,1536]{2,1,0:T(8,128)(2,1)} %bitcast.250), calls=%async_computation.4 | async-start | bytes 6291456 | tf_op jit(solution)/shard_map/all_to_all | solution.py:45
  374.0 16.7 %copy-start.62 = (f32[4,256]{1,0:T(4,128)}, f32[4,256]{1,0:T(4,128)S(1)}, u32[]{:S(2)}) copy-start(f32[4,256]{1,0:T(4,128)S(1)} %psum.14) | copy-start | bytes 12292
  374.0 16.7 %copy-start.66 = (f32[4,256]{1,0:T(4,128)}, f32[4,256]{1,0:T(4,128)S(1)}, u32[]{:S(2)}) copy-start(f32[4,256]{1,0:T(4,128)S(1)} %add_rsqrt_fusion) | copy-start | bytes 12292
  374.2 16.5 %copy-start.72 = (f32[256]{0:T(256)}, f32[256]{0:T(256)S(1)}, u32[]{:S(2)}) copy-start(f32[256]{0:T(256)S(1)} %mul.236) | copy-start | bytes 3076
  394.5 5.6 copy-start.68
  394.5 75.0 %all-to-all-start.5 = ((bf16[4,256,1536]{2,1,0:T(8,128)(2,1)}), bf16[4,256,1536]{2,1,0:T(8,128)(2,1)}, u32[]{:S(2)}, u32[]{:S(2)}) async-start(bf16[4,256,1536]{2,1,0:T(8,128)(2,1)} %broadcast_in_dim.77), calls=%async_computation.5 | async-start | bytes 6291456 | tf_op jit(solution)/shard_map/all_to_all | solution.py:41
  399.7 549.9 %reduce-scatter.3.cloned.1.call-start = ((), (), s32[]{:S(2)}) async-start(), calls=%async_computation.15 | async-start | bytes 23887872 | tf_op jit(solution)/shard_map/reduce_scatter | solution.py:65
  585.4 22.7 %collective-permute-start.1 = (bf16[256,1536]{1,0:T(8,128)(2,1)}, bf16[256,1536]{1,0:T(8,128)(2,1)}, u32[]{:S(2)}, u32[]{:S(2)}) collective-permute-start(bf16[256,1536]{1,0:T(8,128)(2,1)} %get-tuple-element.235), channel_id=1, source_target_pairs={{0,1},{1,2},{2,3},{3,0},{4,5},{5,6},{6,7},{7,4},{8,9},{9,10},{10,1... | collective-permute-start | bytes 2359304 | tf_op jit(solution)/shard_map/ppermute | solution.py:55
  585.4 54.6 %collective-permute-start.2 = (bf16[256,1536]{1,0:T(8,128)(2,1)}, bf16[256,1536]{1,0:T(8,128)(2,1)}, u32[]{:S(2)}, u32[]{:S(2)}) collective-permute-start(bf16[256,1536]{1,0:T(8,128)(2,1)} %get-tuple-element.237), channel_id=1, source_target_pairs={{0,2},{1,3},{2,0},{3,1},{4,6},{5,7},{6,4},{7,5},{8,10},{9,11},{10,... | collective-permute-start | bytes 2359304 | tf_op jit(solution)/shard_map/ppermute | solution.py:55
  587.4 52.6 %collective-permute-start.3 = (bf16[256,1536]{1,0:T(8,128)(2,1)}, bf16[256,1536]{1,0:T(8,128)(2,1)}, u32[]{:S(2)}, u32[]{:S(2)}) collective-permute-start(bf16[256,1536]{1,0:T(8,128)(2,1)} %get-tuple-element.236), channel_id=1, source_target_pairs={{0,3},{1,0},{2,1},{3,2},{4,7},{5,4},{6,5},{7,6},{8,11},{9,8},{10,9... | collective-permute-start | bytes 2359304 | tf_op jit(solution)/shard_map/ppermute | solution.py:55
  589.4 53.7 %copy-start.32 = (f32[256,1536]{1,0:T(8,128)S(1)}, f32[256,1536]{1,0:T(8,128)}, u32[]{:S(2)}) copy-start(f32[256,1536]{1,0:T(8,128)} %copy-done.31) | copy-start | bytes 4718596
  589.4 53.7 %copy-start.42 = (f32[4,64,1536]{2,1,0:T(8,128)S(1)}, f32[4,64,1536]{2,1,0:T(8,128)}, u32[]{:S(2)}) copy-start(f32[4,64,1536]{2,1,0:T(8,128)} %copy-done.41) | copy-start | bytes 4718596
  645.0 87.6 %copy-start.78 = (f32[768]{0:T(1024)S(1)}, f32[768]{0:T(1024)}, u32[]{:S(2)}) copy-start(f32[768]{0:T(1024)} %param.34) | copy-start | bytes 9220
  645.0 87.6 %copy-start.85 = (f32[1024,768]{1,0:T(8,128)S(1)}, f32[1024,768]{1,0:T(8,128)}, u32[]{:S(2)}) copy-start(f32[1024,768]{1,0:T(8,128)} %fusion.15) | copy-start | bytes 9437188
  645.0 87.6 %copy-start.86 = (f32[4,256,768]{2,1,0:T(8,128)S(1)}, f32[4,256,768]{2,1,0:T(8,128)}, u32[]{:S(2)}) copy-start(f32[4,256,768]{2,1,0:T(8,128)} %get-tuple-element.74.y_ref) | copy-start | bytes 9437188
  732.6 7.5 copy-start.34
  732.6 17.4 %copy-start.63 = (f32[4,256]{1,0:T(4,128)S(1)}, f32[4,256]{1,0:T(4,128)}, u32[]{:S(2)}) copy-start(f32[4,256]{1,0:T(4,128)} %copy-done.62) | copy-start | bytes 12292
  763.2 25.1 %all-to-all-start.8 = ((f32[8,384,128]{2,1,0:T(8,128)}), f32[8,384,128]{2,1,0:T(8,128)S(1)}, u32[]{:S(2)}, u32[]{:S(2)}) async-start(f32[8,384,128]{2,1,0:T(8,128)} %bitcast.232), calls=%async_computation.8 | async-start | bytes 3145728 | tf_op jit(solution)/shard_map/all_to_all | solution.py:222
  788.3 72.9 %all-to-all-start.7 = ((bf16[4,256,1536]{2,1,0:T(8,128)(2,1)}), bf16[4,256,1536]{2,1,0:T(8,128)(2,1)}, u32[]{:S(2)}, u32[]{:S(2)}) async-start(bf16[4,256,1536]{2,1,0:T(8,128)(2,1)} %after.8), calls=%async_computation.7 | async-start | bytes 6291456 | tf_op jit(solution)/shard_map/all_to_all | solution.py:45
  829.0 37.4 %copy-start.19 = (bf16[4,4,64,768]{3,2,1,0:T(8,128)(2,1)S(1)}, bf16[4,4,64,768]{3,2,1,0:T(8,128)(2,1)}, u32[]{:S(2)}) copy-start(bf16[4,4,64,768]{3,2,1,0:T(8,128)(2,1)} %copy-done.18) | copy-start | bytes 4718596
  861.2 25.9 %all-to-all-start.9 = ((f32[8,384,128]{2,1,0:T(8,128)}), f32[8,384,128]{2,1,0:T(8,128)}, u32[]{:S(2)}, u32[]{:S(2)}) async-start(f32[8,384,128]{2,1,0:T(8,128)} %copy-done.4), calls=%async_computation.9 | async-start | bytes 3145728 | tf_op jit(solution)/shard_map/all_to_all | solution.py:222
  866.0 6.8 copy-start.17
  866.0 263.8 %reduce-scatter.5.cloned.1.call-start = ((), (), s32[]{:S(2)}) async-start(), calls=%async_computation.16 | async-start | bytes 8404992 | tf_op jit(solution)/shard_map/reduce_scatter | solution.py:65
  866.4 6.4 copy-start.49
  931.6 3.2 collective-permute-start.4
  934.0 7.6 slice-start.1
  934.0 7.6 slice-start.2
  941.4 3.7 slice-start.4
  941.5 3.6 copy-start.44
  941.7 4.1 slice-start.5
  941.7 4.1 copy-start.65
  951.5 5.0 copy-start.51
  951.5 5.0 copy-start.52
  1020.1 5.0 copy-start.71
  1020.1 5.1 copy-start.82
  1020.1 6.4 copy-start.80
  1020.1 6.4 copy-start.33
  1020.1 6.4 copy-start.40
  1020.1 6.4 copy-start.73
  1020.1 84.4 %all-to-all-start.10 = ((bf16[4,256,1536]{2,1,0:T(8,128)(2,1)}), bf16[4,256,1536]{2,1,0:T(8,128)(2,1)}, u32[]{:S(2)}, u32[]{:S(2)}) async-start(bf16[4,256,1536]{2,1,0:T(8,128)(2,1)} %bitcast.57), calls=%async_computation.10 | async-start | bytes 6291456 | tf_op jit(solution)/shard_map/all_to_all | solution.py:45
  1117.4 5.6 slice-start
  (49 other events, 87.0 us)
Sparse Core Ops, SparseCore 0:
  10.8 36.6 all-gather.8
  49.4 40.5 all-gather.10
  91.9 141.4 all-gather.12
  582.5 136.2 reduce-scatter.2
  970.4 71.3 reduce-scatter.4

commit v3 on v2

--- a/solution.py
+++ b/solution.py
@@ -38,23 +38,40 @@
 
 def line_gather(value):
     size = lax.axis_size("tensor")
-    return lax.all_to_all(row_major(jnp.broadcast_to(value[None], (size,) + value.shape)), "tensor", 0, 0)
-
-
-def line_scatter(blocks):
-    got = lax.all_to_all(row_major(blocks), "tensor", 0, 0)
-    return row_major(jnp.sum(got.astype(f32), axis=0))
-
-
-def line_scatter_steps(blocks):
+    return [value] + [
+        row_major(lax.ppermute(row_major(value), "tensor", [(a, (a - step) % size) for a in range(size)]))
+        for step in range(1, size)
+    ]
+
+
+def line_parts(block_of):
     size = lax.axis_size("tensor")
+    return [block_of(0)] + [
+        lax.ppermute(row_major(block_of(step)), "tensor", [(a, (a + step) % size) for a in range(size)])
+        for step in range(1, size)
+    ]
+
+
+def summed(parts):
+    total = parts[0].astype(f32)
+    for part in parts[1:]:
+        total = total + part.astype(f32)
+    return row_major(total)
+
+
+def in_order(blocks):
+    size = len(blocks)
     own = lax.axis_index("tensor")
-    total = lax.dynamic_index_in_dim(blocks, own, 0, False).astype(f32)
-    for step in range(1, size):
-        sent = lax.dynamic_index_in_dim(blocks, (own + step) % size, 0, False)
-        sent = lax.ppermute(row_major(sent), "tensor", [(a, (a + step) % size) for a in range(size)])
-        total = total + sent.astype(f32)
-    return row_major(total)
+    whole = jnp.zeros((size,) + blocks[0].shape, blocks[0].dtype)
+    for k in range(size):
+        whole = lax.dynamic_update_index_in_dim(whole, blocks[k], (own + k) % size, 0)
+    return whole
+
+
+def by_distance(whole):
+    size = whole.shape[0]
+    own = lax.axis_index("tensor")
+    return lambda k: lax.dynamic_index_in_dim(whole, (own + k) % size, 0, False)
 
 
 def weight_gather(shard):
@@ -62,7 +79,7 @@
 
 
 def weight_scatter(grads):
-    return lax.psum_scatter(grads.astype(bf16), "dp", scatter_dimension=0, tiled=False)
+    return row_major(lax.psum_scatter(grads.astype(bf16), "dp", scatter_dimension=0, tiled=False))
 
 
 def rms_scale(values, gain_vec):
@@ -87,6 +104,11 @@
 
 def dot_split(a, b, dims):
     return dot(a[0], b[0], dims) + (dot(a[0], b[1], dims) + dot(a[1], b[0], dims))
+
+
+def dot_ones(values, ones, dims):
+    upper, lower = split_parts(values)
+    return dot(upper, ones, dims) + dot(lower, ones, dims)
 
 
 def after(value, *others):
@@ -109,13 +131,13 @@
 def head_spread(inner):
     row = lax.broadcasted_iota(jnp.int32, (LANES, inner), 0)
     col = lax.broadcasted_iota(jnp.int32, (LANES, inner), 1)
-    return (col // HEAD_DIM == row).astype(f32)
+    return (col // HEAD_DIM == row).astype(bf16)
 
 
 def head_sums(inner):
     row = lax.broadcasted_iota(jnp.int32, (inner, LANES), 0)
     col = lax.broadcasted_iota(jnp.int32, (inner, LANES), 1)
-    return (row // HEAD_DIM == col).astype(f32)
+    return (row // HEAD_DIM == col).astype(bf16)
 
 
 def lower_ones(extent):
@@ -159,7 +181,7 @@
     unused_raw, step = step_sizes(v_ref, hp_ref, width, extent)
     log_sum = dot(lower_ones(extent), -step * jnp.exp(hp_ref[0:1, :]), NN, highest)
     tail = jnp.exp(log_sum[extent - 1 : extent, :] - log_sum) * step
-    spread = dot(tail, head_spread(inner), NN, highest)
+    spread = dot_ones(tail, head_spread(inner), NN)
     xs_ref[0] = xs
     rw_ref[0] = act[:, inner:]
     dl_ref[0, :, 0:LANES] = step
@@ -222,7 +244,7 @@
     return lax.all_to_all(rows, "dp", 0, 0, tiled=False)
 
 
-def states_forward(s_local, log_last):
+def states_forward(beside, s_local, log_last):
     count = lax.axis_size("dp")
     slots, inner, _ = s_local.shape
     share = slots * inner // count
@@ -231,7 +253,7 @@
     per_row = jnp.pad(per_row, ((0, 0), (0, lines * LANES - share))).reshape(count, lines, LANES)
     got = exchanged(jnp.concatenate([s_local.reshape(count, share, STATE_DIM), per_row], axis=1))
     decay = got[:, share:].reshape(count, lines * LANES)[:, :share, None]
-    entering = exchanged(scan_pieces(got[:, :share], decay, False))
+    entering = exchanged(after(scan_pieces(got[:, :share], decay, False), beside))
     return entering.reshape(slots, inner, STATE_DIM), decay
 
 
@@ -283,7 +305,7 @@
     extent = xs_ref.shape[1]
     zs, _, rows, _ = z_ref.shape
     read = split_parts(rw_ref[0, :, STATE_DIM:])
-    grown = dot(jnp.exp(dl_ref[0, :, LANES:]), head_spread(inner), NN, highest)
+    grown = dot_ones(jnp.exp(dl_ref[0, :, LANES:]), head_spread(inner), NN)
     y = yi_ref[0] + grown * dot_split(read, split_parts(h_ref[0]), NT) + hp_ref[3:4, :] * xs_ref[0]
     y_ref[0] = y
     z = z_ref[...].reshape(extent, inner)
@@ -347,7 +369,7 @@
     gy_ref[0] = gy
     gz = gated_grad * y * (logistic * (1.0 + z * (1.0 - logistic)))
     gz_ref[...] = gz.astype(bf16).reshape(zs, 1, rows, inner)
-    grown = dot(jnp.exp(dl_ref[0, :, LANES:]), head_spread(inner), NN, highest)
+    grown = dot_ones(jnp.exp(dl_ref[0, :, LANES:]), head_spread(inner), NN)
     s_ref[0] = dot_split(split_parts(gy * grown), split_parts(rw_ref[0, :, STATE_DIM:]), TN)
 
 
@@ -464,17 +486,19 @@
     spread = head_spread(inner)
     last = log_sum[extent - 1 : extent, :]
     tail_decay = jnp.exp(last - log_sum)
-    tail = dot(tail_decay * step, spread, NN, highest)
-    grown = dot(jnp.exp(log_sum), spread, NN, highest)
+    tail = dot_ones(tail_decay * step, spread, NN)
+    grown = dot_ones(jnp.exp(log_sum), spread, NN)
     gh = gh_ref[0]
     h_in = h_ref[0]
     gh_parts, h_parts = split_parts(gh), split_parts(h_in)
     tail_in = dot(write_low, gh_parts[0], NT)
-    tail_direct = tail_decay * dot(xs * tail_in, sums, NN, highest)
+    tail_direct = tail_decay * dot_ones(xs * tail_in, sums, NN)
     tail_weight = tail_direct * step
     state_part = grown * dot(read_low, h_parts[0], NT)
-    state_weight = dot(gy * state_part, sums, NN, highest)
-    kept = dot(sums, jnp.sum(gh * h_in, axis=1, keepdims=True) * jnp.ones((1, LANES), f32), TN, highest).T[0:1, :]
+    state_weight = dot_ones(gy * state_part, sums, NN)
+    held = split_parts(gh * h_in)
+    row_ones = jnp.ones((8, STATE_DIM), bf16)
+    kept = dot_ones(dot(row_ones, held[0], NT) + dot(row_ones, held[1], NT), sums, NN)[0:1, :]
     log_grad = gdl_ref[0, :, LANES:] + state_weight - tail_weight
     end_grad = jnp.sum(tail_weight, axis=0, keepdims=True) + jnp.exp(last) * kept
     rate_arg_grad = dot(lower_ones(extent), log_grad, TN, highest) + end_grad
@@ -486,7 +510,7 @@
     valid_lane = lax.broadcasted_iota(jnp.int32, (1, LANES), 1) < heads
     rate_grad = jnp.where(valid_lane, jnp.sum(-step * rate * rate_arg_grad, axis=0, keepdims=True), 0.0)
     raw_grad = jnp.where(valid_lane, raw_grad, 0.0)
-    skip_grad = jnp.sum(dot(gy * xs, sums, NN, highest), axis=0, keepdims=True)
+    skip_grad = jnp.sum(dot_ones(gy * xs, sums, NN), axis=0, keepdims=True)
 
     @pl.when(first)
     def _():
@@ -769,14 +793,13 @@
 
     u_slots = by_slot(block_input)
     u_low = [row_major(part(u_slots, c)) for c in chunk_ids]
-    u_all = [line_gather(u_low[c]) for c in chunk_ids]
+    u_all = [in_order(line_gather(u_low[c])) for c in chunk_ids]
     full_enter = weight_gather(enter_shard).reshape(D_MODEL, width + LANES)
     gains = jnp.stack([norm1_gain, norm2_gain], axis=1).astype(f32)
     gains = lax.all_gather(gains, "dp", axis=0, tiled=True)
     gain_one, gain_two = gains[:, 0], gains[:, 1]
     full_side = weight_gather(side_shard).reshape(D_MODEL, 2 * inner + LANES)
     full_z, full_out, full_router = full_side[:, :inner], full_side[:, inner : 2 * inner], full_side[:, 2 * inner :]
-    full_expert = weight_gather(expert_shard)
 
     positions = wide_index * piece_rows + own * rows + jnp.arange(rows, dtype=jnp.int32)
     valid = (positions[None, :] < lengths[:, None]).astype(f32)[:, :, None]
@@ -791,6 +814,8 @@
         (routes[..., None] == jnp.arange(LANES, dtype=jnp.int32)).astype(f32), axis=2
     )
     hot = jnp.transpose(hot.reshape(zs, rows, SLOT_COUNT, LANES), (0, 2, 1, 3))
+
+    hot_at = by_distance(hot)
 
     def flat(values):
         return values.reshape((zs * tokens,) + values.shape[2:])
@@ -808,18 +833,21 @@
         rim_rows = in_slots(n_one[c])[zs - 1, :, rows - rim :]
         prior = dot(passed_along(rim_rows, "dp", 1).reshape(per * rim, D_MODEL), full_enter[:, :width], NN)
         halo.append(jnp.pad(prior.reshape(per, rim, width), ((0, 0), (8 - rim, 0), (0, 0))))
+    g_blocks = [line_gather(after(grad_c[c].astype(bf16), u_all[CHUNKS - 1])) for c in chunk_ids]
+    for c in chunk_ids:
         entered.append(mixer_enter(v[c], halo[c], conv_w, hp, inner))
-    g_moe = [line_gather(after(grad_c[c].astype(bf16), u_all[CHUNKS - 1])) for c in chunk_ids]
     resid, mixed_all, y_all, h_all, decay_all, inv_alls, gg_all, n_two = [], [], [], [], [], [], [], []
     for c in chunk_ids:
         xs, rw, dl, s_local = entered[c]
         yi = mixer_inner(xs, rw, dl)
         z.append(in_slots(dot(n_one[c], full_z, NN)))
-        h_in, decay = states_forward(s_local, dl[:, piece_rows - 1, LANES : LANES + heads])
-        h_in = after(h_in, g_moe[c])
+        s_local = after(s_local, g_blocks[c][1], g_blocks[c][3])
+        h_in, decay = states_forward(g_blocks[c][2], s_local, dl[:, piece_rows - 1, LANES : LANES + heads])
+        if c == 0:
+            full_expert = weight_gather(after(expert_shard, h_in))
         y, gg, squares = mixer_leave(yi, xs, rw, dl, h_in, z[c], skip, gain_row)
         product = dot(flat(gg.reshape(zs, tokens, inner)), full_out, NT).astype(bf16)
-        mixed = line_scatter(product.reshape(zs, tokens, D_MODEL))
+        mixed = summed(line_parts(by_distance(product.reshape(zs, tokens, D_MODEL))))
         square_sum = lax.psum(squares[:, :, 0], "tensor")
         inv_all = lax.rsqrt(square_sum / INNER_DIM + norm_eps)
         mixed = mixed * lax.dynamic_slice_in_dim(inv_all, own * rows, rows, 1).reshape(tokens, 1)
@@ -830,11 +858,11 @@
         decay_all.append(decay)
         inv_alls.append(inv_all)
         gg_all.append(gg)
-        n_two.append(flat(line_gather(row_major(rms_scale(resid[c], gain_two).astype(bf16)))))
-    g_moe = [flat(g_moe[c]) for c in chunk_ids]
+        n_two.append(jnp.concatenate(line_gather(row_major(rms_scale(resid[c], gain_two).astype(bf16))), axis=0))
     moe_part, back_part, logit_grads, acts, hids = [], [], [], [], []
+    g_moe = [jnp.concatenate(g_blocks[c], axis=0) for c in chunk_ids]
     for c in chunk_ids:
-        mask = hot[:, c * per : (c + 1) * per].reshape(zs * tokens, LANES)
+        mask = jnp.concatenate([part(hot_at(k), c) for k in range(zs)], axis=0)
         results = experts(n_two[c], g_moe[c], mask, full_router, full_expert)
         moe_part.append(results[0].reshape(zs, tokens, D_MODEL))
         back_part.append(results[1].reshape(zs, tokens, D_MODEL))
@@ -846,14 +874,18 @@
         return jax.vjp(rms_scale, values, gain_vec)[1](grads)
 
     resid_grad, g_mixed, gain_two_grad = [], [], 0.0
-    unmixed, pairs, gate_gain_grad = [], [], 0.0
+    unmixed, pairs, toks, gate_gain_grad = [], [], [], 0.0
     for c in chunk_ids:
-        n_two_grad = line_scatter_steps(back_part[c])
+        n_two_grad = summed(line_parts(lambda k: back_part[c][k]))
         from_norm, gain_grad = norm_back(resid[c], gain_two, n_two_grad)
         gain_two_grad = gain_two_grad + gain_grad
         resid_grad.append(row_major(grad_c[c] + from_norm))
         low = resid_grad[c].astype(bf16)
-        g_mixed.append(flat(line_gather(low)))
+        if c == CHUNKS - 1:
+            expert_grad = weight_scatter(
+                after(expert_grads([n.T for n in n_two], [g.T for g in g_moe], hids, acts, pieces), low)
+            ).astype(f32)
+        g_mixed.append(flat(in_order(line_gather(low))))
         grad = in_slots(dot(g_mixed[c], full_out, NN))
         xs, rw, dl, _ = entered[c]
         inv_all = inv_alls[c]
@@ -862,14 +894,15 @@
         cross = lax.psum(jnp.transpose(cross, (1, 0, 2)).reshape(per, piece_rows), "tensor")
         tok = jnp.stack([inv_all, cross * (inv_all * inv_all * inv_all) / INNER_DIM], axis=-1)
         gy, gz, g_local, gg_grad = mixer_unmix(grad, y_all[c], z[c], rw, dl, tok, gain_row)
+        toks.append(tok)
         gate_gain_grad = gate_gain_grad + gg_grad[0]
         unmixed.append((gy, gz, g_local))
         pairs.append(mixer_pairs(xs, rw, dl, gy))
 
-    expert_grad = weight_scatter(
-        expert_grads([n.T for n in n_two], [g.T for g in g_moe], hids, acts, pieces)
-    )
-    moe = [line_scatter(after(moe_part[c], g_mixed[CHUNKS - 1])) for c in chunk_ids]
+    moe = []
+    for c in chunk_ids:
+        held = after(moe_part[c], *toks)
+        moe.append(summed(line_parts(lambda k: held[k])))
     output = [resid[c] + moe[c] for c in chunk_ids]
     stat_terms = sum(
         jnp.stack(
@@ -894,6 +927,14 @@
     n_rows = rows_of(n_one)
     z_w_grad = dot(n_rows, rows_of([unmixed[c][1] for c in chunk_ids]), TN).astype(bf16)
 
+    ups, downs = EXPERTS + 2, EXPERTS // 2
+    expert_outs = (
+        expert_grad[:EXPERTS].reshape(EXPERTS, shard, 2, half),
+        expert_grad[ups : ups + downs].transpose(0, 2, 1).reshape(EXPERTS, half, shard),
+        expert_grad[EXPERTS:ups].reshape(2, shard, 2, half).transpose(1, 2, 0, 3).reshape(shard, 2, 2 * half),
+        expert_grad[ups + downs].T,
+    )
+
     v_grads, bc_grads, conv_grad, head_grad = [], [], 0.0, 0.0
     full_x = jnp.concatenate([full_enter[:, :inner], full_enter[:, width:]], axis=1)
     full_bc = full_enter[:, inner:width]
@@ -901,7 +942,7 @@
     for c in chunk_ids:
         gy, gz, g_local = unmixed[c]
         xs, rw, dl, _ = entered[c]
-        gh = after(states_backward(g_local, decay_all[c]), moe[c])
+        gh = after(states_backward(g_local, decay_all[c]), moe[c], *expert_outs)
         gv, gbc, g_rim, gc, ghp = mixer_back(
             v[c], halo[c], conv_w, hp, skip, rw, dl, gy, *pairs[c], h_all[c], gh
         )
@@ -914,7 +955,7 @@
         gbc = lax.dynamic_update_slice(gbc, edge[None], (zs - 1, 0, rows - rim, 0))
         v_grads.append(gv)
         bc_grads.append(jnp.concatenate(split_parts(gbc), axis=-1))
-    u_grad, n_parts, gain_one_grad = [], [], 0.0
+    n_parts, arrived, gain_one_grad = [], [], 0.0
     for c in chunk_ids:
         n_grad = (
             dot(unmixed[c][1].reshape(zs * tokens, inner), full_z, NT)
@@ -925,17 +966,17 @@
         scale = lax.rsqrt(jnp.mean(every * every, axis=-1, keepdims=True) + norm_eps)
         gain_one_grad = gain_one_grad + jnp.sum(n_grad * (every * scale), axis=0)
         n_parts.append(n_grad.astype(bf16))
-        total = line_scatter(n_parts[c].reshape(zs, tokens, D_MODEL))
-        u_grad.append(resid_grad[c] + norm_back(u[c], gain_one, total)[0])
-    v_grads[0] = after(v_grads[0], expert_grad, *n_parts)
-    bc_grads[0] = after(bc_grads[0], *n_parts)
+        received = line_parts(by_distance(n_parts[c].reshape(zs, tokens, D_MODEL)))
+        arrived.append(received)
     enter_w_grad = dot(n_rows, rows_of(v_grads), TN).astype(bf16)
     bc_w_grad = dot(n_rows, rows_of(bc_grads), TN)
     bc_w_grad = bc_w_grad[:, : 2 * STATE_DIM] + bc_w_grad[:, 2 * STATE_DIM :]
-    mixer_grad = weight_scatter(
-        jnp.concatenate([z_w_grad, out_w_grad, enter_w_grad], axis=1).reshape(pieces, shard, 3 * inner + LANES)
-    ).astype(f32)
-
+
+    def mixer_scatter(grads):
+        return weight_scatter(grads.reshape(pieces, shard, -1)).astype(f32)
+
+    out_part, z_part = mixer_scatter(out_w_grad), mixer_scatter(z_w_grad)
+    enter_part = mixer_scatter(enter_w_grad)
     def to_shares(values, dim):
         size = values.shape[dim] // (pieces * zs)
         values = jnp.moveaxis(values, dim, 0).reshape(pieces, zs, size, -1)
@@ -961,8 +1002,16 @@
     shares = jnp.pad(shares, ((0, 0), (0, 0), (0, -length % (8 * LANES))))
     wide_share = bc_w_grad.reshape(pieces, zs, -1, LANES)
     shares = jnp.concatenate([wide_share, shares.reshape(pieces, zs, -1, LANES)], axis=2)
+    shares = after(shares, arrived[CHUNKS - 1][2])
     shares = jnp.sum(lax.all_to_all(shares, "dp", 0, 0), axis=0)
+    first_sum = shares
     shares = jnp.sum(lax.all_to_all(shares, "tensor", 0, 0), axis=0)
+    u_grad = []
+    for c in chunk_ids:
+        received = arrived[c]
+        if c == CHUNKS - 1:
+            received[1] = after(received[1], first_sum)
+        u_grad.append(resid_grad[c] + norm_back(u[c], gain_one, summed(received))[0])
     bc_lines = wide_share.shape[2]
     bc_grad = shares[:bc_lines].reshape(-1, 2 * STATE_DIM)
     shares = shares[bc_lines:].reshape(-1)
@@ -987,17 +1036,13 @@
         whole = jnp.concatenate([value.astype(bf16).reshape(per, rows, D_MODEL) for value in values], axis=0)
         return jnp.transpose(whole, (1, 0, 2))
 
-    expert_grad = expert_grad.astype(f32)
-    ups, downs = EXPERTS + 2, EXPERTS // 2
-    z_part, out_part = mixer_grad[:, :inner], mixer_grad[:, inner : 2 * inner]
-    x_part, dt_part = mixer_grad[:, 2 * inner : 3 * inner], mixer_grad[:, 3 * inner :]
     return (
         placed_back(output),
         placed_back(u_grad),
         took[0],
-        jnp.stack([z_part, x_part], axis=1),
+        jnp.stack([z_part, enter_part[:, :inner]], axis=1),
         bc_grad,
-        dt_part[:, :heads],
+        enter_part[:, inner : inner + heads],
         took[1],
         took[2],
         head_sum,
@@ -1005,10 +1050,7 @@
         out_part.T,
         took[4],
         took[5],
-        expert_grad[:EXPERTS].reshape(EXPERTS, shard, 2, half),
-        expert_grad[ups : ups + downs].transpose(0, 2, 1).reshape(EXPERTS, half, shard),
-        expert_grad[EXPERTS:ups].reshape(2, shard, 2, half).transpose(1, 2, 0, 3).reshape(shard, 2, 2 * half),
-        expert_grad[ups + downs].T,
+        *expert_outs,
         stats,
     )
 

time: 1150 us -> 926 us (0.81)
  blocking collectives: 273 us -> 108 us
  waiting for transfers between devices: 358 us -> 237 us
  local copies, waits for them, and re-layouts: 116 us -> 143 us
  starting transfers between devices: 57.9 us -> 82.6 us
  other arithmetic: 46.6 us -> 67.1 us
  Pallas kernels: 208 us -> 190 us
    all_to_all x6 -> x2, waiting for transfers between devices: 219 us -> 0.01 us  [the longest x1 0.01 us: body(): shares = jnp.sum(lax.all_to_all(shares, 'dp', 0, 0), axis=0)]
    ppermute x3 -> x24, waiting for transfers between devices: 50.6 us -> 209 us  [the longest x12 151 us: line_gather(): lax.ppermute(row_major(value), 'tensor', [(a, (a - step) % size) for a in...]
    all_to_all x3 -> x0, blocking collectives: 132 us -> none  [the longest x1 87.6 us: line_gather(): lax.all_to_all(row_major(jnp.broadcast_to(value[None], (size,) + value.sh...]
    all_to_all x4, waiting for transfers between devices: 88 us -> 27.4 us  [exchanged(): return lax.all_to_all(rows, 'dp', 0, 0, tiled=False)]
    ppermute x3 -> x24, starting transfers between devices: 3.98 us -> 50.3 us  [the longest x12 29.3 us: line_parts(): lax.ppermute(row_major(block_of(step)), 'tensor', [(a, (a + step) % size)...]
    all_gather x1, blocking collectives: 57.7 us -> 19.7 us  [body(): tiles = lax.all_gather(tile, 'tensor')]
    another operation x0 -> x12, local copies, waits for them, and re-layouts: none -> 22 us  [the longest x8 21.5 us: row_major(): with_layout_constraint(value, Layout(major_to_minor=tuple(range(value.ndi...]
    all_to_all x6 -> x2, starting transfers between devices: 30.8 us -> 12.1 us  [the longest x1 7.09 us: body(): shares = jnp.sum(lax.all_to_all(shares, 'dp', 0, 0), axis=0)]
  transfers between devices with their start and end apart: 20 -> 39, of which waited for: 12 -> 12; matrix products, arithmetic and copies ran while one was open for 15% -> 26% of each run, Pallas kernels for 9% -> 13%
where the time goes in v3:
time: 926 us; the launch traced here: 914 us
  waiting for transfers between devices  237 us (26%)
  Pallas kernels  190 us (21%)
  local copies, waits for them, and re-layouts  143 us (15%)
  blocking collectives  108 us (12%)
  starting transfers between devices  82.6 us (9%)
  matrix products  70.3 us (8%)
  other arithmetic  67.1 us (7%)
  between operations  16.5 us (2%)
    ppermute x12, waiting for transfers between devices, line_gather(): lax.ppermute(row_major(value), 'tensor', [(a, (a - step) % size) for a in...  151 us
    pallas_call x1, Pallas kernels, experts(): pl.pallas_call(expert_kernel, grid=(pairs,), in_specs=[pl.BlockSpec((toke...  71.6 us
    dot_general x13, matrix products, dot(): lax.dot_general(a, b, (dims, ((), ())), precision=precision, preferred_el...  70.3 us
    ppermute x12, waiting for transfers between devices, line_parts(): lax.ppermute(row_major(block_of(step)), 'tensor', [(a, (a + step) % size)...  58.1 us
    psum x1, blocking collectives, body(): square_sum = lax.psum(squares[:, :, 0], 'tensor')  53.8 us
    unnamed x211, local copies, waits for them, and re-layouts  38.3 us
    pallas_call x1, Pallas kernels, expert_grads(): pl.pallas_call(functools.partial(expert_grad_kernel, ups, chunks), grid=(...  34.7 us
    ppermute x12, starting transfers between devices, line_parts(): lax.ppermute(row_major(block_of(step)), 'tensor', [(a, (a + step) % size)...  29.3 us
  transfers between devices with their start and end apart: 39, of which 12 were waited for; matrix products, arithmetic and copies ran while one was open for 26% of the time, Pallas kernels for 13%

profile of v3, /device:TPU:0, one launch (start us, length us, event | category | flops | bytes accessed | tf_op | source)
XLA Modules:
  0.0 913.7 jit_solution(2555115888510317203)
XLA Ops:
  12.5 5.0 collective-permute-start
  19.7 8.9 all-gather.4
  32.7 3.1 collective-permute-done
  37.0 48.1 %collective-permute-done.1 = bf16[256,1536]{1,0:T(8,128)(2,1)} collective-permute-done((bf16[256,1536]{1,0:T(8,128)(2,1)}, bf16[256,1536]{1,0:T(8,128)(2,1)}, u32[]{:S(2)}, u32[]{:S(2)}) %collective-permute-start.1) | collective-permute-done | bytes 786464 | tf_op jit(solution)/shard_map/ppermute | solution.py:42
  95.4 8.0 fusion.v_ref
  103.4 11.3 %mixer_enter.1 = (f32[4,256,768]{2,1,0:T(8,128)}, f32[4,256,256]{2,1,0:T(8,128)S(1)}, f32[4,256,256]{2,1,0:T(8,128)S(1)}, f32[4,768,128]{2,1,0:T(8,128)S(1)}) custom-call(f32[4,4,64,1152]{3,2,1,0:T(8,128)} %fusion.v_ref, f32[4,8,1024]{2,1,0:T(8,128)S(1)} %pad.42.halo_ref, f32[8,1024]{1,0:T(8,128)S(1)} %select_maximum_fusion.cw_ref, f32[8,128]{1,0:T(8,128)S(1)} %pad.44.hp_ref), custom_call_target="tpu_custom_call" | custom-call | flops 13516800000 | bytes 1024 | tf_op jit(solution)/shard_map/mixer_enter/pallas_call | solution.py:197
  118.1 10.4 %collective-permute-done.5.refs_2_ = bf16[256,1536]{1,0:T(8,128)(2,1)} collective-permute-done((bf16[256,1536]{1,0:T(8,128)(2,1)}, bf16[256,1536]{1,0:T(8,128)(2,1)}, u32[]{:S(2)}, u32[]{:S(2)}) %collective-permute-start.5) | collective-permute-done | bytes 786464 | tf_op jit(solution)/shard_map/ppermute | solution.py:42
  131.2 4.3 all-to-all-start
  136.4 20.5 %all-to-all-done = f32[8,392,128]{2,1,0:T(8,128)} async-done(((f32[8,392,128]{2,1,0:T(8,128)}), f32[8,392,128]{2,1,0:T(8,128)}, u32[]{:S(2)}, u32[]{:S(2)}) %all-to-all-start) | async-done | bytes 1605664 | tf_op jit(solution)/shard_map/all_to_all | solution.py:244
  161.3 10.9 %collective-permute-done.6.refs_1_ = bf16[256,1536]{1,0:T(8,128)(2,1)S(1)} collective-permute-done((bf16[256,1536]{1,0:T(8,128)(2,1)S(1)}, bf16[256,1536]{1,0:T(8,128)(2,1)S(1)}, u32[]{:S(2)}, u32[]{:S(2)}) %collective-permute-start.6) | collective-permute-done | bytes 786464 | tf_op jit(solution)/shard_map/ppermute | solution.py:42
  173.1 3.9 all-to-all-start.1
  184.3 3.8 reshape.431
  188.1 3.0 pad_maximum_fusion.2.refs_0_
  191.1 6.9 all-to-all-done.1
  203.5 4.6 mixer_inner.1.yi_ref
  209.7 7.2 fusion.15
  216.9 7.2 mixer_leave.1
  224.2 5.3 convolution_convert_fusion
  232.6 3.1 collective-permute-start.9
  236.4 53.8 %psum.14 = f32[4,256]{1,0:T(4,128)S(1)} all-reduce(f32[4,256]{1,0:T(4,128)S(1)} %slice_reduce_fusion), channel_id=1, replica_groups=mesh['dp'=8,'tensor'=4] {'tensor'}, use_global_device_ids=true, to_apply=%region_1.2 | all-reduce | flops 1024 | bytes 8192 | tf_op jit(solution)/shard_map/psum | solution.py:851
  290.4 9.8 %collective-permute-done.8 = bf16[256,1536]{1,0:T(8,128)(2,1)} collective-permute-done((bf16[256,1536]{1,0:T(8,128)(2,1)}, bf16[256,1536]{1,0:T(8,128)(2,1)}, u32[]{:S(2)}, u32[]{:S(2)}) %collective-permute-start.8) | collective-permute-done | bytes 786464 | tf_op jit(solution)/shard_map/ppermute | solution.py:50
  300.2 2.8 multiply_reduce_fusion.4
  304.3 3.0 collective-permute-start.12
  307.3 5.1 collective-permute-start.11
  324.9 4.4 fusion.55
  329.3 4.7 copy.333.g_ref
  340.4 22.1 %collective-permute-done.11 = bf16[256,1536]{1,0:T(8,128)(2,1)} collective-permute-done((bf16[256,1536]{1,0:T(8,128)(2,1)}, bf16[256,1536]{1,0:T(8,128)(2,1)}, u32[]{:S(2)}, u32[]{:S(2)}) %collective-permute-start.11) | collective-permute-done | bytes 786464 | tf_op jit(solution)/shard_map/ppermute | solution.py:42
  367.1 3.3 pad_maximum_fusion
  370.3 4.7 copy.332.n_ref
  375.0 3.2 fusion.78.refs_0_
  378.2 71.6 %experts.1 = (bf16[1024,1536]{1,0:T(8,128)(2,1)}, bf16[1024,1536]{1,0:T(8,128)(2,1)}, bf16[1024,128]{1,0:T(8,128)(2,1)}, bf16[9,1024,256]{2,1,0:T(8,128)(2,1)}, bf16[9,1024,512]{2,1,0:T(8,128)(2,1)}) custom-call(bf16[1024,1536]{1,0:T(8,128)(2,1)} %copy.332.n_ref, bf16[1024,1536]{1,0:T(8,128)(2,1)} %copy.333.g_ref, f32[1024,128]{1,0:T(8,128)} %pad_maximum_fusion.7.mask_ref, ...), custom_call_target="tpu_custom_call" | custom-call | flops 81100800000 | bytes 1024 | tf_op jit(solution)/shard_map/experts/pallas_call | solution.py:655
  451.7 17.3 %collective-permute-start.15 = (bf16[256,1536]{1,0:T(8,128)(2,1)S(1)}, bf16[256,1536]{1,0:T(8,128)(2,1)S(1)}, u32[]{:S(2)}, u32[]{:S(2)}) collective-permute-start(bf16[256,1536]{1,0:T(8,128)(2,1)S(1)} %get-tuple-element.243), channel_id=1, source_target_pairs={{0,3},{1,0},{2,1},{3,2},{4,7},{5,4},{6,5},{7,6},{8,11},{9,8},{10,9... | collective-permute-start | bytes 2359304 | tf_op jit(solution)/shard_map/ppermute | solution.py:50
  469.8 34.7 %expert_grads.1.refs_0_ = bf16[8,27,192,256]{3,2,1,0:T(8,128)(2,1)} custom-call(bf16[1536,1024]{1,0:T(8,128)(2,1)S(1)} %copy-done.6, bf16[1536,1024]{1,0:T(8,128)(2,1)} %get-tuple-element.237.refs_1_, bf16[9,1024,512]{2,1,0:T(8,128)(2,1)} %get-tuple-element.81.refs_2_, bf16[9,1024,256]{2,1,0:T(8,128)(2,1)} %get-tuple-element.82.refs_3_), custom_call_target="tpu_custom_call" | custom-call | flops 45056000000 | bytes 1024 | tf_op jit(solution)/shard_map/expert_grads/pallas_call | solution.py:721
  504.5 31.7 %collective-permute-done.14 = bf16[256,1536]{1,0:T(8,128)(2,1)S(1)} collective-permute-done((bf16[256,1536]{1,0:T(8,128)(2,1)S(1)}, bf16[256,1536]{1,0:T(8,128)(2,1)S(1)}, u32[]{:S(2)}, u32[]{:S(2)}) %collective-permute-start.14) | collective-permute-done | bytes 786464 | tf_op jit(solution)/shard_map/ppermute | solution.py:50
  546.5 3.6 fusion.40
  554.1 8.8 collective-permute-done.16
  565.1 47.4 %collective-permute-done.17 = bf16[256,1536]{1,0:T(8,128)(2,1)} collective-permute-done((bf16[256,1536]{1,0:T(8,128)(2,1)S(1)}, bf16[256,1536]{1,0:T(8,128)(2,1)}, u32[]{:S(2)}, u32[]{:S(2)}) %collective-permute-start.17) | collective-permute-done | bytes 786464 | tf_op jit(solution)/shard_map/ppermute | solution.py:42
  615.6 8.5 fusion.4
  624.2 8.3 psum.15
  633.6 3.3 slice_bitcast_fusion.4
  640.4 8.0 mixer_unmix.1
  650.7 3.7 all-to-all-start.2
  654.6 6.5 convolution_convert_fusion.3
  663.5 23.4 %mixer_pairs.1 = (f32[4,256,768]{2,1,0:T(8,128)}, f32[4,256,256]{2,1,0:T(8,128)S(1)}, f32[4,256,256]{2,1,0:T(8,128)S(1)}) custom-call(f32[4,256,768]{2,1,0:T(8,128)} %get-tuple-element.66.xs_ref, f32[4,256,256]{2,1,0:T(8,128)S(1)} %copy-done.30, f32[4,256,256]{2,1,0:T(8,128)S(1)} %copy-done.19, f32[4,256,768]{2,1,0:T(8,128)} %get-tuple-element.76.gy_ref), custom_call_target="tpu_custom_call" | custom-call | flops 47308800000 | bytes 1024 | tf_op jit(solution)/shard_map/mixer_pairs/pallas_call | solution.py:448
  689.1 4.0 convolution_convert_fusion.2
  694.7 4.4 all-to-all-start.3
  700.2 6.2 fusion.13
  706.5 6.1 fusion.20
  712.6 5.4 copy.340
  717.9 4.1 slice.279
  723.6 3.8 convert_element_type.219
  727.4 6.0 copy.342.refs_2_
  736.6 27.2 %mixer_back.1 = (bf16[4,4,64,896]{3,2,1,0:T(8,128)(2,1)}, f32[4,4,64,256]{3,2,1,0:T(8,128)}, f32[4,8,1024]{2,1,0:T(8,128)}, f32[8,1024]{1,0:T(8,128)}, f32[8,128]{1,0:T(8,128)}) custom-call(f32[4,4,64,1152]{3,2,1,0:T(8,128)} %fusion.v_ref, f32[4,8,1024]{2,1,0:T(8,128)} %copy-done.11, f32[8,1024]{1,0:T(8,128)} %copy-done.12, f32[8,128]{1,0:T(8,128)} %copy-done.14, ...), custom_call_target="tpu_custom_call" | custom-call | flops 20275200000 | bytes 1024 | tf_op jit(solution)/shard_map/mixer_back/pallas_call | solution.py:552
  775.9 5.4 fusion.5
  781.3 4.8 multiply_reduce_fusion
  790.0 4.8 convolution_convert_fusion.1
  794.8 3.5 fusion.61
  798.9 3.2 slice_add_fusion
  804.6 2.8 pad_maximum_fusion.3.refs_0_
  807.4 16.5 %collective-permute-done.24.refs_1_ = bf16[256,1536]{1,0:T(8,128)(2,1)S(1)} collective-permute-done((bf16[256,1536]{1,0:T(8,128)(2,1)}, bf16[256,1536]{1,0:T(8,128)(2,1)S(1)}, u32[]{:S(2)}, u32[]{:S(2)}) %collective-permute-start.24) | collective-permute-done | bytes 786464 | tf_op jit(solution)/shard_map/ppermute | solution.py:50
  824.9 7.1 all-to-all-start.4
  845.6 17.2 %all_gather.44 = f32[8,8,128]{2,1,0:T(8,128)S(1)} all-gather(f32[1,8,128]{2,1,0:T(8,128)S(1)} %scatter.9), channel_id=1, replica_groups=mesh['dp'=8,'tensor'=4] {'dp'}, dimensions={0}, use_global_device_ids=true | all-gather | bytes 36864 | tf_op jit(solution)/shard_map/all_gather | solution.py:1029
  862.8 19.7 %all-gather.3 = f32[32,128]{1,0:T(8,128)S(1)} all-gather(f32[8,128]{1,0:T(8,128)S(1)} %reduce_sum.187), channel_id=5, replica_groups=mesh['dp'=8,'tensor'=4] {'tensor'}, dimensions={0}, use_global_device_ids=true | all-gather | bytes 20480 | tf_op jit(solution)/shard_map/all_gather | solution.py:1030
  886.0 5.0 all-to-all-start.5
  (446 shorter events, 170.9 us)
Async XLA Ops:
  7.2 176.8 %copy-start = (bf16[192,2,256]{2,1,0:T(2,128)(2,1)S(1)}, bf16[192,2,256]{2,1,0:T(2,128)(2,1)}, u32[]{:S(2)}) copy-start(bf16[192,2,256]{2,1,0:T(2,128)(2,1)} %param.40) | copy-start | bytes 589828
  7.2 85.7 %all-gather.9.cloned.1.call-start = ((), (), s32[]{:S(2)}) async-start(), calls=%async_computation.14 | async-start | bytes 3981312 | tf_op jit(solution)/shard_map/all_gather | solution.py:78
  8.2 10.4 %copy-start.82 = (bf16[192,16]{0,1:T(8,128)(2,1)S(1)}, bf16[192,16]{0,1:T(8,128)(2,1)}, u32[]{:S(2)}) copy-start(bf16[192,16]{0,1:T(8,128)(2,1)} %param.37) | copy-start | bytes 18436
  11.4 8.3 copy-start.92
  11.4 8.3 copy-start.93
  11.4 17.3 %copy-start.88 = (s32[4]{0:T(128)S(1)}, s32[4]{0:T(128)}, u32[]{:S(2)}) copy-start(s32[4]{0:T(128)} %param.25) | copy-start | bytes 52
  11.4 17.5 %copy-start.61 = (bf16[64,4,1536]{2,1,0:T(4,128)(2,1)S(1)}, bf16[64,4,1536]{2,1,0:T(4,128)(2,1)}, u32[]{:S(2)}) copy-start(bf16[64,4,1536]{2,1,0:T(4,128)(2,1)} %param.24) | copy-start | bytes 2359300
  11.4 198.3 %all-gather.11.cloned.1.call-start = ((), (), s32[]{:S(2)}) async-start(), calls=%async_computation.15 | async-start | bytes 5750784 | tf_op jit(solution)/shard_map/all_gather | solution.py:78
  12.5 23.4 %collective-permute-start = (bf16[256,1536]{1,0:T(8,128)(2,1)}, bf16[256,1536]{1,0:T(8,128)(2,1)}, u32[]{:S(2)}, u32[]{:S(2)}) collective-permute-start(bf16[256,1536]{1,0:T(8,128)(2,1)} %bitcast.1), channel_id=1, source_target_pairs={{0,3},{1,0},{2,1},{3,2},{4,7},{5,4},{6,5},{7,6},{8,11},{9,8},{10,9... | collective-permute-start | bytes 2359304 | tf_op jit(solution)/shard_map/ppermute | solution.py:42
  17.5 67.6 %collective-permute-start.1 = (bf16[256,1536]{1,0:T(8,128)(2,1)}, bf16[256,1536]{1,0:T(8,128)(2,1)}, u32[]{:S(2)}, u32[]{:S(2)}) collective-permute-start(bf16[256,1536]{1,0:T(8,128)(2,1)} %bitcast.1), channel_id=1, source_target_pairs={{0,2},{1,3},{2,0},{3,1},{4,6},{5,7},{6,4},{7,5},{8,10},{9,11},{10,... | collective-permute-start | bytes 2359304 | tf_op jit(solution)/shard_map/ppermute | solution.py:42
  17.5 68.8 %collective-permute-start.2 = (bf16[256,1536]{1,0:T(8,128)(2,1)}, bf16[256,1536]{1,0:T(8,128)(2,1)}, u32[]{:S(2)}, u32[]{:S(2)}) collective-permute-start(bf16[256,1536]{1,0:T(8,128)(2,1)} %bitcast.1), channel_id=1, source_target_pairs={{0,1},{1,2},{2,3},{3,0},{4,5},{5,6},{6,7},{7,4},{8,9},{9,10},{10,1... | collective-permute-start | bytes 2359304 | tf_op jit(solution)/shard_map/ppermute | solution.py:42
  32.7 55.6 %copy-start.65 = (f32[1536]{0:T(1024)}, f32[1536]{0:T(1024)S(1)}, u32[]{:S(2)}) copy-start(f32[1536]{0:T(1024)S(1)} %get-tuple-element.223) | copy-start | bytes 18436
  89.2 3.7 collective-permute-start.3
  90.8 12.7 %copy-start.12 = (f32[8,1024]{1,0:T(8,128)}, f32[8,1024]{1,0:T(8,128)S(1)}, u32[]{:S(2)}) copy-start(f32[8,1024]{1,0:T(8,128)S(1)} %select_maximum_fusion.cw_ref) | copy-start | bytes 98308
  90.8 12.6 %copy-start.14 = (f32[8,128]{1,0:T(8,128)}, f32[8,128]{1,0:T(8,128)S(1)}, u32[]{:S(2)}) copy-start(f32[8,128]{1,0:T(8,128)S(1)} %pad.44.hp_ref) | copy-start | bytes 12292
  90.8 27.2 %collective-permute-start.4 = (bf16[256,1536]{1,0:T(8,128)(2,1)}, bf16[256,1536]{1,0:T(8,128)(2,1)}, u32[]{:S(2)}, u32[]{:S(2)}) collective-permute-start(bf16[256,1536]{1,0:T(8,128)(2,1)} %after.9), channel_id=1, source_target_pairs={{0,3},{1,0},{2,1},{3,2},{4,7},{5,4},{6,5},{7,6},{8,11},{9,8},{10,9... | collective-permute-start | bytes 2359304 | tf_op jit(solution)/shard_map/ppermute | solution.py:42
  90.9 37.6 %collective-permute-start.5 = (bf16[256,1536]{1,0:T(8,128)(2,1)}, bf16[256,1536]{1,0:T(8,128)(2,1)}, u32[]{:S(2)}, u32[]{:S(2)}) collective-permute-start(bf16[256,1536]{1,0:T(8,128)(2,1)} %after.9), channel_id=1, source_target_pairs={{0,1},{1,2},{2,3},{3,0},{4,5},{5,6},{6,7},{7,4},{8,9},{9,10},{10,1... | collective-permute-start | bytes 2359304 | tf_op jit(solution)/shard_map/ppermute | solution.py:42
  131.2 25.7 %all-to-all-start = ((f32[8,392,128]{2,1,0:T(8,128)}), f32[8,392,128]{2,1,0:T(8,128)}, u32[]{:S(2)}, u32[]{:S(2)}) async-start(f32[8,392,128]{2,1,0:T(8,128)} %pad_maximum_fusion.4), calls=%async_computation | async-start | bytes 3211264 | tf_op jit(solution)/shard_map/all_to_all | solution.py:244
  135.5 36.7 %collective-permute-start.6 = (bf16[256,1536]{1,0:T(8,128)(2,1)S(1)}, bf16[256,1536]{1,0:T(8,128)(2,1)S(1)}, u32[]{:S(2)}, u32[]{:S(2)}) collective-permute-start(bf16[256,1536]{1,0:T(8,128)(2,1)S(1)} %copy-done.46), channel_id=1, source_target_pairs={{0,2},{1,3},{2,0},{3,1},{4,6},{5,7},{6,4},{7,5},{8,10},{9,11},{10,... | collective-permute-start | bytes 2359304 | tf_op jit(solution)/shard_map/ppermute | solution.py:42
  173.1 24.9 %all-to-all-start.1 = ((f32[8,384,128]{2,1,0:T(8,128)}), f32[8,384,128]{2,1,0:T(8,128)S(1)}, u32[]{:S(2)}, u32[]{:S(2)}) async-start(f32[8,384,128]{2,1,0:T(8,128)} %after.11), calls=%async_computation.1 | async-start | bytes 3145728 | tf_op jit(solution)/shard_map/all_to_all | solution.py:244
  176.9 201.3 %all-gather.13.cloned.1.call-start = ((), (), s32[]{:S(2)}) async-start(), calls=%async_computation.16 | async-start | bytes 23887872 | tf_op jit(solution)/shard_map/all_gather | solution.py:78
  199.1 513.4 %reduce-scatter.5.cloned.1.call-start = ((), (), s32[]{:S(2)}) async-start(), calls=%async_computation.10 | async-start | bytes 23887872 | tf_op jit(solution)/shard_map/reduce_scatter | solution.py:82
  199.8 17.1 %copy-start.13 = (f32[8,768]{1,0:T(8,128)}, f32[8,768]{1,0:T(8,128)S(1)}, u32[]{:S(2)}) copy-start(f32[8,768]{1,0:T(8,128)S(1)} %pad.47.hp_ref.skip_ref) | copy-start | bytes 73732
  232.6 57.8 %collective-permute-start.9 = (bf16[256,1536]{1,0:T(8,128)(2,1)}, bf16[256,1536]{1,0:T(8,128)(2,1)S(1)}, u32[]{:S(2)}, u32[]{:S(2)}) collective-permute-start(bf16[256,1536]{1,0:T(8,128)(2,1)} %get-tuple-element.246), channel_id=1, source_target_pairs={{0,3},{1,0},{2,1},{3,2},{4,7},{5,4},{6,5},{7,6},{8,11},{9,8},{10,9... | collective-permute-start | bytes 2359304 | tf_op jit(solution)/shard_map/ppermute | solution.py:50
  235.6 64.6 %collective-permute-start.8 = (bf16[256,1536]{1,0:T(8,128)(2,1)}, bf16[256,1536]{1,0:T(8,128)(2,1)}, u32[]{:S(2)}, u32[]{:S(2)}) collective-permute-start(bf16[256,1536]{1,0:T(8,128)(2,1)} %get-tuple-element.247), channel_id=1, source_target_pairs={{0,2},{1,3},{2,0},{3,1},{4,6},{5,7},{6,4},{7,5},{8,10},{9,11},{10,... | collective-permute-start | bytes 2359304 | tf_op jit(solution)/shard_map/ppermute | solution.py:50
  235.6 64.6 %collective-permute-start.7 = (bf16[256,1536]{1,0:T(8,128)(2,1)}, bf16[256,1536]{1,0:T(8,128)(2,1)}, u32[]{:S(2)}, u32[]{:S(2)}) collective-permute-start(bf16[256,1536]{1,0:T(8,128)(2,1)} %get-tuple-element.245), channel_id=1, source_target_pairs={{0,1},{1,2},{2,3},{3,0},{4,5},{5,6},{6,7},{7,4},{8,9},{9,10},{10,1... | collective-permute-start | bytes 2359304 | tf_op jit(solution)/shard_map/ppermute | solution.py:50
  290.2 12.8 %copy-start.70 = (f32[4,256]{1,0:T(4,128)}, f32[4,256]{1,0:T(4,128)S(1)}, u32[]{:S(2)}) copy-start(f32[4,256]{1,0:T(4,128)S(1)} %psum.14) | copy-start | bytes 12292
  290.2 12.8 %copy-start.74 = (f32[4,256]{1,0:T(4,128)}, f32[4,256]{1,0:T(4,128)S(1)}, u32[]{:S(2)}) copy-start(f32[4,256]{1,0:T(4,128)S(1)} %add_rsqrt_fusion) | copy-start | bytes 12292
  290.4 24.4 %copy-start.80 = (f32[256]{0:T(256)}, f32[256]{0:T(256)S(1)}, u32[]{:S(2)}) copy-start(f32[256]{0:T(256)S(1)} %mul.236) | copy-start | bytes 3076
  290.4 9.8 %copy-start.55 = (bf16[256,1536]{1,0:T(8,128)(2,1)}, bf16[256,1536]{1,0:T(8,128)(2,1)S(1)}, u32[]{:S(2)}) copy-start(bf16[256,1536]{1,0:T(8,128)(2,1)S(1)} %collective-permute-done.9) | copy-start | bytes 2359300
  303.0 234.3 %copy-start.35 = (f32[256,1536]{1,0:T(8,128)}, f32[256,1536]{1,0:T(8,128)S(1)}, u32[]{:S(2)}) copy-start(f32[256,1536]{1,0:T(8,128)S(1)} %get-tuple-element.231) | copy-start | bytes 4718596
  304.3 33.8 %collective-permute-start.12 = (bf16[256,1536]{1,0:T(8,128)(2,1)}, bf16[256,1536]{1,0:T(8,128)(2,1)}, u32[]{:S(2)}, u32[]{:S(2)}) collective-permute-start(bf16[256,1536]{1,0:T(8,128)(2,1)} %multiply_convert_fusion.2), channel_id=1, source_target_pairs={{0,1},{1,2},{2,3},{3,0},{4,5},{5,6},{6,7},{7,4},{8,9},{9,10},{10,1... | collective-permute-start | bytes 2359304 | tf_op jit(solution)/shard_map/ppermute | solution.py:42
  307.3 55.2 %collective-permute-start.11 = (bf16[256,1536]{1,0:T(8,128)(2,1)}, bf16[256,1536]{1,0:T(8,128)(2,1)}, u32[]{:S(2)}, u32[]{:S(2)}) collective-permute-start(bf16[256,1536]{1,0:T(8,128)(2,1)} %multiply_convert_fusion.2), channel_id=1, source_target_pairs={{0,2},{1,3},{2,0},{3,1},{4,6},{5,7},{6,4},{7,5},{8,10},{9,11},{10,... | collective-permute-start | bytes 2359304 | tf_op jit(solution)/shard_map/ppermute | solution.py:42
  312.3 52.4 %collective-permute-start.10 = (bf16[256,1536]{1,0:T(8,128)(2,1)}, bf16[256,1536]{1,0:T(8,128)(2,1)}, u32[]{:S(2)}, u32[]{:S(2)}) collective-permute-start(bf16[256,1536]{1,0:T(8,128)(2,1)} %multiply_convert_fusion.2), channel_id=1, source_target_pairs={{0,3},{1,0},{2,1},{3,2},{4,7},{5,4},{6,5},{7,6},{8,11},{9,8},{10,9... | collective-permute-start | bytes 2359304 | tf_op jit(solution)/shard_map/ppermute | solution.py:42
  449.8 20.0 %copy-start.6 = (bf16[1536,1024]{1,0:T(8,128)(2,1)S(1)}, bf16[1536,1024]{1,0:T(8,128)(2,1)}, u32[]{:S(2)}) copy-start(bf16[1536,1024]{1,0:T(8,128)(2,1)} %fusion.78.refs_0_) | copy-start | bytes 9437188
  451.7 52.8 %collective-permute-start.15 = (bf16[256,1536]{1,0:T(8,128)(2,1)S(1)}, bf16[256,1536]{1,0:T(8,128)(2,1)S(1)}, u32[]{:S(2)}, u32[]{:S(2)}) collective-permute-start(bf16[256,1536]{1,0:T(8,128)(2,1)S(1)} %get-tuple-element.243), channel_id=1, source_target_pairs={{0,3},{1,0},{2,1},{3,2},{4,7},{5,4},{6,5},{7,6},{8,11},{9,8},{10,9... | collective-permute-start | bytes 2359304 | tf_op jit(solution)/shard_map/ppermute | solution.py:50
  469.0 67.3 %collective-permute-start.14 = (bf16[256,1536]{1,0:T(8,128)(2,1)S(1)}, bf16[256,1536]{1,0:T(8,128)(2,1)S(1)}, u32[]{:S(2)}, u32[]{:S(2)}) collective-permute-start(bf16[256,1536]{1,0:T(8,128)(2,1)S(1)} %get-tuple-element.244), channel_id=1, source_target_pairs={{0,2},{1,3},{2,0},{3,1},{4,6},{5,7},{6,4},{7,5},{8,10},{9,11},{10,... | collective-permute-start | bytes 2359304 | tf_op jit(solution)/shard_map/ppermute | solution.py:50
  469.0 67.3 %collective-permute-start.13 = (bf16[256,1536]{1,0:T(8,128)(2,1)S(1)}, bf16[256,1536]{1,0:T(8,128)(2,1)S(1)}, u32[]{:S(2)}, u32[]{:S(2)}) collective-permute-start(bf16[256,1536]{1,0:T(8,128)(2,1)S(1)} %get-tuple-element.242), channel_id=1, source_target_pairs={{0,1},{1,2},{2,3},{3,0},{4,5},{5,6},{6,7},{7,4},{8,9},{9,10},{10,1... | collective-permute-start | bytes 2359304 | tf_op jit(solution)/shard_map/ppermute | solution.py:50
  469.8 66.5 %copy-start.50 = (bf16[1024,1536]{1,0:T(8,128)(2,1)S(1)}, bf16[1024,1536]{1,0:T(8,128)(2,1)}, u32[]{:S(2)}) copy-start(bf16[1024,1536]{1,0:T(8,128)(2,1)} %get-tuple-element.73) | copy-start | bytes 9437188
  543.5 19.4 %collective-permute-start.16 = (bf16[256,1536]{1,0:T(8,128)(2,1)S(1)}, bf16[256,1536]{1,0:T(8,128)(2,1)}, u32[]{:S(2)}, u32[]{:S(2)}) collective-permute-start(bf16[256,1536]{1,0:T(8,128)(2,1)S(1)} %copy-done.58), channel_id=1, source_target_pairs={{0,3},{1,0},{2,1},{3,2},{4,7},{5,4},{6,5},{7,6},{8,11},{9,8},{10,9... | collective-permute-start | bytes 2359304 | tf_op jit(solution)/shard_map/ppermute | solution.py:42
  545.7 66.8 %collective-permute-start.17 = (bf16[256,1536]{1,0:T(8,128)(2,1)S(1)}, bf16[256,1536]{1,0:T(8,128)(2,1)}, u32[]{:S(2)}, u32[]{:S(2)}) collective-permute-start(bf16[256,1536]{1,0:T(8,128)(2,1)S(1)} %copy-done.58), channel_id=1, source_target_pairs={{0,2},{1,3},{2,0},{3,1},{4,6},{5,7},{6,4},{7,5},{8,10},{9,11},{10,... | collective-permute-start | bytes 2359304 | tf_op jit(solution)/shard_map/ppermute | solution.py:42
  550.6 65.0 %copy-start.85 = (f32[768]{0:T(1024)S(1)}, f32[768]{0:T(1024)}, u32[]{:S(2)}) copy-start(f32[768]{0:T(1024)} %param.34) | copy-start | bytes 9220
  551.4 63.2 %collective-permute-start.18 = (bf16[256,1536]{1,0:T(8,128)(2,1)S(1)}, bf16[256,1536]{1,0:T(8,128)(2,1)S(1)}, u32[]{:S(2)}, u32[]{:S(2)}) collective-permute-start(bf16[256,1536]{1,0:T(8,128)(2,1)S(1)} %copy-done.58), channel_id=1, source_target_pairs={{0,1},{1,2},{2,3},{3,0},{4,5},{5,6},{6,7},{7,4},{8,9},{9,10},{10,1... | collective-permute-start | bytes 2359304 | tf_op jit(solution)/shard_map/ppermute | solution.py:42
  554.0 61.5 %copy-start.94 = (f32[1024,768]{1,0:T(8,128)S(1)}, f32[1024,768]{1,0:T(8,128)}, u32[]{:S(2)}) copy-start(f32[1024,768]{1,0:T(8,128)} %fusion.15) | copy-start | bytes 9437188
  615.6 17.0 %copy-start.71 = (f32[4,256]{1,0:T(4,128)S(1)}, f32[4,256]{1,0:T(4,128)}, u32[]{:S(2)}) copy-start(f32[4,256]{1,0:T(4,128)} %copy-done.70) | copy-start | bytes 12292
  637.0 69.5 %collective-permute-start.21 = (bf16[256,1536]{1,0:T(8,128)(2,1)}, bf16[256,1536]{1,0:T(8,128)(2,1)}, u32[]{:S(2)}, u32[]{:S(2)}) collective-permute-start(bf16[256,1536]{1,0:T(8,128)(2,1)} %get-tuple-element.240), channel_id=1, source_target_pairs={{0,3},{1,0},{2,1},{3,2},{4,7},{5,4},{6,5},{7,6},{8,11},{9,8},{10,9... | collective-permute-start | bytes 2359304 | tf_op jit(solution)/shard_map/ppermute | solution.py:50
  638.9 67.6 %collective-permute-start.20 = (bf16[256,1536]{1,0:T(8,128)(2,1)}, bf16[256,1536]{1,0:T(8,128)(2,1)}, u32[]{:S(2)}, u32[]{:S(2)}) collective-permute-start(bf16[256,1536]{1,0:T(8,128)(2,1)} %get-tuple-element.241), channel_id=1, source_target_pairs={{0,2},{1,3},{2,0},{3,1},{4,6},{5,7},{6,4},{7,5},{8,10},{9,11},{10,... | collective-permute-start | bytes 2359304 | tf_op jit(solution)/shard_map/ppermute | solution.py:50
  640.3 66.1 %collective-permute-start.19 = (bf16[256,1536]{1,0:T(8,128)(2,1)}, bf16[256,1536]{1,0:T(8,128)(2,1)}, u32[]{:S(2)}, u32[]{:S(2)}) collective-permute-start(bf16[256,1536]{1,0:T(8,128)(2,1)} %get-tuple-element.239), channel_id=1, source_target_pairs={{0,1},{1,2},{2,3},{3,0},{4,5},{5,6},{6,7},{7,4},{8,9},{9,10},{10,1... | collective-permute-start | bytes 2359304 | tf_op jit(solution)/shard_map/ppermute | solution.py:50
  650.7 42.4 %all-to-all-start.2 = ((f32[8,384,128]{2,1,0:T(8,128)}), f32[8,384,128]{2,1,0:T(8,128)S(1)}, u32[]{:S(2)}, u32[]{:S(2)}) async-start(f32[8,384,128]{2,1,0:T(8,128)} %bitcast.283), calls=%async_computation.2 | async-start | bytes 3145728 | tf_op jit(solution)/shard_map/all_to_all | solution.py:244
  654.3 181.4 %reduce-scatter.7.cloned.1.call-start = ((), (), s32[]{:S(2)}) async-start(), calls=%async_computation.11 | async-start | bytes 2654208 | tf_op jit(solution)/shard_map/reduce_scatter | solution.py:82
  663.5 23.4 %copy-start.45 = (bf16[4,256,1536]{2,1,0:T(8,128)(2,1)S(1)}, bf16[4,256,1536]{2,1,0:T(8,128)(2,1)}, u32[]{:S(2)}) copy-start(bf16[4,256,1536]{2,1,0:T(8,128)(2,1)} %bitcast_dynamic-update-slice_fusion.1) | copy-start | bytes 9437188
  694.7 41.9 %all-to-all-start.3 = ((f32[8,384,128]{2,1,0:T(8,128)}), f32[8,384,128]{2,1,0:T(8,128)}, u32[]{:S(2)}, u32[]{:S(2)}) async-start(f32[8,384,128]{2,1,0:T(8,128)} %scan_pieces.3), calls=%async_computation.3 | async-start | bytes 3145728 | tf_op jit(solution)/shard_map/all_to_all | solution.py:244
  699.2 140.8 %reduce-scatter.11.cloned.1.call-start = ((), (), s32[]{:S(2)}) async-start(), calls=%async_computation.13 | async-start | bytes 2654208 | tf_op jit(solution)/shard_map/reduce_scatter | solution.py:82
  699.8 203.0 %reduce-scatter.9.cloned.1.call-start = ((), (), s32[]{:S(2)}) async-start(), calls=%async_computation.12 | async-start | bytes 3096576 | tf_op jit(solution)/shard_map/reduce_scatter | solution.py:82
  764.7 3.5 collective-permute-start.22
  786.1 8.7 copy-start.39
  787.6 36.3 %collective-permute-start.24 = (bf16[256,1536]{1,0:T(8,128)(2,1)}, bf16[256,1536]{1,0:T(8,128)(2,1)S(1)}, u32[]{:S(2)}, u32[]{:S(2)}) collective-permute-start(bf16[256,1536]{1,0:T(8,128)(2,1)} %get-tuple-element.236), channel_id=1, source_target_pairs={{0,2},{1,3},{2,0},{3,1},{4,6},{5,7},{6,4},{7,5},{8,10},{9,11},{10,... | collective-permute-start | bytes 2359304 | tf_op jit(solution)/shard_map/ppermute | solution.py:50
  824.9 58.8 %all-to-all-start.4 = ((f32[8,4,112,128]{3,2,1,0:T(8,128)}), f32[8,4,112,128]{3,2,1,0:T(8,128)}, u32[]{:S(2)}, u32[]{:S(2)}) async-start(f32[8,4,112,128]{3,2,1,0:T(8,128)} %after.16), calls=%async_computation.5 | async-start | bytes 3670016 | tf_op jit(solution)/shard_map/all_to_all | solution.py:1006
  832.2 9.5 %copy-start.38 = (f32[8,192,256]{1,2,0:T(8,128)S(1)}, f32[8,192,256]{1,2,0:T(8,128)}, u32[]{:S(2)}) copy-start(f32[8,192,256]{1,2,0:T(8,128)} %slice.280) | copy-start | bytes 4718596
  837.6 53.5 %collective-permute-start.25 = (bf16[256,1536]{1,0:T(8,128)(2,1)}, bf16[256,1536]{1,0:T(8,128)(2,1)}, u32[]{:S(2)}, u32[]{:S(2)}) collective-permute-start(bf16[256,1536]{1,0:T(8,128)(2,1)} %get-tuple-element.235), channel_id=1, source_target_pairs={{0,3},{1,0},{2,1},{3,2},{4,7},{5,4},{6,5},{7,6},{8,11},{9,8},{10,9... | collective-permute-start | bytes 2359304 | tf_op jit(solution)/shard_map/ppermute | solution.py:50
  839.9 51.1 %collective-permute-start.23 = (bf16[256,1536]{1,0:T(8,128)(2,1)}, bf16[256,1536]{1,0:T(8,128)(2,1)}, u32[]{:S(2)}, u32[]{:S(2)}) collective-permute-start(bf16[256,1536]{1,0:T(8,128)(2,1)} %get-tuple-element.234), channel_id=1, source_target_pairs={{0,1},{1,2},{2,3},{3,0},{4,5},{5,6},{6,7},{7,4},{8,9},{9,10},{10,1... | collective-permute-start | bytes 2359304 | tf_op jit(solution)/shard_map/ppermute | solution.py:50
  843.5 47.6 %copy-start.40 = (bf16[1024,1536]{1,0:T(8,128)(2,1)S(1)}, bf16[1024,1536]{1,0:T(8,128)(2,1)}, u32[]{:S(2)}) copy-start(bf16[1024,1536]{1,0:T(8,128)(2,1)} %copy-done.39) | copy-start | bytes 9437188
  843.5 47.6 %copy-start.66 = (f32[1536]{0:T(1024)S(1)}, f32[1536]{0:T(1024)}, u32[]{:S(2)}) copy-start(f32[1536]{0:T(1024)} %copy-done.65) | copy-start | bytes 18436
  886.0 11.9 %all-to-all-start.5 = ((f32[4,112,128]{2,1,0:T(8,128)}), f32[4,112,128]{2,1,0:T(8,128)}, u32[]{:S(2)}, u32[]{:S(2)}) async-start(f32[4,112,128]{2,1,0:T(8,128)} %reduce_sum.180.refs_1_), calls=%async_computation.6 | async-start | bytes 458752 | tf_op jit(solution)/shard_map/all_to_all | solution.py:1008
  (75 other events, 271.2 us)
Sparse Core Ops, SparseCore 0:
  11.5 36.6 all-gather.8
  50.2 40.5 all-gather.10
  199.3 107.0 all-gather.12
  542.5 153.5 reduce-scatter.4
  699.3 42.5 reduce-scatter.6
  745.4 42.7 reduce-scatter.10
  799.1 60.5 reduce-scatter.8

commit v4 on v3

--- a/solution.py
+++ b/solution.py
@@ -19,6 +19,7 @@
 INNER_DIM = 3072
 LANES = 128
 CHUNKS = 1
+HALVES = 2
 
 norm_eps = 1e-05
 highest = lax.Precision.HIGHEST
@@ -123,6 +124,11 @@
     )(value, *others)
 
 
+def skipping(kernel, first, count):
+    return lambda *refs: kernel(*refs[:first], *refs[first + count :])
+
+
+ANYWHERE = pl.BlockSpec(memory_space=pl.ANY)
 NN = ((1,), (0,))
 NT = ((1,), (1,))
 TN = ((0,), (0,))
@@ -257,11 +263,11 @@
     return entering.reshape(slots, inner, STATE_DIM), decay
 
 
-def states_backward(g_local, decay):
+def states_scanned(g_local, decay):
     count = lax.axis_size("dp")
     slots, inner, _ = g_local.shape
     got = exchanged(g_local.reshape(count, slots * inner // count, STATE_DIM))
-    return exchanged(scan_pieces(got, decay, True)).reshape(slots, inner, STATE_DIM)
+    return scan_pieces(got, decay, True)
 
 
 def inner_kernel(inner, xs_ref, rw_ref, dl_ref, y_ref):
@@ -441,14 +447,14 @@
     gdl_ref[0, :, LANES:] = cols_buf[...].T - step * step_direct
 
 
-def mixer_pairs(xs, rw, dl, gy):
+def mixer_pairs(xs, rw, dl, gy, *earlier):
     slots, extent, inner = xs.shape
     wide = pl.BlockSpec((1, extent, inner), lambda s: (s, 0, 0))
     two = pl.BlockSpec((1, extent, 2 * LANES), lambda s: (s, 0, 0))
     return pl.pallas_call(
-        functools.partial(pairs_kernel, inner),
+        skipping(functools.partial(pairs_kernel, inner), 4, len(earlier)),
         grid=(slots,),
-        in_specs=[wide, two, two, wide],
+        in_specs=[wide, two, two, wide] + [ANYWHERE] * len(earlier),
         out_specs=[wide, two, two],
         out_shape=[
             jax.ShapeDtypeStruct((slots, extent, inner), f32),
@@ -459,7 +465,7 @@
         compiler_params=kernel_params(48),
         cost_estimate=taking(42, slots * extent),
         name="mixer_pairs",
-    )(xs, rw, dl, gy)
+    )(xs, rw, dl, gy, *earlier)
 
 
 def back_kernel(
@@ -691,45 +697,70 @@
 
 def expert_grad_kernel(up_blocks, chunks, *refs):
     n_refs, g_refs, h_refs, a_refs = (refs[i * chunks : (i + 1) * chunks] for i in range(4))
-    out_ref = refs[4 * chunks]
+    out_ref, turned = refs[4 * chunks :]
     block = pl.program_id(0)
     count, _, rows, cols = out_ref.shape
-
-    def summed(lefts, rights):
-        total = dot(lefts[0][...], rights[0][0], NN)
-        for left, right in zip(lefts[1:], rights[1:]):
-            total = total + dot(left[...], right[0], NN)
+    tokens = n_refs[0].shape[0]
+
+    def turn(sources):
+        for at, source in enumerate(sources):
+            turned[:, at * tokens : (at + 1) * tokens] = source[...].T
+
+    def summed_over(rights):
+        total = dot(turned[:, 0:tokens], rights[0][0], NN)
+        for at in range(1, chunks):
+            total = total + dot(turned[:, at * tokens : (at + 1) * tokens], rights[at][0], NN)
         out_ref[...] = total.astype(bf16).reshape(count, 1, rows, cols)
+
+    @pl.when(block == 0)
+    def _():
+        turn(n_refs)
+
+    @pl.when(block == up_blocks)
+    def _():
+        turn(g_refs)
 
     @pl.when(block < up_blocks)
     def _():
-        summed(n_refs, h_refs)
+        summed_over(h_refs)
 
     @pl.when(block >= up_blocks)
     def _():
-        summed(g_refs, a_refs)
-
-
-def expert_grads(n_list, g_list, hid_list, act_list, count):
+        summed_over(a_refs)
+
+
+def expert_grads(n_list, g_list, hid_list, act_list, count, *earlier):
     chunks = len(n_list)
-    width, tokens = n_list[0].shape
-    pairs, _, cols = act_list[0].shape
-    ups = 2 * pairs
-    blocks = 3 * pairs
-    whole = pl.BlockSpec((width, tokens), lambda b: (0, 0))
-    hid_at = lambda b: (jnp.minimum(b, ups - 1) // 2, 0, jnp.minimum(b, ups - 1) % 2)
+    tokens, width = n_list[0].shape
+    cols = 2 * LANES
+    hid_wide, act_wide = (values[0].shape[2] // cols for values in (hid_list, act_list))
+    ups = hid_list[0].shape[0] * hid_wide
+    downs = act_list[0].shape[0] * act_wide
+    blocks = ups + downs
+    whole = pl.BlockSpec((tokens, width), lambda b: (0, 0))
+
+    def hid_at(b):
+        b = jnp.minimum(b, ups - 1)
+        return b // hid_wide, 0, b % hid_wide
+
+    def act_at(b):
+        b = jnp.maximum(b - ups, 0)
+        return b // act_wide, 0, b % act_wide
+
     return pl.pallas_call(
-        functools.partial(expert_grad_kernel, ups, chunks),
+        skipping(functools.partial(expert_grad_kernel, ups, chunks), 4 * chunks, len(earlier)),
         grid=(blocks,),
         in_specs=[whole] * (2 * chunks)
         + [pl.BlockSpec((1, tokens, cols), hid_at)] * chunks
-        + [pl.BlockSpec((1, tokens, cols), lambda b: (jnp.maximum(b - ups, 0), 0, 0))] * chunks,
+        + [pl.BlockSpec((1, tokens, cols), act_at)] * chunks
+        + [ANYWHERE] * len(earlier),
         out_specs=pl.BlockSpec((count, 1, width // count, cols), lambda b: (0, b, 0, 0)),
         out_shape=jax.ShapeDtypeStruct((count, blocks, width // count, cols), bf16),
+        scratch_shapes=[pltpu.VMEM((width, chunks * tokens), bf16)],
         compiler_params=kernel_params(48),
-        cost_estimate=taking(40, chunks * tokens),
+        cost_estimate=taking(4 * blocks / 3, chunks * tokens),
         name="expert_grads",
-    )(*n_list, *g_list, *hid_list, *act_list)
+    )(*n_list, *g_list, *hid_list, *act_list, *earlier)
 
 
 def body(
@@ -847,25 +878,41 @@
             full_expert = weight_gather(after(expert_shard, h_in))
         y, gg, squares = mixer_leave(yi, xs, rw, dl, h_in, z[c], skip, gain_row)
         product = dot(flat(gg.reshape(zs, tokens, inner)), full_out, NT).astype(bf16)
-        mixed = summed(line_parts(by_distance(product.reshape(zs, tokens, D_MODEL))))
+        product = product.reshape(zs, tokens, D_MODEL)
         square_sum = lax.psum(squares[:, :, 0], "tensor")
         inv_all = lax.rsqrt(square_sum / INNER_DIM + norm_eps)
-        mixed = mixed * lax.dynamic_slice_in_dim(inv_all, own * rows, rows, 1).reshape(tokens, 1)
-        resid.append(row_major(u[c] + mixed))
-        mixed_all.append(mixed)
         y_all.append(y)
         h_all.append(h_in)
         decay_all.append(decay)
         inv_alls.append(inv_all)
         gg_all.append(gg)
-        n_two.append(jnp.concatenate(line_gather(row_major(rms_scale(resid[c], gain_two).astype(bf16))), axis=0))
+
+    few = tokens // HALVES
+    halves = range(HALVES)
+
+    def half_of(values, m):
+        return values[m * few : (m + 1) * few]
+
+    inv_own = lax.dynamic_slice_in_dim(inv_alls[0], own * rows, rows, 1).reshape(tokens, 1)
+    mixed_own = summed(line_parts(by_distance(product))) * inv_own
+    resid_own = row_major(u[0] + mixed_own)
+    normed_two = row_major(rms_scale(resid_own, gain_two).astype(bf16))
+    n_two_low, n_two, g_moe, masks = [], [], [], []
+    for m in halves:
+        low = half_of(normed_two, m)
+        if m > 0:
+            low = after(low, *n_two_low[m - 1][1:])
+        n_two_low.append(line_gather(low))
+        g_moe.append(jnp.concatenate([half_of(block, m) for block in g_blocks[0]], axis=0))
+        masks.append(jnp.concatenate([half_of(part(hot_at(k), 0), m) for k in range(zs)], axis=0))
     moe_part, back_part, logit_grads, acts, hids = [], [], [], [], []
-    g_moe = [jnp.concatenate(g_blocks[c], axis=0) for c in chunk_ids]
-    for c in chunk_ids:
-        mask = jnp.concatenate([part(hot_at(k), c) for k in range(zs)], axis=0)
-        results = experts(n_two[c], g_moe[c], mask, full_router, full_expert)
-        moe_part.append(results[0].reshape(zs, tokens, D_MODEL))
-        back_part.append(results[1].reshape(zs, tokens, D_MODEL))
+    for m in halves:
+        if m > 0:
+            n_two_low[m][1] = after(n_two_low[m][1], back_part[m - 1])
+        n_two.append(jnp.concatenate(n_two_low[m], axis=0))
+        results = experts(n_two[m], g_moe[m], masks[m], full_router, full_expert)
+        moe_part.append(results[0].reshape(zs, few, D_MODEL))
+        back_part.append(results[1].reshape(zs, few, D_MODEL))
         logit_grads.append(results[2])
         acts.append(results[3])
         hids.append(results[4])
@@ -873,19 +920,22 @@
     def norm_back(values, gain_vec, grads):
         return jax.vjp(rms_scale, values, gain_vec)[1](grads)
 
-    resid_grad, g_mixed, gain_two_grad = [], [], 0.0
-    unmixed, pairs, toks, gate_gain_grad = [], [], [], 0.0
+    back_blocks = []
+    for m in halves:
+        sent = back_part[m]
+        if m > 0:
+            sent = after(sent, *back_blocks[m - 1][1:])
+        back_blocks.append(line_parts(lambda k: sent[k]))
+    n_two_grad = jnp.concatenate([summed(blocks) for blocks in back_blocks], axis=0)
+    from_norm, gain_two_grad = norm_back(resid_own, gain_two, n_two_grad)
+    resid_grad = [row_major(grad_c[0] + from_norm)]
+    low = resid_grad[0].astype(bf16)
+    low_blocks = line_gather(low)
+    gathered = in_order(low_blocks)
+    expert_grad = weight_scatter(after(expert_grads(n_two, g_moe, hids, acts, pieces), gathered))
+    g_mixed = [flat(gathered)]
+    unmixed, scanned, pairs, toks, gate_gain_grad = [], [], [], [], 0.0
     for c in chunk_ids:
-        n_two_grad = summed(line_parts(lambda k: back_part[c][k]))
-        from_norm, gain_grad = norm_back(resid[c], gain_two, n_two_grad)
-        gain_two_grad = gain_two_grad + gain_grad
-        resid_grad.append(row_major(grad_c[c] + from_norm))
-        low = resid_grad[c].astype(bf16)
-        if c == CHUNKS - 1:
-            expert_grad = weight_scatter(
-                after(expert_grads([n.T for n in n_two], [g.T for g in g_moe], hids, acts, pieces), low)
-            ).astype(f32)
-        g_mixed.append(flat(in_order(line_gather(low))))
         grad = in_slots(dot(g_mixed[c], full_out, NN))
         xs, rw, dl, _ = entered[c]
         inv_all = inv_alls[c]
@@ -896,25 +946,27 @@
         gy, gz, g_local, gg_grad = mixer_unmix(grad, y_all[c], z[c], rw, dl, tok, gain_row)
         toks.append(tok)
         gate_gain_grad = gate_gain_grad + gg_grad[0]
-        unmixed.append((gy, gz, g_local))
+        unmixed.append((gy, gz))
+        scanned.append(states_scanned(g_local, decay_all[c]))
         pairs.append(mixer_pairs(xs, rw, dl, gy))
 
-    moe = []
-    for c in chunk_ids:
-        held = after(moe_part[c], *toks)
-        moe.append(summed(line_parts(lambda k: held[k])))
-    output = [resid[c] + moe[c] for c in chunk_ids]
-    stat_terms = sum(
-        jnp.stack(
-            [
-                jnp.sum(valid_c[c] * output[c] * output[c]),
-                jnp.sum(valid_c[c] * mixed_all[c] * mixed_all[c]),
-                jnp.sum(valid_c[c] * moe[c] * moe[c]),
-            ]
-        )
-        for c in chunk_ids
-    )
-    router_grad = sum(dot(n_two[c], logit_grads[c], TN)[:, :EXPERTS] for c in chunk_ids)
+    moe_blocks = []
+    for m in halves:
+        held = after(moe_part[m], *toks)
+        moe_blocks.append(line_parts(lambda k: held[k]))
+    sooner = [block for blocks in moe_blocks for block in blocks[1::2]]
+    later = [block for blocks in moe_blocks for block in blocks[2::2]]
+    moe = [summed(blocks) for blocks in moe_blocks]
+    moe_own = jnp.concatenate(moe, axis=0)
+    output = [resid_own + moe_own]
+    stat_terms = jnp.stack(
+        [
+            jnp.sum(valid_c[0] * output[0] * output[0]),
+            jnp.sum(valid_c[0] * mixed_own * mixed_own),
+            jnp.sum(valid_c[0] * moe_own * moe_own),
+        ]
+    )
+    router_grad = sum(dot(n_two[m], logit_grads[m], TN)[:, :EXPERTS] for m in halves)
 
     def rows_of(values):
         return jnp.concatenate([v.reshape(zs * tokens, -1) for v in values], axis=0)
@@ -923,26 +975,18 @@
         jnp.transpose(inv_alls[c].reshape(per, zs, rows), (1, 0, 2)).reshape(zs * tokens, 1) for c in chunk_ids
     ]
     scaled = [(g_mixed[c].astype(f32) * inv_rows[c]).astype(bf16) for c in chunk_ids]
-    out_w_grad = dot(rows_of(scaled), rows_of(gg_all), TN).astype(bf16)
     n_rows = rows_of(n_one)
-    z_w_grad = dot(n_rows, rows_of([unmixed[c][1] for c in chunk_ids]), TN).astype(bf16)
-
-    ups, downs = EXPERTS + 2, EXPERTS // 2
-    expert_outs = (
-        expert_grad[:EXPERTS].reshape(EXPERTS, shard, 2, half),
-        expert_grad[ups : ups + downs].transpose(0, 2, 1).reshape(EXPERTS, half, shard),
-        expert_grad[EXPERTS:ups].reshape(2, shard, 2, half).transpose(1, 2, 0, 3).reshape(shard, 2, 2 * half),
-        expert_grad[ups + downs].T,
-    )
+    gg_row, gz_row = (values.reshape(1, zs * tokens, inner) for values in (gg_all[0], unmixed[0][1]))
+    side_products = expert_grads(scaled, [n_rows], [gg_row], [gz_row], pieces)
 
     v_grads, bc_grads, conv_grad, head_grad = [], [], 0.0, 0.0
     full_x = jnp.concatenate([full_enter[:, :inner], full_enter[:, width:]], axis=1)
     full_bc = full_enter[:, inner:width]
     full_bc = jnp.concatenate([full_bc, full_bc], axis=1)
     for c in chunk_ids:
-        gy, gz, g_local = unmixed[c]
+        gy, gz = unmixed[c]
         xs, rw, dl, _ = entered[c]
-        gh = after(states_backward(g_local, decay_all[c]), moe[c], *expert_outs)
+        gh = exchanged(after(scanned[c], pairs[c][0], *sooner)).reshape(h_all[c].shape)
         gv, gbc, g_rim, gc, ghp = mixer_back(
             v[c], halo[c], conv_w, hp, skip, rw, dl, gy, *pairs[c], h_all[c], gh
         )
@@ -954,7 +998,7 @@
         edge = gbc[zs - 1, :, rows - rim :] + following[:, :, inner:]
         gbc = lax.dynamic_update_slice(gbc, edge[None], (zs - 1, 0, rows - rim, 0))
         v_grads.append(gv)
-        bc_grads.append(jnp.concatenate(split_parts(gbc), axis=-1))
+        bc_grads.append(after(jnp.concatenate(split_parts(gbc), axis=-1), *later))
     n_parts, arrived, gain_one_grad = [], [], 0.0
     for c in chunk_ids:
         n_grad = (
@@ -971,12 +1015,25 @@
     enter_w_grad = dot(n_rows, rows_of(v_grads), TN).astype(bf16)
     bc_w_grad = dot(n_rows, rows_of(bc_grads), TN)
     bc_w_grad = bc_w_grad[:, : 2 * STATE_DIM] + bc_w_grad[:, 2 * STATE_DIM :]
+    side_grad = weight_scatter(after(side_products, expert_grad, conv_grad))
 
     def mixer_scatter(grads):
-        return weight_scatter(grads.reshape(pieces, shard, -1)).astype(f32)
-
-    out_part, z_part = mixer_scatter(out_w_grad), mixer_scatter(z_w_grad)
+        return weight_scatter(after(grads.reshape(pieces, shard, -1), side_grad)).astype(f32)
+
+    side = side_grad.astype(f32)
+    fold = side.shape[0] // 2
+    z_part = jnp.transpose(side[fold:], (1, 0, 2)).reshape(shard, inner)
+    out_part = jnp.transpose(side[:fold], (0, 2, 1)).reshape(inner, shard)
     enter_part = mixer_scatter(enter_w_grad)
+    expert_grad = expert_grad.astype(f32)
+    ups, downs = EXPERTS + 2, EXPERTS // 2
+    expert_outs = (
+        expert_grad[:EXPERTS].reshape(EXPERTS, shard, 2, half),
+        expert_grad[ups : ups + downs].transpose(0, 2, 1).reshape(EXPERTS, half, shard),
+        expert_grad[EXPERTS:ups].reshape(2, shard, 2, half).transpose(1, 2, 0, 3).reshape(shard, 2, 2 * half),
+        expert_grad[ups + downs].T,
+    )
+
     def to_shares(values, dim):
         size = values.shape[dim] // (pieces * zs)
         values = jnp.moveaxis(values, dim, 0).reshape(pieces, zs, size, -1)
@@ -1001,16 +1058,22 @@
     length = shares.shape[2]
     shares = jnp.pad(shares, ((0, 0), (0, 0), (0, -length % (8 * LANES))))
     wide_share = bc_w_grad.reshape(pieces, zs, -1, LANES)
-    shares = jnp.concatenate([wide_share, shares.reshape(pieces, zs, -1, LANES)], axis=2)
-    shares = after(shares, arrived[CHUNKS - 1][2])
+    tile = jnp.zeros((8, LANES), f32)
+    tile = tile.at[:3, :heads].set(head_grad[:3, :heads]).at[3, :3].set(stat_terms)
+    tile = jnp.broadcast_to(tile, (pieces, zs) + tile.shape)
+    shares = jnp.concatenate([wide_share, shares.reshape(pieces, zs, -1, LANES), tile], axis=2)
+    shares = after(shares, arrived[CHUNKS - 1][1])
     shares = jnp.sum(lax.all_to_all(shares, "dp", 0, 0), axis=0)
-    first_sum = shares
-    shares = jnp.sum(lax.all_to_all(shares, "tensor", 0, 0), axis=0)
+    first_sum = after(shares, arrived[0][2])
+    shares = first_sum
+    got = lax.all_to_all(shares, "tensor", 0, 0)
+    tiles = got[:, -8:]
+    shares = jnp.sum(got[:, :-8], axis=0)
     u_grad = []
     for c in chunk_ids:
         received = arrived[c]
         if c == CHUNKS - 1:
-            received[1] = after(received[1], first_sum)
+            received[3] = after(received[3], first_sum, *expert_outs)
         u_grad.append(resid_grad[c] + norm_back(u[c], gain_one, summed(received))[0])
     bc_lines = wide_share.shape[2]
     bc_grad = shares[:bc_lines].reshape(-1, 2 * STATE_DIM)
@@ -1024,10 +1087,6 @@
             share = share.reshape(other, size // other)
             share = share if dim == 1 else share.T
         took.append(share)
-    tile = jnp.zeros((8, LANES), f32)
-    tile = tile.at[:3, :heads].set(head_grad[:3, :heads]).at[3, :3].set(stat_terms)
-    tile = jnp.sum(lax.all_gather(tile, "dp"), axis=0)
-    tiles = lax.all_gather(tile, "tensor")
     head_sum = jnp.transpose(tiles[:, :3, :heads], (1, 0, 2)).reshape(3, HEAD_COUNT)
     stat_sum = jnp.sum(tiles[:, 3, :3], axis=0)
     stats = jnp.sqrt(stat_sum / (jnp.sum(lengths).astype(f32) * D_MODEL))
@@ -1047,7 +1106,7 @@
         took[2],
         head_sum,
         took[3],
-        out_part.T,
+        out_part,
         took[4],
         took[5],
         *expert_outs,

time: 926 us -> 897 us (0.969)
  blocking collectives: 108 us -> 70.8 us
  waiting for transfers between devices: 237 us -> 265 us
  local copies, waits for them, and re-layouts: 143 us -> 122 us
  Pallas kernels: 190 us -> 208 us
    all_gather x2 -> x0, blocking collectives: 36.9 us -> none  [the longest x1 19.7 us: body(): tiles = lax.all_gather(tile, 'tensor')]
    ppermute x12 -> x15, waiting for transfers between devices: 151 us -> 128 us  [line_gather(): lax.ppermute(row_major(value), 'tensor', [(a, (a - step) % size) for a in...]
    all_to_all x4, waiting for transfers between devices: 27.4 us -> 48.8 us  [exchanged(): return lax.all_to_all(rows, 'dp', 0, 0, tiled=False)]
    another operation x8 -> x1, local copies, waits for them, and re-layouts: 21.5 us -> 3.75 us  [row_major(): with_layout_constraint(value, Layout(major_to_minor=tuple(range(value.ndi...]
    all_to_all x1, waiting for transfers between devices: 0.01 us -> 16.8 us  [body(): shares = jnp.sum(lax.all_to_all(shares, 'dp', 0, 0), axis=0)]
    pallas_call x2 -> x3, Pallas kernels: 58.2 us -> 71.3 us  [the longest x2 48 us: expert_grads(): pl.pallas_call(skipping(functools.partial(expert_grad_kernel, ups, chunks...]
    reduce_scatter x4 -> x3, waiting for transfers between devices: 0.01 us -> 9.78 us  [weight_scatter(): lax.psum_scatter(grads.astype(bf16), 'dp', scatter_dimension=0, tiled=False)]
    transpose x3 -> x0, other arithmetic: 9.48 us -> none  [the longest x2 7.66 us: body(): expert_grad = weight_scatter(after(expert_grads([n.T for n in n_two], [g....]
  transfers between devices with their start and end apart: 39 -> 47, of which waited for: 12 -> 20; matrix products, arithmetic and copies ran while one was open for 26% -> 22% of each run, Pallas kernels for 13% -> 23%
where the time goes in v4:
time: 897 us; the launch traced here: 885 us
  waiting for transfers between devices  265 us (30%)
  Pallas kernels  208 us (23%)
  local copies, waits for them, and re-layouts  122 us (14%)
  starting transfers between devices  79.1 us (9%)
  blocking collectives  70.8 us (8%)
  matrix products  63.3 us (7%)
  other arithmetic  60.5 us (7%)
  between operations  16.7 us (2%)
    ppermute x15, waiting for transfers between devices, line_gather(): lax.ppermute(row_major(value), 'tensor', [(a, (a - step) % size) for a in...  128 us
    pallas_call x2, Pallas kernels, experts(): pl.pallas_call(expert_kernel, grid=(pairs,), in_specs=[pl.BlockSpec((toke...  77.3 us
    dot_general x12, matrix products, dot(): lax.dot_general(a, b, (dims, ((), ())), precision=precision, preferred_el...  63.3 us
    ppermute x18, waiting for transfers between devices, line_parts(): lax.ppermute(row_major(block_of(step)), 'tensor', [(a, (a + step) % size)...  59.8 us
    psum x1, blocking collectives, body(): square_sum = lax.psum(squares[:, :, 0], 'tensor')  53.5 us
    all_to_all x4, waiting for transfers between devices, exchanged(): return lax.all_to_all(rows, 'dp', 0, 0, tiled=False)  48.8 us
    pallas_call x2, Pallas kernels, expert_grads(): pl.pallas_call(skipping(functools.partial(expert_grad_kernel, ups, chunks...  48 us
    unnamed x234, local copies, waits for them, and re-layouts  40.1 us
  transfers between devices with their start and end apart: 47, of which 20 were waited for; matrix products, arithmetic and copies ran while one was open for 22% of the time, Pallas kernels for 23%

profile of v4, /device:TPU:0, one launch (start us, length us, event | category | flops | bytes accessed | tf_op | source)
XLA Modules:
  0.0 885.3 jit_solution(10786300792487549709)
XLA Ops:
  12.5 5.0 collective-permute-start
  19.8 8.9 %all-gather.3 = f32[8,192,2]{1,2,0:T(2,128)S(1)} all-gather(f32[1,192,2]{1,2,0:T(2,128)S(1)} %fusion.57), channel_id=1, replica_groups=mesh['dp'=8,'tensor'=4] {'dp'}, dimensions={0}, use_global_device_ids=true | all-gather | bytes 13824 | tf_op jit(solution)/shard_map/all_gather | solution.py:830
  32.8 3.0 collective-permute-done
  37.1 48.1 %collective-permute-done.1 = bf16[256,1536]{1,0:T(8,128)(2,1)} collective-permute-done((bf16[256,1536]{1,0:T(8,128)(2,1)}, bf16[256,1536]{1,0:T(8,128)(2,1)}, u32[]{:S(2)}, u32[]{:S(2)}) %collective-permute-start.1) | collective-permute-done | bytes 786464 | tf_op jit(solution)/shard_map/ppermute | solution.py:43
  95.6 7.9 fusion.1.v_ref
  103.5 11.3 %mixer_enter.1 = (f32[4,256,768]{2,1,0:T(8,128)}, f32[4,256,256]{2,1,0:T(8,128)S(1)}, f32[4,256,256]{2,1,0:T(8,128)S(1)}, f32[4,768,128]{2,1,0:T(8,128)S(1)}) custom-call(f32[4,4,64,1152]{3,2,1,0:T(8,128)} %fusion.1.v_ref, f32[4,8,1024]{2,1,0:T(8,128)S(1)} %pad.42.halo_ref, f32[8,1024]{1,0:T(8,128)S(1)} %select_maximum_fusion.cw_ref, f32[8,128]{1,0:T(8,128)S(1)} %pad.44.hp_ref), custom_call_target="tpu_custom_call" | custom-call | flops 13516800000 | bytes 1024 | tf_op jit(solution)/shard_map/mixer_enter/pallas_call | solution.py:203
  118.2 10.4 %collective-permute-done.5.refs_2_ = bf16[256,1536]{1,0:T(8,128)(2,1)} collective-permute-done((bf16[256,1536]{1,0:T(8,128)(2,1)}, bf16[256,1536]{1,0:T(8,128)(2,1)}, u32[]{:S(2)}, u32[]{:S(2)}) %collective-permute-start.5) | collective-permute-done | bytes 786464 | tf_op jit(solution)/shard_map/ppermute | solution.py:43
  128.7 2.7 pad_maximum_fusion.2
  131.3 4.4 all-to-all-start
  136.6 20.6 %all-to-all-done = f32[8,392,128]{2,1,0:T(8,128)} async-done(((f32[8,392,128]{2,1,0:T(8,128)}), f32[8,392,128]{2,1,0:T(8,128)}, u32[]{:S(2)}, u32[]{:S(2)}) %all-to-all-start) | async-done | bytes 1605664 | tf_op jit(solution)/shard_map/all_to_all | solution.py:250
  161.6 10.8 %collective-permute-done.6.refs_1_ = bf16[256,1536]{1,0:T(8,128)(2,1)S(1)} collective-permute-done((bf16[256,1536]{1,0:T(8,128)(2,1)S(1)}, bf16[256,1536]{1,0:T(8,128)(2,1)S(1)}, u32[]{:S(2)}, u32[]{:S(2)}) %collective-permute-start.6) | collective-permute-done | bytes 786464 | tf_op jit(solution)/shard_map/ppermute | solution.py:43
  173.3 3.9 all-to-all-start.1
  184.6 3.8 reshape.439
  188.4 3.0 pad_maximum_fusion.refs_0_
  191.4 6.8 all-to-all-done.1
  206.0 4.6 mixer_inner.1.yi_ref
  212.3 7.0 fusion.16
  219.3 7.2 mixer_leave.1
  226.6 5.1 convolution_convert_fusion
  238.3 53.5 %psum.14 = f32[4,256]{1,0:T(4,128)S(1)} all-reduce(f32[4,256]{1,0:T(4,128)S(1)} %slice_reduce_fusion), channel_id=1, replica_groups=mesh['dp'=8,'tensor'=4] {'tensor'}, use_global_device_ids=true, to_apply=%region_1.2 | all-reduce | flops 1024 | bytes 8192 | tf_op jit(solution)/shard_map/psum | solution.py:882
  292.0 9.5 %collective-permute-done.8 = bf16[256,1536]{1,0:T(8,128)(2,1)S(1)} collective-permute-done((bf16[256,1536]{1,0:T(8,128)(2,1)}, bf16[256,1536]{1,0:T(8,128)(2,1)S(1)}, u32[]{:S(2)}, u32[]{:S(2)}) %collective-permute-start.8) | collective-permute-done | bytes 786464 | tf_op jit(solution)/shard_map/ppermute | solution.py:51
  302.4 2.8 multiply_reduce_fusion.4
  306.3 7.7 collective-permute-start.10
  319.6 4.0 collective-permute-done.10.refs_1_
  323.6 21.7 %collective-permute-done.11.refs_2_ = bf16[128,1536]{1,0:T(8,128)(2,1)S(1)} collective-permute-done((bf16[128,1536]{1,0:T(8,128)(2,1)S(1)}, bf16[128,1536]{1,0:T(8,128)(2,1)S(1)}, u32[]{:S(2)}, u32[]{:S(2)}) %collective-permute-start.11) | collective-permute-done | bytes 393248 | tf_op jit(solution)/shard_map/ppermute | solution.py:43
  349.7 3.3 collective-permute-start.16
  355.6 38.7 %experts.2 = (bf16[512,1536]{1,0:T(8,128)(2,1)}, bf16[512,1536]{1,0:T(8,128)(2,1)}, bf16[512,128]{1,0:T(8,128)(2,1)}, bf16[9,512,256]{2,1,0:T(8,128)(2,1)}, bf16[9,512,512]{2,1,0:T(8,128)(2,1)}) custom-call(bf16[512,1536]{1,0:T(8,128)(2,1)} %pad_maximum_fusion.3.n_ref.refs_0_, bf16[512,1536]{1,0:T(8,128)(2,1)} %get-tuple-element.300.g_ref.refs_2_, ...), custom_call_target="tpu_custom_call" | custom-call | flops 40550400000 | bytes 1024 | tf_op jit(solution)/shard_map/experts/pallas_call | solution.py:661
  397.1 3.2 collective-permute-start.15
  403.0 38.7 %experts.3 = (bf16[512,1536]{1,0:T(8,128)(2,1)}, bf16[512,1536]{1,0:T(8,128)(2,1)}, bf16[512,128]{1,0:T(8,128)(2,1)}, bf16[9,512,256]{2,1,0:T(8,128)(2,1)}, bf16[9,512,512]{2,1,0:T(8,128)(2,1)}) custom-call(bf16[512,1536]{1,0:T(8,128)(2,1)} %pad_maximum_fusion.5.n_ref.refs_1_, bf16[512,1536]{1,0:T(8,128)(2,1)} %get-tuple-element.301.g_ref.refs_3_, ...), custom_call_target="tpu_custom_call" | custom-call | flops 40550400000 | bytes 1024 | tf_op jit(solution)/shard_map/experts/pallas_call | solution.py:661
  448.7 4.6 collective-permute-done.21
  453.3 23.8 %collective-permute-done.20 = bf16[128,1536]{1,0:T(8,128)(2,1)S(1)} collective-permute-done((bf16[128,1536]{1,0:T(8,128)(2,1)S(1)}, bf16[128,1536]{1,0:T(8,128)(2,1)S(1)}, u32[]{:S(2)}, u32[]{:S(2)}) %collective-permute-start.20) | collective-permute-done | bytes 393248 | tf_op jit(solution)/shard_map/ppermute | solution.py:51
  485.2 35.9 %expert_grads.2.refs_0_ = bf16[8,27,192,256]{3,2,1,0:T(8,128)(2,1)} custom-call(bf16[512,1536]{1,0:T(8,128)(2,1)S(1)} %copy-done.7, bf16[512,1536]{1,0:T(8,128)(2,1)S(1)} %copy-done.4, bf16[512,1536]{1,0:T(8,128)(2,1)S(1)} %copy-done.12, bf16[512,1536]{1,0:T(8,128)(2,1)} %get-tuple-element.301.g_ref.refs_3_, bf16[9,512,512]{2,1,0:T(8,128)(2,1)} %get-tuple-element.96.refs_4_, ...), custom_call_target="tpu_custom_call" | custom-call | flops 40550400000 | bytes 1024 | tf_op jit(solution)/shard_map/expert_grads/pallas_call | solution.py:750
  524.0 29.4 %collective-permute-done.23 = bf16[256,1536]{1,0:T(8,128)(2,1)S(1)} collective-permute-done((bf16[256,1536]{1,0:T(8,128)(2,1)S(1)}, bf16[256,1536]{1,0:T(8,128)(2,1)S(1)}, u32[]{:S(2)}, u32[]{:S(2)}) %collective-permute-start.23) | collective-permute-done | bytes 786464 | tf_op jit(solution)/shard_map/ppermute | solution.py:43
  560.4 11.5 %fusion.5 = (f32[4,4,64]{2,1,0:T(4,128)S(1)}, f32[4,4,64,768]{3,2,1,0:T(8,128)}) fusion(f32[4,4,64,768]{3,2,1,0:T(8,128)} %bitcast.371, f32[4,4,64,768]{3,2,1,0:T(8,128)} %bitcast.369, f32[768]{0:T(1024)S(1)} %copy-done.101, bf16[4,4,64,1536]{3,2,1,0:T(8,128)(2,1)} %bitcast.59, bf16[1536,1664]{1,0:T(8,128)(2,1)} %all-gather.10.cloned.1.call-done), kind=kOutput, calls=%fused_computation.15 | convolution fusion | flops 2422209536 | bytes 14949376 | tf_op jit(solution)/shard_map/dot_general | solution.py:98
  572.0 8.3 psum.15
  589.9 3.8 collective-permute-start.27
  593.7 8.0 mixer_unmix.1
  604.0 4.6 all-to-all-start.2
  611.1 23.3 %mixer_pairs.1 = (f32[4,256,768]{2,1,0:T(8,128)}, f32[4,256,256]{2,1,0:T(8,128)S(1)}, f32[4,256,256]{2,1,0:T(8,128)S(1)}) custom-call(f32[4,256,768]{2,1,0:T(8,128)} %get-tuple-element.71.xs_ref.refs_0_, f32[4,256,256]{2,1,0:T(8,128)S(1)} %copy-done.32, f32[4,256,256]{2,1,0:T(8,128)S(1)} %copy-done.21, f32[4,256,768]{2,1,0:T(8,128)} %get-tuple-element.83.refs_3_.gy_ref), custom_call_target="tpu_custom_call" | custom-call | flops 47308800000 | bytes 1024 | tf_op jit(solution)/shard_map/mixer_pairs/pallas_call | solution.py:454
  636.3 4.2 fusion.refs_0_
  640.5 6.3 all-to-all-done.2.got_ref
  649.1 3.7 all-to-all-start.3
  653.1 6.3 fusion.14
  659.4 12.1 %expert_grads.3.refs_0_ = bf16[8,6,192,256]{3,2,1,0:T(8,128)(2,1)} custom-call(bf16[1024,1536]{1,0:T(8,128)(2,1)} %fusion.refs_0_, bf16[1024,1536]{1,0:T(8,128)(2,1)} %copy-done.54, bf16[1,1024,768]{2,1,0:T(8,128)(2,1)S(1)} %bitcast.304, bf16[1,1024,768]{2,1,0:T(8,128)(2,1)S(1)} %bitcast.306), custom_call_target="tpu_custom_call" | custom-call | flops 9011200000 | bytes 1024 | tf_op jit(solution)/shard_map/expert_grads/pallas_call | solution.py:750
  671.6 15.1 %all-to-all-done.3 = f32[8,384,128]{2,1,0:T(8,128)S(1)} async-done(((f32[8,384,128]{2,1,0:T(8,128)}), f32[8,384,128]{2,1,0:T(8,128)S(1)}, u32[]{:S(2)}, u32[]{:S(2)}) %all-to-all-start.3) | async-done | bytes 1572896 | tf_op jit(solution)/shard_map/all_to_all | solution.py:250
  687.9 27.2 %mixer_back.1 = (bf16[4,4,64,896]{3,2,1,0:T(8,128)(2,1)}, f32[4,4,64,256]{3,2,1,0:T(8,128)}, f32[4,8,1024]{2,1,0:T(8,128)}, f32[8,1024]{1,0:T(8,128)}, f32[8,128]{1,0:T(8,128)}) custom-call(f32[4,4,64,1152]{3,2,1,0:T(8,128)} %fusion.1.v_ref, f32[4,8,1024]{2,1,0:T(8,128)} %copy-done.13, f32[8,1024]{1,0:T(8,128)} %copy-done.14, f32[8,128]{1,0:T(8,128)} %copy-done.16, ...), custom_call_target="tpu_custom_call" | custom-call | flops 20275200000 | bytes 1024 | tf_op jit(solution)/shard_map/mixer_back/pallas_call | solution.py:558
  715.1 9.8 %reduce-scatter.4.cloned.1.call-done = bf16[1,27,192,256]{3,2,1,0:T(8,128)(2,1)} async-done(((bf16[8,27,192,256]{3,2,1,0:T(8,128)(2,1)}), bf16[1,27,192,256]{3,2,1,0:T(8,128)(2,1)}) %reduce-scatter.4.cloned.1.call-update) | async-done | bytes 2654224 | tf_op jit(solution)/shard_map/reduce_scatter | solution.py:83
  729.1 3.9 fusion.19
  744.9 5.1 fusion.6
  750.0 5.3 multiply_reduce_fusion
  759.6 3.5 fusion.76
  763.6 3.3 slice_add_fusion
  769.8 10.5 %collective-permute-done.32.refs_1_ = bf16[256,1536]{1,0:T(8,128)(2,1)S(1)} collective-permute-done((bf16[256,1536]{1,0:T(8,128)(2,1)}, bf16[256,1536]{1,0:T(8,128)(2,1)S(1)}, u32[]{:S(2)}, u32[]{:S(2)}) %collective-permute-start.32) | collective-permute-done | bytes 786464 | tf_op jit(solution)/shard_map/ppermute | solution.py:51
  781.2 3.6 all-to-all-start.4
  785.7 7.5 convolution_convert_fusion.1
  793.2 16.8 %all-to-all-done.4 = f32[8,4,120,128]{3,2,1,0:T(8,128)S(1)} async-done(((f32[8,4,120,128]{3,2,1,0:T(8,128)}), f32[8,4,120,128]{3,2,1,0:T(8,128)S(1)}, u32[]{:S(2)}, u32[]{:S(2)}) %all-to-all-start.4) | async-done | bytes 1966112 | tf_op jit(solution)/shard_map/all_to_all | solution.py:1066
  810.8 11.4 %collective-permute-done.33.refs_1_ = bf16[256,1536]{1,0:T(8,128)(2,1)} collective-permute-done((bf16[256,1536]{1,0:T(8,128)(2,1)}, bf16[256,1536]{1,0:T(8,128)(2,1)}, u32[]{:S(2)}, u32[]{:S(2)}) %collective-permute-start.33) | collective-permute-done | bytes 786464 | tf_op jit(solution)/shard_map/ppermute | solution.py:51
  822.1 3.6 all-to-all-start.5
  829.6 3.8 collective-permute-start.34
  840.2 3.8 copy.298
  843.9 4.3 slice.469
  848.5 3.8 convert_element_type.267
  852.2 6.0 copy.300.refs_2_
  865.8 2.7 fusion.24
  (495 shorter events, 174.2 us)
Async XLA Ops:
  7.2 177.2 %copy-start = (bf16[192,2,256]{2,1,0:T(2,128)(2,1)S(1)}, bf16[192,2,256]{2,1,0:T(2,128)(2,1)}, u32[]{:S(2)}) copy-start(bf16[192,2,256]{2,1,0:T(2,128)(2,1)} %param.40) | copy-start | bytes 589828
  7.2 85.8 %all-gather.8.cloned.1.call-start = ((), (), s32[]{:S(2)}) async-start(), calls=%async_computation.12 | async-start | bytes 3981312 | tf_op jit(solution)/shard_map/all_gather | solution.py:79
  11.4 200.9 %all-gather.10.cloned.1.call-start = ((), (), s32[]{:S(2)}) async-start(), calls=%async_computation.13 | async-start | bytes 5750784 | tf_op jit(solution)/shard_map/all_gather | solution.py:79
  11.5 17.3 %copy-start.104 = (s32[4]{0:T(128)S(1)}, s32[4]{0:T(128)}, u32[]{:S(2)}) copy-start(s32[4]{0:T(128)} %param.25) | copy-start | bytes 52
  11.5 17.5 %copy-start.78 = (bf16[64,4,1536]{2,1,0:T(4,128)(2,1)S(1)}, bf16[64,4,1536]{2,1,0:T(4,128)(2,1)}, u32[]{:S(2)}) copy-start(bf16[64,4,1536]{2,1,0:T(4,128)(2,1)} %param.24) | copy-start | bytes 2359300
  12.5 23.4 %collective-permute-start = (bf16[256,1536]{1,0:T(8,128)(2,1)}, bf16[256,1536]{1,0:T(8,128)(2,1)}, u32[]{:S(2)}, u32[]{:S(2)}) collective-permute-start(bf16[256,1536]{1,0:T(8,128)(2,1)} %bitcast.1), channel_id=1, source_target_pairs={{0,3},{1,0},{2,1},{3,2},{4,7},{5,4},{6,5},{7,6},{8,11},{9,8},{10,9... | collective-permute-start | bytes 2359304 | tf_op jit(solution)/shard_map/ppermute | solution.py:43
  17.6 67.6 %collective-permute-start.1 = (bf16[256,1536]{1,0:T(8,128)(2,1)}, bf16[256,1536]{1,0:T(8,128)(2,1)}, u32[]{:S(2)}, u32[]{:S(2)}) collective-permute-start(bf16[256,1536]{1,0:T(8,128)(2,1)} %bitcast.1), channel_id=1, source_target_pairs={{0,2},{1,3},{2,0},{3,1},{4,6},{5,7},{6,4},{7,5},{8,10},{9,11},{10,... | collective-permute-start | bytes 2359304 | tf_op jit(solution)/shard_map/ppermute | solution.py:43
  17.6 68.8 %collective-permute-start.2 = (bf16[256,1536]{1,0:T(8,128)(2,1)}, bf16[256,1536]{1,0:T(8,128)(2,1)}, u32[]{:S(2)}, u32[]{:S(2)}) collective-permute-start(bf16[256,1536]{1,0:T(8,128)(2,1)} %bitcast.1), channel_id=1, source_target_pairs={{0,1},{1,2},{2,3},{3,0},{4,5},{5,6},{6,7},{7,4},{8,9},{9,10},{10,1... | collective-permute-start | bytes 2359304 | tf_op jit(solution)/shard_map/ppermute | solution.py:43
  32.8 55.5 %copy-start.80 = (f32[1536]{0:T(1024)}, f32[1536]{0:T(1024)S(1)}, u32[]{:S(2)}) copy-start(f32[1536]{0:T(1024)S(1)} %get-tuple-element.233) | copy-start | bytes 18436
  89.3 3.8 collective-permute-start.3
  90.9 12.6 %copy-start.14 = (f32[8,1024]{1,0:T(8,128)}, f32[8,1024]{1,0:T(8,128)S(1)}, u32[]{:S(2)}) copy-start(f32[8,1024]{1,0:T(8,128)S(1)} %select_maximum_fusion.cw_ref) | copy-start | bytes 98308
  90.9 12.6 %copy-start.16 = (f32[8,128]{1,0:T(8,128)}, f32[8,128]{1,0:T(8,128)S(1)}, u32[]{:S(2)}) copy-start(f32[8,128]{1,0:T(8,128)S(1)} %pad.44.hp_ref) | copy-start | bytes 12292
  91.0 27.2 %collective-permute-start.4 = (bf16[256,1536]{1,0:T(8,128)(2,1)}, bf16[256,1536]{1,0:T(8,128)(2,1)}, u32[]{:S(2)}, u32[]{:S(2)}) collective-permute-start(bf16[256,1536]{1,0:T(8,128)(2,1)} %after.17), channel_id=1, source_target_pairs={{0,3},{1,0},{2,1},{3,2},{4,7},{5,4},{6,5},{7,6},{8,11},{9,8},{10,9... | collective-permute-start | bytes 2359304 | tf_op jit(solution)/shard_map/ppermute | solution.py:43
  91.0 37.6 %collective-permute-start.5 = (bf16[256,1536]{1,0:T(8,128)(2,1)}, bf16[256,1536]{1,0:T(8,128)(2,1)}, u32[]{:S(2)}, u32[]{:S(2)}) collective-permute-start(bf16[256,1536]{1,0:T(8,128)(2,1)} %after.17), channel_id=1, source_target_pairs={{0,1},{1,2},{2,3},{3,0},{4,5},{5,6},{6,7},{7,4},{8,9},{9,10},{10,1... | collective-permute-start | bytes 2359304 | tf_op jit(solution)/shard_map/ppermute | solution.py:43
  131.3 25.8 %all-to-all-start = ((f32[8,392,128]{2,1,0:T(8,128)}), f32[8,392,128]{2,1,0:T(8,128)}, u32[]{:S(2)}, u32[]{:S(2)}) async-start(f32[8,392,128]{2,1,0:T(8,128)} %pad_maximum_fusion.2), calls=%async_computation | async-start | bytes 3211264 | tf_op jit(solution)/shard_map/all_to_all | solution.py:250
  135.8 36.6 %collective-permute-start.6 = (bf16[256,1536]{1,0:T(8,128)(2,1)S(1)}, bf16[256,1536]{1,0:T(8,128)(2,1)S(1)}, u32[]{:S(2)}, u32[]{:S(2)}) collective-permute-start(bf16[256,1536]{1,0:T(8,128)(2,1)S(1)} %copy-done.48), channel_id=1, source_target_pairs={{0,2},{1,3},{2,0},{3,1},{4,6},{5,7},{6,4},{7,5},{8,10},{9,11},{10,... | collective-permute-start | bytes 2359304 | tf_op jit(solution)/shard_map/ppermute | solution.py:43
  173.3 24.9 %all-to-all-start.1 = ((f32[8,384,128]{2,1,0:T(8,128)}), f32[8,384,128]{2,1,0:T(8,128)S(1)}, u32[]{:S(2)}, u32[]{:S(2)}) async-start(f32[8,384,128]{2,1,0:T(8,128)} %after.19), calls=%async_computation.1 | async-start | bytes 3145728 | tf_op jit(solution)/shard_map/all_to_all | solution.py:250
  177.2 178.4 %all-gather.12.cloned.1.call-start = ((), (), s32[]{:S(2)}) async-start(), calls=%async_computation.14 | async-start | bytes 23887872 | tf_op jit(solution)/shard_map/all_gather | solution.py:79
  199.4 525.5 %reduce-scatter.4.cloned.1.call-start = ((), (), s32[]{:S(2)}) async-start(), calls=%async_computation.9 | async-start | bytes 23887872 | tf_op jit(solution)/shard_map/reduce_scatter | solution.py:83
  200.0 19.3 %copy-start.15 = (f32[8,768]{1,0:T(8,128)}, f32[8,768]{1,0:T(8,128)S(1)}, u32[]{:S(2)}) copy-start(f32[8,768]{1,0:T(8,128)S(1)} %pad.47.hp_ref.skip_ref) | copy-start | bytes 73732
  234.1 57.9 %collective-permute-start.9 = (bf16[256,1536]{1,0:T(8,128)(2,1)}, bf16[256,1536]{1,0:T(8,128)(2,1)S(1)}, u32[]{:S(2)}, u32[]{:S(2)}) collective-permute-start(bf16[256,1536]{1,0:T(8,128)(2,1)} %get-tuple-element.248), channel_id=1, source_target_pairs={{0,3},{1,0},{2,1},{3,2},{4,7},{5,4},{6,5},{7,6},{8,11},{9,8},{10,9... | collective-permute-start | bytes 2359304 | tf_op jit(solution)/shard_map/ppermute | solution.py:51
  236.6 65.0 %collective-permute-start.8 = (bf16[256,1536]{1,0:T(8,128)(2,1)}, bf16[256,1536]{1,0:T(8,128)(2,1)S(1)}, u32[]{:S(2)}, u32[]{:S(2)}) collective-permute-start(bf16[256,1536]{1,0:T(8,128)(2,1)} %get-tuple-element.249), channel_id=1, source_target_pairs={{0,2},{1,3},{2,0},{3,1},{4,6},{5,7},{6,4},{7,5},{8,10},{9,11},{10,... | collective-permute-start | bytes 2359304 | tf_op jit(solution)/shard_map/ppermute | solution.py:51
  236.6 65.8 %collective-permute-start.7 = (bf16[256,1536]{1,0:T(8,128)(2,1)}, bf16[256,1536]{1,0:T(8,128)(2,1)}, u32[]{:S(2)}, u32[]{:S(2)}) collective-permute-start(bf16[256,1536]{1,0:T(8,128)(2,1)} %get-tuple-element.247), channel_id=1, source_target_pairs={{0,1},{1,2},{2,3},{3,0},{4,5},{5,6},{6,7},{7,4},{8,9},{9,10},{10,1... | collective-permute-start | bytes 2359304 | tf_op jit(solution)/shard_map/ppermute | solution.py:51
  291.8 13.4 %copy-start.86 = (f32[4,256]{1,0:T(4,128)}, f32[4,256]{1,0:T(4,128)S(1)}, u32[]{:S(2)}) copy-start(f32[4,256]{1,0:T(4,128)S(1)} %psum.14) | copy-start | bytes 12292
  291.8 13.4 %copy-start.90 = (f32[4,256]{1,0:T(4,128)}, f32[4,256]{1,0:T(4,128)S(1)}, u32[]{:S(2)}) copy-start(f32[4,256]{1,0:T(4,128)S(1)} %add_rsqrt_fusion) | copy-start | bytes 12292
  292.0 25.8 %copy-start.96 = (f32[256]{0:T(256)}, f32[256]{0:T(256)S(1)}, u32[]{:S(2)}) copy-start(f32[256]{0:T(256)S(1)} %mul.235) | copy-start | bytes 3076
  305.2 173.0 %copy-start.38 = (f32[256,1536]{1,0:T(8,128)}, f32[256,1536]{1,0:T(8,128)S(1)}, u32[]{:S(2)}) copy-start(f32[256,1536]{1,0:T(8,128)S(1)} %get-tuple-element.240) | copy-start | bytes 4718596
  306.3 11.5 %copy-start.72 = (bf16[128,1536]{1,0:T(8,128)(2,1)}, bf16[128,1536]{1,0:T(8,128)(2,1)S(1)}, u32[]{:S(2)}) copy-start(bf16[128,1536]{1,0:T(8,128)(2,1)S(1)} %get-tuple-element.272) | copy-start | bytes 1179652
  306.3 17.3 %collective-permute-start.10 = (bf16[128,1536]{1,0:T(8,128)(2,1)S(1)}, bf16[128,1536]{1,0:T(8,128)(2,1)S(1)}, u32[]{:S(2)}, u32[]{:S(2)}) collective-permute-start(bf16[128,1536]{1,0:T(8,128)(2,1)S(1)} %get-tuple-element.272), channel_id=1, source_target_pairs={{0,3},{1,0},{2,1},{3,2},{4,7},{5,4},{6,5},{7,6},{8,11},{9,8},{10,9... | collective-permute-start | bytes 1179656 | tf_op jit(solution)/shard_map/ppermute | solution.py:43
  314.0 31.4 %collective-permute-start.11 = (bf16[128,1536]{1,0:T(8,128)(2,1)S(1)}, bf16[128,1536]{1,0:T(8,128)(2,1)S(1)}, u32[]{:S(2)}, u32[]{:S(2)}) collective-permute-start(bf16[128,1536]{1,0:T(8,128)(2,1)S(1)} %get-tuple-element.272), channel_id=1, source_target_pairs={{0,2},{1,3},{2,0},{3,1},{4,6},{5,7},{6,4},{7,5},{8,10},{9,11},{10,... | collective-permute-start | bytes 1179656 | tf_op jit(solution)/shard_map/ppermute | solution.py:43
  314.0 31.4 %collective-permute-start.12 = (bf16[128,1536]{1,0:T(8,128)(2,1)S(1)}, bf16[128,1536]{1,0:T(8,128)(2,1)S(1)}, u32[]{:S(2)}, u32[]{:S(2)}) collective-permute-start(bf16[128,1536]{1,0:T(8,128)(2,1)S(1)} %get-tuple-element.272), channel_id=1, source_target_pairs={{0,1},{1,2},{2,3},{3,0},{4,5},{5,6},{6,7},{7,4},{8,9},{9,10},{10,1... | collective-permute-start | bytes 1179656 | tf_op jit(solution)/shard_map/ppermute | solution.py:43
  323.6 21.8 %copy-start.73 = (bf16[128,1536]{1,0:T(8,128)(2,1)}, bf16[128,1536]{1,0:T(8,128)(2,1)S(1)}, u32[]{:S(2)}) copy-start(bf16[128,1536]{1,0:T(8,128)(2,1)S(1)} %collective-permute-done.10.refs_1_) | copy-start | bytes 1179652
  346.8 53.5 %collective-permute-start.18 = (bf16[128,1536]{1,0:T(8,128)(2,1)}, bf16[128,1536]{1,0:T(8,128)(2,1)}, u32[]{:S(2)}, u32[]{:S(2)}) collective-permute-start(bf16[128,1536]{1,0:T(8,128)(2,1)} %after.21), channel_id=1, source_target_pairs={{0,1},{1,2},{2,3},{3,0},{4,5},{5,6},{6,7},{7,4},{8,9},{9,10},{10,1... | collective-permute-start | bytes 1179656 | tf_op jit(solution)/shard_map/ppermute | solution.py:43
  347.7 52.6 %collective-permute-start.17 = (bf16[128,1536]{1,0:T(8,128)(2,1)}, bf16[128,1536]{1,0:T(8,128)(2,1)}, u32[]{:S(2)}, u32[]{:S(2)}) collective-permute-start(bf16[128,1536]{1,0:T(8,128)(2,1)} %after.21), channel_id=1, source_target_pairs={{0,2},{1,3},{2,0},{3,1},{4,6},{5,7},{6,4},{7,5},{8,10},{9,11},{10,... | collective-permute-start | bytes 1179656 | tf_op jit(solution)/shard_map/ppermute | solution.py:43
  349.7 47.4 %collective-permute-start.16 = (bf16[128,1536]{1,0:T(8,128)(2,1)}, bf16[128,1536]{1,0:T(8,128)(2,1)}, u32[]{:S(2)}, u32[]{:S(2)}) collective-permute-start(bf16[128,1536]{1,0:T(8,128)(2,1)} %after.21), channel_id=1, source_target_pairs={{0,3},{1,0},{2,1},{3,2},{4,7},{5,4},{6,5},{7,6},{8,11},{9,8},{10,9... | collective-permute-start | bytes 1179656 | tf_op jit(solution)/shard_map/ppermute | solution.py:43
  396.5 45.1 %collective-permute-start.13 = (bf16[128,1536]{1,0:T(8,128)(2,1)}, bf16[128,1536]{1,0:T(8,128)(2,1)}, u32[]{:S(2)}, u32[]{:S(2)}) collective-permute-start(bf16[128,1536]{1,0:T(8,128)(2,1)} %get-tuple-element.261), channel_id=1, source_target_pairs={{0,1},{1,2},{2,3},{3,0},{4,5},{5,6},{6,7},{7,4},{8,9},{9,10},{10,1... | collective-permute-start | bytes 1179656 | tf_op jit(solution)/shard_map/ppermute | solution.py:51
  396.5 45.1 %collective-permute-start.14 = (bf16[128,1536]{1,0:T(8,128)(2,1)}, bf16[128,1536]{1,0:T(8,128)(2,1)}, u32[]{:S(2)}, u32[]{:S(2)}) collective-permute-start(bf16[128,1536]{1,0:T(8,128)(2,1)} %get-tuple-element.260), channel_id=1, source_target_pairs={{0,2},{1,3},{2,0},{3,1},{4,6},{5,7},{6,4},{7,5},{8,10},{9,11},{10,... | collective-permute-start | bytes 1179656 | tf_op jit(solution)/shard_map/ppermute | solution.py:51
  397.1 44.6 %collective-permute-start.15 = (bf16[128,1536]{1,0:T(8,128)(2,1)}, bf16[128,1536]{1,0:T(8,128)(2,1)}, u32[]{:S(2)}, u32[]{:S(2)}) collective-permute-start(bf16[128,1536]{1,0:T(8,128)(2,1)} %get-tuple-element.259), channel_id=1, source_target_pairs={{0,3},{1,0},{2,1},{3,2},{4,7},{5,4},{6,5},{7,6},{8,11},{9,8},{10,9... | collective-permute-start | bytes 1179656 | tf_op jit(solution)/shard_map/ppermute | solution.py:51
  443.0 10.2 %collective-permute-start.21 = (bf16[128,1536]{1,0:T(8,128)(2,1)S(1)}, bf16[128,1536]{1,0:T(8,128)(2,1)S(1)}, u32[]{:S(2)}, u32[]{:S(2)}) collective-permute-start(bf16[128,1536]{1,0:T(8,128)(2,1)S(1)} %get-tuple-element.257), channel_id=1, source_target_pairs={{0,3},{1,0},{2,1},{3,2},{4,7},{5,4},{6,5},{7,6},{8,11},{9,8},{10,9... | collective-permute-start | bytes 1179656 | tf_op jit(solution)/shard_map/ppermute | solution.py:51
  443.6 33.4 %collective-permute-start.20 = (bf16[128,1536]{1,0:T(8,128)(2,1)S(1)}, bf16[128,1536]{1,0:T(8,128)(2,1)S(1)}, u32[]{:S(2)}, u32[]{:S(2)}) collective-permute-start(bf16[128,1536]{1,0:T(8,128)(2,1)S(1)} %get-tuple-element.258), channel_id=1, source_target_pairs={{0,2},{1,3},{2,0},{3,1},{4,6},{5,7},{6,4},{7,5},{8,10},{9,11},{10,... | collective-permute-start | bytes 1179656 | tf_op jit(solution)/shard_map/ppermute | solution.py:51
  445.2 31.9 %collective-permute-start.19 = (bf16[128,1536]{1,0:T(8,128)(2,1)S(1)}, bf16[128,1536]{1,0:T(8,128)(2,1)S(1)}, u32[]{:S(2)}, u32[]{:S(2)}) collective-permute-start(bf16[128,1536]{1,0:T(8,128)(2,1)S(1)} %get-tuple-element.256), channel_id=1, source_target_pairs={{0,1},{1,2},{2,3},{3,0},{4,5},{5,6},{6,7},{7,4},{8,9},{9,10},{10,1... | collective-permute-start | bytes 1179656 | tf_op jit(solution)/shard_map/ppermute | solution.py:51
  483.5 39.5 %collective-permute-start.22 = (bf16[256,1536]{1,0:T(8,128)(2,1)S(1)}, bf16[256,1536]{1,0:T(8,128)(2,1)S(1)}, u32[]{:S(2)}, u32[]{:S(2)}) collective-permute-start(bf16[256,1536]{1,0:T(8,128)(2,1)S(1)} %get-tuple-element.238), channel_id=1, source_target_pairs={{0,3},{1,0},{2,1},{3,2},{4,7},{5,4},{6,5},{7,6},{8,11},{9,8},{10,9... | collective-permute-start | bytes 2359304 | tf_op jit(solution)/shard_map/ppermute | solution.py:43
  483.7 69.7 %collective-permute-start.23 = (bf16[256,1536]{1,0:T(8,128)(2,1)S(1)}, bf16[256,1536]{1,0:T(8,128)(2,1)S(1)}, u32[]{:S(2)}, u32[]{:S(2)}) collective-permute-start(bf16[256,1536]{1,0:T(8,128)(2,1)S(1)} %get-tuple-element.238), channel_id=1, source_target_pairs={{0,2},{1,3},{2,0},{3,1},{4,6},{5,7},{6,4},{7,5},{8,10},{9,11},{10,... | collective-permute-start | bytes 2359304 | tf_op jit(solution)/shard_map/ppermute | solution.py:43
  521.1 33.3 %collective-permute-start.24 = (bf16[256,1536]{1,0:T(8,128)(2,1)S(1)}, bf16[256,1536]{1,0:T(8,128)(2,1)S(1)}, u32[]{:S(2)}, u32[]{:S(2)}) collective-permute-start(bf16[256,1536]{1,0:T(8,128)(2,1)S(1)} %get-tuple-element.238), channel_id=1, source_target_pairs={{0,1},{1,2},{2,3},{3,0},{4,5},{5,6},{6,7},{7,4},{8,9},{9,10},{10,1... | collective-permute-start | bytes 2359304 | tf_op jit(solution)/shard_map/ppermute | solution.py:43
  560.4 19.9 %copy-start.87 = (f32[4,256]{1,0:T(4,128)S(1)}, f32[4,256]{1,0:T(4,128)}, u32[]{:S(2)}) copy-start(f32[4,256]{1,0:T(4,128)} %copy-done.86) | copy-start | bytes 12292
  583.9 64.5 %collective-permute-start.30 = (bf16[128,1536]{1,0:T(8,128)(2,1)}, bf16[128,1536]{1,0:T(8,128)(2,1)}, u32[]{:S(2)}, u32[]{:S(2)}) collective-permute-start(bf16[128,1536]{1,0:T(8,128)(2,1)} %get-tuple-element.254), channel_id=1, source_target_pairs={{0,3},{1,0},{2,1},{3,2},{4,7},{5,4},{6,5},{7,6},{8,11},{9,8},{10,9... | collective-permute-start | bytes 1179656 | tf_op jit(solution)/shard_map/ppermute | solution.py:51
  586.0 139.8 %collective-permute-start.29 = (bf16[128,1536]{1,0:T(8,128)(2,1)}, bf16[128,1536]{1,0:T(8,128)(2,1)}, u32[]{:S(2)}, u32[]{:S(2)}) collective-permute-start(bf16[128,1536]{1,0:T(8,128)(2,1)} %get-tuple-element.255), channel_id=1, source_target_pairs={{0,2},{1,3},{2,0},{3,1},{4,6},{5,7},{6,4},{7,5},{8,10},{9,11},{10,... | collective-permute-start | bytes 1179656 | tf_op jit(solution)/shard_map/ppermute | solution.py:51
  587.3 61.8 %collective-permute-start.28 = (bf16[128,1536]{1,0:T(8,128)(2,1)}, bf16[128,1536]{1,0:T(8,128)(2,1)}, u32[]{:S(2)}, u32[]{:S(2)}) collective-permute-start(bf16[128,1536]{1,0:T(8,128)(2,1)} %get-tuple-element.253), channel_id=1, source_target_pairs={{0,1},{1,2},{2,3},{3,0},{4,5},{5,6},{6,7},{7,4},{8,9},{9,10},{10,1... | collective-permute-start | bytes 1179656 | tf_op jit(solution)/shard_map/ppermute | solution.py:51
  589.9 59.2 %collective-permute-start.27 = (bf16[128,1536]{1,0:T(8,128)(2,1)}, bf16[128,1536]{1,0:T(8,128)(2,1)}, u32[]{:S(2)}, u32[]{:S(2)}) collective-permute-start(bf16[128,1536]{1,0:T(8,128)(2,1)} %get-tuple-element.251), channel_id=1, source_target_pairs={{0,3},{1,0},{2,1},{3,2},{4,7},{5,4},{6,5},{7,6},{8,11},{9,8},{10,9... | collective-permute-start | bytes 1179656 | tf_op jit(solution)/shard_map/ppermute | solution.py:51
  593.7 55.4 %collective-permute-start.25 = (bf16[128,1536]{1,0:T(8,128)(2,1)}, bf16[128,1536]{1,0:T(8,128)(2,1)}, u32[]{:S(2)}, u32[]{:S(2)}) collective-permute-start(bf16[128,1536]{1,0:T(8,128)(2,1)} %get-tuple-element.250), channel_id=1, source_target_pairs={{0,1},{1,2},{2,3},{3,0},{4,5},{5,6},{6,7},{7,4},{8,9},{9,10},{10,1... | collective-permute-start | bytes 1179656 | tf_op jit(solution)/shard_map/ppermute | solution.py:51
  604.0 42.8 %all-to-all-start.2 = ((f32[8,384,128]{2,1,0:T(8,128)}), f32[8,384,128]{2,1,0:T(8,128)S(1)}, u32[]{:S(2)}, u32[]{:S(2)}) async-start(f32[8,384,128]{2,1,0:T(8,128)} %bitcast.302), calls=%async_computation.2 | async-start | bytes 3145728 | tf_op jit(solution)/shard_map/all_to_all | solution.py:250
  648.4 79.0 %collective-permute-start.26 = (bf16[128,1536]{1,0:T(8,128)(2,1)}, bf16[128,1536]{1,0:T(8,128)(2,1)}, u32[]{:S(2)}, u32[]{:S(2)}) collective-permute-start(bf16[128,1536]{1,0:T(8,128)(2,1)} %get-tuple-element.252), channel_id=1, source_target_pairs={{0,2},{1,3},{2,0},{3,1},{4,6},{5,7},{6,4},{7,5},{8,10},{9,11},{10,... | collective-permute-start | bytes 1179656 | tf_op jit(solution)/shard_map/ppermute | solution.py:51
  649.1 37.6 %all-to-all-start.3 = ((f32[8,384,128]{2,1,0:T(8,128)}), f32[8,384,128]{2,1,0:T(8,128)S(1)}, u32[]{:S(2)}, u32[]{:S(2)}) async-start(f32[8,384,128]{2,1,0:T(8,128)} %after.26), calls=%async_computation.3 | async-start | bytes 3145728 | tf_op jit(solution)/shard_map/all_to_all | solution.py:250
  652.8 140.3 %reduce-scatter.6.cloned.1.call-start = ((), (), s32[]{:S(2)}) async-start(), calls=%async_computation.10 | async-start | bytes 5308416 | tf_op jit(solution)/shard_map/reduce_scatter | solution.py:83
  735.9 3.1 collective-permute-start.31
  758.1 22.2 %collective-permute-start.32 = (bf16[256,1536]{1,0:T(8,128)(2,1)}, bf16[256,1536]{1,0:T(8,128)(2,1)S(1)}, u32[]{:S(2)}, u32[]{:S(2)}) collective-permute-start(bf16[256,1536]{1,0:T(8,128)(2,1)} %get-tuple-element.245), channel_id=1, source_target_pairs={{0,1},{1,2},{2,3},{3,0},{4,5},{5,6},{6,7},{7,4},{8,9},{9,10},{10,1... | collective-permute-start | bytes 2359304 | tf_op jit(solution)/shard_map/ppermute | solution.py:51
  781.2 28.8 %all-to-all-start.4 = ((f32[8,4,120,128]{3,2,1,0:T(8,128)}), f32[8,4,120,128]{3,2,1,0:T(8,128)S(1)}, u32[]{:S(2)}, u32[]{:S(2)}) async-start(f32[8,4,120,128]{3,2,1,0:T(8,128)} %after.28), calls=%async_computation.4 | async-start | bytes 3932160 | tf_op jit(solution)/shard_map/all_to_all | solution.py:1066
  784.8 89.7 %reduce-scatter.8.cloned.1.call-start = ((), (), s32[]{:S(2)}) async-start(), calls=%async_computation.11 | async-start | bytes 3096576 | tf_op jit(solution)/shard_map/reduce_scatter | solution.py:83
  785.0 37.1 %collective-permute-start.33 = (bf16[256,1536]{1,0:T(8,128)(2,1)}, bf16[256,1536]{1,0:T(8,128)(2,1)}, u32[]{:S(2)}, u32[]{:S(2)}) collective-permute-start(bf16[256,1536]{1,0:T(8,128)(2,1)} %get-tuple-element.243), channel_id=1, source_target_pairs={{0,2},{1,3},{2,0},{3,1},{4,6},{5,7},{6,4},{7,5},{8,10},{9,11},{10,... | collective-permute-start | bytes 2359304 | tf_op jit(solution)/shard_map/ppermute | solution.py:51
  793.2 32.5 %copy-start.105 = (s32[4]{0:T(128)S(1)}, s32[4]{0:T(128)}, u32[]{:S(2)}) copy-start(s32[4]{0:T(128)} %param.25) | copy-start | bytes 52
  810.7 29.4 %copy-start.46 = (bf16[1,27,192,256]{3,2,1,0:T(8,128)(2,1)S(1)}, bf16[1,27,192,256]{3,2,1,0:T(8,128)(2,1)}, u32[]{:S(2)}) copy-start(bf16[1,27,192,256]{3,2,1,0:T(8,128)(2,1)} %reduce-scatter.4.cloned.1.call-done) | copy-start | bytes 7962628
  822.1 12.8 %all-to-all-start.5 = ((f32[4,120,128]{2,1,0:T(8,128)}), f32[4,120,128]{2,1,0:T(8,128)S(1)}, u32[]{:S(2)}, u32[]{:S(2)}) async-start(f32[4,120,128]{2,1,0:T(8,128)} %after.29.refs_1_), calls=%async_computation.6 | async-start | bytes 491520 | tf_op jit(solution)/shard_map/all_to_all | solution.py:1069
  829.6 34.3 %collective-permute-start.34 = (bf16[256,1536]{1,0:T(8,128)(2,1)}, bf16[256,1536]{1,0:T(8,128)(2,1)}, u32[]{:S(2)}, u32[]{:S(2)}) collective-permute-start(bf16[256,1536]{1,0:T(8,128)(2,1)} %get-tuple-element.244), channel_id=1, source_target_pairs={{0,3},{1,0},{2,1},{3,2},{4,7},{5,4},{6,5},{7,6},{8,11},{9,8},{10,9... | collective-permute-start | bytes 2359304 | tf_op jit(solution)/shard_map/ppermute | solution.py:51
  848.4 11.3 %copy-start.41 = (f32[8,192,256]{1,2,0:T(8,128)}, f32[8,192,256]{1,2,0:T(8,128)S(1)}, u32[]{:S(2)}) copy-start(f32[8,192,256]{1,2,0:T(8,128)S(1)} %slice.470) | copy-start | bytes 4718596
  (94 other events, 358.9 us)
Sparse Core Ops, SparseCore 0:
  11.5 36.7 all-gather.7
  50.1 40.5 all-gather.9
  199.5 107.1 all-gather.11
  555.5 169.3 reduce-scatter.3
  728.2 53.8 reduce-scatter.5
  793.3 44.5 reduce-scatter.7

commit v5 on v4

--- a/solution.py
+++ b/solution.py
@@ -259,7 +259,7 @@
     per_row = jnp.pad(per_row, ((0, 0), (0, lines * LANES - share))).reshape(count, lines, LANES)
     got = exchanged(jnp.concatenate([s_local.reshape(count, share, STATE_DIM), per_row], axis=1))
     decay = got[:, share:].reshape(count, lines * LANES)[:, :share, None]
-    entering = exchanged(after(scan_pieces(got[:, :share], decay, False), beside))
+    entering = exchanged(after(scan_pieces(got[:, :share], decay, False), *beside))
     return entering.reshape(slots, inner, STATE_DIM), decay
 
 
@@ -873,7 +873,7 @@
         yi = mixer_inner(xs, rw, dl)
         z.append(in_slots(dot(n_one[c], full_z, NN)))
         s_local = after(s_local, g_blocks[c][1], g_blocks[c][3])
-        h_in, decay = states_forward(g_blocks[c][2], s_local, dl[:, piece_rows - 1, LANES : LANES + heads])
+        h_in, decay = states_forward((g_blocks[c][2], yi, z[c]), s_local, dl[:, piece_rows - 1, LANES : LANES + heads])
         if c == 0:
             full_expert = weight_gather(after(expert_shard, h_in))
         y, gg, squares = mixer_leave(yi, xs, rw, dl, h_in, z[c], skip, gain_row)
@@ -956,16 +956,6 @@
         moe_blocks.append(line_parts(lambda k: held[k]))
     sooner = [block for blocks in moe_blocks for block in blocks[1::2]]
     later = [block for blocks in moe_blocks for block in blocks[2::2]]
-    moe = [summed(blocks) for blocks in moe_blocks]
-    moe_own = jnp.concatenate(moe, axis=0)
-    output = [resid_own + moe_own]
-    stat_terms = jnp.stack(
-        [
-            jnp.sum(valid_c[0] * output[0] * output[0]),
-            jnp.sum(valid_c[0] * mixed_own * mixed_own),
-            jnp.sum(valid_c[0] * moe_own * moe_own),
-        ]
-    )
     router_grad = sum(dot(n_two[m], logit_grads[m], TN)[:, :EXPERTS] for m in halves)
 
     def rows_of(values):
@@ -1012,10 +1002,22 @@
         n_parts.append(n_grad.astype(bf16))
         received = line_parts(by_distance(n_parts[c].reshape(zs, tokens, D_MODEL)))
         arrived.append(received)
+    for blocks in moe_blocks:
+        blocks[1] = after(blocks[1], n_parts[0])
+    moe = [summed(blocks) for blocks in moe_blocks]
+    moe_own = jnp.concatenate(moe, axis=0)
+    output = [resid_own + moe_own]
+    stat_terms = jnp.stack(
+        [
+            jnp.sum(valid_c[0] * output[0] * output[0]),
+            jnp.sum(valid_c[0] * mixed_own * mixed_own),
+            jnp.sum(valid_c[0] * moe_own * moe_own),
+        ]
+    )
     enter_w_grad = dot(n_rows, rows_of(v_grads), TN).astype(bf16)
     bc_w_grad = dot(n_rows, rows_of(bc_grads), TN)
     bc_w_grad = bc_w_grad[:, : 2 * STATE_DIM] + bc_w_grad[:, 2 * STATE_DIM :]
-    side_grad = weight_scatter(after(side_products, expert_grad, conv_grad))
+    side_grad = weight_scatter(after(side_products, expert_grad, *n_parts))
 
     def mixer_scatter(grads):
         return weight_scatter(after(grads.reshape(pieces, shard, -1), side_grad)).astype(f32)
@@ -1062,9 +1064,9 @@
     tile = tile.at[:3, :heads].set(head_grad[:3, :heads]).at[3, :3].set(stat_terms)
     tile = jnp.broadcast_to(tile, (pieces, zs) + tile.shape)
     shares = jnp.concatenate([wide_share, shares.reshape(pieces, zs, -1, LANES), tile], axis=2)
-    shares = after(shares, arrived[CHUNKS - 1][1])
+    shares = after(shares, arrived[0][1], arrived[0][2], *expert_outs)
     shares = jnp.sum(lax.all_to_all(shares, "dp", 0, 0), axis=0)
-    first_sum = after(shares, arrived[0][2])
+    first_sum = after(shares, arrived[0][3])
     shares = first_sum
     got = lax.all_to_all(shares, "tensor", 0, 0)
     tiles = got[:, -8:]
@@ -1072,8 +1074,6 @@
     u_grad = []
     for c in chunk_ids:
         received = arrived[c]
-        if c == CHUNKS - 1:
-            received[3] = after(received[3], first_sum, *expert_outs)
         u_grad.append(resid_grad[c] + norm_back(u[c], gain_one, summed(received))[0])
     bc_lines = wide_share.shape[2]
     bc_grad = shares[:bc_lines].reshape(-1, 2 * STATE_DIM)

time: 897 us -> 865 us (0.964)
  waiting for transfers between devices: 265 us -> 239 us
  local copies, waits for them, and re-layouts: 122 us -> 113 us
    reduce_scatter x3, waiting for transfers between devices: 9.78 us -> 0.01 us  [weight_scatter(): lax.psum_scatter(grads.astype(bf16), 'dp', scatter_dimension=0, tiled=False)]
    unnamed x234 -> x224, local copies, waits for them, and re-layouts: 40.1 us -> 32.1 us
  transfers between devices with their start and end apart: 47 -> 47, of which waited for: 20 -> 17; matrix products, arithmetic and copies ran while one was open for 22% -> 23% of each run, Pallas kernels for 23% -> 25%
where the time goes in v5:
time: 865 us; the launch traced here: 853 us
  waiting for transfers between devices  239 us (28%)
  Pallas kernels  209 us (24%)
  local copies, waits for them, and re-layouts  113 us (13%)
  starting transfers between devices  80.7 us (9%)
  blocking collectives  68.5 us (8%)
  matrix products  62.9 us (7%)
  other arithmetic  62.8 us (7%)
  between operations  16.8 us (2%)
    ppermute x15, waiting for transfers between devices, line_gather(): lax.ppermute(row_major(value), 'tensor', [(a, (a - step) % size) for a in...  122 us
    pallas_call x2, Pallas kernels, experts(): pl.pallas_call(expert_kernel, grid=(pairs,), in_specs=[pl.BlockSpec((toke...  77.2 us
    dot_general x12, matrix products, dot(): lax.dot_general(a, b, (dims, ((), ())), precision=precision, preferred_el...  62.9 us
    ppermute x18, waiting for transfers between devices, line_parts(): lax.ppermute(row_major(block_of(step)), 'tensor', [(a, (a + step) % size)...  58.9 us
    psum x1, blocking collectives, body(): square_sum = lax.psum(squares[:, :, 0], 'tensor')  51.2 us
    all_to_all x4, waiting for transfers between devices, exchanged(): return lax.all_to_all(rows, 'dp', 0, 0, tiled=False)  48.5 us
    pallas_call x2, Pallas kernels, expert_grads(): pl.pallas_call(skipping(functools.partial(expert_grad_kernel, ups, chunks...  48.1 us
    unnamed x224, local copies, waits for them, and re-layouts  32.1 us
  transfers between devices with their start and end apart: 47, of which 17 were waited for; matrix products, arithmetic and copies ran while one was open for 23% of the time, Pallas kernels for 25%

profile of v5, /device:TPU:0, one launch (start us, length us, event | category | flops | bytes accessed | tf_op | source)
XLA Modules:
  0.0 852.9 jit_solution(6224908998498080384)
XLA Ops:
  11.6 5.1 collective-permute-start
  19.0 8.9 %all-gather.3 = f32[8,192,2]{1,2,0:T(2,128)S(1)} all-gather(f32[1,192,2]{1,2,0:T(2,128)S(1)} %fusion.57), channel_id=1, replica_groups=mesh['dp'=8,'tensor'=4] {'dp'}, dimensions={0}, use_global_device_ids=true | all-gather | bytes 13824 | tf_op jit(solution)/shard_map/all_gather | solution.py:830
  36.0 48.0 %collective-permute-done.1 = bf16[256,1536]{1,0:T(8,128)(2,1)S(1)} collective-permute-done((bf16[256,1536]{1,0:T(8,128)(2,1)S(1)}, bf16[256,1536]{1,0:T(8,128)(2,1)S(1)}, u32[]{:S(2)}, u32[]{:S(2)}) %collective-permute-start.1) | collective-permute-done | bytes 786464 | tf_op jit(solution)/shard_map/ppermute | solution.py:43
  92.1 9.5 %fusion.1.v_ref = f32[4,4,64,1152]{3,2,1,0:T(8,128)} fusion(bf16[4,4,64,1536]{3,2,1,0:T(8,128)(2,1)} %bitcast.330, bf16[1536,1152]{1,0:T(8,128)(2,1)} %all-gather.8.cloned.1.call-done), kind=kOutput, calls=%fused_computation.9 | convolution fusion | flops 3623878656 | bytes 11403264 | tf_op jit(solution)/shard_map/dot_general | solution.py:98
  101.6 11.3 %mixer_enter.1 = (f32[4,256,768]{2,1,0:T(8,128)}, f32[4,256,256]{2,1,0:T(8,128)S(1)}, f32[4,256,256]{2,1,0:T(8,128)S(1)}, f32[4,768,128]{2,1,0:T(8,128)S(1)}) custom-call(f32[4,4,64,1152]{3,2,1,0:T(8,128)} %fusion.1.v_ref, f32[4,8,1024]{2,1,0:T(8,128)S(1)} %pad.42.halo_ref, f32[8,1024]{1,0:T(8,128)S(1)} %select_maximum_fusion.cw_ref, f32[8,128]{1,0:T(8,128)S(1)} %pad.44.hp_ref), custom_call_target="tpu_custom_call" | custom-call | flops 13516800000 | bytes 1024 | tf_op jit(solution)/shard_map/mixer_enter/pallas_call | solution.py:203
  114.3 12.0 %collective-permute-done.5.refs_2_ = bf16[256,1536]{1,0:T(8,128)(2,1)} collective-permute-done((bf16[256,1536]{1,0:T(8,128)(2,1)}, bf16[256,1536]{1,0:T(8,128)(2,1)}, u32[]{:S(2)}, u32[]{:S(2)}) %collective-permute-start.5) | collective-permute-done | bytes 786464 | tf_op jit(solution)/shard_map/ppermute | solution.py:43
  126.4 2.7 pad_maximum_fusion.2
  129.1 4.7 all-to-all-start
  135.8 4.6 mixer_inner.1.refs_2_.yi_ref
  142.0 13.1 %all-to-all-done = f32[8,392,128]{2,1,0:T(8,128)} async-done(((f32[8,392,128]{2,1,0:T(8,128)}), f32[8,392,128]{2,1,0:T(8,128)}, u32[]{:S(2)}, u32[]{:S(2)}) %all-to-all-start) | async-done | bytes 1605664 | tf_op jit(solution)/shard_map/all_to_all | solution.py:250
  159.6 6.9 fusion.16
  166.4 3.1 collective-permute-done.6.refs_1_
  169.5 3.9 all-to-all-start.1
  180.5 3.8 reshape.439
  184.3 3.0 pad_maximum_fusion.refs_0_
  187.3 7.1 all-to-all-done.1
  202.2 8.2 mixer_leave.1
  210.3 5.1 convolution_convert_fusion
  217.8 2.7 collective-permute-start.9
  223.4 51.2 %psum.14 = f32[4,256]{1,0:T(4,128)S(1)} all-reduce(f32[4,256]{1,0:T(4,128)S(1)} %slice_reduce_fusion), channel_id=1, replica_groups=mesh['dp'=8,'tensor'=4] {'tensor'}, use_global_device_ids=true, to_apply=%region_1.2 | all-reduce | flops 1024 | bytes 8192 | tf_op jit(solution)/shard_map/psum | solution.py:882
  274.8 9.7 %collective-permute-done.8 = bf16[256,1536]{1,0:T(8,128)(2,1)S(1)} collective-permute-done((bf16[256,1536]{1,0:T(8,128)(2,1)}, bf16[256,1536]{1,0:T(8,128)(2,1)S(1)}, u32[]{:S(2)}, u32[]{:S(2)}) %collective-permute-start.8) | collective-permute-done | bytes 786464 | tf_op jit(solution)/shard_map/ppermute | solution.py:51
  285.5 3.0 multiply_reduce_fusion.4
  289.6 7.3 collective-permute-start.10
  301.2 5.2 collective-permute-done.10.refs_1_
  306.4 21.7 %collective-permute-done.11.refs_2_ = bf16[128,1536]{1,0:T(8,128)(2,1)S(1)} collective-permute-done((bf16[128,1536]{1,0:T(8,128)(2,1)S(1)}, bf16[128,1536]{1,0:T(8,128)(2,1)S(1)}, u32[]{:S(2)}, u32[]{:S(2)}) %collective-permute-start.11) | collective-permute-done | bytes 393248 | tf_op jit(solution)/shard_map/ppermute | solution.py:43
  332.5 3.3 collective-permute-start.16
  335.8 2.6 pad_maximum_fusion.3.n_ref.refs_0_
  338.5 38.6 %experts.2 = (bf16[512,1536]{1,0:T(8,128)(2,1)}, bf16[512,1536]{1,0:T(8,128)(2,1)}, bf16[512,128]{1,0:T(8,128)(2,1)}, bf16[9,512,256]{2,1,0:T(8,128)(2,1)}, bf16[9,512,512]{2,1,0:T(8,128)(2,1)}) custom-call(bf16[512,1536]{1,0:T(8,128)(2,1)} %pad_maximum_fusion.3.n_ref.refs_0_, bf16[512,1536]{1,0:T(8,128)(2,1)} %get-tuple-element.300.g_ref.refs_2_, ...), custom_call_target="tpu_custom_call" | custom-call | flops 40550400000 | bytes 1024 | tf_op jit(solution)/shard_map/experts/pallas_call | solution.py:661
  379.9 3.2 collective-permute-start.15
  385.8 38.6 %experts.3 = (bf16[512,1536]{1,0:T(8,128)(2,1)}, bf16[512,1536]{1,0:T(8,128)(2,1)}, bf16[512,128]{1,0:T(8,128)(2,1)}, bf16[9,512,256]{2,1,0:T(8,128)(2,1)}, bf16[9,512,512]{2,1,0:T(8,128)(2,1)}) custom-call(bf16[512,1536]{1,0:T(8,128)(2,1)} %pad_maximum_fusion.5.n_ref.refs_1_, bf16[512,1536]{1,0:T(8,128)(2,1)} %get-tuple-element.301.g_ref.refs_3_, ...), custom_call_target="tpu_custom_call" | custom-call | flops 40550400000 | bytes 1024 | tf_op jit(solution)/shard_map/experts/pallas_call | solution.py:661
  431.4 4.6 collective-permute-done.21
  436.0 23.8 %collective-permute-done.20 = bf16[128,1536]{1,0:T(8,128)(2,1)S(1)} collective-permute-done((bf16[128,1536]{1,0:T(8,128)(2,1)S(1)}, bf16[128,1536]{1,0:T(8,128)(2,1)S(1)}, u32[]{:S(2)}, u32[]{:S(2)}) %collective-permute-start.20) | collective-permute-done | bytes 393248 | tf_op jit(solution)/shard_map/ppermute | solution.py:51
  467.4 35.9 %expert_grads.2.refs_0_ = bf16[8,27,192,256]{3,2,1,0:T(8,128)(2,1)} custom-call(bf16[512,1536]{1,0:T(8,128)(2,1)S(1)} %copy-done.8, bf16[512,1536]{1,0:T(8,128)(2,1)S(1)} %copy-done.4, bf16[512,1536]{1,0:T(8,128)(2,1)S(1)} %copy-done.14, bf16[512,1536]{1,0:T(8,128)(2,1)} %get-tuple-element.301.g_ref.refs_3_, bf16[9,512,512]{2,1,0:T(8,128)(2,1)} %get-tuple-element.96.refs_4_, ...), custom_call_target="tpu_custom_call" | custom-call | flops 40550400000 | bytes 1024 | tf_op jit(solution)/shard_map/expert_grads/pallas_call | solution.py:750
  506.2 29.4 %collective-permute-done.23 = bf16[256,1536]{1,0:T(8,128)(2,1)S(1)} collective-permute-done((bf16[256,1536]{1,0:T(8,128)(2,1)S(1)}, bf16[256,1536]{1,0:T(8,128)(2,1)S(1)}, u32[]{:S(2)}, u32[]{:S(2)}) %collective-permute-start.23) | collective-permute-done | bytes 786464 | tf_op jit(solution)/shard_map/ppermute | solution.py:43
  538.4 9.7 %fusion.5 = (f32[4,4,64]{2,1,0:T(4,128)S(1)}, f32[4,4,64,768]{3,2,1,0:T(8,128)}) fusion(f32[4,4,64,768]{3,2,1,0:T(8,128)} %bitcast.375, f32[4,4,64,768]{3,2,1,0:T(8,128)} %bitcast.335, f32[768]{0:T(1024)S(1)} %copy-done.96, bf16[4,4,64,1536]{3,2,1,0:T(8,128)(2,1)} %bitcast.59, bf16[1536,1664]{1,0:T(8,128)(2,1)} %all-gather.10.cloned.1.call-done), kind=kOutput, calls=%fused_computation.15 | convolution fusion | flops 2422209536 | bytes 14949376 | tf_op jit(solution)/shard_map/dot_general | solution.py:98
  548.1 8.3 psum.15
  563.6 8.6 %mixer_unmix.1 = (f32[4,256,768]{2,1,0:T(8,128)}, bf16[4,4,64,768]{3,2,1,0:T(8,128)(2,1)S(1)}, f32[4,768,128]{2,1,0:T(8,128)S(1)}, f32[8,768]{1,0:T(8,128)S(1)}) custom-call(f32[4,4,64,768]{3,2,1,0:T(8,128)} %get-tuple-element.298.gn_ref, f32[4,256,768]{2,1,0:T(8,128)} %get-tuple-element.80.y_ref, f32[4,4,64,768]{3,2,1,0:T(8,128)} %bitcast.336, ...), custom_call_target="tpu_custom_call" | custom-call | flops 10137600000 | bytes 1024 | tf_op jit(solution)/shard_map/mixer_unmix/pallas_call | solution.py:385
  574.6 5.5 all-to-all-start.2
  586.4 23.1 %mixer_pairs.1 = (f32[4,256,768]{2,1,0:T(8,128)}, f32[4,256,256]{2,1,0:T(8,128)S(1)}, f32[4,256,256]{2,1,0:T(8,128)S(1)}) custom-call(f32[4,256,768]{2,1,0:T(8,128)} %get-tuple-element.71.xs_ref.refs_0_, f32[4,256,256]{2,1,0:T(8,128)S(1)} %copy-done.31, f32[4,256,256]{2,1,0:T(8,128)S(1)} %copy-done.22, f32[4,256,768]{2,1,0:T(8,128)} %get-tuple-element.82.refs_3_.gy_ref), custom_call_target="tpu_custom_call" | custom-call | flops 47308800000 | bytes 1024 | tf_op jit(solution)/shard_map/mixer_pairs/pallas_call | solution.py:454
  611.5 6.8 all-to-all-done.2.got_ref
  621.3 4.3 all-to-all-start.3
  625.9 4.3 fusion.refs_0_
  630.2 12.2 %expert_grads.3.refs_0_ = bf16[8,6,192,256]{3,2,1,0:T(8,128)(2,1)} custom-call(bf16[1024,1536]{1,0:T(8,128)(2,1)} %fusion.refs_0_, bf16[1024,1536]{1,0:T(8,128)(2,1)} %copy-done.50, bf16[1,1024,768]{2,1,0:T(8,128)(2,1)S(1)} %bitcast.304, bf16[1,1024,768]{2,1,0:T(8,128)(2,1)S(1)} %bitcast.305), custom_call_target="tpu_custom_call" | custom-call | flops 9011200000 | bytes 1024 | tf_op jit(solution)/shard_map/expert_grads/pallas_call | solution.py:750
  642.3 21.5 %all-to-all-done.3 = f32[8,384,128]{2,1,0:T(8,128)} async-done(((f32[8,384,128]{2,1,0:T(8,128)}), f32[8,384,128]{2,1,0:T(8,128)}, u32[]{:S(2)}, u32[]{:S(2)}) %all-to-all-start.3) | async-done | bytes 1572896 | tf_op jit(solution)/shard_map/all_to_all | solution.py:250
  663.8 27.2 %mixer_back.1 = (bf16[4,4,64,896]{3,2,1,0:T(8,128)(2,1)}, f32[4,4,64,256]{3,2,1,0:T(8,128)}, f32[4,8,1024]{2,1,0:T(8,128)}, f32[8,1024]{1,0:T(8,128)}, f32[8,128]{1,0:T(8,128)}) custom-call(f32[4,4,64,1152]{3,2,1,0:T(8,128)} %fusion.1.v_ref, f32[4,8,1024]{2,1,0:T(8,128)} %copy-done.15, f32[8,1024]{1,0:T(8,128)} %copy-done.16, f32[8,128]{1,0:T(8,128)} %copy-done.18, ...), custom_call_target="tpu_custom_call" | custom-call | flops 20275200000 | bytes 1024 | tf_op jit(solution)/shard_map/mixer_back/pallas_call | solution.py:558
  693.6 6.4 fusion.14
  705.9 5.1 fusion.6
  711.0 5.9 multiply_reduce_fusion
  721.9 3.2 dynamic-slice_bitcast_fusion.2
  730.3 3.9 fusion.76
  737.9 3.9 fusion.21
  746.6 6.5 convolution_convert_fusion.1
  753.1 3.7 copy.300
  756.8 4.3 slice.469
  762.6 3.8 convert_element_type.269
  766.4 6.0 copy.302.refs_3_
  775.6 4.7 collective-permute-done.33.refs_2_
  780.3 4.6 all-to-all-start.4
  786.3 2.7 copy.341
  789.0 16.1 %collective-permute-done.34.refs_1_ = bf16[256,1536]{1,0:T(8,128)(2,1)} collective-permute-done((bf16[256,1536]{1,0:T(8,128)(2,1)}, bf16[256,1536]{1,0:T(8,128)(2,1)}, u32[]{:S(2)}, u32[]{:S(2)}) %collective-permute-start.34) | collective-permute-done | bytes 786464 | tf_op jit(solution)/shard_map/ppermute | solution.py:51
  807.5 10.1 %all-to-all-done.4 = f32[8,4,120,128]{3,2,1,0:T(8,128)} async-done(((f32[8,4,120,128]{3,2,1,0:T(8,128)}), f32[8,4,120,128]{3,2,1,0:T(8,128)}, u32[]{:S(2)}, u32[]{:S(2)}) %all-to-all-start.4) | async-done | bytes 1966112 | tf_op jit(solution)/shard_map/all_to_all | solution.py:1068
  819.9 4.2 all-to-all-start.5
  824.2 3.2 fusion.20
  828.8 2.9 copy.310
  (486 shorter events, 161.9 us)
Async XLA Ops:
  7.2 173.0 %copy-start = (bf16[192,2,256]{2,1,0:T(2,128)(2,1)S(1)}, bf16[192,2,256]{2,1,0:T(2,128)(2,1)}, u32[]{:S(2)}) copy-start(bf16[192,2,256]{2,1,0:T(2,128)(2,1)} %param.40) | copy-start | bytes 589828
  7.2 82.4 %all-gather.8.cloned.1.call-start = ((), (), s32[]{:S(2)}) async-start(), calls=%async_computation.12 | async-start | bytes 3981312 | tf_op jit(solution)/shard_map/all_gather | solution.py:79
  11.4 148.2 %all-gather.10.cloned.1.call-start = ((), (), s32[]{:S(2)}) async-start(), calls=%async_computation.13 | async-start | bytes 5750784 | tf_op jit(solution)/shard_map/all_gather | solution.py:79
  11.6 20.9 %copy-start.40 = (bf16[4,64,1536]{2,1,0:T(8,128)(2,1)}, bf16[4,64,1536]{2,1,0:T(8,128)(2,1)S(1)}, u32[]{:S(2)}) copy-start(bf16[4,64,1536]{2,1,0:T(8,128)(2,1)S(1)} %copy.272) | copy-start | bytes 2359300
  11.6 23.1 %collective-permute-start = (bf16[256,1536]{1,0:T(8,128)(2,1)S(1)}, bf16[256,1536]{1,0:T(8,128)(2,1)}, u32[]{:S(2)}, u32[]{:S(2)}) collective-permute-start(bf16[256,1536]{1,0:T(8,128)(2,1)S(1)} %bitcast.310), channel_id=1, source_target_pairs={{0,3},{1,0},{2,1},{3,2},{4,7},{5,4},{6,5},{7,6},{8,11},{9,8},{10,9... | collective-permute-start | bytes 2359304 | tf_op jit(solution)/shard_map/ppermute | solution.py:43
  16.7 67.3 %collective-permute-start.1 = (bf16[256,1536]{1,0:T(8,128)(2,1)S(1)}, bf16[256,1536]{1,0:T(8,128)(2,1)S(1)}, u32[]{:S(2)}, u32[]{:S(2)}) collective-permute-start(bf16[256,1536]{1,0:T(8,128)(2,1)S(1)} %bitcast.311), channel_id=1, source_target_pairs={{0,2},{1,3},{2,0},{3,1},{4,6},{5,7},{6,4},{7,5},{8,10},{9,11},{10,... | collective-permute-start | bytes 2359304 | tf_op jit(solution)/shard_map/ppermute | solution.py:43
  16.7 67.3 %collective-permute-start.2 = (bf16[256,1536]{1,0:T(8,128)(2,1)S(1)}, bf16[256,1536]{1,0:T(8,128)(2,1)S(1)}, u32[]{:S(2)}, u32[]{:S(2)}) collective-permute-start(bf16[256,1536]{1,0:T(8,128)(2,1)S(1)} %bitcast.312), channel_id=1, source_target_pairs={{0,1},{1,2},{2,3},{3,0},{4,5},{5,6},{6,7},{7,4},{8,9},{9,10},{10,1... | collective-permute-start | bytes 2359304 | tf_op jit(solution)/shard_map/ppermute | solution.py:43
  32.2 52.6 %copy-start.74 = (f32[1536]{0:T(1024)}, f32[1536]{0:T(1024)S(1)}, u32[]{:S(2)}) copy-start(f32[1536]{0:T(1024)S(1)} %get-tuple-element.233) | copy-start | bytes 18436
  85.9 3.8 collective-permute-start.3
  87.5 14.1 %copy-start.16 = (f32[8,1024]{1,0:T(8,128)}, f32[8,1024]{1,0:T(8,128)S(1)}, u32[]{:S(2)}) copy-start(f32[8,1024]{1,0:T(8,128)S(1)} %select_maximum_fusion.cw_ref) | copy-start | bytes 98308
  87.5 14.1 %copy-start.18 = (f32[8,128]{1,0:T(8,128)}, f32[8,128]{1,0:T(8,128)S(1)}, u32[]{:S(2)}) copy-start(f32[8,128]{1,0:T(8,128)S(1)} %pad.44.hp_ref) | copy-start | bytes 12292
  87.5 26.8 %collective-permute-start.4 = (bf16[256,1536]{1,0:T(8,128)(2,1)}, bf16[256,1536]{1,0:T(8,128)(2,1)S(1)}, u32[]{:S(2)}, u32[]{:S(2)}) collective-permute-start(bf16[256,1536]{1,0:T(8,128)(2,1)} %after.18), channel_id=1, source_target_pairs={{0,3},{1,0},{2,1},{3,2},{4,7},{5,4},{6,5},{7,6},{8,11},{9,8},{10,9... | collective-permute-start | bytes 2359304 | tf_op jit(solution)/shard_map/ppermute | solution.py:43
  87.6 38.8 %collective-permute-start.5 = (bf16[256,1536]{1,0:T(8,128)(2,1)}, bf16[256,1536]{1,0:T(8,128)(2,1)}, u32[]{:S(2)}, u32[]{:S(2)}) collective-permute-start(bf16[256,1536]{1,0:T(8,128)(2,1)} %after.18), channel_id=1, source_target_pairs={{0,1},{1,2},{2,3},{3,0},{4,5},{5,6},{6,7},{7,4},{8,9},{9,10},{10,1... | collective-permute-start | bytes 2359304 | tf_op jit(solution)/shard_map/ppermute | solution.py:43
  114.0 19.8 %copy-start.19 = (f32[4,256,256]{2,1,0:T(8,128)}, f32[4,256,256]{2,1,0:T(8,128)S(1)}, u32[]{:S(2)}) copy-start(f32[4,256,256]{2,1,0:T(8,128)S(1)} %get-tuple-element.73.dl_ref.refs_2_) | copy-start | bytes 3145732
  114.0 19.8 %copy-start.28 = (f32[4,256,256]{2,1,0:T(8,128)}, f32[4,256,256]{2,1,0:T(8,128)S(1)}, u32[]{:S(2)}) copy-start(f32[4,256,256]{2,1,0:T(8,128)S(1)} %get-tuple-element.72.rw_ref.refs_1_) | copy-start | bytes 3145732
  129.1 26.1 %all-to-all-start = ((f32[8,392,128]{2,1,0:T(8,128)}), f32[8,392,128]{2,1,0:T(8,128)}, u32[]{:S(2)}, u32[]{:S(2)}) async-start(f32[8,392,128]{2,1,0:T(8,128)} %pad_maximum_fusion.2), calls=%async_computation | async-start | bytes 3211264 | tf_op jit(solution)/shard_map/all_to_all | solution.py:250
  133.8 35.7 %collective-permute-start.6 = (bf16[256,1536]{1,0:T(8,128)(2,1)S(1)}, bf16[256,1536]{1,0:T(8,128)(2,1)}, u32[]{:S(2)}, u32[]{:S(2)}) collective-permute-start(bf16[256,1536]{1,0:T(8,128)(2,1)S(1)} %copy-done.47), channel_id=1, source_target_pairs={{0,2},{1,3},{2,0},{3,1},{4,6},{5,7},{6,4},{7,5},{8,10},{9,11},{10,... | collective-permute-start | bytes 2359304 | tf_op jit(solution)/shard_map/ppermute | solution.py:43
  169.5 24.9 %all-to-all-start.1 = ((f32[8,384,128]{2,1,0:T(8,128)}), f32[8,384,128]{2,1,0:T(8,128)S(1)}, u32[]{:S(2)}, u32[]{:S(2)}) async-start(f32[8,384,128]{2,1,0:T(8,128)} %after.20), calls=%async_computation.1 | async-start | bytes 3145728 | tf_op jit(solution)/shard_map/all_to_all | solution.py:250
  173.4 165.1 %all-gather.12.cloned.1.call-start = ((), (), s32[]{:S(2)}) async-start(), calls=%async_computation.14 | async-start | bytes 23887872 | tf_op jit(solution)/shard_map/all_gather | solution.py:79
  195.6 521.3 %reduce-scatter.4.cloned.1.call-start = ((), (), s32[]{:S(2)}) async-start(), calls=%async_computation.9 | async-start | bytes 23887872 | tf_op jit(solution)/shard_map/reduce_scatter | solution.py:83
  217.8 57.0 %collective-permute-start.9 = (bf16[256,1536]{1,0:T(8,128)(2,1)}, bf16[256,1536]{1,0:T(8,128)(2,1)S(1)}, u32[]{:S(2)}, u32[]{:S(2)}) collective-permute-start(bf16[256,1536]{1,0:T(8,128)(2,1)} %get-tuple-element.248), channel_id=1, source_target_pairs={{0,3},{1,0},{2,1},{3,2},{4,7},{5,4},{6,5},{7,6},{8,11},{9,8},{10,9... | collective-permute-start | bytes 2359304 | tf_op jit(solution)/shard_map/ppermute | solution.py:51
  220.6 64.0 %collective-permute-start.8 = (bf16[256,1536]{1,0:T(8,128)(2,1)}, bf16[256,1536]{1,0:T(8,128)(2,1)S(1)}, u32[]{:S(2)}, u32[]{:S(2)}) collective-permute-start(bf16[256,1536]{1,0:T(8,128)(2,1)} %get-tuple-element.249), channel_id=1, source_target_pairs={{0,2},{1,3},{2,0},{3,1},{4,6},{5,7},{6,4},{7,5},{8,10},{9,11},{10,... | collective-permute-start | bytes 2359304 | tf_op jit(solution)/shard_map/ppermute | solution.py:51
  220.6 64.9 %collective-permute-start.7 = (bf16[256,1536]{1,0:T(8,128)(2,1)}, bf16[256,1536]{1,0:T(8,128)(2,1)}, u32[]{:S(2)}, u32[]{:S(2)}) collective-permute-start(bf16[256,1536]{1,0:T(8,128)(2,1)} %get-tuple-element.247), channel_id=1, source_target_pairs={{0,1},{1,2},{2,3},{3,0},{4,5},{5,6},{6,7},{7,4},{8,9},{9,10},{10,1... | collective-permute-start | bytes 2359304 | tf_op jit(solution)/shard_map/ppermute | solution.py:51
  274.7 13.8 %copy-start.79 = (f32[4,256]{1,0:T(4,128)}, f32[4,256]{1,0:T(4,128)S(1)}, u32[]{:S(2)}) copy-start(f32[4,256]{1,0:T(4,128)S(1)} %psum.14) | copy-start | bytes 12292
  274.7 13.8 %copy-start.85 = (f32[4,256]{1,0:T(4,128)}, f32[4,256]{1,0:T(4,128)S(1)}, u32[]{:S(2)}) copy-start(f32[4,256]{1,0:T(4,128)S(1)} %add_rsqrt_fusion) | copy-start | bytes 12292
  274.8 24.6 %copy-start.91 = (f32[256]{0:T(256)}, f32[256]{0:T(256)S(1)}, u32[]{:S(2)}) copy-start(f32[256]{0:T(256)S(1)} %mul.235) | copy-start | bytes 3076
  288.5 175.4 %copy-start.38 = (f32[256,1536]{1,0:T(8,128)}, f32[256,1536]{1,0:T(8,128)S(1)}, u32[]{:S(2)}) copy-start(f32[256,1536]{1,0:T(8,128)S(1)} %get-tuple-element.240) | copy-start | bytes 4718596
  289.6 16.9 %collective-permute-start.10 = (bf16[128,1536]{1,0:T(8,128)(2,1)S(1)}, bf16[128,1536]{1,0:T(8,128)(2,1)S(1)}, u32[]{:S(2)}, u32[]{:S(2)}) collective-permute-start(bf16[128,1536]{1,0:T(8,128)(2,1)S(1)} %get-tuple-element.272), channel_id=1, source_target_pairs={{0,3},{1,0},{2,1},{3,2},{4,7},{5,4},{6,5},{7,6},{8,11},{9,8},{10,9... | collective-permute-start | bytes 1179656 | tf_op jit(solution)/shard_map/ppermute | solution.py:43
  296.8 31.3 %collective-permute-start.11 = (bf16[128,1536]{1,0:T(8,128)(2,1)S(1)}, bf16[128,1536]{1,0:T(8,128)(2,1)S(1)}, u32[]{:S(2)}, u32[]{:S(2)}) collective-permute-start(bf16[128,1536]{1,0:T(8,128)(2,1)S(1)} %get-tuple-element.272), channel_id=1, source_target_pairs={{0,2},{1,3},{2,0},{3,1},{4,6},{5,7},{6,4},{7,5},{8,10},{9,11},{10,... | collective-permute-start | bytes 1179656 | tf_op jit(solution)/shard_map/ppermute | solution.py:43
  296.8 31.3 %collective-permute-start.12 = (bf16[128,1536]{1,0:T(8,128)(2,1)S(1)}, bf16[128,1536]{1,0:T(8,128)(2,1)S(1)}, u32[]{:S(2)}, u32[]{:S(2)}) collective-permute-start(bf16[128,1536]{1,0:T(8,128)(2,1)S(1)} %get-tuple-element.272), channel_id=1, source_target_pairs={{0,1},{1,2},{2,3},{3,0},{4,5},{5,6},{6,7},{7,4},{8,9},{9,10},{10,1... | collective-permute-start | bytes 1179656 | tf_op jit(solution)/shard_map/ppermute | solution.py:43
  306.4 21.7 %copy-start.67 = (bf16[128,1536]{1,0:T(8,128)(2,1)}, bf16[128,1536]{1,0:T(8,128)(2,1)S(1)}, u32[]{:S(2)}) copy-start(bf16[128,1536]{1,0:T(8,128)(2,1)S(1)} %collective-permute-done.10.refs_1_) | copy-start | bytes 1179652
  329.6 53.6 %collective-permute-start.18 = (bf16[128,1536]{1,0:T(8,128)(2,1)}, bf16[128,1536]{1,0:T(8,128)(2,1)}, u32[]{:S(2)}, u32[]{:S(2)}) collective-permute-start(bf16[128,1536]{1,0:T(8,128)(2,1)} %after.22), channel_id=1, source_target_pairs={{0,1},{1,2},{2,3},{3,0},{4,5},{5,6},{6,7},{7,4},{8,9},{9,10},{10,1... | collective-permute-start | bytes 1179656 | tf_op jit(solution)/shard_map/ppermute | solution.py:43
  330.6 52.6 %collective-permute-start.17 = (bf16[128,1536]{1,0:T(8,128)(2,1)}, bf16[128,1536]{1,0:T(8,128)(2,1)}, u32[]{:S(2)}, u32[]{:S(2)}) collective-permute-start(bf16[128,1536]{1,0:T(8,128)(2,1)} %after.22), channel_id=1, source_target_pairs={{0,2},{1,3},{2,0},{3,1},{4,6},{5,7},{6,4},{7,5},{8,10},{9,11},{10,... | collective-permute-start | bytes 1179656 | tf_op jit(solution)/shard_map/ppermute | solution.py:43
  332.5 47.4 %collective-permute-start.16 = (bf16[128,1536]{1,0:T(8,128)(2,1)}, bf16[128,1536]{1,0:T(8,128)(2,1)}, u32[]{:S(2)}, u32[]{:S(2)}) collective-permute-start(bf16[128,1536]{1,0:T(8,128)(2,1)} %after.22), channel_id=1, source_target_pairs={{0,3},{1,0},{2,1},{3,2},{4,7},{5,4},{6,5},{7,6},{8,11},{9,8},{10,9... | collective-permute-start | bytes 1179656 | tf_op jit(solution)/shard_map/ppermute | solution.py:43
  379.4 45.0 %collective-permute-start.13 = (bf16[128,1536]{1,0:T(8,128)(2,1)}, bf16[128,1536]{1,0:T(8,128)(2,1)}, u32[]{:S(2)}, u32[]{:S(2)}) collective-permute-start(bf16[128,1536]{1,0:T(8,128)(2,1)} %get-tuple-element.261), channel_id=1, source_target_pairs={{0,1},{1,2},{2,3},{3,0},{4,5},{5,6},{6,7},{7,4},{8,9},{9,10},{10,1... | collective-permute-start | bytes 1179656 | tf_op jit(solution)/shard_map/ppermute | solution.py:51
  379.4 45.0 %collective-permute-start.14 = (bf16[128,1536]{1,0:T(8,128)(2,1)}, bf16[128,1536]{1,0:T(8,128)(2,1)}, u32[]{:S(2)}, u32[]{:S(2)}) collective-permute-start(bf16[128,1536]{1,0:T(8,128)(2,1)} %get-tuple-element.260), channel_id=1, source_target_pairs={{0,2},{1,3},{2,0},{3,1},{4,6},{5,7},{6,4},{7,5},{8,10},{9,11},{10,... | collective-permute-start | bytes 1179656 | tf_op jit(solution)/shard_map/ppermute | solution.py:51
  379.9 44.5 %collective-permute-start.15 = (bf16[128,1536]{1,0:T(8,128)(2,1)}, bf16[128,1536]{1,0:T(8,128)(2,1)}, u32[]{:S(2)}, u32[]{:S(2)}) collective-permute-start(bf16[128,1536]{1,0:T(8,128)(2,1)} %get-tuple-element.259), channel_id=1, source_target_pairs={{0,3},{1,0},{2,1},{3,2},{4,7},{5,4},{6,5},{7,6},{8,11},{9,8},{10,9... | collective-permute-start | bytes 1179656 | tf_op jit(solution)/shard_map/ppermute | solution.py:51
  425.8 10.2 %collective-permute-start.21 = (bf16[128,1536]{1,0:T(8,128)(2,1)S(1)}, bf16[128,1536]{1,0:T(8,128)(2,1)S(1)}, u32[]{:S(2)}, u32[]{:S(2)}) collective-permute-start(bf16[128,1536]{1,0:T(8,128)(2,1)S(1)} %get-tuple-element.257), channel_id=1, source_target_pairs={{0,3},{1,0},{2,1},{3,2},{4,7},{5,4},{6,5},{7,6},{8,11},{9,8},{10,9... | collective-permute-start | bytes 1179656 | tf_op jit(solution)/shard_map/ppermute | solution.py:51
  426.4 33.4 %collective-permute-start.20 = (bf16[128,1536]{1,0:T(8,128)(2,1)S(1)}, bf16[128,1536]{1,0:T(8,128)(2,1)S(1)}, u32[]{:S(2)}, u32[]{:S(2)}) collective-permute-start(bf16[128,1536]{1,0:T(8,128)(2,1)S(1)} %get-tuple-element.258), channel_id=1, source_target_pairs={{0,2},{1,3},{2,0},{3,1},{4,6},{5,7},{6,4},{7,5},{8,10},{9,11},{10,... | collective-permute-start | bytes 1179656 | tf_op jit(solution)/shard_map/ppermute | solution.py:51
  427.9 31.9 %collective-permute-start.19 = (bf16[128,1536]{1,0:T(8,128)(2,1)S(1)}, bf16[128,1536]{1,0:T(8,128)(2,1)S(1)}, u32[]{:S(2)}, u32[]{:S(2)}) collective-permute-start(bf16[128,1536]{1,0:T(8,128)(2,1)S(1)} %get-tuple-element.256), channel_id=1, source_target_pairs={{0,1},{1,2},{2,3},{3,0},{4,5},{5,6},{6,7},{7,4},{8,9},{9,10},{10,1... | collective-permute-start | bytes 1179656 | tf_op jit(solution)/shard_map/ppermute | solution.py:51
  465.8 39.5 %collective-permute-start.22 = (bf16[256,1536]{1,0:T(8,128)(2,1)S(1)}, bf16[256,1536]{1,0:T(8,128)(2,1)S(1)}, u32[]{:S(2)}, u32[]{:S(2)}) collective-permute-start(bf16[256,1536]{1,0:T(8,128)(2,1)S(1)} %get-tuple-element.238), channel_id=1, source_target_pairs={{0,3},{1,0},{2,1},{3,2},{4,7},{5,4},{6,5},{7,6},{8,11},{9,8},{10,9... | collective-permute-start | bytes 2359304 | tf_op jit(solution)/shard_map/ppermute | solution.py:43
  465.9 69.7 %collective-permute-start.23 = (bf16[256,1536]{1,0:T(8,128)(2,1)S(1)}, bf16[256,1536]{1,0:T(8,128)(2,1)S(1)}, u32[]{:S(2)}, u32[]{:S(2)}) collective-permute-start(bf16[256,1536]{1,0:T(8,128)(2,1)S(1)} %get-tuple-element.238), channel_id=1, source_target_pairs={{0,2},{1,3},{2,0},{3,1},{4,6},{5,7},{6,4},{7,5},{8,10},{9,11},{10,... | collective-permute-start | bytes 2359304 | tf_op jit(solution)/shard_map/ppermute | solution.py:43
  503.3 33.2 %collective-permute-start.24 = (bf16[256,1536]{1,0:T(8,128)(2,1)S(1)}, bf16[256,1536]{1,0:T(8,128)(2,1)S(1)}, u32[]{:S(2)}, u32[]{:S(2)}) collective-permute-start(bf16[256,1536]{1,0:T(8,128)(2,1)S(1)} %get-tuple-element.238), channel_id=1, source_target_pairs={{0,1},{1,2},{2,3},{3,0},{4,5},{5,6},{6,7},{7,4},{8,9},{9,10},{10,1... | collective-permute-start | bytes 2359304 | tf_op jit(solution)/shard_map/ppermute | solution.py:43
  538.4 18.1 %copy-start.80 = (f32[4,256]{1,0:T(4,128)S(1)}, f32[4,256]{1,0:T(4,128)}, u32[]{:S(2)}) copy-start(f32[4,256]{1,0:T(4,128)} %copy-done.79) | copy-start | bytes 12292
  538.4 25.2 %copy-start.30 = (f32[4,256,256]{2,1,0:T(8,128)S(1)}, f32[4,256,256]{2,1,0:T(8,128)}, u32[]{:S(2)}) copy-start(f32[4,256,256]{2,1,0:T(8,128)} %copy-done.28) | copy-start | bytes 3145732
  560.1 59.7 %collective-permute-start.28 = (bf16[128,1536]{1,0:T(8,128)(2,1)}, bf16[128,1536]{1,0:T(8,128)(2,1)}, u32[]{:S(2)}, u32[]{:S(2)}) collective-permute-start(bf16[128,1536]{1,0:T(8,128)(2,1)} %get-tuple-element.255), channel_id=1, source_target_pairs={{0,3},{1,0},{2,1},{3,2},{4,7},{5,4},{6,5},{7,6},{8,11},{9,8},{10,9... | collective-permute-start | bytes 1179656 | tf_op jit(solution)/shard_map/ppermute | solution.py:51
  562.2 141.8 %collective-permute-start.31 = (bf16[128,1536]{1,0:T(8,128)(2,1)}, bf16[128,1536]{1,0:T(8,128)(2,1)}, u32[]{:S(2)}, u32[]{:S(2)}) collective-permute-start(bf16[128,1536]{1,0:T(8,128)(2,1)} %get-tuple-element.254), channel_id=1, source_target_pairs={{0,2},{1,3},{2,0},{3,1},{4,6},{5,7},{6,4},{7,5},{8,10},{9,11},{10,... | collective-permute-start | bytes 1179656 | tf_op jit(solution)/shard_map/ppermute | solution.py:51
  563.6 57.7 %collective-permute-start.27 = (bf16[128,1536]{1,0:T(8,128)(2,1)}, bf16[128,1536]{1,0:T(8,128)(2,1)}, u32[]{:S(2)}, u32[]{:S(2)}) collective-permute-start(bf16[128,1536]{1,0:T(8,128)(2,1)} %get-tuple-element.253), channel_id=1, source_target_pairs={{0,1},{1,2},{2,3},{3,0},{4,5},{5,6},{6,7},{7,4},{8,9},{9,10},{10,1... | collective-permute-start | bytes 1179656 | tf_op jit(solution)/shard_map/ppermute | solution.py:51
  574.6 43.7 %all-to-all-start.2 = ((f32[8,384,128]{2,1,0:T(8,128)}), f32[8,384,128]{2,1,0:T(8,128)S(1)}, u32[]{:S(2)}, u32[]{:S(2)}) async-start(f32[8,384,128]{2,1,0:T(8,128)} %bitcast.302), calls=%async_computation.2 | async-start | bytes 3145728 | tf_op jit(solution)/shard_map/all_to_all | solution.py:250
  582.5 38.8 %collective-permute-start.25 = (bf16[128,1536]{1,0:T(8,128)(2,1)}, bf16[128,1536]{1,0:T(8,128)(2,1)}, u32[]{:S(2)}, u32[]{:S(2)}) collective-permute-start(bf16[128,1536]{1,0:T(8,128)(2,1)} %get-tuple-element.252), channel_id=1, source_target_pairs={{0,1},{1,2},{2,3},{3,0},{4,5},{5,6},{6,7},{7,4},{8,9},{9,10},{10,1... | collective-permute-start | bytes 1179656 | tf_op jit(solution)/shard_map/ppermute | solution.py:51
  584.5 36.8 %collective-permute-start.26 = (bf16[128,1536]{1,0:T(8,128)(2,1)}, bf16[128,1536]{1,0:T(8,128)(2,1)}, u32[]{:S(2)}, u32[]{:S(2)}) collective-permute-start(bf16[128,1536]{1,0:T(8,128)(2,1)} %get-tuple-element.251), channel_id=1, source_target_pairs={{0,3},{1,0},{2,1},{3,2},{4,7},{5,4},{6,5},{7,6},{8,11},{9,8},{10,9... | collective-permute-start | bytes 1179656 | tf_op jit(solution)/shard_map/ppermute | solution.py:51
  619.8 84.2 %collective-permute-start.30 = (bf16[128,1536]{1,0:T(8,128)(2,1)}, bf16[128,1536]{1,0:T(8,128)(2,1)}, u32[]{:S(2)}, u32[]{:S(2)}) collective-permute-start(bf16[128,1536]{1,0:T(8,128)(2,1)} %get-tuple-element.250), channel_id=1, source_target_pairs={{0,2},{1,3},{2,0},{3,1},{4,6},{5,7},{6,4},{7,5},{8,10},{9,11},{10,... | collective-permute-start | bytes 1179656 | tf_op jit(solution)/shard_map/ppermute | solution.py:51
  621.3 42.5 %all-to-all-start.3 = ((f32[8,384,128]{2,1,0:T(8,128)}), f32[8,384,128]{2,1,0:T(8,128)}, u32[]{:S(2)}, u32[]{:S(2)}) async-start(f32[8,384,128]{2,1,0:T(8,128)} %after.27), calls=%async_computation.3 | async-start | bytes 3145728 | tf_op jit(solution)/shard_map/all_to_all | solution.py:250
  625.6 148.3 %reduce-scatter.6.cloned.1.call-start = ((), (), s32[]{:S(2)}) async-start(), calls=%async_computation.10 | async-start | bytes 5308416 | tf_op jit(solution)/shard_map/reduce_scatter | solution.py:83
  691.9 8.1 collective-permute-start.29
  717.0 125.1 %reduce-scatter.8.cloned.1.call-start = ((), (), s32[]{:S(2)}) async-start(), calls=%async_computation.11 | async-start | bytes 3096576 | tf_op jit(solution)/shard_map/reduce_scatter | solution.py:83
  725.1 55.2 %collective-permute-start.33 = (bf16[256,1536]{1,0:T(8,128)(2,1)}, bf16[256,1536]{1,0:T(8,128)(2,1)}, u32[]{:S(2)}, u32[]{:S(2)}) collective-permute-start(bf16[256,1536]{1,0:T(8,128)(2,1)} %get-tuple-element.246), channel_id=1, source_target_pairs={{0,2},{1,3},{2,0},{3,1},{4,6},{5,7},{6,4},{7,5},{8,10},{9,11},{10,... | collective-permute-start | bytes 2359304 | tf_op jit(solution)/shard_map/ppermute | solution.py:51
  727.0 53.3 %collective-permute-start.32 = (bf16[256,1536]{1,0:T(8,128)(2,1)}, bf16[256,1536]{1,0:T(8,128)(2,1)}, u32[]{:S(2)}, u32[]{:S(2)}) collective-permute-start(bf16[256,1536]{1,0:T(8,128)(2,1)} %get-tuple-element.244), channel_id=1, source_target_pairs={{0,1},{1,2},{2,3},{3,0},{4,5},{5,6},{6,7},{7,4},{8,9},{9,10},{10,1... | collective-permute-start | bytes 2359304 | tf_op jit(solution)/shard_map/ppermute | solution.py:51
  780.3 24.8 %copy-start.34 = (bf16[1024,1536]{1,0:T(8,128)(2,1)S(1)}, bf16[1024,1536]{1,0:T(8,128)(2,1)}, u32[]{:S(2)}) copy-start(bf16[1024,1536]{1,0:T(8,128)(2,1)} %get-tuple-element.242.refs_1_.refs_2_) | copy-start | bytes 9437188
  780.3 24.8 %copy-start.75 = (f32[1536]{0:T(1024)S(1)}, f32[1536]{0:T(1024)}, u32[]{:S(2)}) copy-start(f32[1536]{0:T(1024)} %copy-done.74) | copy-start | bytes 18436
  780.3 37.3 %all-to-all-start.4 = ((f32[8,4,120,128]{3,2,1,0:T(8,128)}), f32[8,4,120,128]{3,2,1,0:T(8,128)}, u32[]{:S(2)}, u32[]{:S(2)}) async-start(f32[8,4,120,128]{3,2,1,0:T(8,128)} %after.32), calls=%async_computation.5 | async-start | bytes 3932160 | tf_op jit(solution)/shard_map/all_to_all | solution.py:1068
  784.9 20.1 %collective-permute-start.34 = (bf16[256,1536]{1,0:T(8,128)(2,1)}, bf16[256,1536]{1,0:T(8,128)(2,1)}, u32[]{:S(2)}, u32[]{:S(2)}) collective-permute-start(bf16[256,1536]{1,0:T(8,128)(2,1)} %get-tuple-element.245), channel_id=1, source_target_pairs={{0,3},{1,0},{2,1},{3,2},{4,7},{5,4},{6,5},{7,6},{8,11},{9,8},{10,9... | collective-permute-start | bytes 2359304 | tf_op jit(solution)/shard_map/ppermute | solution.py:51
  786.3 18.8 %copy-start.41 = (bf16[4,64,1536]{2,1,0:T(8,128)(2,1)S(1)}, bf16[4,64,1536]{2,1,0:T(8,128)(2,1)}, u32[]{:S(2)}) copy-start(bf16[4,64,1536]{2,1,0:T(8,128)(2,1)} %copy-done.40) | copy-start | bytes 2359300
  819.9 12.6 %all-to-all-start.5 = ((f32[4,120,128]{2,1,0:T(8,128)}), f32[4,120,128]{2,1,0:T(8,128)}, u32[]{:S(2)}, u32[]{:S(2)}) async-start(f32[4,120,128]{2,1,0:T(8,128)} %after.33), calls=%async_computation.6 | async-start | bytes 491520 | tf_op jit(solution)/shard_map/all_to_all | solution.py:1071
  (89 other events, 376.4 us)
Sparse Core Ops, SparseCore 0:
  11.5 36.6 all-gather.7
  50.1 40.5 all-gather.9
  195.7 107.1 all-gather.11
  537.6 170.6 reduce-scatter.3
  717.1 53.4 reduce-scatter.5
  774.2 54.1 reduce-scatter.7

commit v6 on v5

--- a/solution.py
+++ b/solution.py
@@ -969,6 +969,7 @@
     gg_row, gz_row = (values.reshape(1, zs * tokens, inner) for values in (gg_all[0], unmixed[0][1]))
     side_products = expert_grads(scaled, [n_rows], [gg_row], [gz_row], pieces)
 
+    z_backs = []
     v_grads, bc_grads, conv_grad, head_grad = [], [], 0.0, 0.0
     full_x = jnp.concatenate([full_enter[:, :inner], full_enter[:, width:]], axis=1)
     full_bc = full_enter[:, inner:width]
@@ -977,6 +978,8 @@
         gy, gz = unmixed[c]
         xs, rw, dl, _ = entered[c]
         gh = exchanged(after(scanned[c], pairs[c][0], *sooner)).reshape(h_all[c].shape)
+        z_backs.append(dot(gz.reshape(zs * tokens, inner), full_z, NT))
+        gh = after(gh, z_backs[c], side_products, *later)
         gv, gbc, g_rim, gc, ghp = mixer_back(
             v[c], halo[c], conv_w, hp, skip, rw, dl, gy, *pairs[c], h_all[c], gh
         )
@@ -988,11 +991,11 @@
         edge = gbc[zs - 1, :, rows - rim :] + following[:, :, inner:]
         gbc = lax.dynamic_update_slice(gbc, edge[None], (zs - 1, 0, rows - rim, 0))
         v_grads.append(gv)
-        bc_grads.append(after(jnp.concatenate(split_parts(gbc), axis=-1), *later))
+        bc_grads.append(jnp.concatenate(split_parts(gbc), axis=-1))
     n_parts, arrived, gain_one_grad = [], [], 0.0
     for c in chunk_ids:
         n_grad = (
-            dot(unmixed[c][1].reshape(zs * tokens, inner), full_z, NT)
+            z_backs[c]
             + dot(v_grads[c].reshape(zs * tokens, inner + LANES), full_x, NT)
             + dot(bc_grads[c].reshape(zs * tokens, 4 * STATE_DIM), full_bc, NT)
         )

time: 865 us -> 860 us (level)
    all_to_all x4, waiting for transfers between devices: 48.5 us -> 35 us  [exchanged(): return lax.all_to_all(rows, 'dp', 0, 0, tiled=False)]
    ppermute x18, waiting for transfers between devices: 58.9 us -> 69.4 us  [line_parts(): lax.ppermute(row_major(block_of(step)), 'tensor', [(a, (a + step) % size)...]
    unnamed x224 -> x232, local copies, waits for them, and re-layouts: 32.1 us -> 35.8 us
  transfers between devices with their start and end apart: 47 -> 47, of which waited for: 17 -> 20; matrix products, arithmetic and copies ran while one was open for 23% -> 23% of each run, Pallas kernels for 25% -> 25%
where the time goes in v6:
time: 860 us; the launch traced here: 849 us
  waiting for transfers between devices  238 us (28%)
  Pallas kernels  209 us (24%)
  local copies, waits for them, and re-layouts  116 us (13%)
  starting transfers between devices  80.9 us (9%)
  blocking collectives  68.5 us (8%)
  other arithmetic  61 us (7%)
  matrix products  58.9 us (7%)
  between operations  16.8 us (2%)
    ppermute x15, waiting for transfers between devices, line_gather(): lax.ppermute(row_major(value), 'tensor', [(a, (a - step) % size) for a in...  122 us
    pallas_call x2, Pallas kernels, experts(): pl.pallas_call(expert_kernel, grid=(pairs,), in_specs=[pl.BlockSpec((toke...  77.3 us
    ppermute x18, waiting for transfers between devices, line_parts(): lax.ppermute(row_major(block_of(step)), 'tensor', [(a, (a + step) % size)...  69.4 us
    dot_general x12, matrix products, dot(): lax.dot_general(a, b, (dims, ((), ())), precision=precision, preferred_el...  58.9 us
    psum x1, blocking collectives, body(): square_sum = lax.psum(squares[:, :, 0], 'tensor')  51.3 us
    pallas_call x2, Pallas kernels, expert_grads(): pl.pallas_call(skipping(functools.partial(expert_grad_kernel, ups, chunks...  48 us
    unnamed x232, local copies, waits for them, and re-layouts  35.8 us
    all_to_all x4, waiting for transfers between devices, exchanged(): return lax.all_to_all(rows, 'dp', 0, 0, tiled=False)  35 us
  transfers between devices with their start and end apart: 47, of which 20 were waited for; matrix products, arithmetic and copies ran while one was open for 23% of the time, Pallas kernels for 25%

profile of v6, /device:TPU:0, one launch (start us, length us, event | category | flops | bytes accessed | tf_op | source)
XLA Modules:
  0.0 848.7 jit_solution(12348744476660464954)
XLA Ops:
  11.6 5.1 collective-permute-start
  19.0 8.9 %all-gather.3 = f32[8,192,2]{1,2,0:T(2,128)S(1)} all-gather(f32[1,192,2]{1,2,0:T(2,128)S(1)} %fusion.57), channel_id=1, replica_groups=mesh['dp'=8,'tensor'=4] {'dp'}, dimensions={0}, use_global_device_ids=true | all-gather | bytes 13824 | tf_op jit(solution)/shard_map/all_gather | solution.py:830
  36.0 48.0 %collective-permute-done.1 = bf16[256,1536]{1,0:T(8,128)(2,1)S(1)} collective-permute-done((bf16[256,1536]{1,0:T(8,128)(2,1)S(1)}, bf16[256,1536]{1,0:T(8,128)(2,1)S(1)}, u32[]{:S(2)}, u32[]{:S(2)}) %collective-permute-start.1) | collective-permute-done | bytes 786464 | tf_op jit(solution)/shard_map/ppermute | solution.py:43
  92.2 9.3 %fusion.1.v_ref = f32[4,4,64,1152]{3,2,1,0:T(8,128)} fusion(bf16[4,4,64,1536]{3,2,1,0:T(8,128)(2,1)} %bitcast.332, bf16[1536,1152]{1,0:T(8,128)(2,1)} %all-gather.8.cloned.1.call-done), kind=kOutput, calls=%fused_computation.9 | convolution fusion | flops 3623878656 | bytes 11403264 | tf_op jit(solution)/shard_map/dot_general | solution.py:98
  101.5 11.3 %mixer_enter.1 = (f32[4,256,768]{2,1,0:T(8,128)}, f32[4,256,256]{2,1,0:T(8,128)S(1)}, f32[4,256,256]{2,1,0:T(8,128)S(1)}, f32[4,768,128]{2,1,0:T(8,128)S(1)}) custom-call(f32[4,4,64,1152]{3,2,1,0:T(8,128)} %fusion.1.v_ref, f32[4,8,1024]{2,1,0:T(8,128)S(1)} %pad.42.halo_ref, f32[8,1024]{1,0:T(8,128)S(1)} %select_maximum_fusion.cw_ref, f32[8,128]{1,0:T(8,128)S(1)} %pad.44.hp_ref), custom_call_target="tpu_custom_call" | custom-call | flops 13516800000 | bytes 1024 | tf_op jit(solution)/shard_map/mixer_enter/pallas_call | solution.py:203
  114.3 12.2 %collective-permute-done.5.refs_2_ = bf16[256,1536]{1,0:T(8,128)(2,1)} collective-permute-done((bf16[256,1536]{1,0:T(8,128)(2,1)}, bf16[256,1536]{1,0:T(8,128)(2,1)}, u32[]{:S(2)}, u32[]{:S(2)}) %collective-permute-start.5) | collective-permute-done | bytes 786464 | tf_op jit(solution)/shard_map/ppermute | solution.py:43
  126.4 2.7 pad_maximum_fusion.2
  129.1 4.6 all-to-all-start
  135.7 4.6 mixer_inner.1.refs_2_.yi_ref
  142.0 13.1 %all-to-all-done = f32[8,392,128]{2,1,0:T(8,128)} async-done(((f32[8,392,128]{2,1,0:T(8,128)}), f32[8,392,128]{2,1,0:T(8,128)}, u32[]{:S(2)}, u32[]{:S(2)}) %all-to-all-start) | async-done | bytes 1605664 | tf_op jit(solution)/shard_map/all_to_all | solution.py:250
  159.5 6.9 fusion.16
  166.4 3.1 collective-permute-done.6.refs_1_
  169.5 3.9 all-to-all-start.1
  180.7 3.8 reshape.439
  184.5 3.0 pad_maximum_fusion.refs_0_
  187.5 6.9 all-to-all-done.1
  202.2 8.1 mixer_leave.1
  210.3 5.1 convolution_convert_fusion
  217.8 2.8 collective-permute-start.9
  223.4 51.3 %psum.14 = f32[4,256]{1,0:T(4,128)S(1)} all-reduce(f32[4,256]{1,0:T(4,128)S(1)} %slice_reduce_fusion), channel_id=1, replica_groups=mesh['dp'=8,'tensor'=4] {'tensor'}, use_global_device_ids=true, to_apply=%region_1.2 | all-reduce | flops 1024 | bytes 8192 | tf_op jit(solution)/shard_map/psum | solution.py:882
  274.9 9.8 %collective-permute-done.8 = bf16[256,1536]{1,0:T(8,128)(2,1)S(1)} collective-permute-done((bf16[256,1536]{1,0:T(8,128)(2,1)}, bf16[256,1536]{1,0:T(8,128)(2,1)S(1)}, u32[]{:S(2)}, u32[]{:S(2)}) %collective-permute-start.8) | collective-permute-done | bytes 786464 | tf_op jit(solution)/shard_map/ppermute | solution.py:51
  285.6 3.1 multiply_reduce_fusion.4
  289.8 7.2 collective-permute-start.10
  301.3 5.3 collective-permute-done.10.refs_1_
  306.6 21.7 %collective-permute-done.11.refs_2_ = bf16[128,1536]{1,0:T(8,128)(2,1)S(1)} collective-permute-done((bf16[128,1536]{1,0:T(8,128)(2,1)S(1)}, bf16[128,1536]{1,0:T(8,128)(2,1)S(1)}, u32[]{:S(2)}, u32[]{:S(2)}) %collective-permute-start.11) | collective-permute-done | bytes 393248 | tf_op jit(solution)/shard_map/ppermute | solution.py:43
  332.7 3.3 collective-permute-start.16
  338.6 38.6 %experts.2 = (bf16[512,1536]{1,0:T(8,128)(2,1)}, bf16[512,1536]{1,0:T(8,128)(2,1)}, bf16[512,128]{1,0:T(8,128)(2,1)}, bf16[9,512,256]{2,1,0:T(8,128)(2,1)}, bf16[9,512,512]{2,1,0:T(8,128)(2,1)}) custom-call(bf16[512,1536]{1,0:T(8,128)(2,1)} %pad_maximum_fusion.3.n_ref.refs_0_, bf16[512,1536]{1,0:T(8,128)(2,1)} %get-tuple-element.300.g_ref.refs_2_, ...), custom_call_target="tpu_custom_call" | custom-call | flops 40550400000 | bytes 1024 | tf_op jit(solution)/shard_map/experts/pallas_call | solution.py:661
  380.1 3.2 collective-permute-start.15
  386.0 38.6 %experts.3 = (bf16[512,1536]{1,0:T(8,128)(2,1)}, bf16[512,1536]{1,0:T(8,128)(2,1)}, bf16[512,128]{1,0:T(8,128)(2,1)}, bf16[9,512,256]{2,1,0:T(8,128)(2,1)}, bf16[9,512,512]{2,1,0:T(8,128)(2,1)}) custom-call(bf16[512,1536]{1,0:T(8,128)(2,1)} %pad_maximum_fusion.5.n_ref.refs_1_, bf16[512,1536]{1,0:T(8,128)(2,1)} %get-tuple-element.301.g_ref.refs_3_, ...), custom_call_target="tpu_custom_call" | custom-call | flops 40550400000 | bytes 1024 | tf_op jit(solution)/shard_map/experts/pallas_call | solution.py:661
  431.6 4.6 collective-permute-done.21
  436.2 23.8 %collective-permute-done.20 = bf16[128,1536]{1,0:T(8,128)(2,1)S(1)} collective-permute-done((bf16[128,1536]{1,0:T(8,128)(2,1)S(1)}, bf16[128,1536]{1,0:T(8,128)(2,1)S(1)}, u32[]{:S(2)}, u32[]{:S(2)}) %collective-permute-start.20) | collective-permute-done | bytes 393248 | tf_op jit(solution)/shard_map/ppermute | solution.py:51
  467.7 35.8 %expert_grads.3.refs_0_ = bf16[8,27,192,256]{3,2,1,0:T(8,128)(2,1)} custom-call(bf16[512,1536]{1,0:T(8,128)(2,1)S(1)} %copy-done.8, bf16[512,1536]{1,0:T(8,128)(2,1)S(1)} %copy-done.4, bf16[512,1536]{1,0:T(8,128)(2,1)S(1)} %copy-done.14, bf16[512,1536]{1,0:T(8,128)(2,1)} %get-tuple-element.301.g_ref.refs_3_, bf16[9,512,512]{2,1,0:T(8,128)(2,1)} %get-tuple-element.96.refs_4_, ...), custom_call_target="tpu_custom_call" | custom-call | flops 40550400000 | bytes 1024 | tf_op jit(solution)/shard_map/expert_grads/pallas_call | solution.py:750
  506.4 29.5 %collective-permute-done.23 = bf16[256,1536]{1,0:T(8,128)(2,1)S(1)} collective-permute-done((bf16[256,1536]{1,0:T(8,128)(2,1)S(1)}, bf16[256,1536]{1,0:T(8,128)(2,1)S(1)}, u32[]{:S(2)}, u32[]{:S(2)}) %collective-permute-start.23) | collective-permute-done | bytes 786464 | tf_op jit(solution)/shard_map/ppermute | solution.py:43
  538.6 9.6 %fusion.5 = (f32[4,4,64]{2,1,0:T(4,128)S(1)}, f32[4,4,64,768]{3,2,1,0:T(8,128)}) fusion(f32[4,4,64,768]{3,2,1,0:T(8,128)} %bitcast.377, f32[4,4,64,768]{3,2,1,0:T(8,128)} %bitcast.337, f32[768]{0:T(1024)S(1)} %copy-done.96, bf16[4,4,64,1536]{3,2,1,0:T(8,128)(2,1)} %bitcast.59, bf16[1536,1664]{1,0:T(8,128)(2,1)} %all-gather.10.cloned.1.call-done), kind=kOutput, calls=%fused_computation.15 | convolution fusion | flops 2422209536 | bytes 14949376 | tf_op jit(solution)/shard_map/dot_general | solution.py:98
  548.3 8.3 psum.15
  563.8 8.6 %mixer_unmix.1 = (f32[4,256,768]{2,1,0:T(8,128)}, bf16[4,4,64,768]{3,2,1,0:T(8,128)(2,1)S(1)}, f32[4,768,128]{2,1,0:T(8,128)S(1)}, f32[8,768]{1,0:T(8,128)S(1)}) custom-call(f32[4,4,64,768]{3,2,1,0:T(8,128)} %get-tuple-element.298.gn_ref, f32[4,256,768]{2,1,0:T(8,128)} %get-tuple-element.80.y_ref, f32[4,4,64,768]{3,2,1,0:T(8,128)} %bitcast.338, ...), custom_call_target="tpu_custom_call" | custom-call | flops 10137600000 | bytes 1024 | tf_op jit(solution)/shard_map/mixer_unmix/pallas_call | solution.py:385
  574.6 5.6 all-to-all-start.2
  582.7 23.2 %mixer_pairs.1 = (f32[4,256,768]{2,1,0:T(8,128)}, f32[4,256,256]{2,1,0:T(8,128)S(1)}, f32[4,256,256]{2,1,0:T(8,128)S(1)}) custom-call(f32[4,256,768]{2,1,0:T(8,128)} %get-tuple-element.71.xs_ref.refs_0_, f32[4,256,256]{2,1,0:T(8,128)S(1)} %copy-done.31, f32[4,256,256]{2,1,0:T(8,128)S(1)} %copy-done.22, f32[4,256,768]{2,1,0:T(8,128)} %get-tuple-element.82.refs_3_.gy_ref), custom_call_target="tpu_custom_call" | custom-call | flops 47308800000 | bytes 1024 | tf_op jit(solution)/shard_map/mixer_pairs/pallas_call | solution.py:454
  614.1 4.2 fusion.refs_0_
  621.5 2.9 collective-permute-done.25.refs_2_.refs_0_
  624.3 7.7 collective-permute-done.26.refs_3_
  632.0 4.5 all-to-all-start.3
  636.9 12.1 %expert_grads.2.refs_2_.refs_0_ = bf16[8,6,192,256]{3,2,1,0:T(8,128)(2,1)} custom-call(bf16[1024,1536]{1,0:T(8,128)(2,1)} %fusion.refs_0_, bf16[1024,1536]{1,0:T(8,128)(2,1)} %copy-done.50, bf16[1,1024,768]{2,1,0:T(8,128)(2,1)S(1)} %bitcast.304, bf16[1,1024,768]{2,1,0:T(8,128)(2,1)S(1)} %bitcast.305), custom_call_target="tpu_custom_call" | custom-call | flops 9011200000 | bytes 1024 | tf_op jit(solution)/shard_map/expert_grads/pallas_call | solution.py:750
  649.0 6.2 fusion.14.refs_1_
  655.2 14.9 %all-to-all-done.3 = f32[8,384,128]{2,1,0:T(8,128)} async-done(((f32[8,384,128]{2,1,0:T(8,128)}), f32[8,384,128]{2,1,0:T(8,128)}, u32[]{:S(2)}, u32[]{:S(2)}) %all-to-all-start.3) | async-done | bytes 1572896 | tf_op jit(solution)/shard_map/all_to_all | solution.py:250
  670.2 27.2 %mixer_back.1 = (bf16[4,4,64,896]{3,2,1,0:T(8,128)(2,1)}, f32[4,4,64,256]{3,2,1,0:T(8,128)}, f32[4,8,1024]{2,1,0:T(8,128)}, f32[8,1024]{1,0:T(8,128)}, f32[8,128]{1,0:T(8,128)}) custom-call(f32[4,4,64,1152]{3,2,1,0:T(8,128)} %fusion.1.v_ref, f32[4,8,1024]{2,1,0:T(8,128)} %copy-done.15, f32[8,1024]{1,0:T(8,128)} %copy-done.16, f32[8,128]{1,0:T(8,128)} %copy-done.18, ...), custom_call_target="tpu_custom_call" | custom-call | flops 20275200000 | bytes 1024 | tf_op jit(solution)/shard_map/mixer_back/pallas_call | solution.py:558
  705.4 3.4 fusion.6
  708.9 3.7 multiply_reduce_fusion
  717.7 3.3 dynamic-slice_bitcast_fusion.2
  726.1 4.0 fusion.76
  733.8 3.9 fusion.21
  742.4 6.6 convolution_convert_fusion.1
  749.0 3.8 copy.301
  752.8 4.1 slice.469
  758.5 3.7 convert_element_type.272
  762.2 6.0 copy.303.refs_3_
  771.4 4.6 collective-permute-done.33.refs_2_
  776.0 4.7 all-to-all-start.4
  782.1 2.7 copy.341
  784.8 16.0 %collective-permute-done.34.refs_1_ = bf16[256,1536]{1,0:T(8,128)(2,1)} collective-permute-done((bf16[256,1536]{1,0:T(8,128)(2,1)}, bf16[256,1536]{1,0:T(8,128)(2,1)}, u32[]{:S(2)}, u32[]{:S(2)}) %collective-permute-start.34) | collective-permute-done | bytes 786464 | tf_op jit(solution)/shard_map/ppermute | solution.py:51
  803.2 10.1 %all-to-all-done.4 = f32[8,4,120,128]{3,2,1,0:T(8,128)} async-done(((f32[8,4,120,128]{3,2,1,0:T(8,128)}), f32[8,4,120,128]{3,2,1,0:T(8,128)}, u32[]{:S(2)}, u32[]{:S(2)}) %all-to-all-start.4) | async-done | bytes 1966112 | tf_op jit(solution)/shard_map/all_to_all | solution.py:1071
  815.7 4.2 all-to-all-start.5
  819.9 3.1 fusion.20
  824.6 2.9 copy.310
  (495 shorter events, 166.7 us)
Async XLA Ops:
  7.2 173.2 %copy-start = (bf16[192,2,256]{2,1,0:T(2,128)(2,1)S(1)}, bf16[192,2,256]{2,1,0:T(2,128)(2,1)}, u32[]{:S(2)}) copy-start(bf16[192,2,256]{2,1,0:T(2,128)(2,1)} %param.40) | copy-start | bytes 589828
  7.2 82.4 %all-gather.8.cloned.1.call-start = ((), (), s32[]{:S(2)}) async-start(), calls=%async_computation.12 | async-start | bytes 3981312 | tf_op jit(solution)/shard_map/all_gather | solution.py:79
  11.4 148.1 %all-gather.10.cloned.1.call-start = ((), (), s32[]{:S(2)}) async-start(), calls=%async_computation.13 | async-start | bytes 5750784 | tf_op jit(solution)/shard_map/all_gather | solution.py:79
  11.6 21.0 %copy-start.40 = (bf16[4,64,1536]{2,1,0:T(8,128)(2,1)}, bf16[4,64,1536]{2,1,0:T(8,128)(2,1)S(1)}, u32[]{:S(2)}) copy-start(bf16[4,64,1536]{2,1,0:T(8,128)(2,1)S(1)} %copy.272) | copy-start | bytes 2359300
  11.6 23.1 %collective-permute-start = (bf16[256,1536]{1,0:T(8,128)(2,1)S(1)}, bf16[256,1536]{1,0:T(8,128)(2,1)}, u32[]{:S(2)}, u32[]{:S(2)}) collective-permute-start(bf16[256,1536]{1,0:T(8,128)(2,1)S(1)} %bitcast.312), channel_id=1, source_target_pairs={{0,3},{1,0},{2,1},{3,2},{4,7},{5,4},{6,5},{7,6},{8,11},{9,8},{10,9... | collective-permute-start | bytes 2359304 | tf_op jit(solution)/shard_map/ppermute | solution.py:43
  16.7 67.3 %collective-permute-start.1 = (bf16[256,1536]{1,0:T(8,128)(2,1)S(1)}, bf16[256,1536]{1,0:T(8,128)(2,1)S(1)}, u32[]{:S(2)}, u32[]{:S(2)}) collective-permute-start(bf16[256,1536]{1,0:T(8,128)(2,1)S(1)} %bitcast.313), channel_id=1, source_target_pairs={{0,2},{1,3},{2,0},{3,1},{4,6},{5,7},{6,4},{7,5},{8,10},{9,11},{10,... | collective-permute-start | bytes 2359304 | tf_op jit(solution)/shard_map/ppermute | solution.py:43
  16.7 67.3 %collective-permute-start.2 = (bf16[256,1536]{1,0:T(8,128)(2,1)S(1)}, bf16[256,1536]{1,0:T(8,128)(2,1)S(1)}, u32[]{:S(2)}, u32[]{:S(2)}) collective-permute-start(bf16[256,1536]{1,0:T(8,128)(2,1)S(1)} %bitcast.314), channel_id=1, source_target_pairs={{0,1},{1,2},{2,3},{3,0},{4,5},{5,6},{6,7},{7,4},{8,9},{9,10},{10,1... | collective-permute-start | bytes 2359304 | tf_op jit(solution)/shard_map/ppermute | solution.py:43
  32.3 52.6 %copy-start.74 = (f32[1536]{0:T(1024)}, f32[1536]{0:T(1024)S(1)}, u32[]{:S(2)}) copy-start(f32[1536]{0:T(1024)S(1)} %get-tuple-element.233) | copy-start | bytes 18436
  85.9 3.8 collective-permute-start.3
  87.5 14.0 %copy-start.16 = (f32[8,1024]{1,0:T(8,128)}, f32[8,1024]{1,0:T(8,128)S(1)}, u32[]{:S(2)}) copy-start(f32[8,1024]{1,0:T(8,128)S(1)} %select_maximum_fusion.cw_ref) | copy-start | bytes 98308
  87.6 14.0 %copy-start.18 = (f32[8,128]{1,0:T(8,128)}, f32[8,128]{1,0:T(8,128)S(1)}, u32[]{:S(2)}) copy-start(f32[8,128]{1,0:T(8,128)S(1)} %pad.44.hp_ref) | copy-start | bytes 12292
  87.6 26.7 %collective-permute-start.4 = (bf16[256,1536]{1,0:T(8,128)(2,1)}, bf16[256,1536]{1,0:T(8,128)(2,1)S(1)}, u32[]{:S(2)}, u32[]{:S(2)}) collective-permute-start(bf16[256,1536]{1,0:T(8,128)(2,1)} %after.18), channel_id=1, source_target_pairs={{0,3},{1,0},{2,1},{3,2},{4,7},{5,4},{6,5},{7,6},{8,11},{9,8},{10,9... | collective-permute-start | bytes 2359304 | tf_op jit(solution)/shard_map/ppermute | solution.py:43
  87.6 38.8 %collective-permute-start.5 = (bf16[256,1536]{1,0:T(8,128)(2,1)}, bf16[256,1536]{1,0:T(8,128)(2,1)}, u32[]{:S(2)}, u32[]{:S(2)}) collective-permute-start(bf16[256,1536]{1,0:T(8,128)(2,1)} %after.18), channel_id=1, source_target_pairs={{0,1},{1,2},{2,3},{3,0},{4,5},{5,6},{6,7},{7,4},{8,9},{9,10},{10,1... | collective-permute-start | bytes 2359304 | tf_op jit(solution)/shard_map/ppermute | solution.py:43
  113.9 19.9 %copy-start.19 = (f32[4,256,256]{2,1,0:T(8,128)}, f32[4,256,256]{2,1,0:T(8,128)S(1)}, u32[]{:S(2)}) copy-start(f32[4,256,256]{2,1,0:T(8,128)S(1)} %get-tuple-element.73.dl_ref.refs_2_) | copy-start | bytes 3145732
  113.9 19.9 %copy-start.28 = (f32[4,256,256]{2,1,0:T(8,128)}, f32[4,256,256]{2,1,0:T(8,128)S(1)}, u32[]{:S(2)}) copy-start(f32[4,256,256]{2,1,0:T(8,128)S(1)} %get-tuple-element.72.rw_ref.refs_1_) | copy-start | bytes 3145732
  129.1 26.1 %all-to-all-start = ((f32[8,392,128]{2,1,0:T(8,128)}), f32[8,392,128]{2,1,0:T(8,128)}, u32[]{:S(2)}, u32[]{:S(2)}) async-start(f32[8,392,128]{2,1,0:T(8,128)} %pad_maximum_fusion.2), calls=%async_computation | async-start | bytes 3211264 | tf_op jit(solution)/shard_map/all_to_all | solution.py:250
  133.7 35.7 %collective-permute-start.6 = (bf16[256,1536]{1,0:T(8,128)(2,1)S(1)}, bf16[256,1536]{1,0:T(8,128)(2,1)}, u32[]{:S(2)}, u32[]{:S(2)}) collective-permute-start(bf16[256,1536]{1,0:T(8,128)(2,1)S(1)} %copy-done.45), channel_id=1, source_target_pairs={{0,2},{1,3},{2,0},{3,1},{4,6},{5,7},{6,4},{7,5},{8,10},{9,11},{10,... | collective-permute-start | bytes 2359304 | tf_op jit(solution)/shard_map/ppermute | solution.py:43
  169.5 24.9 %all-to-all-start.1 = ((f32[8,384,128]{2,1,0:T(8,128)}), f32[8,384,128]{2,1,0:T(8,128)S(1)}, u32[]{:S(2)}, u32[]{:S(2)}) async-start(f32[8,384,128]{2,1,0:T(8,128)} %after.20), calls=%async_computation.1 | async-start | bytes 3145728 | tf_op jit(solution)/shard_map/all_to_all | solution.py:250
  173.4 165.3 %all-gather.12.cloned.1.call-start = ((), (), s32[]{:S(2)}) async-start(), calls=%async_computation.14 | async-start | bytes 23887872 | tf_op jit(solution)/shard_map/all_gather | solution.py:79
  195.6 517.1 %reduce-scatter.4.cloned.1.call-start = ((), (), s32[]{:S(2)}) async-start(), calls=%async_computation.9 | async-start | bytes 23887872 | tf_op jit(solution)/shard_map/reduce_scatter | solution.py:83
  217.8 57.0 %collective-permute-start.9 = (bf16[256,1536]{1,0:T(8,128)(2,1)}, bf16[256,1536]{1,0:T(8,128)(2,1)S(1)}, u32[]{:S(2)}, u32[]{:S(2)}) collective-permute-start(bf16[256,1536]{1,0:T(8,128)(2,1)} %get-tuple-element.248), channel_id=1, source_target_pairs={{0,3},{1,0},{2,1},{3,2},{4,7},{5,4},{6,5},{7,6},{8,11},{9,8},{10,9... | collective-permute-start | bytes 2359304 | tf_op jit(solution)/shard_map/ppermute | solution.py:51
  220.6 64.0 %collective-permute-start.8 = (bf16[256,1536]{1,0:T(8,128)(2,1)}, bf16[256,1536]{1,0:T(8,128)(2,1)S(1)}, u32[]{:S(2)}, u32[]{:S(2)}) collective-permute-start(bf16[256,1536]{1,0:T(8,128)(2,1)} %get-tuple-element.249), channel_id=1, source_target_pairs={{0,2},{1,3},{2,0},{3,1},{4,6},{5,7},{6,4},{7,5},{8,10},{9,11},{10,... | collective-permute-start | bytes 2359304 | tf_op jit(solution)/shard_map/ppermute | solution.py:51
  220.6 65.0 %collective-permute-start.7 = (bf16[256,1536]{1,0:T(8,128)(2,1)}, bf16[256,1536]{1,0:T(8,128)(2,1)}, u32[]{:S(2)}, u32[]{:S(2)}) collective-permute-start(bf16[256,1536]{1,0:T(8,128)(2,1)} %get-tuple-element.247), channel_id=1, source_target_pairs={{0,1},{1,2},{2,3},{3,0},{4,5},{5,6},{6,7},{7,4},{8,9},{9,10},{10,1... | collective-permute-start | bytes 2359304 | tf_op jit(solution)/shard_map/ppermute | solution.py:51
  274.7 14.0 %copy-start.79 = (f32[4,256]{1,0:T(4,128)}, f32[4,256]{1,0:T(4,128)S(1)}, u32[]{:S(2)}) copy-start(f32[4,256]{1,0:T(4,128)S(1)} %psum.14) | copy-start | bytes 12292
  274.7 14.0 %copy-start.85 = (f32[4,256]{1,0:T(4,128)}, f32[4,256]{1,0:T(4,128)S(1)}, u32[]{:S(2)}) copy-start(f32[4,256]{1,0:T(4,128)S(1)} %add_rsqrt_fusion) | copy-start | bytes 12292
  274.9 24.7 %copy-start.91 = (f32[256]{0:T(256)}, f32[256]{0:T(256)S(1)}, u32[]{:S(2)}) copy-start(f32[256]{0:T(256)S(1)} %mul.235) | copy-start | bytes 3076
  288.7 175.3 %copy-start.38 = (f32[256,1536]{1,0:T(8,128)}, f32[256,1536]{1,0:T(8,128)S(1)}, u32[]{:S(2)}) copy-start(f32[256,1536]{1,0:T(8,128)S(1)} %get-tuple-element.240) | copy-start | bytes 4718596
  289.8 16.8 %collective-permute-start.10 = (bf16[128,1536]{1,0:T(8,128)(2,1)S(1)}, bf16[128,1536]{1,0:T(8,128)(2,1)S(1)}, u32[]{:S(2)}, u32[]{:S(2)}) collective-permute-start(bf16[128,1536]{1,0:T(8,128)(2,1)S(1)} %get-tuple-element.272), channel_id=1, source_target_pairs={{0,3},{1,0},{2,1},{3,2},{4,7},{5,4},{6,5},{7,6},{8,11},{9,8},{10,9... | collective-permute-start | bytes 1179656 | tf_op jit(solution)/shard_map/ppermute | solution.py:43
  297.0 31.3 %collective-permute-start.11 = (bf16[128,1536]{1,0:T(8,128)(2,1)S(1)}, bf16[128,1536]{1,0:T(8,128)(2,1)S(1)}, u32[]{:S(2)}, u32[]{:S(2)}) collective-permute-start(bf16[128,1536]{1,0:T(8,128)(2,1)S(1)} %get-tuple-element.272), channel_id=1, source_target_pairs={{0,2},{1,3},{2,0},{3,1},{4,6},{5,7},{6,4},{7,5},{8,10},{9,11},{10,... | collective-permute-start | bytes 1179656 | tf_op jit(solution)/shard_map/ppermute | solution.py:43
  297.0 31.3 %collective-permute-start.12 = (bf16[128,1536]{1,0:T(8,128)(2,1)S(1)}, bf16[128,1536]{1,0:T(8,128)(2,1)S(1)}, u32[]{:S(2)}, u32[]{:S(2)}) collective-permute-start(bf16[128,1536]{1,0:T(8,128)(2,1)S(1)} %get-tuple-element.272), channel_id=1, source_target_pairs={{0,1},{1,2},{2,3},{3,0},{4,5},{5,6},{6,7},{7,4},{8,9},{9,10},{10,1... | collective-permute-start | bytes 1179656 | tf_op jit(solution)/shard_map/ppermute | solution.py:43
  306.6 21.7 %copy-start.67 = (bf16[128,1536]{1,0:T(8,128)(2,1)}, bf16[128,1536]{1,0:T(8,128)(2,1)S(1)}, u32[]{:S(2)}) copy-start(bf16[128,1536]{1,0:T(8,128)(2,1)S(1)} %collective-permute-done.10.refs_1_) | copy-start | bytes 1179652
  329.8 53.6 %collective-permute-start.18 = (bf16[128,1536]{1,0:T(8,128)(2,1)}, bf16[128,1536]{1,0:T(8,128)(2,1)}, u32[]{:S(2)}, u32[]{:S(2)}) collective-permute-start(bf16[128,1536]{1,0:T(8,128)(2,1)} %after.22), channel_id=1, source_target_pairs={{0,1},{1,2},{2,3},{3,0},{4,5},{5,6},{6,7},{7,4},{8,9},{9,10},{10,1... | collective-permute-start | bytes 1179656 | tf_op jit(solution)/shard_map/ppermute | solution.py:43
  330.8 52.6 %collective-permute-start.17 = (bf16[128,1536]{1,0:T(8,128)(2,1)}, bf16[128,1536]{1,0:T(8,128)(2,1)}, u32[]{:S(2)}, u32[]{:S(2)}) collective-permute-start(bf16[128,1536]{1,0:T(8,128)(2,1)} %after.22), channel_id=1, source_target_pairs={{0,2},{1,3},{2,0},{3,1},{4,6},{5,7},{6,4},{7,5},{8,10},{9,11},{10,... | collective-permute-start | bytes 1179656 | tf_op jit(solution)/shard_map/ppermute | solution.py:43
  332.7 47.4 %collective-permute-start.16 = (bf16[128,1536]{1,0:T(8,128)(2,1)}, bf16[128,1536]{1,0:T(8,128)(2,1)}, u32[]{:S(2)}, u32[]{:S(2)}) collective-permute-start(bf16[128,1536]{1,0:T(8,128)(2,1)} %after.22), channel_id=1, source_target_pairs={{0,3},{1,0},{2,1},{3,2},{4,7},{5,4},{6,5},{7,6},{8,11},{9,8},{10,9... | collective-permute-start | bytes 1179656 | tf_op jit(solution)/shard_map/ppermute | solution.py:43
  379.5 45.1 %collective-permute-start.13 = (bf16[128,1536]{1,0:T(8,128)(2,1)}, bf16[128,1536]{1,0:T(8,128)(2,1)}, u32[]{:S(2)}, u32[]{:S(2)}) collective-permute-start(bf16[128,1536]{1,0:T(8,128)(2,1)} %get-tuple-element.261), channel_id=1, source_target_pairs={{0,1},{1,2},{2,3},{3,0},{4,5},{5,6},{6,7},{7,4},{8,9},{9,10},{10,1... | collective-permute-start | bytes 1179656 | tf_op jit(solution)/shard_map/ppermute | solution.py:51
  379.5 45.1 %collective-permute-start.14 = (bf16[128,1536]{1,0:T(8,128)(2,1)}, bf16[128,1536]{1,0:T(8,128)(2,1)}, u32[]{:S(2)}, u32[]{:S(2)}) collective-permute-start(bf16[128,1536]{1,0:T(8,128)(2,1)} %get-tuple-element.260), channel_id=1, source_target_pairs={{0,2},{1,3},{2,0},{3,1},{4,6},{5,7},{6,4},{7,5},{8,10},{9,11},{10,... | collective-permute-start | bytes 1179656 | tf_op jit(solution)/shard_map/ppermute | solution.py:51
  380.1 44.5 %collective-permute-start.15 = (bf16[128,1536]{1,0:T(8,128)(2,1)}, bf16[128,1536]{1,0:T(8,128)(2,1)}, u32[]{:S(2)}, u32[]{:S(2)}) collective-permute-start(bf16[128,1536]{1,0:T(8,128)(2,1)} %get-tuple-element.259), channel_id=1, source_target_pairs={{0,3},{1,0},{2,1},{3,2},{4,7},{5,4},{6,5},{7,6},{8,11},{9,8},{10,9... | collective-permute-start | bytes 1179656 | tf_op jit(solution)/shard_map/ppermute | solution.py:51
  425.9 10.2 %collective-permute-start.21 = (bf16[128,1536]{1,0:T(8,128)(2,1)S(1)}, bf16[128,1536]{1,0:T(8,128)(2,1)S(1)}, u32[]{:S(2)}, u32[]{:S(2)}) collective-permute-start(bf16[128,1536]{1,0:T(8,128)(2,1)S(1)} %get-tuple-element.257), channel_id=1, source_target_pairs={{0,3},{1,0},{2,1},{3,2},{4,7},{5,4},{6,5},{7,6},{8,11},{9,8},{10,9... | collective-permute-start | bytes 1179656 | tf_op jit(solution)/shard_map/ppermute | solution.py:51
  426.6 33.4 %collective-permute-start.20 = (bf16[128,1536]{1,0:T(8,128)(2,1)S(1)}, bf16[128,1536]{1,0:T(8,128)(2,1)S(1)}, u32[]{:S(2)}, u32[]{:S(2)}) collective-permute-start(bf16[128,1536]{1,0:T(8,128)(2,1)S(1)} %get-tuple-element.258), channel_id=1, source_target_pairs={{0,2},{1,3},{2,0},{3,1},{4,6},{5,7},{6,4},{7,5},{8,10},{9,11},{10,... | collective-permute-start | bytes 1179656 | tf_op jit(solution)/shard_map/ppermute | solution.py:51
  428.1 31.9 %collective-permute-start.19 = (bf16[128,1536]{1,0:T(8,128)(2,1)S(1)}, bf16[128,1536]{1,0:T(8,128)(2,1)S(1)}, u32[]{:S(2)}, u32[]{:S(2)}) collective-permute-start(bf16[128,1536]{1,0:T(8,128)(2,1)S(1)} %get-tuple-element.256), channel_id=1, source_target_pairs={{0,1},{1,2},{2,3},{3,0},{4,5},{5,6},{6,7},{7,4},{8,9},{9,10},{10,1... | collective-permute-start | bytes 1179656 | tf_op jit(solution)/shard_map/ppermute | solution.py:51
  466.0 39.5 %collective-permute-start.22 = (bf16[256,1536]{1,0:T(8,128)(2,1)S(1)}, bf16[256,1536]{1,0:T(8,128)(2,1)S(1)}, u32[]{:S(2)}, u32[]{:S(2)}) collective-permute-start(bf16[256,1536]{1,0:T(8,128)(2,1)S(1)} %get-tuple-element.238), channel_id=1, source_target_pairs={{0,3},{1,0},{2,1},{3,2},{4,7},{5,4},{6,5},{7,6},{8,11},{9,8},{10,9... | collective-permute-start | bytes 2359304 | tf_op jit(solution)/shard_map/ppermute | solution.py:43
  466.1 69.7 %collective-permute-start.23 = (bf16[256,1536]{1,0:T(8,128)(2,1)S(1)}, bf16[256,1536]{1,0:T(8,128)(2,1)S(1)}, u32[]{:S(2)}, u32[]{:S(2)}) collective-permute-start(bf16[256,1536]{1,0:T(8,128)(2,1)S(1)} %get-tuple-element.238), channel_id=1, source_target_pairs={{0,2},{1,3},{2,0},{3,1},{4,6},{5,7},{6,4},{7,5},{8,10},{9,11},{10,... | collective-permute-start | bytes 2359304 | tf_op jit(solution)/shard_map/ppermute | solution.py:43
  503.5 33.3 %collective-permute-start.24 = (bf16[256,1536]{1,0:T(8,128)(2,1)S(1)}, bf16[256,1536]{1,0:T(8,128)(2,1)S(1)}, u32[]{:S(2)}, u32[]{:S(2)}) collective-permute-start(bf16[256,1536]{1,0:T(8,128)(2,1)S(1)} %get-tuple-element.238), channel_id=1, source_target_pairs={{0,1},{1,2},{2,3},{3,0},{4,5},{5,6},{6,7},{7,4},{8,9},{9,10},{10,1... | collective-permute-start | bytes 2359304 | tf_op jit(solution)/shard_map/ppermute | solution.py:43
  538.6 18.1 %copy-start.80 = (f32[4,256]{1,0:T(4,128)S(1)}, f32[4,256]{1,0:T(4,128)}, u32[]{:S(2)}) copy-start(f32[4,256]{1,0:T(4,128)} %copy-done.79) | copy-start | bytes 12292
  538.6 25.1 %copy-start.30 = (f32[4,256,256]{2,1,0:T(8,128)S(1)}, f32[4,256,256]{2,1,0:T(8,128)}, u32[]{:S(2)}) copy-start(f32[4,256,256]{2,1,0:T(8,128)} %copy-done.28) | copy-start | bytes 3145732
  560.3 59.6 %collective-permute-start.28 = (bf16[128,1536]{1,0:T(8,128)(2,1)}, bf16[128,1536]{1,0:T(8,128)(2,1)}, u32[]{:S(2)}, u32[]{:S(2)}) collective-permute-start(bf16[128,1536]{1,0:T(8,128)(2,1)} %get-tuple-element.255), channel_id=1, source_target_pairs={{0,3},{1,0},{2,1},{3,2},{4,7},{5,4},{6,5},{7,6},{8,11},{9,8},{10,9... | collective-permute-start | bytes 1179656 | tf_op jit(solution)/shard_map/ppermute | solution.py:51
  562.4 92.8 %collective-permute-start.30 = (bf16[128,1536]{1,0:T(8,128)(2,1)}, bf16[128,1536]{1,0:T(8,128)(2,1)}, u32[]{:S(2)}, u32[]{:S(2)}) collective-permute-start(bf16[128,1536]{1,0:T(8,128)(2,1)} %get-tuple-element.254), channel_id=1, source_target_pairs={{0,2},{1,3},{2,0},{3,1},{4,6},{5,7},{6,4},{7,5},{8,10},{9,11},{10,... | collective-permute-start | bytes 1179656 | tf_op jit(solution)/shard_map/ppermute | solution.py:51
  563.7 57.8 %collective-permute-start.27 = (bf16[128,1536]{1,0:T(8,128)(2,1)}, bf16[128,1536]{1,0:T(8,128)(2,1)}, u32[]{:S(2)}, u32[]{:S(2)}) collective-permute-start(bf16[128,1536]{1,0:T(8,128)(2,1)} %get-tuple-element.253), channel_id=1, source_target_pairs={{0,1},{1,2},{2,3},{3,0},{4,5},{5,6},{6,7},{7,4},{8,9},{9,10},{10,1... | collective-permute-start | bytes 1179656 | tf_op jit(solution)/shard_map/ppermute | solution.py:51
  574.6 43.8 %all-to-all-start.2 = ((f32[8,384,128]{2,1,0:T(8,128)}), f32[8,384,128]{2,1,0:T(8,128)S(1)}, u32[]{:S(2)}, u32[]{:S(2)}) async-start(f32[8,384,128]{2,1,0:T(8,128)} %bitcast.302), calls=%async_computation.2 | async-start | bytes 3145728 | tf_op jit(solution)/shard_map/all_to_all | solution.py:250
  610.1 14.2 %collective-permute-start.25 = (bf16[128,1536]{1,0:T(8,128)(2,1)}, bf16[128,1536]{1,0:T(8,128)(2,1)}, u32[]{:S(2)}, u32[]{:S(2)}) collective-permute-start(bf16[128,1536]{1,0:T(8,128)(2,1)} %get-tuple-element.252), channel_id=1, source_target_pairs={{0,1},{1,2},{2,3},{3,0},{4,5},{5,6},{6,7},{7,4},{8,9},{9,10},{10,1... | collective-permute-start | bytes 1179656 | tf_op jit(solution)/shard_map/ppermute | solution.py:51
  612.2 19.8 %collective-permute-start.26 = (bf16[128,1536]{1,0:T(8,128)(2,1)}, bf16[128,1536]{1,0:T(8,128)(2,1)}, u32[]{:S(2)}, u32[]{:S(2)}) collective-permute-start(bf16[128,1536]{1,0:T(8,128)(2,1)} %get-tuple-element.251), channel_id=1, source_target_pairs={{0,3},{1,0},{2,1},{3,2},{4,7},{5,4},{6,5},{7,6},{8,11},{9,8},{10,9... | collective-permute-start | bytes 1179656 | tf_op jit(solution)/shard_map/ppermute | solution.py:51
  620.0 35.2 %collective-permute-start.29 = (bf16[128,1536]{1,0:T(8,128)(2,1)}, bf16[128,1536]{1,0:T(8,128)(2,1)}, u32[]{:S(2)}, u32[]{:S(2)}) collective-permute-start(bf16[128,1536]{1,0:T(8,128)(2,1)} %get-tuple-element.250), channel_id=1, source_target_pairs={{0,2},{1,3},{2,0},{3,1},{4,6},{5,7},{6,4},{7,5},{8,10},{9,11},{10,... | collective-permute-start | bytes 1179656 | tf_op jit(solution)/shard_map/ppermute | solution.py:51
  632.0 38.1 %all-to-all-start.3 = ((f32[8,384,128]{2,1,0:T(8,128)}), f32[8,384,128]{2,1,0:T(8,128)}, u32[]{:S(2)}, u32[]{:S(2)}) async-start(f32[8,384,128]{2,1,0:T(8,128)} %after.27), calls=%async_computation.3 | async-start | bytes 3145728 | tf_op jit(solution)/shard_map/all_to_all | solution.py:250
  636.6 133.1 %reduce-scatter.6.cloned.1.call-start = ((), (), s32[]{:S(2)}) async-start(), calls=%async_computation.10 | async-start | bytes 5308416 | tf_op jit(solution)/shard_map/reduce_scatter | solution.py:83
  698.3 3.1 collective-permute-start.31
  712.7 125.0 %reduce-scatter.8.cloned.1.call-start = ((), (), s32[]{:S(2)}) async-start(), calls=%async_computation.11 | async-start | bytes 3096576 | tf_op jit(solution)/shard_map/reduce_scatter | solution.py:83
  721.0 55.0 %collective-permute-start.33 = (bf16[256,1536]{1,0:T(8,128)(2,1)}, bf16[256,1536]{1,0:T(8,128)(2,1)}, u32[]{:S(2)}, u32[]{:S(2)}) collective-permute-start(bf16[256,1536]{1,0:T(8,128)(2,1)} %get-tuple-element.246), channel_id=1, source_target_pairs={{0,2},{1,3},{2,0},{3,1},{4,6},{5,7},{6,4},{7,5},{8,10},{9,11},{10,... | collective-permute-start | bytes 2359304 | tf_op jit(solution)/shard_map/ppermute | solution.py:51
  723.3 52.7 %collective-permute-start.32 = (bf16[256,1536]{1,0:T(8,128)(2,1)}, bf16[256,1536]{1,0:T(8,128)(2,1)}, u32[]{:S(2)}, u32[]{:S(2)}) collective-permute-start(bf16[256,1536]{1,0:T(8,128)(2,1)} %get-tuple-element.244), channel_id=1, source_target_pairs={{0,1},{1,2},{2,3},{3,0},{4,5},{5,6},{6,7},{7,4},{8,9},{9,10},{10,1... | collective-permute-start | bytes 2359304 | tf_op jit(solution)/shard_map/ppermute | solution.py:51
  776.0 24.8 %copy-start.34 = (bf16[1024,1536]{1,0:T(8,128)(2,1)S(1)}, bf16[1024,1536]{1,0:T(8,128)(2,1)}, u32[]{:S(2)}) copy-start(bf16[1024,1536]{1,0:T(8,128)(2,1)} %get-tuple-element.242.refs_1_.refs_2_) | copy-start | bytes 9437188
  776.0 24.8 %copy-start.75 = (f32[1536]{0:T(1024)S(1)}, f32[1536]{0:T(1024)}, u32[]{:S(2)}) copy-start(f32[1536]{0:T(1024)} %copy-done.74) | copy-start | bytes 18436
  776.0 37.3 %all-to-all-start.4 = ((f32[8,4,120,128]{3,2,1,0:T(8,128)}), f32[8,4,120,128]{3,2,1,0:T(8,128)}, u32[]{:S(2)}, u32[]{:S(2)}) async-start(f32[8,4,120,128]{3,2,1,0:T(8,128)} %after.32), calls=%async_computation.5 | async-start | bytes 3932160 | tf_op jit(solution)/shard_map/all_to_all | solution.py:1071
  780.7 20.1 %collective-permute-start.34 = (bf16[256,1536]{1,0:T(8,128)(2,1)}, bf16[256,1536]{1,0:T(8,128)(2,1)}, u32[]{:S(2)}, u32[]{:S(2)}) collective-permute-start(bf16[256,1536]{1,0:T(8,128)(2,1)} %get-tuple-element.245), channel_id=1, source_target_pairs={{0,3},{1,0},{2,1},{3,2},{4,7},{5,4},{6,5},{7,6},{8,11},{9,8},{10,9... | collective-permute-start | bytes 2359304 | tf_op jit(solution)/shard_map/ppermute | solution.py:51
  782.1 18.8 %copy-start.41 = (bf16[4,64,1536]{2,1,0:T(8,128)(2,1)S(1)}, bf16[4,64,1536]{2,1,0:T(8,128)(2,1)}, u32[]{:S(2)}) copy-start(bf16[4,64,1536]{2,1,0:T(8,128)(2,1)} %copy-done.40) | copy-start | bytes 2359300
  815.7 12.5 %all-to-all-start.5 = ((f32[4,120,128]{2,1,0:T(8,128)}), f32[4,120,128]{2,1,0:T(8,128)}, u32[]{:S(2)}, u32[]{:S(2)}) async-start(f32[4,120,128]{2,1,0:T(8,128)} %after.33), calls=%async_computation.6 | async-start | bytes 491520 | tf_op jit(solution)/shard_map/all_to_all | solution.py:1074
  (93 other events, 371.9 us)
Sparse Core Ops, SparseCore 0:
  11.5 36.6 all-gather.7
  50.1 40.5 all-gather.9
  195.7 107.1 all-gather.11
  537.9 170.5 reduce-scatter.3
  712.9 54.9 reduce-scatter.5
  771.4 53.3 reduce-scatter.7
